TPU v7x, 32 devices: a whole 2x2x4 slice. The times are simulated.
32 devices in a mesh: rep: 4 (over z), fsdp: 4 (over x, core), sp: 2 (over y).
Axes of the slice: x: 2, y: 2, z: 4, core: 2. Of those that a mesh axis runs over, the one named last changes fastest.
Arguments:
- latent_in: bfloat16 [16, 1024, 1152], P(('rep', 'fsdp'), 'sp'), may hold values from -6 to 6
- condition: bfloat16 [16, 1152], P(('rep', 'fsdp')), may hold values from -6 to 6
- valid_slots: int32 [16], P(('rep', 'fsdp')), may hold values 0 or 1
- ada_weight: bfloat16 [1152, 6912], P(('fsdp', 'sp')), may hold values from -0.1875 to 0.1875
- ada_bias: bfloat16 [6912], P(('fsdp', 'sp')), may hold values from -3 to 3
- qkv_weight: bfloat16 [1152, 3456], P(('fsdp', 'sp')), may hold values from -0.1875 to 0.1875
- qv_bias: bfloat16 [2304], P(('fsdp', 'sp')), may hold values from -3 to 3
- out_weight: bfloat16 [1152, 1152], P(('fsdp', 'sp')), may hold values from -2 to 2
- out_bias: bfloat16 [1152], P(('fsdp', 'sp')), may hold values from -3 to 3
- up_weight: bfloat16 [1152, 4608], P(('fsdp', 'sp')), may hold values from -0.1875 to 0.1875
- up_bias: bfloat16 [4608], P(('fsdp', 'sp')), may hold values from -3 to 3
- down_weight: bfloat16 [4608, 1152], P(('fsdp', 'sp')), may hold values from -0.09375 to 0.09375
- down_bias: bfloat16 [1152], P(('fsdp', 'sp')), may hold values from -3 to 3
- cotangent: bfloat16 [16, 1024, 1152], P(('rep', 'fsdp'), 'sp'), may hold values from -6 to 6
Outputs:
- block_out: bfloat16 [16, 1024, 1152], P(('rep', 'fsdp'), 'sp')
- latent_grad: float32 [16, 1024, 1152], P(('rep', 'fsdp'), 'sp')
- cond_grad: float32 [16, 1152], P(('rep', 'fsdp'))
- ada_wgrad: float32 [1152, 6912], P(('fsdp', 'sp'))
- ada_bgrad: float32 [6912], P(('fsdp', 'sp'))
- qkv_wgrad: float32 [1152, 3456], P(('fsdp', 'sp'))
- qv_bgrad: float32 [2304], P(('fsdp', 'sp'))
- out_wgrad: float32 [1152, 1152], P(('fsdp', 'sp'))
- out_bgrad: float32 [1152], P(('fsdp', 'sp'))
- up_wgrad: float32 [1152, 4608], P(('fsdp', 'sp'))
- up_bgrad: float32 [4608], P(('fsdp', 'sp'))
- down_wgrad: float32 [4608, 1152], P(('fsdp', 'sp'))
- down_bgrad: float32 [1152], P(('fsdp', 'sp'))
All inputs are finite; a program needn't handle non-finite values. No bound on the sum of `valid_slots` on one device may be relied on, other than what follows from the above.
Results may differ from a plain program's by a relative error of at most 0.013.
The roundings to bfloat16 on the way count: a program that leaves them out, or rounds other values in their place, can miss the bound.
Values may be sent and summed in bfloat16 or wider, within the bound.
No kernel may reach another device: no remote copies, remote signals or barrier semaphores. Data moves between devices by JAX's collectives and lax.ppermute only.
A program may use at most 256 MiB of HBM per device.

v0:
```python
import jax
import jax.numpy as jnp
from jax import lax
from jax.sharding import PartitionSpec as P

HEAD = 72


exact_mode = lax.Precision.HIGHEST
epsilon = 1e-06


def normalize(values):
    average = jnp.mean(values, -1, keepdims=True)
    centered = values - average
    inverse = lax.rsqrt(jnp.mean(centered * centered, -1, keepdims=True) + epsilon)
    return (centered * inverse, inverse)


def norm_back(upstream, normed, inverse):
    return (
        upstream
        - jnp.mean(upstream, -1, keepdims=True)
        - normed * jnp.mean(upstream * normed, -1, keepdims=True)
    ) * inverse


def matmul(left, right):
    return jnp.dot(left, right, preferred_element_type=jnp.float32)


def matmul_left(left, right):
    return lax.dot_general(
        left, right, (((0,), (0,)), ((), ())), preferred_element_type=jnp.float32
    )


def matmul_right(left, right):
    return lax.dot_general(
        left, right, (((1,), (1,)), ((), ())), preferred_element_type=jnp.float32
    )


def head_slice(values, group_index, group_width):
    number, length, model_width = values.shape
    piece = lax.dynamic_slice_in_dim(values, group_index * group_width, group_width, 2)
    return piece.reshape(number, length, 4, HEAD)


def join_groups(stacked):
    groups, number, length, group_width = stacked.shape
    return jnp.moveaxis(stacked, 0, 2).reshape(number, length, groups * group_width)


def attn_forward(query, keys, values, score_scale):
    group_width = 4 * HEAD
    groups = query.shape[2] // group_width

    def per_group(group_index):
        query_part = head_slice(query, group_index, group_width)
        keys_part = head_slice(keys, group_index, group_width)
        values_part = head_slice(values, group_index, group_width)
        scores = (
            jnp.einsum("lqhd,lkhd->lhqk", query_part, keys_part, preferred_element_type=jnp.float32)
            * score_scale
        )
        row_max = jnp.max(scores, -1, keepdims=True)
        weights = jnp.exp(scores - row_max)
        row_total = jnp.sum(weights, -1, keepdims=True)
        probs = (weights / row_total).astype(jnp.bfloat16)
        mixed = jnp.einsum(
            "lhqk,lkhd->lqhd", probs, values_part, preferred_element_type=jnp.float32
        )
        log_total = row_max[..., 0] + jnp.log(row_total[..., 0])
        return (mixed.reshape(mixed.shape[0], mixed.shape[1], group_width), log_total)

    mixed_all, log_totals = lax.map(per_group, jnp.arange(groups))
    return (join_groups(mixed_all), log_totals)


def attn_backward(query, keys, values, upstream, log_totals, score_scale):
    group_width = 4 * HEAD
    groups = query.shape[2] // group_width

    def per_group(group_item):
        group_index, log_total = group_item
        query_part = head_slice(query, group_index, group_width)
        keys_part = head_slice(keys, group_index, group_width)
        values_part = head_slice(values, group_index, group_width)
        upstream_part = head_slice(upstream, group_index, group_width)
        scores = (
            jnp.einsum("lqhd,lkhd->lhqk", query_part, keys_part, preferred_element_type=jnp.float32)
            * score_scale
        )
        probs = jnp.exp(scores - log_total[..., None])
        d_probs = jnp.einsum(
            "lqhd,lkhd->lhqk", upstream_part, values_part, preferred_element_type=jnp.float32
        )
        d_scores = (probs * (d_probs - jnp.sum(probs * d_probs, -1, keepdims=True))).astype(
            jnp.bfloat16
        )
        d_query = (
            jnp.einsum("lhqk,lkhd->lqhd", d_scores, keys_part, preferred_element_type=jnp.float32)
            * score_scale
        )
        d_keys = (
            jnp.einsum("lhqk,lqhd->lkhd", d_scores, query_part, preferred_element_type=jnp.float32)
            * score_scale
        )
        d_values = jnp.einsum(
            "lhqk,lqhd->lkhd",
            probs.astype(jnp.bfloat16),
            upstream_part,
            preferred_element_type=jnp.float32,
        )
        number = d_query.shape[0]
        return (
            d_query.reshape(number, d_query.shape[1], group_width),
            d_keys.reshape(number, d_keys.shape[1], group_width),
            d_values.reshape(number, d_values.shape[1], group_width),
        )

    d_query, d_keys, d_values = lax.map(per_group, (jnp.arange(groups), log_totals))
    return (join_groups(d_query), join_groups(d_keys), join_groups(d_values))


def per_device(
    latent_in,
    condition,
    valid_slots,
    ada_weight,
    ada_bias,
    qkv_weight,
    qv_bias,
    out_weight,
    out_bias,
    up_weight,
    up_bias,
    down_weight,
    down_bias,
    cotangent,
):
    number, length, model_width = latent_in.shape
    tokens = number * length
    score_scale = float(HEAD) ** (-0.5)
    attn_set = (
        lax.all_gather(ada_weight, ("fsdp", "sp"), axis=0, tiled=True),
        lax.all_gather(ada_bias, ("fsdp", "sp"), axis=0, tiled=True),
        lax.all_gather(qkv_weight, ("fsdp", "sp"), axis=0, tiled=True),
        lax.all_gather(qv_bias, ("fsdp", "sp"), axis=0, tiled=True),
        lax.all_gather(out_weight, ("fsdp", "sp"), axis=0, tiled=True),
        lax.all_gather(out_bias, ("fsdp", "sp"), axis=0, tiled=True),
    )
    full_ada, full_ada_bias, full_qkv, full_qv_bias, full_out, full_out_bias = attn_set
    latent = latent_in.astype(jnp.float32)
    cond_rows = condition.astype(jnp.float32)
    silu_cond = jax.nn.silu(cond_rows).astype(jnp.bfloat16)
    modulation = matmul(silu_cond, full_ada) + full_ada_bias.astype(jnp.float32)
    shift_one, scale_one, gate_one, shift_two, scale_two, gate_two = jnp.split(
        modulation[:, None, :], 6, axis=-1
    )
    normed_one, inverse_one = normalize(latent)
    hidden_one = (
        (normed_one * (1.0 + scale_one) + shift_one)
        .astype(jnp.bfloat16)
        .reshape(tokens, model_width)
    )
    qv_float = full_qv_bias.astype(jnp.float32)
    bias_full = jnp.concatenate(
        [qv_float[:model_width], jnp.zeros((model_width,), jnp.float32), qv_float[model_width:]]
    )
    projected = (
        (matmul(hidden_one, full_qkv) + bias_full)
        .astype(jnp.bfloat16)
        .reshape(number, length, 3 * model_width)
    )
    query = projected[..., :model_width]
    key_part = projected[..., model_width : 2 * model_width]
    value_part = projected[..., 2 * model_width :]
    keys, values = (
        lax.all_gather(key_part, "sp", axis=1, tiled=True),
        lax.all_gather(value_part, "sp", axis=1, tiled=True),
    )
    attended, log_totals = attn_forward(query, keys, values, score_scale)
    attended_low = attended.astype(jnp.bfloat16).reshape(tokens, model_width)
    branch_one = (matmul(attended_low, full_out) + full_out_bias.astype(jnp.float32)).reshape(
        number, length, model_width
    )
    middle = latent + gate_one * branch_one
    mlp_set = (
        lax.all_gather(up_weight, ("fsdp", "sp"), axis=0, tiled=True),
        lax.all_gather(up_bias, ("fsdp", "sp"), axis=0, tiled=True),
        lax.all_gather(down_weight, ("fsdp", "sp"), axis=0, tiled=True),
        lax.all_gather(down_bias, ("fsdp", "sp"), axis=0, tiled=True),
    )
    full_up, full_up_bias, full_down, full_down_bias = mlp_set
    normed_two, inverse_two = normalize(middle)
    hidden_two = (
        (normed_two * (1.0 + scale_two) + shift_two)
        .astype(jnp.bfloat16)
        .reshape(tokens, model_width)
    )
    preact = matmul(hidden_two, full_up) + full_up_bias.astype(jnp.float32)
    activated, gelu_pull = jax.vjp(lambda inner: jax.nn.gelu(inner, approximate=True), preact)
    activated_low = activated.astype(jnp.bfloat16)
    branch_two = (matmul(activated_low, full_down) + full_down_bias.astype(jnp.float32)).reshape(
        number, length, model_width
    )
    slot_mask = valid_slots.astype(jnp.float32)[:, None, None]
    block_out = (slot_mask * (middle + gate_two * branch_two)).astype(jnp.bfloat16)
    back_mlp = (
        lax.all_gather(up_weight, ("fsdp", "sp"), axis=0, tiled=True),
        lax.all_gather(up_bias, ("fsdp", "sp"), axis=0, tiled=True),
        lax.all_gather(down_weight, ("fsdp", "sp"), axis=0, tiled=True),
        lax.all_gather(down_bias, ("fsdp", "sp"), axis=0, tiled=True),
    )
    full_up, full_up_bias, full_down, full_down_bias = back_mlp
    d_out = cotangent.astype(jnp.float32) * slot_mask
    d_gate_two = jnp.sum(d_out * branch_two, axis=1)
    d_branch_two = (gate_two * d_out).astype(jnp.bfloat16).reshape(tokens, model_width)
    down_grad = matmul_left(activated_low, d_branch_two)
    down_bias_grad = jnp.sum(d_branch_two.astype(jnp.float32), axis=0)
    d_activated = matmul_right(d_branch_two, full_down)
    d_preact = gelu_pull(d_activated)[0].astype(jnp.bfloat16)
    up_grad = matmul_left(hidden_two, d_preact)
    up_bias_grad = jnp.sum(d_preact.astype(jnp.float32), axis=0)
    d_hidden_two = matmul_right(d_preact, full_up).reshape(number, length, model_width)
    d_shift_two = jnp.sum(d_hidden_two, axis=1)
    d_scale_two = jnp.sum(d_hidden_two * normed_two, axis=1)
    d_middle = d_out + norm_back(d_hidden_two * (1.0 + scale_two), normed_two, inverse_two)
    back_attn = (
        lax.all_gather(ada_weight, ("fsdp", "sp"), axis=0, tiled=True),
        lax.all_gather(ada_bias, ("fsdp", "sp"), axis=0, tiled=True),
        lax.all_gather(qkv_weight, ("fsdp", "sp"), axis=0, tiled=True),
        lax.all_gather(qv_bias, ("fsdp", "sp"), axis=0, tiled=True),
        lax.all_gather(out_weight, ("fsdp", "sp"), axis=0, tiled=True),
        lax.all_gather(out_bias, ("fsdp", "sp"), axis=0, tiled=True),
    )
    full_ada, full_ada_bias, full_qkv, full_qv_bias, full_out, full_out_bias = back_attn
    d_gate_one = jnp.sum(d_middle * branch_one, axis=1)
    d_branch_one = (gate_one * d_middle).astype(jnp.bfloat16).reshape(tokens, model_width)
    out_grad = matmul_left(attended_low, d_branch_one)
    out_bias_grad = jnp.sum(d_branch_one.astype(jnp.float32), axis=0)
    d_attended = (
        matmul_right(d_branch_one, full_out)
        .astype(jnp.bfloat16)
        .reshape(number, length, model_width)
    )
    d_query, d_keys_all, d_values_all = attn_backward(
        query, keys, values, d_attended, log_totals, score_scale
    )
    d_keys, d_values = (
        lax.psum_scatter(d_keys_all, "sp", scatter_dimension=1, tiled=True),
        lax.psum_scatter(d_values_all, "sp", scatter_dimension=1, tiled=True),
    )
    d_projected = (
        jnp.concatenate([d_query, d_keys, d_values], axis=-1)
        .astype(jnp.bfloat16)
        .reshape(tokens, 3 * model_width)
    )
    qkv_grad = matmul_left(hidden_one, d_projected)
    column_sums = jnp.sum(d_projected.astype(jnp.float32), axis=0)
    qv_bias_grad = jnp.concatenate([column_sums[:model_width], column_sums[2 * model_width :]])
    d_hidden_one = matmul_right(d_projected, full_qkv).reshape(number, length, model_width)
    d_shift_one = jnp.sum(d_hidden_one, axis=1)
    d_scale_one = jnp.sum(d_hidden_one * normed_one, axis=1)
    latent_grad = d_middle + norm_back(d_hidden_one * (1.0 + scale_one), normed_one, inverse_one)
    d_modulation = jnp.concatenate(
        [d_shift_one, d_scale_one, d_gate_one, d_shift_two, d_scale_two, d_gate_two], axis=-1
    )
    ada_grad = jnp.dot(silu_cond.astype(jnp.float32).T, d_modulation, precision=exact_mode)
    ada_bias_grad = jnp.sum(d_modulation, axis=0)
    d_silu = jnp.dot(d_modulation, full_ada.astype(jnp.float32).T, precision=exact_mode)
    silu_pull = jax.vjp(jax.nn.silu, cond_rows)[1]
    cond_part = silu_pull(d_silu)[0]
    cond_grad = lax.psum(cond_part, "sp")
    shards = (
        lax.psum_scatter(ada_grad, ("fsdp", "sp"), scatter_dimension=0, tiled=True),
        lax.psum_scatter(ada_bias_grad, ("fsdp", "sp"), scatter_dimension=0, tiled=True),
        lax.psum_scatter(qkv_grad, ("fsdp", "sp"), scatter_dimension=0, tiled=True),
        lax.psum_scatter(qv_bias_grad, ("fsdp", "sp"), scatter_dimension=0, tiled=True),
        lax.psum_scatter(out_grad, ("fsdp", "sp"), scatter_dimension=0, tiled=True),
        lax.psum_scatter(out_bias_grad, ("fsdp", "sp"), scatter_dimension=0, tiled=True),
        lax.psum_scatter(up_grad, ("fsdp", "sp"), scatter_dimension=0, tiled=True),
        lax.psum_scatter(up_bias_grad, ("fsdp", "sp"), scatter_dimension=0, tiled=True),
        lax.psum_scatter(down_grad, ("fsdp", "sp"), scatter_dimension=0, tiled=True),
        lax.psum_scatter(down_bias_grad, ("fsdp", "sp"), scatter_dimension=0, tiled=True),
    )
    totals = lax.psum(
        (
            shards[0],
            shards[1],
            shards[2],
            shards[3],
            shards[4],
            shards[5],
            shards[6],
            shards[7],
            shards[8],
            shards[9],
        ),
        "rep",
    )
    return (
        block_out,
        latent_grad,
        cond_grad,
        totals[0],
        totals[1],
        totals[2],
        totals[3],
        totals[4],
        totals[5],
        totals[6],
        totals[7],
        totals[8],
        totals[9],
    )


def solution(mesh):
    return jax.shard_map(
        per_device,
        mesh=mesh,
        in_specs=(
            P(("rep", "fsdp"), "sp", None),
            P(("rep", "fsdp"), None),
            P(("rep", "fsdp")),
            P(("fsdp", "sp"), None),
            P(("fsdp", "sp")),
            P(("fsdp", "sp"), None),
            P(("fsdp", "sp")),
            P(("fsdp", "sp"), None),
            P(("fsdp", "sp")),
            P(("fsdp", "sp"), None),
            P(("fsdp", "sp")),
            P(("fsdp", "sp"), None),
            P(("fsdp", "sp")),
            P(("rep", "fsdp"), "sp", None),
        ),
        out_specs=(
            P(("rep", "fsdp"), "sp", None),
            P(("rep", "fsdp"), "sp", None),
            P(("rep", "fsdp"), None),
            P(("fsdp", "sp"), None),
            P(("fsdp", "sp")),
            P(("fsdp", "sp"), None),
            P(("fsdp", "sp")),
            P(("fsdp", "sp"), None),
            P(("fsdp", "sp")),
            P(("fsdp", "sp"), None),
            P(("fsdp", "sp")),
            P(("fsdp", "sp"), None),
            P(("fsdp", "sp")),
        ),
        check_vma=False,
    )
```

profile of v0, /device:TPU:9, one launch (start us, length us, event | category | flops | bytes accessed | tf_op | source)
XLA Modules:
  0.0 1737.9 jit_solution(9683369832360070576)
XLA Ops:
  13.3 26.1 %all-reduce.13 = (bf16[2304]{0:T(1024)(128)(2,1)S(1)}, bf16[6912]{0:T(1024)(128)(2,1)S(1)}, bf16[1152]{0:T(1024)(128)(2,1)S(1)}, bf16[1152]{0:T(1024)(128)(2,1)S(1)}, bf16[4608]{0:T(1024)(128)(2,1)S(1)}) all-reduce(bf16[2304]{0:T(1024)(128)(2,1)S(1)} %dynamic-update-slice.1, ...), channel_id=1, replica_groups=mesh['rep'=4,'fsdp'=4,'sp'=2] {'fsdp','sp'}, use_global_device_ids=true, to_apply=%add.1 | all-reduce | flops 16128 | bytes 64512
  40.2 59.5 %all-gather.8.cloned.1.call-done = bf16[1152,6912]{1,0:T(8,128)(2,1)} async-done(((bf16[144,6912]{1,0:T(8,128)(2,1)}), bf16[1152,6912]{1,0:T(8,128)(2,1)}) %all-gather.8.cloned.1.call-update) | async-done | bytes 15925264 | tf_op jit(solution)/shard_map/all_gather | solution.py:147
  99.6 7.7 convolution_reduce_fusion
  108.0 46.1 %all-gather.10.cloned.1.call-done = bf16[1152,3456]{1,0:T(8,128)(2,1)} async-done(((bf16[144,3456]{1,0:T(8,128)(2,1)}), bf16[1152,3456]{1,0:T(8,128)(2,1)}) %all-gather.10.cloned.1.call-update) | async-done | bytes 7962640 | tf_op jit(solution)/shard_map/all_gather | solution.py:149
  154.1 8.7 fusion.16
  170.7 29.7 %all-gather.12.cloned.1.call-done = bf16[1,1024,1152]{2,1,0:T(8,128)(2,1)} async-done(((bf16[1,512,1152]{2,1,0:T(8,128)(2,1)}), bf16[1,1024,1152]{2,1,0:T(8,128)(2,1)}) %all-gather.12.cloned.1.call-update) | async-done | bytes 2359312 | tf_op jit(solution)/shard_map/all_gather | solution.py:182
  200.4 2.8 copy.34
  203.2 35.2 %all-gather.14.cloned.1.call-done = bf16[1,1024,1152]{2,1,0:T(8,128)(2,1)} async-done(((bf16[1,512,1152]{2,1,0:T(8,128)(2,1)}), bf16[1,1024,1152]{2,1,0:T(8,128)(2,1)}) %all-gather.14.cloned.1.call-update) | async-done | bytes 2359312 | tf_op jit(solution)/shard_map/all_gather | solution.py:181
  238.5 4.3 copy.36
  244.4 44.2 %while.26 = (s32[]{:T(128)}, bf16[4,1,512,288]{2,3,1,0:T(8,128)(2,1)}, f32[4,1,4,512]{3,2,1,0:T(4,128)}, s32[4]{0:T(128)}, bf16[1,1024,1152]{1,2,0:T(8,128)(2,1)...) while((s32[]{:T(128)}, ...), condition=%wide.region_5.6_spmd, body=%wide.region_2.5_spmd.sunk | while | flops 622852096 | bytes 30540976 | solution.py:77
  252.3 2.4 fusion.128
  263.3 2.4 fusion.128
  274.3 2.4 fusion.128
  285.4 2.4 fusion.128
  288.5 5.6 fusion.72
  296.5 40.0 %all-gather.18.cloned.1.call-done = bf16[1152,4608]{1,0:T(8,128)(2,1)} async-done(((bf16[144,4608]{1,0:T(8,128)(2,1)}), bf16[1152,4608]{1,0:T(8,128)(2,1)}) %all-gather.18.cloned.1.call-update) | async-done | bytes 10616848 | tf_op jit(solution)/shard_map/all_gather | solution.py:191
  336.5 12.4 fusion.66
  348.9 53.3 %all-gather.20.cloned.1.call-done = bf16[4608,1152]{1,0:T(8,128)(2,1)} async-done(((bf16[576,1152]{1,0:T(8,128)(2,1)}), bf16[4608,1152]{1,0:T(8,128)(2,1)}) %all-gather.20.cloned.1.call-update) | async-done | bytes 10616848 | tf_op jit(solution)/shard_map/all_gather | solution.py:193
  402.3 17.9 %convert_reduce_fusion = (f32[4608]{0:T(1024)}, bf16[512,4608]{1,0:T(8,128)(2,1)}) fusion(f32[512,4608]{1,0:T(8,128)} %fusion.66, f32[4608]{0:T(1024)} %convert_element_type.114, bf16[4608,1152]{1,0:T(8,128)(2,1)} %all-gather.20.cloned.1.call-done, bf16[1,512,1152]{2,1,0:T(8,128)(2,1)S(1)} %copy-done.11, f32[1152]{0:T(1024)S(1)} %copy-done.20, f32[]{:T(128)} %bitcast.23), kind=kOutput, calls=%fused_computation.39 | convolution fusion | flops 5492436480 | bytes 25993732 | tf_op jit(solution)/shard_map/dot_general | solution.py:39
  420.2 12.1 fusion.68
  432.3 14.8 fusion.32
  447.1 3.6 convert_reduce_fusion.4
  451.8 2.9 fusion.23
  457.4 67.7 %while.27 = (s32[]{:T(128)}, bf16[4,1,512,288]{2,3,1,0:T(8,128)(2,1)}, f32[4,1,1024,288]{2,3,1,0:T(8,128)}, f32[4,1,1024,288]{2,3,1,0:T(8,128)}, s32[4]{0:T(128)...) while((s32[]{:T(128)}, ...), condition=%wide.region_12.13_spmd, body=%wide.region_10.12_spmd.sunk | while | flops 1535703040 | bytes 77423824 | solution.py:123
  462.8 2.9 multiply_reduce_fusion.8
  479.7 2.9 multiply_reduce_fusion.8
  496.7 2.9 multiply_reduce_fusion.8
  513.6 2.9 multiply_reduce_fusion.8
  526.5 5.4 fusion.78
  533.7 12.5 fusion.64
  547.5 15.1 fusion.44
  562.7 22.2 %reduce-scatter.10.cloned.1.call-done = f32[1,512,1152]{1,2,0:T(8,128)} async-done(((f32[1,1024,1152]{1,2,0:T(8,128)}), f32[1,512,1152]{1,2,0:T(8,128)}) %reduce-scatter.10.cloned.1.call-update) | async-done | bytes 2359312 | tf_op jit(solution)/shard_map/reduce_scatter | solution.py:254
  586.7 60.6 %reduce-scatter.8.cloned.1.call-done = f32[1,512,1152]{1,2,0:T(8,128)} async-done(((f32[1,1024,1152]{1,2,0:T(8,128)}), f32[1,512,1152]{1,2,0:T(8,128)}) %reduce-scatter.8.cloned.1.call-update) | async-done | bytes 2359312 | tf_op jit(solution)/shard_map/reduce_scatter | solution.py:253
  649.2 13.3 fusion.60
  663.8 9.7 fusion.30
  675.8 2.4 fusion.34
  681.4 11.5 broadcast_multiply_fusion
  693.0 14.5 reduce-scatter.16.cloned.1.call-done
  707.5 141.2 %reduce-scatter.18.cloned.1.call-done = f32[144,4608]{1,0:T(8,128)} async-done(((f32[1152,4608]{1,0:T(8,128)}), f32[144,4608]{1,0:T(8,128)}) %reduce-scatter.18.cloned.1.call-update) | async-done | bytes 2654224 | tf_op jit(solution)/shard_map/reduce_scatter | solution.py:284
  848.7 141.1 %reduce-scatter.20.cloned.1.call-done = f32[576,1152]{1,0:T(8,128)} async-done(((f32[4608,1152]{1,0:T(8,128)}), f32[576,1152]{1,0:T(8,128)}) %reduce-scatter.20.cloned.1.call-update) | async-done | bytes 2654224 | tf_op jit(solution)/shard_map/reduce_scatter | solution.py:286
  989.8 117.0 %reduce-scatter.14.cloned.1.call-done = f32[144,3456]{1,0:T(8,128)} async-done(((f32[1152,3456]{1,0:T(8,128)}), f32[144,3456]{1,0:T(8,128)}) %reduce-scatter.14.cloned.1.call-update) | async-done | bytes 1990672 | tf_op jit(solution)/shard_map/reduce_scatter | solution.py:280
  1106.8 202.1 %reduce-scatter.12.cloned.1.call-done = f32[144,6912]{1,0:T(8,128)} async-done(((f32[1152,6912]{1,0:T(8,128)}), f32[144,6912]{1,0:T(8,128)}) %reduce-scatter.12.cloned.1.call-update) | async-done | bytes 3981328 | tf_op jit(solution)/shard_map/reduce_scatter | solution.py:278
  1313.7 25.9 %all-reduce.10 = (f32[6912]{0:T(1024)S(1)}, f32[2304]{0:T(1024)S(1)}, f32[1152]{0:T(1024)S(1)}, f32[4608]{0:T(1024)S(1)}, f32[1152]{0:T(1024)S(1)}) all-reduce(f32[6912]{0:T(1024)S(1)} %reduce.32, f32[2304]{0:T(1024)S(1)} %pad_maximum_fusion.2, ...), channel_id=5, replica_groups=mesh['rep'=4,'fsdp'=4,'sp'=2] {'fsdp','sp'}, use_global_device_ids=true, to_apply=%region_26.27.clone | all-reduce | flops 16128 | bytes 129024
  1340.0 18.7 %all-reduce.11 = (f32[864]{0:T(1024)}, f32[288]{0:T(512)}, f32[144]{0:T(256)}, f32[576]{0:T(1024)}, f32[144]{0:T(256)}) all-reduce(f32[864]{0:T(1024)S(1)} %dynamic-slice.6, f32[288]{0:T(512)S(1)} %dynamic-slice.8, f32[144]{0:T(256)S(1)} %dynamic-slice.10, ...), channel_id=1, replica_groups=mesh['rep'=4,'fsdp'=4,'sp'=2] {'rep'}, use_global_device_ids=true, to_apply=%region_27.28 | all-reduce | flops 2016 | bytes 16128 | tf_op jit(solution)/shard_map/psum | solution.py:289
  1358.7 16.0 fusion.53
  1374.8 4.9 psum.77
  1379.6 339.7 %all-reduce.16.cloned.1.call-done = (f32[144,6912]{1,0:T(8,128)}, f32[144,3456]{1,0:T(8,128)}, f32[144,1152]{1,0:T(8,128)}, f32[144,4608]{1,0:T(8,128)}, f32[576,1152]{1,0:T(8,128)}) async-done(((f32[144,6912]{1,0:T(8,128)}, f32[144,3456]{1,0:T(8,128)}, f32[144,1152]{1,0:T(8,128)}, f32[144,4608]{1,0:T(8,128)}, f32[576,1152]{1,0:T(8,128)}), (f32[144,6912]{1,0:T(8,128)}, f32[144,3456]{1,0:T(8,128)}, ...) | async-done | bytes 11943952 | tf_op jit(solution)/shard_map/psum | solution.py:289
  1719.3 4.5 copy.83
  (279 shorter events, 130.1 us)
Async XLA Ops:
  7.2 4.8 copy-start.50
  7.2 5.1 copy-start.51
  7.2 5.3 copy-start.47
  7.2 5.5 copy-start.48
  7.2 5.8 copy-start.49
  7.2 32.2 %copy-start.3 = (bf16[1,512,1152]{2,1,0:T(8,128)(2,1)S(1)}, bf16[1,512,1152]{2,1,0:T(8,128)(2,1)}, u32[]{:S(2)}) copy-start(bf16[1,512,1152]{2,1,0:T(8,128)(2,1)} %param.18) | copy-start | bytes 3538948
  7.3 92.4 %copy-start.18 = (bf16[1,1152]{1,0:T(2,128)(2,1)S(1)}, bf16[1,1152]{1,0:T(2,128)(2,1)}, u32[]{:S(2)}) copy-start(bf16[1,1152]{1,0:T(2,128)(2,1)} %param.19) | copy-start | bytes 6916
  7.3 92.3 %all-gather.8.cloned.1.call-start = ((), (), s32[]{:S(2)}) async-start(), calls=%async_computation.7 | async-start | bytes 17915904 | tf_op jit(solution)/shard_map/all_gather | solution.py:147
  8.0 146.1 %all-gather.10.cloned.1.call-start = ((), (), s32[]{:S(2)}) async-start(), calls=%async_computation.8 | async-start | bytes 8957952 | tf_op jit(solution)/shard_map/all_gather | solution.py:149
  8.8 191.7 %all-gather.12.cloned.1.call-start = ((), (), s32[]{:S(2)}) async-start(), calls=%async_computation.9 | async-start | bytes 3538944 | tf_op jit(solution)/shard_map/all_gather | solution.py:182
  39.7 114.5 %copy-start.28 = (f32[512]{0:T(512)}, f32[512]{0:T(512)S(1)}, u32[]{:S(2)}) copy-start(f32[512]{0:T(512)S(1)} %broadcast_multiply_fusion.6) | copy-start | bytes 6148
  40.1 114.0 %copy-start.34 = (f32[512]{0:T(512)}, f32[512]{0:T(512)S(1)}, u32[]{:S(2)}) copy-start(f32[512]{0:T(512)S(1)} %add_rsqrt_fusion.1) | copy-start | bytes 6148
  108.0 46.1 %copy-start.16 = (f32[1152]{0:T(1024)}, f32[1152]{0:T(1024)S(1)}, u32[]{:S(2)}) copy-start(f32[1152]{0:T(1024)S(1)} %get-tuple-element.156) | copy-start | bytes 13828
  108.0 46.1 %copy-start.39 = (f32[1152]{0:T(1024)}, f32[1152]{0:T(1024)S(1)}, u32[]{:S(2)}) copy-start(f32[1152]{0:T(1024)S(1)} %get-tuple-element.155) | copy-start | bytes 13828
  164.6 73.9 %all-gather.14.cloned.1.call-start = ((), (), s32[]{:S(2)}) async-start(), calls=%async_computation.10 | async-start | bytes 3538944 | tf_op jit(solution)/shard_map/all_gather | solution.py:181
  165.2 123.4 %all-gather.16.cloned.1.call-start = ((), (), s32[]{:S(2)}) async-start(), calls=%async_computation.11 | async-start | bytes 2985984 | tf_op jit(solution)/shard_map/all_gather | solution.py:151
  165.8 170.8 %all-gather.18.cloned.1.call-start = ((), (), s32[]{:S(2)}) async-start(), calls=%async_computation.12 | async-start | bytes 11943936 | tf_op jit(solution)/shard_map/all_gather | solution.py:191
  166.3 235.9 %all-gather.20.cloned.1.call-start = ((), (), s32[]{:S(2)}) async-start(), calls=%async_computation.13 | async-start | bytes 11943936 | tf_op jit(solution)/shard_map/all_gather | solution.py:193
  167.1 417.8 %reduce-scatter.10.cloned.1.call-start = ((), (), s32[]{:S(2)}) async-start(), calls=%async_computation.15 | async-start | bytes 7077888 | tf_op jit(solution)/shard_map/reduce_scatter | solution.py:254
  336.5 65.7 %copy-start.11 = (bf16[1,512,1152]{2,1,0:T(8,128)(2,1)S(1)}, bf16[1,512,1152]{2,1,0:T(8,128)(2,1)}, u32[]{:S(2)}) copy-start(bf16[1,512,1152]{2,1,0:T(8,128)(2,1)} %param.31) | copy-start | bytes 3538948
  336.5 65.7 %copy-start.20 = (f32[1152]{0:T(1024)S(1)}, f32[1152]{0:T(1024)}, u32[]{:S(2)}) copy-start(f32[1152]{0:T(1024)} %get-tuple-element.152) | copy-start | bytes 13828
  402.3 17.9 %copy-start.21 = (f32[1152]{0:T(1024)S(1)}, f32[1152]{0:T(1024)}, u32[]{:S(2)}) copy-start(f32[1152]{0:T(1024)} %get-tuple-element.154) | copy-start | bytes 13828
  420.1 12.2 copy-start.1
  420.1 12.2 copy-start.25
  420.1 12.2 copy-start.32
  420.2 12.1 copy-start.37
  420.2 12.1 copy-start.42
  447.1 4.7 copy-start.9
  525.2 122.2 %reduce-scatter.8.cloned.1.call-start = ((), (), s32[]{:S(2)}) async-start(), calls=%async_computation.14 | async-start | bytes 7077888 | tf_op jit(solution)/shard_map/reduce_scatter | solution.py:253
  525.9 181.6 %reduce-scatter.16.cloned.1.call-start = ((), (), s32[]{:S(2)}) async-start(), calls=%async_computation.18 | async-start | bytes 5971968 | tf_op jit(solution)/shard_map/reduce_scatter | solution.py:282
  531.9 316.9 %reduce-scatter.18.cloned.1.call-start = ((), (), s32[]{:S(2)}) async-start(), calls=%async_computation.19 | async-start | bytes 23887872 | tf_op jit(solution)/shard_map/reduce_scatter | solution.py:284
  546.2 443.7 %reduce-scatter.20.cloned.1.call-start = ((), (), s32[]{:S(2)}) async-start(), calls=%async_computation.20 | async-start | bytes 23887872 | tf_op jit(solution)/shard_map/reduce_scatter | solution.py:286
  562.6 544.1 %reduce-scatter.14.cloned.1.call-start = ((), (), s32[]{:S(2)}) async-start(), calls=%async_computation.17 | async-start | bytes 17915904 | tf_op jit(solution)/shard_map/reduce_scatter | solution.py:280
  586.7 62.5 %copy-start.4 = (bf16[1,512,1152]{2,1,0:T(8,128)(2,1)S(1)}, bf16[1,512,1152]{2,1,0:T(8,128)(2,1)}, u32[]{:S(2)}) copy-start(bf16[1,512,1152]{2,1,0:T(8,128)(2,1)} %param.18) | copy-start | bytes 3538948
  586.7 62.5 %copy-start.17 = (f32[1152]{0:T(1024)S(1)}, f32[1152]{0:T(1024)}, u32[]{:S(2)}) copy-start(f32[1152]{0:T(1024)} %copy-done.16) | copy-start | bytes 13828
  586.7 62.5 %copy-start.29 = (f32[512]{0:T(512)S(1)}, f32[512]{0:T(512)}, u32[]{:S(2)}) copy-start(f32[512]{0:T(512)} %copy-done.28) | copy-start | bytes 6148
  586.7 62.5 %copy-start.35 = (f32[512]{0:T(512)S(1)}, f32[512]{0:T(512)}, u32[]{:S(2)}) copy-start(f32[512]{0:T(512)} %copy-done.34) | copy-start | bytes 6148
  662.5 646.4 %reduce-scatter.12.cloned.1.call-start = ((), (), s32[]{:S(2)}) async-start(), calls=%async_computation.16 | async-start | bytes 35831808 | tf_op jit(solution)/shard_map/reduce_scatter | solution.py:278
  663.8 11.2 copy-start.6
  675.8 3.0 copy-start.44
  675.8 3.6 copy-start.45
  675.8 4.2 copy-start.43
  692.9 1026.4 %all-reduce.16.cloned.1.call-start = ((), (), s32[]{:S(2)}) async-start(), calls=%async_computation.21 | async-start | bytes 23887872 | tf_op jit(solution)/shard_map/psum | solution.py:289
  1308.9 4.8 copy-start.23
  1308.9 4.8 copy-start.24
  1308.9 4.8 copy-start.27
  1719.3 4.5 copy-start.10
  1723.8 2.9 copy-start.8
  (19 other events, 32.7 us)
Sparse Core Ops, SparseCore 0:
  10.0 89.5 all-gather.7
  101.5 52.5 all-gather.9
  164.7 35.6 all-gather.11
  202.4 36.0 all-gather.13
  240.2 30.6 all-gather.15
  272.7 63.8 all-gather.17
  338.4 63.7 all-gather.19
  525.3 59.5 reduce-scatter.9
  587.3 59.9 reduce-scatter.7
  650.6 56.9 reduce-scatter.15
  711.6 137.1 reduce-scatter.17
  852.6 137.1 reduce-scatter.19
  993.9 112.8 reduce-scatter.13
  1110.3 198.5 reduce-scatter.11
  1312.1 407.1 all-reduce.15
where the time goes:
time: 1750 us; the launch traced here: 1740 us
  waiting for transfers between devices  1310 us (75%)
  matrix products  202 us (12%)
  local copies, waits for them, and re-layouts  79.5 us (5%)
  blocking collectives  75.6 us (4%)
  other arithmetic  46.7 us (3%)
  between operations  20.8 us (1%)
    psum x1, waiting for transfers between devices, per_device(): lax.psum((shards[0], shards[1], shards[2], shards[3], shards[4], shards[5...  340 us
    reduce_scatter x1, waiting for transfers between devices, per_device(): lax.psum_scatter(ada_grad, ('fsdp', 'sp'), scatter_dimension=0, tiled=True)  202 us
    reduce_scatter x1, waiting for transfers between devices, per_device(): lax.psum_scatter(up_grad, ('fsdp', 'sp'), scatter_dimension=0, tiled=True)  141 us
    reduce_scatter x1, waiting for transfers between devices, per_device(): lax.psum_scatter(down_grad, ('fsdp', 'sp'), scatter_dimension=0, tiled=True)  141 us
    reduce_scatter x1, waiting for transfers between devices, per_device(): lax.psum_scatter(qkv_grad, ('fsdp', 'sp'), scatter_dimension=0, tiled=True)  117 us
    reduce_scatter x1, waiting for transfers between devices, per_device(): lax.psum_scatter(d_keys_all, 'sp', scatter_dimension=1, tiled=True)  60.6 us
    all_gather x1, waiting for transfers between devices, per_device(): lax.all_gather(ada_weight, ('fsdp', 'sp'), axis=0, tiled=True)  59.5 us
    all_gather x1, waiting for transfers between devices, per_device(): lax.all_gather(down_weight, ('fsdp', 'sp'), axis=0, tiled=True)  53.3 us
  transfers between devices with their start and end apart: 15, of which 14 were waited for; matrix products, arithmetic and copies ran while one was open for 10% of the time, Pallas kernels for 0%

commit v1 on v0

v1 whole, which is shorter than its diff:
```python
import jax
import jax.numpy as jnp
from jax import lax
from jax.sharding import PartitionSpec as P

HEAD = 72
GROUP = ("fsdp", "sp")
SHARDS = 8

exact_mode = lax.Precision.HIGHEST
epsilon = 1e-06


def normalize(values):
    average = jnp.mean(values, -1, keepdims=True)
    centered = values - average
    inverse = lax.rsqrt(jnp.mean(centered * centered, -1, keepdims=True) + epsilon)
    return (centered * inverse, inverse)


def norm_back(upstream, normed, inverse):
    return (
        upstream
        - jnp.mean(upstream, -1, keepdims=True)
        - normed * jnp.mean(upstream * normed, -1, keepdims=True)
    ) * inverse


def matmul(left, right):
    return jnp.dot(left, right, preferred_element_type=jnp.float32)


def matmul_left(left, right):
    return lax.dot_general(
        left, right, (((0,), (0,)), ((), ())), preferred_element_type=jnp.float32
    )


def matmul_right(left, right):
    return lax.dot_general(
        left, right, (((1,), (1,)), ((), ())), preferred_element_type=jnp.float32
    )


def place_of():
    return lax.axis_index("fsdp") * 2 + lax.axis_index("sp")


def pairs_by(rule):
    return [(place, rule(place)) for place in range(SHARDS)]


def swap_rule(place):
    return (place & 4) | ((place & 1) << 1) | ((place >> 1) & 1)


def core_rule(place):
    return place ^ 2


def first_rule(place):
    return place ^ (1 if place & 2 else 4)


def second_rule(place):
    return place ^ (4 if place & 2 else 1)


def permute(values, rule):
    return lax.ppermute(values, GROUP, pairs_by(rule))


def reduce_scatter(partial):
    low = partial.dtype
    place = place_of()
    core = (place >> 1) & 1
    _, rows, columns = partial.shape
    spread = partial.reshape(2, 2, 2, rows, columns)

    def core_half(which):
        return lax.dynamic_index_in_dim(spread, which, 1, keepdims=False)

    received = permute(core_half(1 - core), core_rule)
    kept = (core_half(core).astype(jnp.float32) + received.astype(jnp.float32)).astype(low)
    kept = kept.reshape(4, rows, columns)
    mine = ((place >> 2) << 1) | (place & 1)
    near = jnp.where(core == 0, 2, 1)
    far = 3 - near

    def block(which):
        return lax.dynamic_slice_in_dim(kept, which, 1, 0)

    received = permute(jnp.concatenate([block(mine ^ near), block(mine ^ 3)]), first_rule)
    halved = jnp.concatenate([block(mine), block(mine ^ far)]).astype(jnp.float32)
    halved = halved + received.astype(jnp.float32)
    received = permute(halved[1].astype(low), second_rule)
    return halved[0] + received.astype(jnp.float32)


def head_slice(values, group_index, group_width):
    number, length, model_width = values.shape
    piece = lax.dynamic_slice_in_dim(values, group_index * group_width, group_width, 2)
    return piece.reshape(number, length, 4, HEAD)


def join_groups(stacked):
    groups, number, length, group_width = stacked.shape
    return jnp.moveaxis(stacked, 0, 2).reshape(number, length, groups * group_width)


def attn_forward(query, keys, values, score_scale):
    group_width = 4 * HEAD
    groups = query.shape[2] // group_width

    def per_group(group_index):
        query_part = head_slice(query, group_index, group_width)
        keys_part = head_slice(keys, group_index, group_width)
        values_part = head_slice(values, group_index, group_width)
        scores = (
            jnp.einsum("lqhd,lkhd->lhqk", query_part, keys_part, preferred_element_type=jnp.float32)
            * score_scale
        )
        row_max = jnp.max(scores, -1, keepdims=True)
        weights = jnp.exp(scores - row_max)
        row_total = jnp.sum(weights, -1, keepdims=True)
        probs = (weights / row_total).astype(jnp.bfloat16)
        mixed = jnp.einsum(
            "lhqk,lkhd->lqhd", probs, values_part, preferred_element_type=jnp.float32
        )
        log_total = row_max[..., 0] + jnp.log(row_total[..., 0])
        return (mixed.reshape(mixed.shape[0], mixed.shape[1], group_width), log_total)

    mixed_all, log_totals = lax.map(per_group, jnp.arange(groups))
    return (join_groups(mixed_all), log_totals)


def attn_backward(query, keys, values, upstream, log_totals, score_scale):
    group_width = 4 * HEAD
    groups = query.shape[2] // group_width

    def per_group(group_item):
        group_index, log_total = group_item
        query_part = head_slice(query, group_index, group_width)
        keys_part = head_slice(keys, group_index, group_width)
        values_part = head_slice(values, group_index, group_width)
        upstream_part = head_slice(upstream, group_index, group_width)
        scores = (
            jnp.einsum("lqhd,lkhd->lhqk", query_part, keys_part, preferred_element_type=jnp.float32)
            * score_scale
        )
        probs = jnp.exp(scores - log_total[..., None])
        d_probs = jnp.einsum(
            "lqhd,lkhd->lhqk", upstream_part, values_part, preferred_element_type=jnp.float32
        )
        d_scores = (probs * (d_probs - jnp.sum(probs * d_probs, -1, keepdims=True))).astype(
            jnp.bfloat16
        )
        d_query = (
            jnp.einsum("lhqk,lkhd->lqhd", d_scores, keys_part, preferred_element_type=jnp.float32)
            * score_scale
        )
        d_keys = (
            jnp.einsum("lhqk,lqhd->lkhd", d_scores, query_part, preferred_element_type=jnp.float32)
            * score_scale
        )
        d_values = jnp.einsum(
            "lhqk,lqhd->lkhd",
            probs.astype(jnp.bfloat16),
            upstream_part,
            preferred_element_type=jnp.float32,
        )
        number = d_query.shape[0]
        return (
            d_query.reshape(number, d_query.shape[1], group_width),
            d_keys.reshape(number, d_keys.shape[1], group_width),
            d_values.reshape(number, d_values.shape[1], group_width),
        )

    d_query, d_keys, d_values = lax.map(per_group, (jnp.arange(groups), log_totals))
    return (join_groups(d_query), join_groups(d_keys), join_groups(d_values))


def per_device(
    latent_in,
    condition,
    valid_slots,
    ada_weight,
    ada_bias,
    qkv_weight,
    qv_bias,
    out_weight,
    out_bias,
    up_weight,
    up_bias,
    down_weight,
    down_bias,
    cotangent,
):
    number, length, width = latent_in.shape
    hidden_width = up_weight.shape[1]
    score_scale = float(HEAD) ** (-0.5)
    place = place_of()
    fsdp_index = lax.axis_index("fsdp")
    held = (place >> 2) * 2 + (place & 1)
    rows = width // SHARDS

    small = jnp.concatenate(
        [
            condition[0],
            qv_bias,
            out_bias,
            up_bias,
            down_bias,
            jnp.broadcast_to(valid_slots.astype(jnp.bfloat16), (128,)),
        ]
    )
    small_all = lax.all_gather(small, GROUP, axis=0)
    full_qkv = lax.all_gather(qkv_weight, GROUP, axis=0, tiled=True)
    latent_low = permute(latent_in, swap_rule)
    cotangent_low = permute(cotangent, swap_rule)
    full_out = lax.all_gather(out_weight, GROUP, axis=0, tiled=True)
    full_up = lax.all_gather(up_weight, GROUP, axis=0, tiled=True)
    full_down = lax.all_gather(down_weight, GROUP, axis=0, tiled=True)

    bounds = [0, width]
    for bias in (qv_bias, out_bias, up_bias, down_bias):
        bounds.append(bounds[-1] + bias.shape[0])
    cond_group = small_all[::2, :width].astype(jnp.float32)
    full_qv_bias, full_out_bias, full_up_bias, full_down_bias = (
        small_all[:, low:high].reshape(-1).astype(jnp.float32)
        for low, high in zip(bounds[1:-1], bounds[2:])
    )
    valid_group = small_all[::2, bounds[-1]].astype(jnp.float32)
    slot_mask = lax.dynamic_slice_in_dim(valid_group, held, 1)[:, None, None]

    silu_group = jax.nn.silu(cond_group).astype(jnp.bfloat16)
    silu_mine = lax.dynamic_slice_in_dim(silu_group, place * rows, rows, 1)
    ada_bias_row = lax.dynamic_update_slice_in_dim(
        jnp.zeros((ada_weight.shape[1],), jnp.float32),
        ada_bias.astype(jnp.float32),
        place * ada_bias.shape[0],
        0,
    )
    modulation_all = lax.psum(matmul(silu_mine, ada_weight) + ada_bias_row, GROUP)
    modulation = lax.dynamic_slice_in_dim(modulation_all, held, 1, 0)
    shift_one, scale_one, gate_one, shift_two, scale_two, gate_two = jnp.split(
        modulation, 6, axis=-1
    )

    latent = latent_low[0].astype(jnp.float32)
    normed_one, inverse_one = normalize(latent)
    hidden_one = (normed_one * (1.0 + scale_one) + shift_one).astype(jnp.bfloat16)
    bias_full = jnp.concatenate(
        [full_qv_bias[:width], jnp.zeros((width,), jnp.float32), full_qv_bias[width:]]
    )
    projected = (matmul(hidden_one, full_qkv) + bias_full).astype(jnp.bfloat16)
    query = projected[:, :width]
    pair_own = projected[:, width:]
    pair_other = permute(pair_own, core_rule)
    pair_all = jnp.concatenate([pair_own, pair_other], axis=0)[None]
    keys = pair_all[..., :width]
    values = pair_all[..., width:]
    attended, log_totals = attn_forward(query[None], keys, values, score_scale)
    attended_low = attended[0].astype(jnp.bfloat16)
    branch_one = matmul(attended_low, full_out) + full_out_bias
    middle = latent + gate_one * branch_one

    normed_two, inverse_two = normalize(middle)
    hidden_two = (normed_two * (1.0 + scale_two) + shift_two).astype(jnp.bfloat16)
    preact = matmul(hidden_two, full_up) + full_up_bias
    activated, gelu_pull = jax.vjp(lambda inner: jax.nn.gelu(inner, approximate=True), preact)
    activated_low = activated.astype(jnp.bfloat16)
    branch_two = matmul(activated_low, full_down) + full_down_bias
    mask_row = slot_mask[0]
    block_out = (mask_row * (middle + gate_two * branch_two)).astype(jnp.bfloat16)
    block_out = permute(block_out[None], swap_rule)

    d_out = cotangent_low[0].astype(jnp.float32) * mask_row
    d_gate_two = jnp.sum(d_out * branch_two, axis=0)
    d_branch_two = (gate_two * d_out).astype(jnp.bfloat16)
    down_grad = matmul_left(activated_low, d_branch_two).astype(jnp.bfloat16)
    down_shard = lax.psum_scatter(down_grad, GROUP, scatter_dimension=0, tiled=True)
    down_total = lax.psum(down_shard, "rep").astype(jnp.float32)
    down_bias_grad = jnp.sum(d_branch_two.astype(jnp.float32), axis=0)
    d_activated = matmul_right(d_branch_two, full_down)
    d_preact = gelu_pull(d_activated)[0].astype(jnp.bfloat16)

    up_grad = matmul_left(hidden_two, d_preact).astype(jnp.bfloat16)
    up_shard = reduce_scatter(up_grad.reshape(SHARDS, rows, hidden_width))
    up_total = lax.psum(up_shard.astype(jnp.bfloat16), "rep").astype(jnp.float32)
    up_bias_grad = jnp.sum(d_preact.astype(jnp.float32), axis=0)
    d_hidden_two = matmul_right(d_preact, full_up)
    d_shift_two = jnp.sum(d_hidden_two, axis=0)
    d_scale_two = jnp.sum(d_hidden_two * normed_two, axis=0)
    d_middle = d_out + norm_back(d_hidden_two * (1.0 + scale_two), normed_two, inverse_two)
    d_gate_one = jnp.sum(d_middle * branch_one, axis=0)
    d_branch_one = (gate_one * d_middle).astype(jnp.bfloat16)

    out_grad = matmul_left(attended_low, d_branch_one).astype(jnp.bfloat16)
    out_shard = reduce_scatter(out_grad.reshape(SHARDS, rows, width))
    out_total = lax.psum(out_shard.astype(jnp.bfloat16), "rep").astype(jnp.float32)
    out_bias_grad = jnp.sum(d_branch_one.astype(jnp.float32), axis=0)
    d_attended = matmul_right(d_branch_one, full_out).astype(jnp.bfloat16)
    d_query, d_keys_all, d_values_all = attn_backward(
        query[None], keys, values, d_attended[None], log_totals, score_scale
    )
    d_pair = jnp.concatenate([d_keys_all[0], d_values_all[0]], axis=-1)
    d_pair_other = permute(d_pair[length:].astype(jnp.bfloat16), core_rule)
    d_pair = d_pair[:length] + d_pair_other.astype(jnp.float32)
    d_projected = jnp.concatenate([d_query[0], d_pair], axis=-1).astype(jnp.bfloat16)

    qkv_grad = matmul_left(hidden_one, d_projected).astype(jnp.bfloat16)
    qkv_shard = reduce_scatter(qkv_grad.reshape(SHARDS, rows, 3 * width))
    qkv_total = lax.psum(qkv_shard.astype(jnp.bfloat16), "rep").astype(jnp.float32)
    column_sums = jnp.sum(d_projected.astype(jnp.float32), axis=0)
    d_hidden_one = matmul_right(d_projected, full_qkv)
    d_shift_one = jnp.sum(d_hidden_one, axis=0)
    d_scale_one = jnp.sum(d_hidden_one * normed_one, axis=0)
    latent_grad = d_middle + norm_back(d_hidden_one * (1.0 + scale_one), normed_one, inverse_one)
    latent_grad = permute(latent_grad.astype(jnp.bfloat16)[None], swap_rule).astype(jnp.float32)

    bias_grads = (
        jnp.concatenate([column_sums[:width], column_sums[2 * width :]]),
        out_bias_grad,
        up_bias_grad,
        down_bias_grad,
    )
    sums = [d_shift_one, d_scale_one, d_gate_one, d_shift_two, d_scale_two, d_gate_two]
    ada_width = 6 * width
    sums_all = lax.all_gather(jnp.concatenate(sums + list(bias_grads)), GROUP, axis=0)
    d_group = sums_all[:, :ada_width].reshape(2, 2, 2, ada_width).sum(1).reshape(4, ada_width)
    bias_mine = []
    start = ada_width
    for grad in bias_grads:
        total = jnp.sum(sums_all[:, start : start + grad.shape[0]], axis=0)
        piece = grad.shape[0] // SHARDS
        bias_mine.append(lax.dynamic_slice_in_dim(total, place * piece, piece))
        start += grad.shape[0]
    d_silu = lax.dot_general(
        d_group,
        ada_weight.astype(jnp.float32),
        (((1,), (1,)), ((), ())),
        precision=exact_mode,
    )
    cond_mine = lax.dynamic_slice_in_dim(cond_group, place * rows, rows, 1)
    cond_part = jax.vjp(jax.nn.silu, cond_mine)[1](d_silu)[0]
    cond_all = lax.all_gather(cond_part, GROUP, axis=1, tiled=True)
    cond_grad = lax.dynamic_slice_in_dim(cond_all, fsdp_index, 1, 0)

    packed = jnp.concatenate(
        [d_group.reshape(-1), silu_mine.astype(jnp.float32).reshape(-1)] + bias_mine
    )
    packed_all = lax.all_gather(packed, "rep", axis=0)
    d_all = packed_all[:, : 4 * ada_width].reshape(-1, ada_width)
    silu_all = packed_all[:, 4 * ada_width : 4 * ada_width + 4 * rows].reshape(-1, rows)
    ada_total = lax.dot_general(
        silu_all, d_all, (((0,), (0,)), ((), ())), precision=exact_mode
    )
    ada_bias_total = jnp.sum(
        lax.dynamic_slice_in_dim(d_all, place * ada_bias.shape[0], ada_bias.shape[0], 1), axis=0
    )
    bias_totals = jnp.sum(packed_all[:, 4 * ada_width + 4 * rows :], axis=0)
    cuts = [0]
    for piece in bias_mine:
        cuts.append(cuts[-1] + piece.shape[0])
    qv_total, out_bias_total, up_bias_total, down_bias_total = (
        bias_totals[low:high] for low, high in zip(cuts[:-1], cuts[1:])
    )
    return (
        block_out,
        latent_grad,
        cond_grad,
        ada_total,
        ada_bias_total,
        qkv_total,
        qv_total,
        out_total,
        out_bias_total,
        up_total,
        up_bias_total,
        down_total,
        down_bias_total,
    )


def solution(mesh):
    tokens = P(("rep", "fsdp"), "sp", None)
    rows = P(("rep", "fsdp"), None)
    matrix = P(GROUP, None)
    vector = P(GROUP)
    weights = (matrix, vector) * 5
    return jax.shard_map(
        per_device,
        mesh=mesh,
        in_specs=(tokens, rows, P(("rep", "fsdp"))) + weights + (tokens,),
        out_specs=(tokens, tokens, rows) + weights,
        check_vma=False,
    )
```

time: 1750 us -> 787 us (0.45)
  waiting for transfers between devices: 1310 us -> 338 us
  matrix products: 202 us -> 179 us
  blocking collectives: 75.6 us -> 56.5 us
  other arithmetic: 46.7 us -> 65.3 us
    reduce_scatter x7 -> x1, waiting for transfers between devices: 699 us -> 0.01 us  [per_device(): lax.psum_scatter(down_grad, GROUP, scatter_dimension=0, tiled=True)]
    psum x1 -> x2, waiting for transfers between devices: 340 us -> 143 us  [the longest x1 95 us: per_device(): lax.psum(qkv_shard.astype(jnp.bfloat16), 'rep').astype(jnp.float32)]
    all_gather x7 -> x4, waiting for transfers between devices: 264 us -> 125 us  [the longest x1 53.5 us: per_device(): full_qkv = lax.all_gather(qkv_weight, GROUP, axis=0, tiled=True)]
    ppermute x0 -> x15, waiting for transfers between devices: none -> 68.7 us  [permute(): return lax.ppermute(values, GROUP, pairs_by(rule))]
    all_gather x0 -> x3, blocking collectives: none -> 56.5 us  [the longest x1 22.1 us: per_device(): cond_all = lax.all_gather(cond_part, GROUP, axis=1, tiled=True)]
    unnamed x2 -> x0, blocking collectives: 52 us -> none
    convert_element_type x4 -> x16, other arithmetic: 1.25 us -> 24.8 us  [the longest x3 11.5 us: reduce_scatter(): (core_half(core).astype(jnp.float32) + received.astype(jnp.float32)).asty...]
    psum x2 -> x0, blocking collectives: 23.6 us -> none  [the longest x1 18.7 us: per_device(): lax.psum((shards[0], shards[1], shards[2], shards[3], shards[4], shards[5...]
  transfers between devices with their start and end apart: 15 -> 23, of which waited for: 14 -> 9; matrix products, arithmetic and copies ran while one was open for 10% -> 33% of each run, Pallas kernels for 0% -> 0%
where the time goes in v1:
time: 787 us; the launch traced here: 776 us
  waiting for transfers between devices  338 us (43%)
  matrix products  179 us (23%)
  local copies, waits for them, and re-layouts  96.4 us (12%)
  other arithmetic  65.3 us (8%)
  blocking collectives  56.5 us (7%)
  starting transfers between devices  18.1 us (2%)
  between operations  17.1 us (2%)
    psum x1, waiting for transfers between devices, per_device(): lax.psum(qkv_shard.astype(jnp.bfloat16), 'rep').astype(jnp.float32)  95 us
    ppermute x15, waiting for transfers between devices, permute(): return lax.ppermute(values, GROUP, pairs_by(rule))  68.7 us
    all_gather x1, waiting for transfers between devices, per_device(): full_qkv = lax.all_gather(qkv_weight, GROUP, axis=0, tiled=True)  53.5 us
    all_gather x1, waiting for transfers between devices, per_device(): full_down = lax.all_gather(down_weight, GROUP, axis=0, tiled=True)  53.5 us
    psum x1, waiting for transfers between devices, per_device(): lax.psum(matmul(silu_mine, ada_weight) + ada_bias_row, GROUP)  47.8 us
    dot_general x4, matrix products, matmul_right(): lax.dot_general(left, right, (((1,), (1,)), ((), ())), preferred_element_...  44.7 us
    dot_general x5, matrix products, matmul(): return jnp.dot(left, right, preferred_element_type=jnp.float32)  43.9 us
    dot_general x4, matrix products, matmul_left(): lax.dot_general(left, right, (((0,), (0,)), ((), ())), preferred_element_...  33.7 us
  transfers between devices with their start and end apart: 23, of which 9 were waited for; matrix products, arithmetic and copies ran while one was open for 33% of the time, Pallas kernels for 0%

profile of v1, /device:TPU:9, one launch (start us, length us, event | category | flops | bytes accessed | tf_op | source)
XLA Modules:
  0.0 775.9 jit_solution(7648652924539691562)
XLA Ops:
  8.8 2.8 concatenate.40
  11.6 17.0 %all-gather.3 = bf16[8,1,2432]{2,1,0:T(2,128)(2,1)S(1)} all-gather(bf16[1,1,2432]{2,1,0:T(2,128)(2,1)S(1)} %reshape.294), channel_id=2, replica_groups=mesh['rep'=4,'fsdp'=4,'sp'=2] {'fsdp','sp'}, dimensions={0}, use_global_device_ids=true | all-gather | bytes 43776 | tf_op jit(solution)/shard_map/all_gather | solution.py:217
  35.0 47.8 %all-reduce.6.cloned.1.call-done = f32[4,6912]{1,0:T(4,128)} async-done(((f32[4,6912]{1,0:T(4,128)}), f32[4,6912]{1,0:T(4,128)}) %all-reduce.6.cloned.1.call-update) | async-done | bytes 110608 | tf_op jit(solution)/shard_map/psum | solution.py:244
  84.5 53.5 %all-gather.11.cloned.1.call-done = bf16[1152,3456]{1,0:T(8,128)(2,1)} async-done(((bf16[144,3456]{1,0:T(8,128)(2,1)}), bf16[1152,3456]{1,0:T(8,128)(2,1)}) %all-gather.11.cloned.1.call-update) | async-done | bytes 7962640 | tf_op jit(solution)/shard_map/all_gather | solution.py:218
  138.1 8.7 %add_convert_fusion = bf16[512,3456]{1,0:T(8,128)(2,1)S(1)} fusion(bf16[1152,3456]{1,0:T(8,128)(2,1)} %all-gather.11.cloned.1.call-done, f32[3456]{0:T(1024)S(1)} %pad_maximum_fusion.7, bf16[1,512,1152]{2,1,0:T(8,128)(2,1)S(1)} %collective-permute-done, f32[1152]{0:T(1024)S(1)} %get-tuple-element.209, f32[1152]{0:T(1024)S(1)} %get-tuple-element.210, ...), kind=kOutput, calls=%fused_computation.52 | convolution fusion | flops 4083941376 | bytes 12708352 | tf_op jit(solution)/shard_map/dot_general | solution.py:30
  149.7 3.1 collective-permute-start.3
  159.9 2.7 maximum_bitcast_fusion
  162.6 2.5 fusion.75
  165.1 4.3 copy.58
  169.4 4.3 copy.60
  174.8 39.9 %while.26 = (s32[]{:T(128)}, bf16[4,1,512,288]{2,3,1,0:T(8,128)(2,1)}, f32[4,1,4,512]{3,2,1,0:T(4,128)S(1)}, s32[4]{0:T(128)S(1)}, bf16[1,1024,1152]{1,2,0:T(8,1...) while((s32[]{:T(128)}, ...), condition=%wide.region_6.7_spmd, body=%wide.region_3.6_spmd.sunk | while | flops 622852096 | bytes 30539968 | solution.py:133
  214.8 5.6 fusion.73
  222.2 17.5 %all-gather.15.cloned.1.call-done = bf16[1152,4608]{1,0:T(8,128)(2,1)} async-done(((bf16[144,4608]{1,0:T(8,128)(2,1)}), bf16[1152,4608]{1,0:T(8,128)(2,1)}) %all-gather.15.cloned.1.call-update) | async-done | bytes 10616848 | tf_op jit(solution)/shard_map/all_gather | solution.py:222
  239.7 12.2 %fusion.72 = f32[512,4608]{1,0:T(8,128)} fusion(bf16[1152,4608]{1,0:T(8,128)(2,1)} %all-gather.15.cloned.1.call-done, f32[512,1152]{1,0:T(8,128)} %copy-done.4, f32[1152]{0:T(1024)S(1)} %get-tuple-element.212, f32[1152]{0:T(1024)S(1)} %get-tuple-element.208, f32[512]{0:T(512)S(1)} %add_rsqrt_fusion, f32[512]{0:T(512)S(1)} %broadcast_multiply_fusion.4), kind=kOutput, calls=%fused_computation.199 | convolution fusion | flops 5438767104 | bytes 22426624 | tf_op jit(solution)/shard_map/dot_general | solution.py:30
  252.0 53.5 %all-gather.17.cloned.1.call-done = bf16[4608,1152]{1,0:T(8,128)(2,1)} async-done(((bf16[576,1152]{1,0:T(8,128)(2,1)}), bf16[4608,1152]{1,0:T(8,128)(2,1)}) %all-gather.17.cloned.1.call-update) | async-done | bytes 10616848 | tf_op jit(solution)/shard_map/all_gather | solution.py:223
  305.5 19.2 %convert_reduce_fusion = (f32[4608]{0:T(1024)}, bf16[512,4608]{1,0:T(8,128)(2,1)}) fusion(f32[512,4608]{1,0:T(8,128)} %fusion.72, f32[4608]{0:T(1024)S(1)} %reshape.281, bf16[4608,1152]{1,0:T(8,128)(2,1)} %all-gather.17.cloned.1.call-done, bf16[1,512,1152]{2,1,0:T(8,128)(2,1)} %collective-permute-done.3, f32[]{:T(128)} %bitcast.24, ...), kind=kOutput, calls=%fused_computation.45 | convolution fusion | flops 5492436480 | bytes 25993732 | tf_op jit(solution)/shard_map/dot_general | solution.py:40
  324.7 13.2 %multiply_reduce_fusion.2 = (f32[1152]{0:T(1024)}, f32[512]{0:T(512)S(1)}, f32[512]{0:T(512)S(1)}, f32[1152]{0:T(1024)}, f32[512,1152]{1,0:T(8,128)}) fusion(f32[512,1152]{1,0:T(8,128)S(1)} %copy-done.5, f32[512]{0:T(512)S(1)} %add_rsqrt_fusion, f32[512]{0:T(512)S(1)} %broadcast_multiply_fusion.4, f32[1152]{0:T(1024)S(1)} %get-tuple-element.208, ...), kind=kOutput, calls=%fused_computation.101 | convolution fusion | flops 5441123328 | bytes 20076032 | tf_op jit(solution)/shard_map/dot_general | solution.py:40
  338.0 16.2 %convert_reduce_fusion.3 = (f32[1152]{0:T(1024)}, f32[1152]{0:T(1024)}, bf16[1,512,1152]{2,1,0:T(8,128)(2,1)}, f32[1152]{0:T(1024)}, bf16[512,1152]{1,0:T(8,128)(2,1)S(1)}, /*index=5*/f32[512,1152]{1,0:T(8,128)}) fusion(f32[]{:T(128)} %bitcast.24, bf16[1,512,1152]{2,1,0:T(8,128)(2,1)} %collective-permute-done.3, f32[1152]{0:T(1024)S(1)} %get-tuple-element.207, ...), kind=kOutput, calls=%fused_computation.99 | convolution fusion | flops 5474153472 | bytes 30729732 | tf_op jit(solution)/shard_map/dot_general | solution.py:30
  354.2 3.2 convolution_convert_fusion.3
  357.4 2.9 fusion.30
  364.6 14.3 %convolution_convert_fusion = bf16[4608,1152]{1,0:T(8,128)(2,1)} fusion(bf16[1,512,1152]{2,1,0:T(8,128)(2,1)} %collective-permute-done.3, f32[]{:T(128)} %bitcast.24, f32[1152]{0:T(1024)S(1)} %get-tuple-element.207, f32[512,4608]{1,0:T(8,128)} %fusion.72, f32[4608]{0:T(1024)S(1)} %reshape.281), kind=kOutput, calls=%fused_computation.29 | convolution fusion | flops 5467078656 | bytes 21256708 | tf_op jit(solution)/shard_map/dot_general | solution.py:34
  380.1 69.5 %while.27 = (s32[]{:T(128)}, bf16[4,1,512,288]{2,3,1,0:T(8,128)(2,1)}, f32[4,1,1024,288]{2,3,1,0:T(8,128)}, f32[4,1,1024,288]{2,3,1,0:T(8,128)}, s32[4]{0:T(128)...) while((s32[]{:T(128)}, ...), condition=%wide.region_13.14_spmd, body=%wide.region_11.13_spmd.sunk | while | flops 1535703040 | bytes 77422808 | solution.py:179
  386.1 2.9 multiply_reduce_fusion.11
  403.4 2.9 multiply_reduce_fusion.11
  420.8 2.9 multiply_reduce_fusion.11
  438.2 2.9 multiply_reduce_fusion.11
  449.7 4.2 fusion.21
  457.8 9.3 %convolution_convert_fusion.1 = bf16[1152,4608]{1,0:T(8,128)(2,1)S(1)} fusion(bf16[512,4608]{1,0:T(8,128)(2,1)} %get-tuple-element.296, f32[512,1152]{1,0:T(8,128)S(1)} %copy-done.6, f32[1152]{0:T(1024)S(1)} %copy-done.32, f32[1152]{0:T(1024)S(1)} %get-tuple-element.208, f32[512]{0:T(512)S(1)} %add_rsqrt_fusion, f32[512]{0:T(512)S(1)} %broadcast_multiply_fusion.4), kind=kOutput, calls=%fused_computation.30 | convolution fusion | flops 5444075520 | bytes 17708032 | tf_op jit(solution)/shard_map/dot_general | solution.py:34
  468.5 2.9 dynamic-slice_bitcast_fusion.1
  471.4 2.5 copy-done.3
  474.9 2.8 fusion.20
  477.7 6.8 convolution_convert_fusion.2
  489.5 9.4 %fusion.41 = (f32[1152]{0:T(1024)S(1)}, f32[512]{0:T(512)S(1)}, f32[512]{0:T(512)S(1)}, f32[1152]{0:T(1024)S(1)}, f32[512,1152]{1,0:T(8,128)S(1)}) fusion(bf16[1,512,1152]{2,1,0:T(8,128)(2,1)S(1)} %copy-done.2, f32[512]{0:T(512)S(1)} %copy-done.39, f32[512]{0:T(512)S(1)} %copy-done.28, f32[1152]{0:T(1024)S(1)} %copy-done.25, ...), kind=kOutput, calls=%fused_computation.92 | convolution fusion | flops 4089836544 | bytes 15062528 | tf_op jit(solution)/shard_map/dot_general | solution.py:40
  502.1 17.4 %all-gather.4 = f32[8,1,16128]{2,1,0:T(1,128)S(1)} all-gather(f32[1,1,16128]{2,1,0:T(1,128)S(1)} %reshape.296), channel_id=3, replica_groups=mesh['rep'=4,'fsdp'=4,'sp'=2] {'fsdp','sp'}, dimensions={0}, use_global_device_ids=true | all-gather | bytes 580608 | tf_op jit(solution)/shard_map/all_gather | solution.py:330
  520.8 5.6 fusion.9
  530.0 2.8 fusion.69
  542.3 4.3 fusion.17
  548.3 12.7 %collective-permute-done.13 = bf16[2,144,4608]{2,1,0:T(8,128)(2,1)} collective-permute-done((bf16[2,144,4608]{2,1,0:T(8,128)(2,1)}, bf16[2,144,4608]{2,1,0:T(8,128)(2,1)}, u32[]{:S(2)}, u32[]{:S(2)}) %collective-permute-start.13) | collective-permute-done | bytes 2654240 | tf_op jit(solution)/shard_map/ppermute | solution.py:70
  561.0 2.5 convert_add_fusion.2
  564.4 32.0 %collective-permute-done.7 = bf16[2,144,3456]{2,1,0:T(8,128)(2,1)S(1)} collective-permute-done((bf16[2,144,3456]{2,1,0:T(8,128)(2,1)S(1)}, bf16[2,144,3456]{2,1,0:T(8,128)(2,1)S(1)}, u32[]{:S(2)}, u32[]{:S(2)}) %collective-permute-start.7) | collective-permute-done | bytes 1990688 | tf_op jit(solution)/shard_map/ppermute | solution.py:70
  599.1 11.4 %collective-permute-done.8 = bf16[144,3456]{1,0:T(8,128)(2,1)S(1)} collective-permute-done((bf16[144,3456]{1,0:T(8,128)(2,1)S(1)}, bf16[144,3456]{1,0:T(8,128)(2,1)S(1)}, u32[]{:S(2)}, u32[]{:S(2)}) %collective-permute-start.8) | collective-permute-done | bytes 995360 | tf_op jit(solution)/shard_map/ppermute | solution.py:70
  611.6 4.0 collective-permute-start.2
  617.6 12.6 %collective-permute-done.2 = bf16[1,512,1152]{2,1,0:T(8,128)(2,1)S(1)} collective-permute-done((bf16[1,512,1152]{2,1,0:T(8,128)(2,1)}, bf16[1,512,1152]{2,1,0:T(8,128)(2,1)S(1)}, u32[]{:S(2)}, u32[]{:S(2)}) %collective-permute-start.2) | collective-permute-done | bytes 1179680 | tf_op jit(solution)/shard_map/ppermute | solution.py:70
  630.1 22.1 %all-gather.5 = f32[8,144,4]{1,2,0:T(4,128)S(1)} all-gather(f32[1,144,4]{1,2,0:T(4,128)S(1)} %get-tuple-element.287), channel_id=1, replica_groups=mesh['rep'=4,'fsdp'=4,'sp'=2] {'fsdp','sp'}, dimensions={0}, use_global_device_ids=true | all-gather | bytes 20736 | tf_op jit(solution)/shard_map/all_gather | solution.py:347
  657.4 5.2 fusion.79
  662.6 2.9 convert_element_type.270
  665.5 95.0 %all-reduce.10.cloned.1.call-done = (bf16[144,3456]{1,0:T(8,128)(2,1)}, bf16[144,1152]{1,0:T(8,128)(2,1)}, bf16[144,4608]{1,0:T(8,128)(2,1)}, bf16[576,1152]{1,0:T(8,128)(2,1)}) async-done(((bf16[144,3456]{1,0:T(8,128)(2,1)}, bf16[144,1152]{1,0:T(8,128)(2,1)}, bf16[144,4608]{1,0:T(8,128)(2,1)}, bf16[576,1152]{1,0:T(8,128)(2,1)}), (bf16[144,3456]{1,0:T(8,128)(2,1)}, bf16[144,1152]{1,0:T(8,128)(2,1)}, ...) | async-done | bytes 3981328 | tf_op jit(solution)/shard_map/psum | solution.py:314
  760.5 2.7 convert_element_type.285
  (337 shorter events, 165.7 us)
Async XLA Ops:
  7.2 22.3 %copy-start = (bf16[144,6912]{1,0:T(8,128)(2,1)S(1)}, bf16[144,6912]{1,0:T(8,128)(2,1)}, u32[]{:S(2)}) copy-start(bf16[144,6912]{1,0:T(8,128)(2,1)} %param.21) | copy-start | bytes 5971972
  7.2 75.6 %all-reduce.6.cloned.1.call-start = ((), (), s32[]{:S(2)}) async-start(), calls=%async_computation.1 | async-start | bytes 221184 | tf_op jit(solution)/shard_map/psum | solution.py:244
  30.6 107.5 %all-gather.11.cloned.1.call-start = ((), (), s32[]{:S(2)}) async-start(), calls=%async_computation.2 | async-start | bytes 8957952 | tf_op jit(solution)/shard_map/all_gather | solution.py:218
  31.3 183.4 %all-gather.13.cloned.1.call-start = ((), (), s32[]{:S(2)}) async-start(), calls=%async_computation.3 | async-start | bytes 2985984 | tf_op jit(solution)/shard_map/all_gather | solution.py:221
  32.1 207.7 %all-gather.15.cloned.1.call-start = ((), (), s32[]{:S(2)}) async-start(), calls=%async_computation.4 | async-start | bytes 11943936 | tf_op jit(solution)/shard_map/all_gather | solution.py:222
  32.6 272.8 %all-gather.17.cloned.1.call-start = ((), (), s32[]{:S(2)}) async-start(), calls=%async_computation.5 | async-start | bytes 11943936 | tf_op jit(solution)/shard_map/all_gather | solution.py:223
  32.7 51.1 %collective-permute-start = (bf16[1,512,1152]{2,1,0:T(8,128)(2,1)}, bf16[1,512,1152]{2,1,0:T(8,128)(2,1)S(1)}, u32[]{:S(2)}, u32[]{:S(2)}) collective-permute-start(bf16[1,512,1152]{2,1,0:T(8,128)(2,1)} %param.18), channel_id=1, source_target_pairs={{0,0},{1,2},{2,1},{3,3},{4,4},{5,6},{6,5},{7,7},{8,8},{9,10},{10,9... | collective-permute-start | bytes 3538952 | tf_op jit(solution)/shard_map/ppermute | solution.py:70
  34.8 576.8 %reduce-scatter.2.cloned.1.call-start = ((), (), s32[]{:S(2)}) async-start(), calls=%async_computation.6 | async-start | bytes 11943936 | tf_op jit(solution)/shard_map/reduce_scatter | solution.py:282
  83.8 63.0 %copy-start.24 = (f32[1152]{0:T(1024)}, f32[1152]{0:T(1024)S(1)}, u32[]{:S(2)}) copy-start(f32[1152]{0:T(1024)S(1)} %get-tuple-element.210) | copy-start | bytes 13828
  83.8 63.0 %copy-start.29 = (f32[1152]{0:T(1024)}, f32[1152]{0:T(1024)S(1)}, u32[]{:S(2)}) copy-start(f32[1152]{0:T(1024)S(1)} %get-tuple-element.209) | copy-start | bytes 13828
  83.8 156.0 %copy-start.31 = (f32[1152]{0:T(1024)}, f32[1152]{0:T(1024)S(1)}, u32[]{:S(2)}) copy-start(f32[1152]{0:T(1024)S(1)} %get-tuple-element.212) | copy-start | bytes 13828
  83.8 131.0 %copy-start.1 = (bf16[1,512,1152]{2,1,0:T(8,128)(2,1)}, bf16[1,512,1152]{2,1,0:T(8,128)(2,1)S(1)}, u32[]{:S(2)}) copy-start(bf16[1,512,1152]{2,1,0:T(8,128)(2,1)S(1)} %collective-permute-done) | copy-start | bytes 3538948
  84.1 62.8 %copy-start.27 = (f32[512]{0:T(512)}, f32[512]{0:T(512)S(1)}, u32[]{:S(2)}) copy-start(f32[512]{0:T(512)S(1)} %broadcast_multiply_fusion.5) | copy-start | bytes 6148
  84.5 62.3 %copy-start.38 = (f32[512]{0:T(512)}, f32[512]{0:T(512)S(1)}, u32[]{:S(2)}) copy-start(f32[512]{0:T(512)S(1)} %add_rsqrt_fusion.1) | copy-start | bytes 6148
  146.9 7.0 copy-start.40
  149.4 10.5 %collective-permute-start.1 = (bf16[512,2304]{1,0:T(8,128)(2,1)}, bf16[512,2304]{1,0:T(8,128)(2,1)}, u32[]{:S(2)}, u32[]{:S(2)}) collective-permute-start(bf16[512,2304]{1,0:T(8,128)(2,1)} %slice.151), channel_id=1, source_target_pairs={{0,2},{1,3},{2,0},{3,1},{4,6},{5,7},{6,4},{7,5},{8,10},{9,11},{10,... | collective-permute-start | bytes 7077896 | tf_op jit(solution)/shard_map/ppermute | solution.py:70
  149.7 102.3 %collective-permute-start.3 = (bf16[1,512,1152]{2,1,0:T(8,128)(2,1)}, bf16[1,512,1152]{2,1,0:T(8,128)(2,1)}, u32[]{:S(2)}, u32[]{:S(2)}) collective-permute-start(bf16[1,512,1152]{2,1,0:T(8,128)(2,1)} %param.31), channel_id=1, source_target_pairs={{0,0},{1,2},{2,1},{3,3},{4,4},{5,6},{6,5},{7,7},{8,8},{9,10},{10,9... | collective-permute-start | bytes 3538952 | tf_op jit(solution)/shard_map/ppermute | solution.py:70
  305.5 19.3 %copy-start.5 = (f32[512,1152]{1,0:T(8,128)S(1)}, f32[512,1152]{1,0:T(8,128)}, u32[]{:S(2)}) copy-start(f32[512,1152]{1,0:T(8,128)} %copy-done.4) | copy-start | bytes 7077892
  305.5 32.4 %slice-start.4 = ((s8[9437184]{0:T(1024)(128)(4,1)}), s8[4194304]{0:T(1024)(128)(4,1)S(1)}, s32[]{:S(2)}) async-start(s8[9437184]{0:T(1024)(128)(4,1)} %bitcast.305), calls=%async_computation.13 | async-start | bytes 8388608
  305.5 32.4 %slice-start.5 = ((s8[9437184]{0:T(1024)(128)(4,1)}), s8[4194304]{0:T(1024)(128)(4,1)S(1)}, s32[]{:S(2)}) async-start(s8[9437184]{0:T(1024)(128)(4,1)} %bitcast.305), calls=%async_computation.14 | async-start | bytes 8388608
  324.7 13.2 %slice-start.6 = ((s8[9437184]{0:T(1024)(128)(4,1)}), s8[1048576]{0:T(1024)(128)(4,1)S(1)}, s32[]{:S(2)}) async-start(s8[9437184]{0:T(1024)(128)(4,1)} %bitcast.305), calls=%async_computation.15 | async-start | bytes 2097152
  338.0 16.2 %copy-start.11 = (bf16[4,1,512,288]{2,3,1,0:T(8,128)(2,1)S(1)}, bf16[4,1,512,288]{2,3,1,0:T(8,128)(2,1)}, u32[]{:S(2)}) copy-start(bf16[4,1,512,288]{2,3,1,0:T(8,128)(2,1)} %get-tuple-element.105) | copy-start | bytes 3538948
  364.4 90.0 %collective-permute-start.9 = (bf16[2,2,144,1152]{3,2,1,0:T(8,128)(2,1)}, bf16[2,2,144,1152]{3,2,1,0:T(8,128)(2,1)}, u32[]{:S(2)}, u32[]{:S(2)}) collective-permute-start(bf16[2,2,144,1152]{3,2,1,0:T(8,128)(2,1)} %dynamic-slice_bitcast_fusion.3), channel_id=1, source_target_pairs={{0,2},{1,3},{2,0},{3,1},{4,6},{5,7},{6,4},{7,5},{8,10},{9,11},{10,... | collective-permute-start | bytes 3981320 | tf_op jit(solution)/shard_map/ppermute | solution.py:70
  379.0 274.0 %all-reduce.8.cloned.1.call-start = ((), (), s32[]{:S(2)}) async-start(), calls=%async_computation.7 | async-start | bytes 942080
  449.7 4.7 copy-start.14
  453.9 20.9 %collective-permute-start.4 = (bf16[512,2304]{0,1:T(8,128)(2,1)}, bf16[512,2304]{0,1:T(8,128)(2,1)}, u32[]{:S(2)}, u32[]{:S(2)}) collective-permute-start(bf16[512,2304]{0,1:T(8,128)(2,1)} %fusion.21), channel_id=1, source_target_pairs={{0,2},{1,3},{2,0},{3,1},{4,6},{5,7},{6,4},{7,5},{8,10},{9,11},{10,... | collective-permute-start | bytes 7077896 | tf_op jit(solution)/shard_map/ppermute | solution.py:70
  456.2 18.6 %slice-start.2 = ((s8[4718592]{0:T(1024)(128)(4,1)}), s8[4194304]{0:T(1024)(128)(4,1)S(1)}, s32[]{:S(2)}) async-start(s8[4718592]{0:T(1024)(128)(4,1)} %bitcast.278), calls=%async_computation.11 | async-start | bytes 8388608
  456.3 18.6 %slice-start.3 = ((s8[4718592]{0:T(1024)(128)(4,1)}), s8[524288]{0:T(1024)(128)(4,1)S(1)}, s32[]{:S(2)}) async-start(s8[4718592]{0:T(1024)(128)(4,1)} %bitcast.278), calls=%async_computation.12 | async-start | bytes 1048576
  456.3 10.8 %collective-permute-start.10 = (bf16[2,144,1152]{2,1,0:T(8,128)(2,1)S(1)}, bf16[2,144,1152]{2,1,0:T(8,128)(2,1)S(1)}, u32[]{:S(2)}, u32[]{:S(2)}) collective-permute-start(bf16[2,144,1152]{2,1,0:T(8,128)(2,1)S(1)} %pad_maximum_fusion.6), channel_id=1, source_target_pairs={{0,4},{1,5},{2,3},{3,2},{4,0},{5,1},{6,7},{7,6},{8,12},{9,13},{10,... | collective-permute-start | bytes 1990664 | tf_op jit(solution)/shard_map/ppermute | solution.py:70
  467.1 6.8 copy-start.3
  467.3 6.7 collective-permute-start.11
  468.5 6.3 slice-start
  468.5 6.3 slice-start.1
  473.9 46.8 %collective-permute-start.12 = (bf16[2,2,144,4608]{3,2,1,0:T(8,128)(2,1)}, bf16[2,2,144,4608]{3,2,1,0:T(8,128)(2,1)}, u32[]{:S(2)}, u32[]{:S(2)}) collective-permute-start(bf16[2,2,144,4608]{3,2,1,0:T(8,128)(2,1)} %dynamic-slice_bitcast_fusion.1), channel_id=1, source_target_pairs={{0,2},{1,3},{2,0},{3,1},{4,6},{5,7},{6,4},{7,5},{8,10},{9,11},{10,... | collective-permute-start | bytes 15925256 | tf_op jit(solution)/shard_map/ppermute | solution.py:70
  484.6 4.4 copy-start.8
  489.0 10.0 %copy-start.22 = (f32[16128]{0:T(1024)S(1)}, f32[16128]{0:T(1024)}, u32[]{:S(2)}) copy-start(f32[16128]{0:T(1024)} %custom-call) | copy-start | bytes 193540
  489.0 10.0 %copy-start.7 = (f32[512,1152]{1,0:T(8,128)S(1)}, f32[512,1152]{1,0:T(8,128)}, u32[]{:S(2)}) copy-start(f32[512,1152]{1,0:T(8,128)} %get-tuple-element.292) | copy-start | bytes 7077892
  489.0 53.3 %collective-permute-start.6 = (bf16[2,2,144,3456]{3,2,1,0:T(8,128)(2,1)}, bf16[2,2,144,3456]{3,2,1,0:T(8,128)(2,1)}, u32[]{:S(2)}, u32[]{:S(2)}) collective-permute-start(bf16[2,2,144,3456]{3,2,1,0:T(8,128)(2,1)} %dynamic-slice_bitcast_fusion.2), channel_id=1, source_target_pairs={{0,2},{1,3},{2,0},{3,1},{4,6},{5,7},{6,4},{7,5},{8,10},{9,11},{10,... | collective-permute-start | bytes 11943944 | tf_op jit(solution)/shard_map/ppermute | solution.py:70
  489.5 9.5 %copy-start.15 = (f32[512,1152]{1,0:T(8,128)S(1)}, f32[512,1152]{1,0:T(8,128)}, u32[]{:S(2)}) copy-start(f32[512,1152]{1,0:T(8,128)} %get-tuple-element.277) | copy-start | bytes 7077892
  529.6 31.5 %collective-permute-start.13 = (bf16[2,144,4608]{2,1,0:T(8,128)(2,1)}, bf16[2,144,4608]{2,1,0:T(8,128)(2,1)}, u32[]{:S(2)}, u32[]{:S(2)}) collective-permute-start(bf16[2,144,4608]{2,1,0:T(8,128)(2,1)} %pad_maximum_fusion.2), channel_id=1, source_target_pairs={{0,4},{1,5},{2,3},{3,2},{4,0},{5,1},{6,7},{7,6},{8,12},{9,13},{10,... | collective-permute-start | bytes 7962632 | tf_op jit(solution)/shard_map/ppermute | solution.py:70
  542.2 218.2 %all-reduce.10.cloned.1.call-start = ((), (), s32[]{:S(2)}) async-start(), calls=%async_computation.8 | async-start | bytes 7962624 | tf_op jit(solution)/shard_map/psum | solution.py:314
  547.0 14.0 %copy-start.9 = (bf16[1,144,4608]{2,1,0:T(8,128)(2,1)S(1)}, bf16[1,144,4608]{2,1,0:T(8,128)(2,1)}, u32[]{:S(2)}) copy-start(bf16[1,144,4608]{2,1,0:T(8,128)(2,1)} %get-tuple-element.267) | copy-start | bytes 3981316
  547.2 49.2 %collective-permute-start.7 = (bf16[2,144,3456]{2,1,0:T(8,128)(2,1)S(1)}, bf16[2,144,3456]{2,1,0:T(8,128)(2,1)S(1)}, u32[]{:S(2)}, u32[]{:S(2)}) collective-permute-start(bf16[2,144,3456]{2,1,0:T(8,128)(2,1)S(1)} %pad_maximum_fusion.3), channel_id=1, source_target_pairs={{0,4},{1,5},{2,3},{3,2},{4,0},{5,1},{6,7},{7,6},{8,12},{9,13},{10,... | collective-permute-start | bytes 5971976 | tf_op jit(solution)/shard_map/ppermute | solution.py:70
  563.7 34.1 %collective-permute-start.14 = (bf16[144,4608]{1,0:T(8,128)(2,1)S(1)}, bf16[144,4608]{1,0:T(8,128)(2,1)S(1)}, u32[]{:S(2)}, u32[]{:S(2)}) collective-permute-start(bf16[144,4608]{1,0:T(8,128)(2,1)S(1)} %fusion.47), channel_id=1, source_target_pairs={{0,1},{1,0},{2,6},{3,7},{4,5},{5,4},{6,2},{7,3},{8,9},{9,8},{10,14... | collective-permute-start | bytes 3981320 | tf_op jit(solution)/shard_map/ppermute | solution.py:70
  597.0 13.4 %collective-permute-start.8 = (bf16[144,3456]{1,0:T(8,128)(2,1)S(1)}, bf16[144,3456]{1,0:T(8,128)(2,1)S(1)}, u32[]{:S(2)}, u32[]{:S(2)}) collective-permute-start(bf16[144,3456]{1,0:T(8,128)(2,1)S(1)} %fusion.51), channel_id=1, source_target_pairs={{0,1},{1,0},{2,6},{3,7},{4,5},{5,4},{6,2},{7,3},{8,9},{9,8},{10,14... | collective-permute-start | bytes 2985992 | tf_op jit(solution)/shard_map/ppermute | solution.py:70
  611.6 18.5 %collective-permute-start.2 = (bf16[1,512,1152]{2,1,0:T(8,128)(2,1)}, bf16[1,512,1152]{2,1,0:T(8,128)(2,1)S(1)}, u32[]{:S(2)}, u32[]{:S(2)}) collective-permute-start(bf16[1,512,1152]{2,1,0:T(8,128)(2,1)} %get-tuple-element.274), channel_id=1, source_target_pairs={{0,0},{1,2},{2,1},{3,3},{4,4},{5,6},{6,5},{7,7},{8,8},{9,10},{10,9... | collective-permute-start | bytes 3538952 | tf_op jit(solution)/shard_map/ppermute | solution.py:70
  615.7 47.0 %collective-permute-start.5 = (bf16[1,512,1152]{2,1,0:T(8,128)(2,1)}, bf16[1,512,1152]{2,1,0:T(8,128)(2,1)}, u32[]{:S(2)}, u32[]{:S(2)}) collective-permute-start(bf16[1,512,1152]{2,1,0:T(8,128)(2,1)} %get-tuple-element.279), channel_id=1, source_target_pairs={{0,0},{1,2},{2,1},{3,3},{4,4},{5,6},{6,5},{7,7},{8,8},{9,10},{10,9... | collective-permute-start | bytes 3538952 | tf_op jit(solution)/shard_map/ppermute | solution.py:70
  630.1 22.8 %copy-start.19 = (bf16[1,512,1152]{2,1,0:T(8,128)(2,1)}, bf16[1,512,1152]{2,1,0:T(8,128)(2,1)S(1)}, u32[]{:S(2)}) copy-start(bf16[1,512,1152]{2,1,0:T(8,128)(2,1)S(1)} %collective-permute-done.2) | copy-start | bytes 3538948
  (23 other events, 53.0 us)
Sparse Core Ops, SparseCore 0:
  30.7 52.0 all-reduce.5
  84.9 53.1 all-gather.10
  140.1 33.8 all-gather.12
  175.9 63.7 all-gather.14
  241.6 63.8 all-gather.16
  379.1 81.7 reduce-scatter.1
  542.4 36.6 all-reduce.7
  611.7 148.6 all-reduce.9

commit v2 on v1

--- a/solution.py
+++ b/solution.py
@@ -1,6 +1,8 @@
 import jax
 import jax.numpy as jnp
 from jax import lax
+from jax.experimental import pallas as pl
+from jax.experimental.pallas import tpu as pltpu
 from jax.sharding import PartitionSpec as P
 
 HEAD = 72
@@ -68,6 +70,115 @@
 
 def permute(values, rule):
     return lax.ppermute(values, GROUP, pairs_by(rule))
+
+
+def swap_halves(values):
+    place = place_of()
+    pairs = [pair for pair in pairs_by(swap_rule) if pair[0] != pair[1]]
+    received = lax.ppermute(values, GROUP, pairs)
+    stays = ((place >> 1) & 1) == (place & 1)
+    return jnp.where(stays, values, received)
+
+
+def gather_group(values):
+    place = place_of()
+    stacked = values[None]
+    for bit in (1, 2, 4):
+        received = permute(stacked, lambda at: at ^ bit)
+        stacked = jnp.where(
+            (place & bit) == 0,
+            jnp.concatenate([stacked, received]),
+            jnp.concatenate([received, stacked]),
+        )
+    return stacked
+
+
+def gather_replicas(values, replicas):
+    stacked = [values]
+    for shift in range(1, replicas):
+        pairs = [(at, (at + shift) % replicas) for at in range(replicas)]
+        stacked.append(lax.ppermute(values, "rep", pairs))
+    return jnp.stack(stacked)
+
+
+def reduce_replicas(partial, replicas):
+    low = jnp.bfloat16
+    rows, columns = partial.shape
+    own = lax.axis_index("rep")
+    pieces = partial.astype(low).reshape(replicas, rows // replicas, columns)
+    total = lax.dynamic_index_in_dim(
+        partial.reshape(pieces.shape), own, 0, keepdims=False
+    )
+    for shift in range(1, replicas):
+        pairs = [(at, (at + shift) % replicas) for at in range(replicas)]
+        piece = lax.dynamic_index_in_dim(pieces, (own + shift) % replicas, 0, keepdims=False)
+        total = total + lax.ppermute(piece, "rep", pairs).astype(jnp.float32)
+    stacked = gather_replicas(total.astype(low), replicas)
+    ordered = [
+        lax.dynamic_index_in_dim(stacked, (own - at) % replicas, 0, keepdims=False)
+        for at in range(replicas)
+    ]
+    return jnp.stack(ordered).reshape(rows, columns).astype(jnp.float32)
+
+
+def assemble_kernel(order_ref, *refs):
+    pieces, whole, buffer, load_sems, store_sems = (
+        refs[:SHARDS],
+        refs[SHARDS],
+        refs[SHARDS + 1],
+        refs[SHARDS + 2],
+        refs[SHARDS + 3],
+    )
+    rows = buffer.shape[1]
+    loads = [
+        pltpu.make_async_copy(piece, buffer.at[at], load_sems.at[at])
+        for at, piece in enumerate(pieces)
+    ]
+    for load in loads:
+        load.start()
+    stores = []
+    for at, load in enumerate(loads):
+        load.wait()
+        target = pl.ds(pl.multiple_of(order_ref[at] * rows, 16), rows)
+        store = pltpu.make_async_copy(buffer.at[at], whole.at[target], store_sems.at[at])
+        store.start()
+        stores.append(store)
+    for store in stores:
+        store.wait()
+
+
+def assemble(pieces, order):
+    rows, columns = pieces[0].shape
+    size = SHARDS * rows * columns * 2
+    return pl.pallas_call(
+        assemble_kernel,
+        out_shape=jax.ShapeDtypeStruct((SHARDS * rows, columns), pieces[0].dtype),
+        in_specs=[pl.BlockSpec(memory_space=pltpu.SMEM)]
+        + [pl.BlockSpec(memory_space=pl.ANY)] * SHARDS,
+        out_specs=pl.BlockSpec(memory_space=pl.ANY),
+        scratch_shapes=[
+            pltpu.VMEM((SHARDS, rows, columns), pieces[0].dtype),
+            pltpu.SemaphoreType.DMA((SHARDS,)),
+            pltpu.SemaphoreType.DMA((SHARDS,)),
+        ],
+        compiler_params=pltpu.CompilerParams(vmem_limit_bytes=size + (4 << 20)),
+        cost_estimate=pl.CostEstimate(flops=0, bytes_accessed=2 * size, transcendentals=0),
+    )(order, *pieces)
+
+
+def gather_weight(shard):
+    place = place_of()
+    near = jnp.where((place & 2) == 0, 4, 1)
+    far = 5 - near
+    other = place ^ 2
+    first = permute(shard, first_rule)
+    second = permute(shard, second_rule)
+    both = permute(first, second_rule)
+    held = [shard, first, second, both]
+    pieces = held + [permute(piece, core_rule) for piece in held]
+    order = [place, place ^ near, place ^ far, place ^ 5]
+    order += [other, other ^ far, other ^ near, other ^ 5]
+    return assemble(pieces, jnp.stack(order).astype(jnp.int32))
 
 
 def reduce_scatter(partial):
@@ -203,6 +314,7 @@
     fsdp_index = lax.axis_index("fsdp")
     held = (place >> 2) * 2 + (place & 1)
     rows = width // SHARDS
+    replicas = lax.axis_size("rep")
 
     small = jnp.concatenate(
         [
@@ -214,13 +326,13 @@
             jnp.broadcast_to(valid_slots.astype(jnp.bfloat16), (128,)),
         ]
     )
-    small_all = lax.all_gather(small, GROUP, axis=0)
-    full_qkv = lax.all_gather(qkv_weight, GROUP, axis=0, tiled=True)
-    latent_low = permute(latent_in, swap_rule)
-    cotangent_low = permute(cotangent, swap_rule)
-    full_out = lax.all_gather(out_weight, GROUP, axis=0, tiled=True)
-    full_up = lax.all_gather(up_weight, GROUP, axis=0, tiled=True)
-    full_down = lax.all_gather(down_weight, GROUP, axis=0, tiled=True)
+    small_all = gather_group(small)
+    full_qkv = gather_weight(qkv_weight)
+    latent_low = swap_halves(latent_in)
+    full_out = gather_weight(out_weight)
+    cotangent_low = swap_halves(cotangent)
+    full_up = gather_weight(up_weight)
+    full_down = gather_weight(down_weight)
 
     bounds = [0, width]
     for bias in (qv_bias, out_bias, up_bias, down_bias):
@@ -241,8 +353,13 @@
         place * ada_bias.shape[0],
         0,
     )
-    modulation_all = lax.psum(matmul(silu_mine, ada_weight) + ada_bias_row, GROUP)
-    modulation = lax.dynamic_slice_in_dim(modulation_all, held, 1, 0)
+    modulation = matmul(silu_mine, ada_weight) + ada_bias_row
+    for bit, count in ((4, 2), (1, 1)):
+        upper = (place & bit) != 0
+        sent = jnp.where(upper, modulation[:count], modulation[count:])
+        kept = jnp.where(upper, modulation[count:], modulation[:count])
+        modulation = kept + permute(sent, lambda at: at ^ bit)
+    modulation = modulation + permute(modulation, core_rule)
     shift_one, scale_one, gate_one, shift_two, scale_two, gate_two = jnp.split(
         modulation, 6, axis=-1
     )
@@ -273,21 +390,21 @@
     branch_two = matmul(activated_low, full_down) + full_down_bias
     mask_row = slot_mask[0]
     block_out = (mask_row * (middle + gate_two * branch_two)).astype(jnp.bfloat16)
-    block_out = permute(block_out[None], swap_rule)
+    block_out = swap_halves(block_out[None])
 
     d_out = cotangent_low[0].astype(jnp.float32) * mask_row
     d_gate_two = jnp.sum(d_out * branch_two, axis=0)
     d_branch_two = (gate_two * d_out).astype(jnp.bfloat16)
     down_grad = matmul_left(activated_low, d_branch_two).astype(jnp.bfloat16)
-    down_shard = lax.psum_scatter(down_grad, GROUP, scatter_dimension=0, tiled=True)
-    down_total = lax.psum(down_shard, "rep").astype(jnp.float32)
+    down_shard = reduce_scatter(down_grad.reshape(SHARDS, hidden_width // SHARDS, width))
+    down_total = reduce_replicas(down_shard, replicas)
     down_bias_grad = jnp.sum(d_branch_two.astype(jnp.float32), axis=0)
     d_activated = matmul_right(d_branch_two, full_down)
     d_preact = gelu_pull(d_activated)[0].astype(jnp.bfloat16)
 
     up_grad = matmul_left(hidden_two, d_preact).astype(jnp.bfloat16)
     up_shard = reduce_scatter(up_grad.reshape(SHARDS, rows, hidden_width))
-    up_total = lax.psum(up_shard.astype(jnp.bfloat16), "rep").astype(jnp.float32)
+    up_total = reduce_replicas(up_shard, replicas)
     up_bias_grad = jnp.sum(d_preact.astype(jnp.float32), axis=0)
     d_hidden_two = matmul_right(d_preact, full_up)
     d_shift_two = jnp.sum(d_hidden_two, axis=0)
@@ -298,7 +415,7 @@
 
     out_grad = matmul_left(attended_low, d_branch_one).astype(jnp.bfloat16)
     out_shard = reduce_scatter(out_grad.reshape(SHARDS, rows, width))
-    out_total = lax.psum(out_shard.astype(jnp.bfloat16), "rep").astype(jnp.float32)
+    out_total = reduce_replicas(out_shard, replicas)
     out_bias_grad = jnp.sum(d_branch_one.astype(jnp.float32), axis=0)
     d_attended = matmul_right(d_branch_one, full_out).astype(jnp.bfloat16)
     d_query, d_keys_all, d_values_all = attn_backward(
@@ -311,13 +428,13 @@
 
     qkv_grad = matmul_left(hidden_one, d_projected).astype(jnp.bfloat16)
     qkv_shard = reduce_scatter(qkv_grad.reshape(SHARDS, rows, 3 * width))
-    qkv_total = lax.psum(qkv_shard.astype(jnp.bfloat16), "rep").astype(jnp.float32)
+    qkv_total = reduce_replicas(qkv_shard, replicas)
     column_sums = jnp.sum(d_projected.astype(jnp.float32), axis=0)
     d_hidden_one = matmul_right(d_projected, full_qkv)
     d_shift_one = jnp.sum(d_hidden_one, axis=0)
     d_scale_one = jnp.sum(d_hidden_one * normed_one, axis=0)
     latent_grad = d_middle + norm_back(d_hidden_one * (1.0 + scale_one), normed_one, inverse_one)
-    latent_grad = permute(latent_grad.astype(jnp.bfloat16)[None], swap_rule).astype(jnp.float32)
+    latent_grad = swap_halves(latent_grad.astype(jnp.bfloat16)[None]).astype(jnp.float32)
 
     bias_grads = (
         jnp.concatenate([column_sums[:width], column_sums[2 * width :]]),
@@ -327,7 +444,7 @@
     )
     sums = [d_shift_one, d_scale_one, d_gate_one, d_shift_two, d_scale_two, d_gate_two]
     ada_width = 6 * width
-    sums_all = lax.all_gather(jnp.concatenate(sums + list(bias_grads)), GROUP, axis=0)
+    sums_all = gather_group(jnp.concatenate(sums + list(bias_grads)))
     d_group = sums_all[:, :ada_width].reshape(2, 2, 2, ada_width).sum(1).reshape(4, ada_width)
     bias_mine = []
     start = ada_width
@@ -344,13 +461,14 @@
     )
     cond_mine = lax.dynamic_slice_in_dim(cond_group, place * rows, rows, 1)
     cond_part = jax.vjp(jax.nn.silu, cond_mine)[1](d_silu)[0]
-    cond_all = lax.all_gather(cond_part, GROUP, axis=1, tiled=True)
-    cond_grad = lax.dynamic_slice_in_dim(cond_all, fsdp_index, 1, 0)
+    cond_all = gather_group(cond_part)
+    cond_grad = lax.dynamic_index_in_dim(cond_all, fsdp_index, 1, keepdims=False)
+    cond_grad = cond_grad.reshape(1, width)
 
     packed = jnp.concatenate(
         [d_group.reshape(-1), silu_mine.astype(jnp.float32).reshape(-1)] + bias_mine
     )
-    packed_all = lax.all_gather(packed, "rep", axis=0)
+    packed_all = gather_replicas(packed, replicas)
     d_all = packed_all[:, : 4 * ada_width].reshape(-1, ada_width)
     silu_all = packed_all[:, 4 * ada_width : 4 * ada_width + 4 * rows].reshape(-1, rows)
     ada_total = lax.dot_general(

time: 787 us -> 873 us (1.11)
  starting transfers between devices: 18.1 us -> 110 us
  blocking collectives: 56.5 us -> 0 us
  local copies, waits for them, and re-layouts: 96.4 us -> 146 us
  other arithmetic: 65.3 us -> 103 us
  waiting for transfers between devices: 338 us -> 308 us
  Pallas kernels: 0 us -> 15.7 us
  between operations: 17.1 us -> 3.06 us
  matrix products: 179 us -> 169 us
    psum x2 -> x0, waiting for transfers between devices: 143 us -> none  [the longest x1 95 us: per_device(): lax.psum(qkv_shard.astype(jnp.bfloat16), 'rep').astype(jnp.float32)]
    all_gather x4 -> x0, waiting for transfers between devices: 125 us -> none  [the longest x1 53.5 us: per_device(): full_qkv = lax.all_gather(qkv_weight, GROUP, axis=0, tiled=True)]
    ppermute x0 -> x31, waiting for transfers between devices: none -> 124 us  [the longest x15 58.5 us: gather_replicas(): stacked.append(lax.ppermute(values, 'rep', pairs))]
    ppermute x15 -> x54, waiting for transfers between devices: 68.7 us -> 184 us  [permute(): return lax.ppermute(values, GROUP, pairs_by(rule))]
    all_gather x3 -> x0, blocking collectives: 56.5 us -> none  [the longest x1 22.1 us: per_device(): cond_all = lax.all_gather(cond_part, GROUP, axis=1, tiled=True)]
    ppermute x0 -> x31, starting transfers between devices: none -> 55.2 us  [the longest x15 24.1 us: gather_replicas(): stacked.append(lax.ppermute(values, 'rep', pairs))]
    ppermute x15 -> x54, starting transfers between devices: 17.7 us -> 54.3 us  [permute(): return lax.ppermute(values, GROUP, pairs_by(rule))]
    unnamed x115 -> x170, local copies, waits for them, and re-layouts: 12.8 us -> 32.2 us
  transfers between devices with their start and end apart: 23 -> 85, of which waited for: 9 -> 34; matrix products, arithmetic and copies ran while one was open for 33% -> 36% of each run, Pallas kernels for 0% -> 2%
where the time goes in v2:
time: 873 us; the launch traced here: 861 us
  waiting for transfers between devices  308 us (35%)
  matrix products  169 us (19%)
  local copies, waits for them, and re-layouts  146 us (17%)
  starting transfers between devices  110 us (13%)
  other arithmetic  103 us (12%)
  Pallas kernels  15.7 us (2%)
    ppermute x54, waiting for transfers between devices, permute(): return lax.ppermute(values, GROUP, pairs_by(rule))  184 us
    ppermute x15, waiting for transfers between devices, gather_replicas(): stacked.append(lax.ppermute(values, 'rep', pairs))  58.5 us
    ppermute x54, starting transfers between devices, permute(): return lax.ppermute(values, GROUP, pairs_by(rule))  54.3 us
    ppermute x12, waiting for transfers between devices, reduce_replicas(): total = total + lax.ppermute(piece, 'rep', pairs).astype(jnp.float32)  52.5 us
    dot_general x4, matrix products, matmul_right(): lax.dot_general(left, right, (((1,), (1,)), ((), ())), preferred_element_...  41.1 us
    dot_general x5, matrix products, matmul(): return jnp.dot(left, right, preferred_element_type=jnp.float32)  38 us
    dot_general x4, matrix products, matmul_left(): lax.dot_general(left, right, (((0,), (0,)), ((), ())), preferred_element_...  33 us
    unnamed x170, local copies, waits for them, and re-layouts  32.2 us
  transfers between devices with their start and end apart: 85, of which 34 were waited for; matrix products, arithmetic and copies ran while one was open for 36% of the time, Pallas kernels for 2%

profile of v2, /device:TPU:9, one launch (start us, length us, event | category | flops | bytes accessed | tf_op | source)
XLA Modules:
  0.0 860.6 jit_solution(14821141603474208974)
XLA Ops:
  36.6 17.8 %collective-permute-done.17.refs_3_ = bf16[144,1152]{1,0:T(8,128)(2,1)S(1)} collective-permute-done((bf16[144,1152]{1,0:T(8,128)(2,1)S(1)}, bf16[144,1152]{1,0:T(8,128)(2,1)S(1)}, u32[]{:S(2)}, u32[]{:S(2)}) %collective-permute-start.17) | collective-permute-done | bytes 331808 | tf_op jit(solution)/shard_map/ppermute | solution.py:72
  63.9 17.3 %collective-permute-done.9.refs_3_ = bf16[144,3456]{1,0:T(8,128)(2,1)} collective-permute-done((bf16[144,3456]{1,0:T(8,128)(2,1)}, bf16[144,3456]{1,0:T(8,128)(2,1)}, u32[]{:S(2)}, u32[]{:S(2)}) %collective-permute-start.9) | collective-permute-done | bytes 995360 | tf_op jit(solution)/shard_map/ppermute | solution.py:72
  83.2 13.1 %collective-permute-done.3 = bf16[1,512,1152]{2,1,0:T(8,128)(2,1)} collective-permute-done((bf16[1,512,1152]{2,1,0:T(8,128)(2,1)}, bf16[1,512,1152]{2,1,0:T(8,128)(2,1)}, u32[]{:S(2)}, u32[]{:S(2)}) %collective-permute-start.3) | collective-permute-done | bytes 1179680 | tf_op jit(solution)/shard_map/ppermute | solution.py:78
  102.3 4.5 shard_map.237
  108.0 17.1 %collective-permute-done.30.refs_2_ = bf16[576,1152]{1,0:T(8,128)(2,1)} collective-permute-done((bf16[576,1152]{1,0:T(8,128)(2,1)S(1)}, bf16[576,1152]{1,0:T(8,128)(2,1)}, u32[]{:S(2)}, u32[]{:S(2)}) %collective-permute-start.30) | collective-permute-done | bytes 1327136 | tf_op jit(solution)/shard_map/ppermute | solution.py:72
  130.6 11.2 %collective-permute-done.31.refs_3_ = bf16[576,1152]{1,0:T(8,128)(2,1)} collective-permute-done((bf16[576,1152]{1,0:T(8,128)(2,1)}, bf16[576,1152]{1,0:T(8,128)(2,1)}, u32[]{:S(2)}, u32[]{:S(2)}) %collective-permute-start.31) | collective-permute-done | bytes 1327136 | tf_op jit(solution)/shard_map/ppermute | solution.py:72
  142.2 5.5 add_convert_fusion
  150.3 5.8 collective-permute-done.23.refs_2_
  159.0 11.2 %collective-permute-done.24.refs_3_ = bf16[144,4608]{1,0:T(8,128)(2,1)} collective-permute-done((bf16[144,4608]{1,0:T(8,128)(2,1)}, bf16[144,4608]{1,0:T(8,128)(2,1)}, u32[]{:S(2)}, u32[]{:S(2)}) %collective-permute-start.24) | collective-permute-done | bytes 1327136 | tf_op jit(solution)/shard_map/ppermute | solution.py:72
  197.1 3.9 copy-done.1
  201.0 4.1 collective-permute-start.37
  205.1 4.9 shard_map.239
  210.0 4.0 copy-done.2
  219.3 4.3 copy.41
  223.5 4.3 copy.43
  228.9 39.8 %while.26 = (s32[]{:T(128)}, bf16[4,1,512,288]{2,3,1,0:T(8,128)(2,1)}, f32[4,1,4,512]{3,2,1,0:T(4,128)S(1)}, s32[4]{0:T(128)S(1)}, bf16[1,1024,1152]{1,2,0:T(8,1...) while((s32[]{:T(128)}, ...), condition=%wide.region_5.6_spmd, body=%wide.region_2.5_spmd.sunk | while | flops 622852096 | bytes 30539968 | solution.py:244
  268.7 5.8 fusion.95
  274.9 13.5 %fusion.86 = f32[512,4608]{1,0:T(8,128)} fusion(bf16[1152,4608]{1,0:T(8,128)(2,1)} %copy-done.2, f32[512,1152]{1,0:T(8,128)S(1)} %get-tuple-element.226, f32[1152]{0:T(1024)S(1)} %get-tuple-element.174, f32[1152]{0:T(1024)S(1)} %get-tuple-element.175, f32[512]{0:T(512)S(1)} %add_rsqrt_fusion, f32[512]{0:T(512)S(1)} %broadcast_multiply_fusion.4), kind=kOutput, calls=%fused_computation.284 | convolution fusion | flops 5438767104 | bytes 22426624 | tf_op jit(solution)/shard_map/dot_general | solution.py:32
  288.5 12.8 %convert_reduce_fusion.3 = (f32[1152]{0:T(1024)}, f32[1152]{0:T(1024)}, bf16[1,512,1152]{2,1,0:T(8,128)(2,1)S(1)}, bf16[1,512,1152]{2,1,0:T(8,128)(2,1)}) fusion(f32[]{:T(128)} %bitcast.24, f32[1152]{0:T(1024)S(1)} %get-tuple-element.173, bf16[1,512,1152]{2,1,0:T(8,128)(2,1)} %param.31, bf16[1,512,1152]{2,1,0:T(8,128)(2,1)} %collective-permute-done.37, ...), kind=kOutput, calls=%fused_computation.106 | convolution fusion | flops 5467666432 | bytes 27168772 | tf_op jit(solution)/shard_map/dot_general | solution.py:32
  301.2 16.2 %convert_reduce_fusion = (f32[4608]{0:T(1024)}, bf16[512,4608]{1,0:T(8,128)(2,1)}) fusion(f32[512,4608]{1,0:T(8,128)} %fusion.86, f32[4608]{0:T(1024)S(1)} %reshape.337, bf16[4608,1152]{1,0:T(8,128)(2,1)S(1)} %bitcast.344, bf16[1,512,1152]{2,1,0:T(8,128)(2,1)S(1)} %get-tuple-element.224, f32[]{:T(128)} %bitcast.24, f32[1152]{0:T(1024)S(1)} %get-tuple-element.173), kind=kOutput, calls=%fused_computation.47 | convolution fusion | flops 5492436480 | bytes 25993732 | tf_op jit(solution)/shard_map/dot_general | solution.py:42
  317.4 12.7 %multiply_reduce_fusion.2 = (f32[1152]{0:T(1024)}, f32[512]{0:T(512)S(1)}, f32[512]{0:T(512)S(1)}, f32[1152]{0:T(1024)}, f32[512,1152]{1,0:T(8,128)S(1)}) fusion(f32[512,1152]{1,0:T(8,128)} %copy-done.32, f32[512]{0:T(512)S(1)} %add_rsqrt_fusion, f32[512]{0:T(512)S(1)} %broadcast_multiply_fusion.4, f32[1152]{0:T(1024)S(1)} %get-tuple-element.175, ...), kind=kOutput, calls=%fused_computation.108 | convolution fusion | flops 5441123328 | bytes 20076032 | tf_op jit(solution)/shard_map/dot_general | solution.py:42
  330.1 4.3 convert_reduce_fusion.4
  340.6 11.8 %convolution_convert_fusion = bf16[4608,1152]{1,0:T(8,128)(2,1)} fusion(bf16[1,512,1152]{2,1,0:T(8,128)(2,1)S(1)} %get-tuple-element.224, f32[]{:T(128)} %bitcast.24, f32[1152]{0:T(1024)S(1)} %get-tuple-element.173, f32[512,4608]{1,0:T(8,128)S(1)} %bitcast.397, f32[4608]{0:T(1024)S(1)} %reshape.337), kind=kOutput, calls=%fused_computation.29 | convolution fusion | flops 5467078656 | bytes 21256708 | tf_op jit(solution)/shard_map/dot_general | solution.py:36
  357.1 69.3 %while.27 = (s32[]{:T(128)}, bf16[4,1,512,288]{2,3,1,0:T(8,128)(2,1)}, f32[4,1,1024,288]{2,3,1,0:T(8,128)}, f32[4,1,1024,288]{2,3,1,0:T(8,128)}, s32[4]{0:T(128)...) while((s32[]{:T(128)}, ...), condition=%wide.region_12.13_spmd, body=%wide.region_10.12_spmd.sunk | while | flops 1535703040 | bytes 77422808 | solution.py:290
  429.0 4.2 fusion.22
  433.7 9.0 %convolution_convert_fusion.1 = bf16[1152,4608]{1,0:T(8,128)(2,1)S(1)} fusion(bf16[512,4608]{1,0:T(8,128)(2,1)} %get-tuple-element.298, f32[512,1152]{1,0:T(8,128)S(1)} %copy-done.34, f32[1152]{0:T(1024)S(1)} %copy-done.64, f32[1152]{0:T(1024)S(1)} %get-tuple-element.175, f32[512]{0:T(512)S(1)} %add_rsqrt_fusion, f32[512]{0:T(512)S(1)} %broadcast_multiply_fusion.4), kind=kOutput, calls=%fused_computation.30 | convolution fusion | flops 5444075520 | bytes 17708032 | tf_op jit(solution)/shard_map/dot_general | solution.py:36
  442.8 4.2 fusion.34
  472.5 4.0 fusion.21
  476.6 9.3 %fusion.42 = (f32[1152]{0:T(1024)S(1)}, f32[512]{0:T(512)S(1)}, f32[512]{0:T(512)S(1)}, f32[1152]{0:T(1024)S(1)}, f32[512,1152]{1,0:T(8,128)S(1)}) fusion(bf16[1,512,1152]{2,1,0:T(8,128)(2,1)S(1)} %copy-done.37, f32[512]{0:T(512)S(1)} %copy-done.70, f32[512]{0:T(512)S(1)} %copy-done.60, f32[1152]{0:T(1024)S(1)} %copy-done.57, ...), kind=kOutput, calls=%fused_computation.99 | convolution fusion | flops 4089836544 | bytes 15062528 | tf_op jit(solution)/shard_map/dot_general | solution.py:42
  486.5 9.0 %convolution_convert_fusion.2 = bf16[1152,3456]{1,0:T(8,128)(2,1)} fusion(bf16[512,2304]{0,1:T(8,128)(2,1)S(1)} %fusion.21, bf16[512,1152]{0,1:T(8,128)(2,1)S(1)} %bitcast.377, bf16[1,512,1152]{2,1,0:T(8,128)(2,1)S(1)} %copy-done.37, f32[1152]{0:T(1024)S(1)} %copy-done.62, f32[1152]{0:T(1024)S(1)} %copy-done.57, f32[512]{0:T(512)S(1)} %copy-done.70, ...), kind=kOutput, calls=%fused_computation.31 | convolution fusion | flops 4091461632 | bytes 12694528 | tf_op jit(solution)/shard_map/dot_general | solution.py:36
  554.8 6.2 fusion.101
  563.9 5.5 fusion.10
  570.2 5.4 fusion.9
  577.9 4.3 fusion.18
  582.8 18.6 %collective-permute-done.68 = bf16[2,144,4608]{2,1,0:T(8,128)(2,1)} collective-permute-done((bf16[2,144,4608]{2,1,0:T(8,128)(2,1)S(1)}, bf16[2,144,4608]{2,1,0:T(8,128)(2,1)}, u32[]{:S(2)}, u32[]{:S(2)}) %collective-permute-start.68) | collective-permute-done | bytes 2654240 | tf_op jit(solution)/shard_map/ppermute | solution.py:72
  604.5 39.5 %collective-permute-done.77 = bf16[2,576,1152]{2,1,0:T(8,128)(2,1)} collective-permute-done((bf16[2,576,1152]{2,1,0:T(8,128)(2,1)S(1)}, bf16[2,576,1152]{2,1,0:T(8,128)(2,1)}, u32[]{:S(2)}, u32[]{:S(2)}) %collective-permute-start.77) | collective-permute-done | bytes 2654240 | tf_op jit(solution)/shard_map/ppermute | solution.py:72
  648.1 31.2 %collective-permute-done.50 = bf16[2,144,3456]{2,1,0:T(8,128)(2,1)S(1)} collective-permute-done((bf16[2,144,3456]{2,1,0:T(8,128)(2,1)S(1)}, bf16[2,144,3456]{2,1,0:T(8,128)(2,1)S(1)}, u32[]{:S(2)}, u32[]{:S(2)}) %collective-permute-start.50) | collective-permute-done | bytes 1990688 | tf_op jit(solution)/shard_map/ppermute | solution.py:72
  690.5 4.1 fusion.87
  709.5 27.5 %collective-permute-done.54 = bf16[36,3456]{1,0:T(8,128)(2,1)} collective-permute-done((bf16[36,3456]{1,0:T(8,128)(2,1)}, bf16[36,3456]{1,0:T(8,128)(2,1)}, u32[]{:S(2)}, u32[]{:S(2)}) %collective-permute-start.54) | collective-permute-done | bytes 248864 | tf_op jit(solution)/shard_map/ppermute | solution.py:115
  737.0 7.1 collective-permute-start.81
  752.0 13.8 %collective-permute-done.80 = bf16[144,1152]{1,0:T(8,128)(2,1)S(1)} collective-permute-done((bf16[144,1152]{1,0:T(8,128)(2,1)S(1)}, bf16[144,1152]{1,0:T(8,128)(2,1)S(1)}, u32[]{:S(2)}, u32[]{:S(2)}) %collective-permute-start.80) | collective-permute-done | bytes 331808 | tf_op jit(solution)/shard_map/ppermute | solution.py:115
  765.9 9.1 %collective-permute-start.75 = (bf16[36,4608]{1,0:T(8,128)(2,1)S(1)}, bf16[36,4608]{1,0:T(8,128)(2,1)S(1)}, u32[]{:S(2)}, u32[]{:S(2)}) collective-permute-start(bf16[36,4608]{1,0:T(8,128)(2,1)S(1)} %fusion.55), channel_id=1, source_target_pairs={{0,24},{8,0},{16,8},{24,16},{1,25},{9,1},{17,9},{25,17},{2,26},{10... | collective-permute-start | bytes 995336 | tf_op jit(solution)/shard_map/ppermute | solution.py:100
  774.9 10.9 %collective-permute-done.79 = bf16[144,1152]{1,0:T(8,128)(2,1)S(1)} collective-permute-done((bf16[144,1152]{1,0:T(8,128)(2,1)S(1)}, bf16[144,1152]{1,0:T(8,128)(2,1)S(1)}, u32[]{:S(2)}, u32[]{:S(2)}) %collective-permute-start.79) | collective-permute-done | bytes 331808 | tf_op jit(solution)/shard_map/ppermute | solution.py:115
  789.9 12.8 %collective-permute-done.56 = bf16[36,3456]{1,0:T(8,128)(2,1)S(1)} collective-permute-done((bf16[36,3456]{1,0:T(8,128)(2,1)S(1)}, bf16[36,3456]{1,0:T(8,128)(2,1)S(1)}, u32[]{:S(2)}, u32[]{:S(2)}) %collective-permute-start.56) | collective-permute-done | bytes 248864 | tf_op jit(solution)/shard_map/ppermute | solution.py:100
  803.5 12.6 %collective-permute-done.55 = bf16[36,3456]{1,0:T(8,128)(2,1)S(1)} collective-permute-done((bf16[36,3456]{1,0:T(8,128)(2,1)S(1)}, bf16[36,3456]{1,0:T(8,128)(2,1)S(1)}, u32[]{:S(2)}, u32[]{:S(2)}) %collective-permute-start.55) | collective-permute-done | bytes 248864 | tf_op jit(solution)/shard_map/ppermute | solution.py:100
  823.0 11.6 %collective-permute-done.74 = bf16[36,4608]{1,0:T(8,128)(2,1)S(1)} collective-permute-done((bf16[36,4608]{1,0:T(8,128)(2,1)S(1)}, bf16[36,4608]{1,0:T(8,128)(2,1)S(1)}, u32[]{:S(2)}, u32[]{:S(2)}) %collective-permute-start.74) | collective-permute-done | bytes 331808 | tf_op jit(solution)/shard_map/ppermute | solution.py:100
  834.6 8.0 collective-permute-done.73
  849.7 7.1 collective-permute-done.82
  (564 shorter events, 370.7 us)
Async XLA Ops:
  20.7 36.2 %collective-permute-start.7 = (bf16[144,3456]{1,0:T(8,128)(2,1)}, bf16[144,3456]{1,0:T(8,128)(2,1)}, u32[]{:S(2)}, u32[]{:S(2)}) collective-permute-start(bf16[144,3456]{1,0:T(8,128)(2,1)} %refs_0_.4), channel_id=1, source_target_pairs={{0,4},{1,5},{2,3},{3,2},{4,0},{5,1},{6,7},{7,6},{8,12},{9,13},{10,... | collective-permute-start | bytes 2985992 | tf_op jit(solution)/shard_map/ppermute | solution.py:72
  25.8 36.4 %collective-permute-start.8 = (bf16[144,3456]{1,0:T(8,128)(2,1)}, bf16[144,3456]{1,0:T(8,128)(2,1)}, u32[]{:S(2)}, u32[]{:S(2)}) collective-permute-start(bf16[144,3456]{1,0:T(8,128)(2,1)} %refs_0_.4), channel_id=1, source_target_pairs={{0,1},{1,0},{2,6},{3,7},{4,5},{5,4},{6,2},{7,3},{8,9},{9,8},{10,14... | collective-permute-start | bytes 2985992 | tf_op jit(solution)/shard_map/ppermute | solution.py:72
  27.1 35.3 %collective-permute-start.10 = (bf16[144,3456]{1,0:T(8,128)(2,1)}, bf16[144,3456]{1,0:T(8,128)(2,1)S(1)}, u32[]{:S(2)}, u32[]{:S(2)}) collective-permute-start(bf16[144,3456]{1,0:T(8,128)(2,1)} %refs_0_.4), channel_id=1, source_target_pairs={{0,2},{1,3},{2,0},{3,1},{4,6},{5,7},{6,4},{7,5},{8,10},{9,11},{10,... | collective-permute-start | bytes 2985992 | tf_op jit(solution)/shard_map/ppermute | solution.py:72
  56.3 41.3 %collective-permute-start.29 = (bf16[576,1152]{1,0:T(8,128)(2,1)S(1)}, bf16[576,1152]{1,0:T(8,128)(2,1)}, u32[]{:S(2)}, u32[]{:S(2)}) collective-permute-start(bf16[576,1152]{1,0:T(8,128)(2,1)S(1)} %copy-done.6), channel_id=1, source_target_pairs={{0,4},{1,5},{2,3},{3,2},{4,0},{5,1},{6,7},{7,6},{8,12},{9,13},{10,... | collective-permute-start | bytes 3981320 | tf_op jit(solution)/shard_map/ppermute | solution.py:72
  58.8 37.6 %collective-permute-start.3 = (bf16[1,512,1152]{2,1,0:T(8,128)(2,1)}, bf16[1,512,1152]{2,1,0:T(8,128)(2,1)}, u32[]{:S(2)}, u32[]{:S(2)}) collective-permute-start(bf16[1,512,1152]{2,1,0:T(8,128)(2,1)} %param.18), channel_id=1, source_target_pairs={{1,2},{2,1},{5,6},{6,5},{9,10},{10,9},{13,14},{14,13},{17,18},{18,... | collective-permute-start | bytes 3538952 | tf_op jit(solution)/shard_map/ppermute | solution.py:78
  62.3 35.6 %collective-permute-start.11 = (bf16[144,3456]{1,0:T(8,128)(2,1)}, bf16[144,3456]{1,0:T(8,128)(2,1)}, u32[]{:S(2)}, u32[]{:S(2)}) collective-permute-start(bf16[144,3456]{1,0:T(8,128)(2,1)} %collective-permute-done.7.refs_1_), channel_id=1, source_target_pairs={{0,2},{1,3},{2,0},{3,1},{4,6},{5,7},{6,4},{7,5},{8,10},{9,11},{10,... | collective-permute-start | bytes 2985992 | tf_op jit(solution)/shard_map/ppermute | solution.py:72
  63.3 34.6 %collective-permute-start.12 = (bf16[144,3456]{1,0:T(8,128)(2,1)}, bf16[144,3456]{1,0:T(8,128)(2,1)}, u32[]{:S(2)}, u32[]{:S(2)}) collective-permute-start(bf16[144,3456]{1,0:T(8,128)(2,1)} %collective-permute-done.8.refs_2_), channel_id=1, source_target_pairs={{0,2},{1,3},{2,0},{3,1},{4,6},{5,7},{6,4},{7,5},{8,10},{9,11},{10,... | collective-permute-start | bytes 2985992 | tf_op jit(solution)/shard_map/ppermute | solution.py:72
  97.6 29.8 %collective-permute-start.32 = (bf16[576,1152]{1,0:T(8,128)(2,1)S(1)}, bf16[576,1152]{1,0:T(8,128)(2,1)}, u32[]{:S(2)}, u32[]{:S(2)}) collective-permute-start(bf16[576,1152]{1,0:T(8,128)(2,1)S(1)} %copy-done.6), channel_id=1, source_target_pairs={{0,2},{1,3},{2,0},{3,1},{4,6},{5,7},{6,4},{7,5},{8,10},{9,11},{10,... | collective-permute-start | bytes 3981320 | tf_op jit(solution)/shard_map/ppermute | solution.py:72
  97.9 31.5 %collective-permute-start.22 = (bf16[144,4608]{1,0:T(8,128)(2,1)}, bf16[144,4608]{1,0:T(8,128)(2,1)}, u32[]{:S(2)}, u32[]{:S(2)}) collective-permute-start(bf16[144,4608]{1,0:T(8,128)(2,1)} %refs_0_.6), channel_id=1, source_target_pairs={{0,4},{1,5},{2,3},{3,2},{4,0},{5,1},{6,7},{7,6},{8,12},{9,13},{10,... | collective-permute-start | bytes 3981320 | tf_op jit(solution)/shard_map/ppermute | solution.py:72
  97.9 44.0 %collective-permute-start.31 = (bf16[576,1152]{1,0:T(8,128)(2,1)}, bf16[576,1152]{1,0:T(8,128)(2,1)}, u32[]{:S(2)}, u32[]{:S(2)}) collective-permute-start(bf16[576,1152]{1,0:T(8,128)(2,1)} %collective-permute-done.29.refs_1_), channel_id=1, source_target_pairs={{0,1},{1,0},{2,6},{3,7},{4,5},{5,4},{6,2},{7,3},{8,9},{9,8},{10,14... | collective-permute-start | bytes 3981320 | tf_op jit(solution)/shard_map/ppermute | solution.py:72
  107.6 48.5 %collective-permute-start.23 = (bf16[144,4608]{1,0:T(8,128)(2,1)}, bf16[144,4608]{1,0:T(8,128)(2,1)}, u32[]{:S(2)}, u32[]{:S(2)}) collective-permute-start(bf16[144,4608]{1,0:T(8,128)(2,1)} %refs_0_.6), channel_id=1, source_target_pairs={{0,1},{1,0},{2,6},{3,7},{4,5},{5,4},{6,2},{7,3},{8,9},{9,8},{10,14... | collective-permute-start | bytes 3981320 | tf_op jit(solution)/shard_map/ppermute | solution.py:72
  125.1 31.3 %collective-permute-start.33 = (bf16[576,1152]{1,0:T(8,128)(2,1)}, bf16[576,1152]{1,0:T(8,128)(2,1)S(1)}, u32[]{:S(2)}, u32[]{:S(2)}) collective-permute-start(bf16[576,1152]{1,0:T(8,128)(2,1)} %collective-permute-done.29.refs_1_), channel_id=1, source_target_pairs={{0,2},{1,3},{2,0},{3,1},{4,6},{5,7},{6,4},{7,5},{8,10},{9,11},{10,... | collective-permute-start | bytes 3981320 | tf_op jit(solution)/shard_map/ppermute | solution.py:72
  127.4 30.3 %collective-permute-start.34 = (bf16[576,1152]{1,0:T(8,128)(2,1)}, bf16[576,1152]{1,0:T(8,128)(2,1)S(1)}, u32[]{:S(2)}, u32[]{:S(2)}) collective-permute-start(bf16[576,1152]{1,0:T(8,128)(2,1)} %collective-permute-done.30.refs_2_), channel_id=1, source_target_pairs={{0,2},{1,3},{2,0},{3,1},{4,6},{5,7},{6,4},{7,5},{8,10},{9,11},{10,... | collective-permute-start | bytes 3981320 | tf_op jit(solution)/shard_map/ppermute | solution.py:72
  129.4 40.8 %collective-permute-start.24 = (bf16[144,4608]{1,0:T(8,128)(2,1)}, bf16[144,4608]{1,0:T(8,128)(2,1)}, u32[]{:S(2)}, u32[]{:S(2)}) collective-permute-start(bf16[144,4608]{1,0:T(8,128)(2,1)} %collective-permute-done.22.refs_1_), channel_id=1, source_target_pairs={{0,1},{1,0},{2,6},{3,7},{4,5},{5,4},{6,2},{7,3},{8,9},{9,8},{10,14... | collective-permute-start | bytes 3981320 | tf_op jit(solution)/shard_map/ppermute | solution.py:72
  156.1 58.0 %collective-permute-start.14 = (bf16[512,2304]{1,0:T(8,128)(2,1)}, bf16[512,2304]{1,0:T(8,128)(2,1)}, u32[]{:S(2)}, u32[]{:S(2)}) collective-permute-start(bf16[512,2304]{1,0:T(8,128)(2,1)} %slice.184), channel_id=1, source_target_pairs={{0,2},{1,3},{2,0},{3,1},{4,6},{5,7},{6,4},{7,5},{8,10},{9,11},{10,... | collective-permute-start | bytes 7077896 | tf_op jit(solution)/shard_map/ppermute | solution.py:72
  157.5 43.5 %collective-permute-start.25 = (bf16[144,4608]{1,0:T(8,128)(2,1)}, bf16[144,4608]{1,0:T(8,128)(2,1)}, u32[]{:S(2)}, u32[]{:S(2)}) collective-permute-start(bf16[144,4608]{1,0:T(8,128)(2,1)} %refs_0_.6), channel_id=1, source_target_pairs={{0,2},{1,3},{2,0},{3,1},{4,6},{5,7},{6,4},{7,5},{8,10},{9,11},{10,... | collective-permute-start | bytes 3981320 | tf_op jit(solution)/shard_map/ppermute | solution.py:72
  158.7 46.4 %collective-permute-start.26 = (bf16[144,4608]{1,0:T(8,128)(2,1)}, bf16[144,4608]{1,0:T(8,128)(2,1)}, u32[]{:S(2)}, u32[]{:S(2)}) collective-permute-start(bf16[144,4608]{1,0:T(8,128)(2,1)} %collective-permute-done.22.refs_1_), channel_id=1, source_target_pairs={{0,2},{1,3},{2,0},{3,1},{4,6},{5,7},{6,4},{7,5},{8,10},{9,11},{10,... | collective-permute-start | bytes 3981320 | tf_op jit(solution)/shard_map/ppermute | solution.py:72
  170.2 34.9 %collective-permute-start.27 = (bf16[144,4608]{1,0:T(8,128)(2,1)}, bf16[144,4608]{1,0:T(8,128)(2,1)}, u32[]{:S(2)}, u32[]{:S(2)}) collective-permute-start(bf16[144,4608]{1,0:T(8,128)(2,1)} %collective-permute-done.23.refs_2_), channel_id=1, source_target_pairs={{0,2},{1,3},{2,0},{3,1},{4,6},{5,7},{6,4},{7,5},{8,10},{9,11},{10,... | collective-permute-start | bytes 3981320 | tf_op jit(solution)/shard_map/ppermute | solution.py:72
  171.7 33.4 %collective-permute-start.28 = (bf16[144,4608]{1,0:T(8,128)(2,1)}, bf16[144,4608]{1,0:T(8,128)(2,1)}, u32[]{:S(2)}, u32[]{:S(2)}) collective-permute-start(bf16[144,4608]{1,0:T(8,128)(2,1)} %collective-permute-done.24.refs_3_), channel_id=1, source_target_pairs={{0,2},{1,3},{2,0},{3,1},{4,6},{5,7},{6,4},{7,5},{8,10},{9,11},{10,... | collective-permute-start | bytes 3981320 | tf_op jit(solution)/shard_map/ppermute | solution.py:72
  201.0 87.4 %collective-permute-start.37 = (bf16[1,512,1152]{2,1,0:T(8,128)(2,1)}, bf16[1,512,1152]{2,1,0:T(8,128)(2,1)}, u32[]{:S(2)}, u32[]{:S(2)}) collective-permute-start(bf16[1,512,1152]{2,1,0:T(8,128)(2,1)} %param.31), channel_id=1, source_target_pairs={{1,2},{2,1},{5,6},{6,5},{9,10},{10,9},{13,14},{14,13},{17,18},{18,... | collective-permute-start | bytes 3538952 | tf_op jit(solution)/shard_map/ppermute | solution.py:78
  352.4 108.4 %collective-permute-start.36 = (bf16[1,512,1152]{2,1,0:T(8,128)(2,1)}, bf16[1,512,1152]{2,1,0:T(8,128)(2,1)}, u32[]{:S(2)}, u32[]{:S(2)}) collective-permute-start(bf16[1,512,1152]{2,1,0:T(8,128)(2,1)} %get-tuple-element.251), channel_id=1, source_target_pairs={{1,2},{2,1},{5,6},{6,5},{9,10},{10,9},{13,14},{14,13},{17,18},{18,... | collective-permute-start | bytes 3538952 | tf_op jit(solution)/shard_map/ppermute | solution.py:78
  433.2 39.2 %collective-permute-start.38 = (bf16[512,2304]{0,1:T(8,128)(2,1)}, bf16[512,2304]{0,1:T(8,128)(2,1)}, u32[]{:S(2)}, u32[]{:S(2)}) collective-permute-start(bf16[512,2304]{0,1:T(8,128)(2,1)} %fusion.22), channel_id=1, source_target_pairs={{0,2},{1,3},{2,0},{3,1},{4,6},{5,7},{6,4},{7,5},{8,10},{9,11},{10,... | collective-permute-start | bytes 7077896 | tf_op jit(solution)/shard_map/ppermute | solution.py:72
  452.2 111.7 %collective-permute-start.67 = (bf16[2,2,144,4608]{3,2,1,0:T(8,128)(2,1)}, bf16[2,2,144,4608]{3,2,1,0:T(8,128)(2,1)}, u32[]{:S(2)}, u32[]{:S(2)}) collective-permute-start(bf16[2,2,144,4608]{3,2,1,0:T(8,128)(2,1)} %dynamic-slice_bitcast_fusion.2), channel_id=1, source_target_pairs={{0,2},{1,3},{2,0},{3,1},{4,6},{5,7},{6,4},{7,5},{8,10},{9,11},{10,... | collective-permute-start | bytes 15925256 | tf_op jit(solution)/shard_map/ppermute | solution.py:72
  466.6 37.9 %collective-permute-start.63 = (bf16[36,1152]{1,0:T(8,128)(2,1)}, bf16[36,1152]{1,0:T(8,128)(2,1)S(1)}, u32[]{:S(2)}, u32[]{:S(2)}) collective-permute-start(bf16[36,1152]{1,0:T(8,128)(2,1)} %get-tuple-element.284), channel_id=1, source_target_pairs={{0,24},{8,0},{16,8},{24,16},{1,25},{9,1},{17,9},{25,17},{2,26},{10... | collective-permute-start | bytes 248840 | tf_op jit(solution)/shard_map/ppermute | solution.py:115
  466.8 37.7 %collective-permute-start.62 = (bf16[36,1152]{1,0:T(8,128)(2,1)S(1)}, bf16[36,1152]{1,0:T(8,128)(2,1)}, u32[]{:S(2)}, u32[]{:S(2)}) collective-permute-start(bf16[36,1152]{1,0:T(8,128)(2,1)S(1)} %get-tuple-element.285), channel_id=1, source_target_pairs={{0,16},{8,24},{16,0},{24,8},{1,17},{9,25},{17,1},{25,9},{2,18},{10... | collective-permute-start | bytes 248840 | tf_op jit(solution)/shard_map/ppermute | solution.py:115
  469.1 35.4 %collective-permute-start.61 = (bf16[36,1152]{1,0:T(8,128)(2,1)S(1)}, bf16[36,1152]{1,0:T(8,128)(2,1)}, u32[]{:S(2)}, u32[]{:S(2)}) collective-permute-start(bf16[36,1152]{1,0:T(8,128)(2,1)S(1)} %get-tuple-element.283), channel_id=1, source_target_pairs={{0,8},{8,16},{16,24},{24,0},{1,9},{9,17},{17,25},{25,1},{2,10},{10... | collective-permute-start | bytes 248840 | tf_op jit(solution)/shard_map/ppermute | solution.py:115
  537.5 32.7 %collective-permute-start.76 = (bf16[2,2,576,1152]{3,2,1,0:T(8,128)(2,1)}, bf16[2,2,576,1152]{3,2,1,0:T(8,128)(2,1)}, u32[]{:S(2)}, u32[]{:S(2)}) collective-permute-start(bf16[2,2,576,1152]{3,2,1,0:T(8,128)(2,1)} %dynamic-slice_bitcast_fusion.1), channel_id=1, source_target_pairs={{0,2},{1,3},{2,0},{3,1},{4,6},{5,7},{6,4},{7,5},{8,10},{9,11},{10,... | collective-permute-start | bytes 15925256 | tf_op jit(solution)/shard_map/ppermute | solution.py:72
  545.0 32.9 %collective-permute-start.49 = (bf16[2,2,144,3456]{3,2,1,0:T(8,128)(2,1)}, bf16[2,2,144,3456]{3,2,1,0:T(8,128)(2,1)}, u32[]{:S(2)}, u32[]{:S(2)}) collective-permute-start(bf16[2,2,144,3456]{3,2,1,0:T(8,128)(2,1)} %dynamic-slice_bitcast_fusion.3), channel_id=1, source_target_pairs={{0,2},{1,3},{2,0},{3,1},{4,6},{5,7},{6,4},{7,5},{8,10},{9,11},{10,... | collective-permute-start | bytes 11943944 | tf_op jit(solution)/shard_map/ppermute | solution.py:72
  570.1 31.3 %collective-permute-start.68 = (bf16[2,144,4608]{2,1,0:T(8,128)(2,1)S(1)}, bf16[2,144,4608]{2,1,0:T(8,128)(2,1)}, u32[]{:S(2)}, u32[]{:S(2)}) collective-permute-start(bf16[2,144,4608]{2,1,0:T(8,128)(2,1)S(1)} %pad_maximum_fusion.2), channel_id=1, source_target_pairs={{0,4},{1,5},{2,3},{3,2},{4,0},{5,1},{6,7},{7,6},{8,12},{9,13},{10,... | collective-permute-start | bytes 7962632 | tf_op jit(solution)/shard_map/ppermute | solution.py:72
  576.3 67.6 %collective-permute-start.77 = (bf16[2,576,1152]{2,1,0:T(8,128)(2,1)S(1)}, bf16[2,576,1152]{2,1,0:T(8,128)(2,1)}, u32[]{:S(2)}, u32[]{:S(2)}) collective-permute-start(bf16[2,576,1152]{2,1,0:T(8,128)(2,1)S(1)} %pad_maximum_fusion.3), channel_id=1, source_target_pairs={{0,4},{1,5},{2,3},{3,2},{4,0},{5,1},{6,7},{7,6},{8,12},{9,13},{10,... | collective-permute-start | bytes 7962632 | tf_op jit(solution)/shard_map/ppermute | solution.py:72
  582.7 96.5 %collective-permute-start.50 = (bf16[2,144,3456]{2,1,0:T(8,128)(2,1)S(1)}, bf16[2,144,3456]{2,1,0:T(8,128)(2,1)S(1)}, u32[]{:S(2)}, u32[]{:S(2)}) collective-permute-start(bf16[2,144,3456]{2,1,0:T(8,128)(2,1)S(1)} %pad_maximum_fusion.4), channel_id=1, source_target_pairs={{0,4},{1,5},{2,3},{3,2},{4,0},{5,1},{6,7},{7,6},{8,12},{9,13},{10,... | collective-permute-start | bytes 5971976 | tf_op jit(solution)/shard_map/ppermute | solution.py:72
  604.2 77.0 %collective-permute-start.69 = (bf16[144,4608]{1,0:T(8,128)(2,1)S(1)}, bf16[144,4608]{1,0:T(8,128)(2,1)S(1)}, u32[]{:S(2)}, u32[]{:S(2)}) collective-permute-start(bf16[144,4608]{1,0:T(8,128)(2,1)S(1)} %fusion.47), channel_id=1, source_target_pairs={{0,1},{1,0},{2,6},{3,7},{4,5},{5,4},{6,2},{7,3},{8,9},{9,8},{10,14... | collective-permute-start | bytes 3981320 | tf_op jit(solution)/shard_map/ppermute | solution.py:72
  647.6 42.9 %collective-permute-start.78 = (bf16[576,1152]{1,0:T(8,128)(2,1)}, bf16[576,1152]{1,0:T(8,128)(2,1)}, u32[]{:S(2)}, u32[]{:S(2)}) collective-permute-start(bf16[576,1152]{1,0:T(8,128)(2,1)} %fusion.48), channel_id=1, source_target_pairs={{0,1},{1,0},{2,6},{3,7},{4,5},{5,4},{6,2},{7,3},{8,9},{9,8},{10,14... | collective-permute-start | bytes 3981320 | tf_op jit(solution)/shard_map/ppermute | solution.py:72
  686.6 59.0 %collective-permute-start.72 = (bf16[36,4608]{1,0:T(8,128)(2,1)}, bf16[36,4608]{1,0:T(8,128)(2,1)}, u32[]{:S(2)}, u32[]{:S(2)}) collective-permute-start(bf16[36,4608]{1,0:T(8,128)(2,1)} %get-tuple-element.259), channel_id=1, source_target_pairs={{0,24},{8,0},{16,8},{24,16},{1,25},{9,1},{17,9},{25,17},{2,26},{10... | collective-permute-start | bytes 995336 | tf_op jit(solution)/shard_map/ppermute | solution.py:115
  686.6 60.3 %collective-permute-start.71 = (bf16[36,4608]{1,0:T(8,128)(2,1)}, bf16[36,4608]{1,0:T(8,128)(2,1)}, u32[]{:S(2)}, u32[]{:S(2)}) collective-permute-start(bf16[36,4608]{1,0:T(8,128)(2,1)} %get-tuple-element.260), channel_id=1, source_target_pairs={{0,16},{8,24},{16,0},{24,8},{1,17},{9,25},{17,1},{25,9},{2,18},{10... | collective-permute-start | bytes 995336 | tf_op jit(solution)/shard_map/ppermute | solution.py:115
  701.9 35.1 %collective-permute-start.54 = (bf16[36,3456]{1,0:T(8,128)(2,1)}, bf16[36,3456]{1,0:T(8,128)(2,1)}, u32[]{:S(2)}, u32[]{:S(2)}) collective-permute-start(bf16[36,3456]{1,0:T(8,128)(2,1)} %get-tuple-element.277), channel_id=1, source_target_pairs={{0,24},{8,0},{16,8},{24,16},{1,25},{9,1},{17,9},{25,17},{2,26},{10... | collective-permute-start | bytes 746504 | tf_op jit(solution)/shard_map/ppermute | solution.py:115
  703.6 33.4 %collective-permute-start.53 = (bf16[36,3456]{1,0:T(8,128)(2,1)}, bf16[36,3456]{1,0:T(8,128)(2,1)}, u32[]{:S(2)}, u32[]{:S(2)}) collective-permute-start(bf16[36,3456]{1,0:T(8,128)(2,1)} %get-tuple-element.278), channel_id=1, source_target_pairs={{0,16},{8,24},{16,0},{24,8},{1,17},{9,25},{17,1},{25,9},{2,18},{10... | collective-permute-start | bytes 746504 | tf_op jit(solution)/shard_map/ppermute | solution.py:115
  705.2 39.0 %collective-permute-start.52 = (bf16[36,3456]{1,0:T(8,128)(2,1)}, bf16[36,3456]{1,0:T(8,128)(2,1)}, u32[]{:S(2)}, u32[]{:S(2)}) collective-permute-start(bf16[36,3456]{1,0:T(8,128)(2,1)} %get-tuple-element.276), channel_id=1, source_target_pairs={{0,8},{8,16},{16,24},{24,0},{1,9},{9,17},{17,25},{25,1},{2,10},{10... | collective-permute-start | bytes 746504 | tf_op jit(solution)/shard_map/ppermute | solution.py:115
  745.6 40.2 %collective-permute-start.79 = (bf16[144,1152]{1,0:T(8,128)(2,1)S(1)}, bf16[144,1152]{1,0:T(8,128)(2,1)S(1)}, u32[]{:S(2)}, u32[]{:S(2)}) collective-permute-start(bf16[144,1152]{1,0:T(8,128)(2,1)S(1)} %copy-done.50), channel_id=1, source_target_pairs={{0,8},{8,16},{16,24},{24,0},{1,9},{9,17},{17,25},{25,1},{2,10},{10... | collective-permute-start | bytes 995336 | tf_op jit(solution)/shard_map/ppermute | solution.py:115
  746.9 41.6 %collective-permute-start.57 = (bf16[36,3456]{1,0:T(8,128)(2,1)S(1)}, bf16[36,3456]{1,0:T(8,128)(2,1)S(1)}, u32[]{:S(2)}, u32[]{:S(2)}) collective-permute-start(bf16[36,3456]{1,0:T(8,128)(2,1)S(1)} %fusion.67), channel_id=1, source_target_pairs={{0,24},{8,0},{16,8},{24,16},{1,25},{9,1},{17,9},{25,17},{2,26},{10... | collective-permute-start | bytes 746504 | tf_op jit(solution)/shard_map/ppermute | solution.py:100
  747.1 55.5 %collective-permute-start.56 = (bf16[36,3456]{1,0:T(8,128)(2,1)S(1)}, bf16[36,3456]{1,0:T(8,128)(2,1)S(1)}, u32[]{:S(2)}, u32[]{:S(2)}) collective-permute-start(bf16[36,3456]{1,0:T(8,128)(2,1)S(1)} %fusion.67), channel_id=1, source_target_pairs={{0,16},{8,24},{16,0},{24,8},{1,17},{9,25},{17,1},{25,9},{2,18},{10... | collective-permute-start | bytes 746504 | tf_op jit(solution)/shard_map/ppermute | solution.py:100
  751.2 64.8 %collective-permute-start.55 = (bf16[36,3456]{1,0:T(8,128)(2,1)S(1)}, bf16[36,3456]{1,0:T(8,128)(2,1)S(1)}, u32[]{:S(2)}, u32[]{:S(2)}) collective-permute-start(bf16[36,3456]{1,0:T(8,128)(2,1)S(1)} %fusion.67), channel_id=1, source_target_pairs={{0,8},{8,16},{16,24},{24,0},{1,9},{9,17},{17,25},{25,1},{2,10},{10... | collective-permute-start | bytes 746504 | tf_op jit(solution)/shard_map/ppermute | solution.py:100
  765.9 54.8 %collective-permute-start.75 = (bf16[36,4608]{1,0:T(8,128)(2,1)S(1)}, bf16[36,4608]{1,0:T(8,128)(2,1)S(1)}, u32[]{:S(2)}, u32[]{:S(2)}) collective-permute-start(bf16[36,4608]{1,0:T(8,128)(2,1)S(1)} %fusion.55), channel_id=1, source_target_pairs={{0,24},{8,0},{16,8},{24,16},{1,25},{9,1},{17,9},{25,17},{2,26},{10... | collective-permute-start | bytes 995336 | tf_op jit(solution)/shard_map/ppermute | solution.py:100
  785.8 48.7 %collective-permute-start.74 = (bf16[36,4608]{1,0:T(8,128)(2,1)S(1)}, bf16[36,4608]{1,0:T(8,128)(2,1)S(1)}, u32[]{:S(2)}, u32[]{:S(2)}) collective-permute-start(bf16[36,4608]{1,0:T(8,128)(2,1)S(1)} %fusion.55), channel_id=1, source_target_pairs={{0,16},{8,24},{16,0},{24,8},{1,17},{9,25},{17,1},{25,9},{2,18},{10... | collective-permute-start | bytes 995336 | tf_op jit(solution)/shard_map/ppermute | solution.py:100
  788.5 54.1 %collective-permute-start.73 = (bf16[36,4608]{1,0:T(8,128)(2,1)S(1)}, bf16[36,4608]{1,0:T(8,128)(2,1)}, u32[]{:S(2)}, u32[]{:S(2)}) collective-permute-start(bf16[36,4608]{1,0:T(8,128)(2,1)S(1)} %fusion.55), channel_id=1, source_target_pairs={{0,8},{8,16},{16,24},{24,0},{1,9},{9,17},{17,25},{25,1},{2,10},{10... | collective-permute-start | bytes 995336 | tf_op jit(solution)/shard_map/ppermute | solution.py:100
  802.7 46.3 %collective-permute-start.84 = (bf16[144,1152]{1,0:T(8,128)(2,1)S(1)}, bf16[144,1152]{1,0:T(8,128)(2,1)}, u32[]{:S(2)}, u32[]{:S(2)}) collective-permute-start(bf16[144,1152]{1,0:T(8,128)(2,1)S(1)} %fusion.59), channel_id=1, source_target_pairs={{0,24},{8,0},{16,8},{24,16},{1,25},{9,1},{17,9},{25,17},{2,26},{10... | collective-permute-start | bytes 995336 | tf_op jit(solution)/shard_map/ppermute | solution.py:100
  816.1 33.6 %collective-permute-start.83 = (bf16[144,1152]{1,0:T(8,128)(2,1)S(1)}, bf16[144,1152]{1,0:T(8,128)(2,1)}, u32[]{:S(2)}, u32[]{:S(2)}) collective-permute-start(bf16[144,1152]{1,0:T(8,128)(2,1)S(1)} %fusion.59), channel_id=1, source_target_pairs={{0,16},{8,24},{16,0},{24,8},{1,17},{9,25},{17,1},{25,9},{2,18},{10... | collective-permute-start | bytes 995336 | tf_op jit(solution)/shard_map/ppermute | solution.py:100
  820.6 36.2 %collective-permute-start.82 = (bf16[144,1152]{1,0:T(8,128)(2,1)S(1)}, bf16[144,1152]{1,0:T(8,128)(2,1)}, u32[]{:S(2)}, u32[]{:S(2)}) collective-permute-start(bf16[144,1152]{1,0:T(8,128)(2,1)S(1)} %fusion.59), channel_id=1, source_target_pairs={{0,8},{8,16},{16,24},{24,0},{1,9},{9,17},{17,25},{25,1},{2,10},{10... | collective-permute-start | bytes 995336 | tf_op jit(solution)/shard_map/ppermute | solution.py:100
  (117 other events, 1397.0 us)

commit v3 on v2

--- a/solution.py
+++ b/solution.py
@@ -99,26 +99,6 @@
         pairs = [(at, (at + shift) % replicas) for at in range(replicas)]
         stacked.append(lax.ppermute(values, "rep", pairs))
     return jnp.stack(stacked)
-
-
-def reduce_replicas(partial, replicas):
-    low = jnp.bfloat16
-    rows, columns = partial.shape
-    own = lax.axis_index("rep")
-    pieces = partial.astype(low).reshape(replicas, rows // replicas, columns)
-    total = lax.dynamic_index_in_dim(
-        partial.reshape(pieces.shape), own, 0, keepdims=False
-    )
-    for shift in range(1, replicas):
-        pairs = [(at, (at + shift) % replicas) for at in range(replicas)]
-        piece = lax.dynamic_index_in_dim(pieces, (own + shift) % replicas, 0, keepdims=False)
-        total = total + lax.ppermute(piece, "rep", pairs).astype(jnp.float32)
-    stacked = gather_replicas(total.astype(low), replicas)
-    ordered = [
-        lax.dynamic_index_in_dim(stacked, (own - at) % replicas, 0, keepdims=False)
-        for at in range(replicas)
-    ]
-    return jnp.stack(ordered).reshape(rows, columns).astype(jnp.float32)
 
 
 def assemble_kernel(order_ref, *refs):
@@ -208,87 +188,172 @@
     return halved[0] + received.astype(jnp.float32)
 
 
-def head_slice(values, group_index, group_width):
-    number, length, model_width = values.shape
-    piece = lax.dynamic_slice_in_dim(values, group_index * group_width, group_width, 2)
-    return piece.reshape(number, length, 4, HEAD)
-
-
-def join_groups(stacked):
-    groups, number, length, group_width = stacked.shape
-    return jnp.moveaxis(stacked, 0, 2).reshape(number, length, groups * group_width)
-
-
-def attn_forward(query, keys, values, score_scale):
-    group_width = 4 * HEAD
-    groups = query.shape[2] // group_width
-
-    def per_group(group_index):
-        query_part = head_slice(query, group_index, group_width)
-        keys_part = head_slice(keys, group_index, group_width)
-        values_part = head_slice(values, group_index, group_width)
-        scores = (
-            jnp.einsum("lqhd,lkhd->lhqk", query_part, keys_part, preferred_element_type=jnp.float32)
-            * score_scale
+WINDOW = 256
+
+
+def head_window(width):
+    first = pl.program_id(0) * HEAD
+    start = jnp.minimum(first // 128 * 128, width - WINDOW)
+    start = pl.multiple_of(start, 128)
+    lane = lax.broadcasted_iota(jnp.int32, (1, WINDOW), 1) + start
+    inside = (lane >= first) & (lane < first + HEAD)
+    mask = jnp.where(inside, 1.0, 0.0).astype(jnp.bfloat16)
+    return pl.ds(start, WINDOW), pl.ds(pl.multiple_of(start + width, 128), WINDOW), mask
+
+
+def dot_last(left, right):
+    return lax.dot_general(
+        left, right, (((1,), (1,)), ((), ())), preferred_element_type=jnp.float32
+    )
+
+
+def dot_first(left, right):
+    return lax.dot_general(
+        left, right, (((0,), (0,)), ((), ())), preferred_element_type=jnp.float32
+    )
+
+
+def attend_kernel(query_ref, own_ref, other_ref, out_ref, log_ref, total_ref):
+    length, width = query_ref.shape
+    head = pl.program_id(0)
+    key_lanes, value_lanes, mask = head_window(width)
+    score_scale = float(HEAD) ** (-0.5)
+
+    @pl.when(head == 0)
+    def _():
+        total_ref[...] = jnp.zeros_like(total_ref)
+        log_ref[...] = jnp.zeros_like(log_ref)
+
+    keys = jnp.concatenate([own_ref[:, key_lanes], other_ref[:, key_lanes]]) * mask
+    values = jnp.concatenate([own_ref[:, value_lanes], other_ref[:, value_lanes]]) * mask
+    rows = min(256, length)
+    for at in range(0, length, rows):
+        block = pl.ds(at, rows)
+        scores = dot_last(query_ref[block, key_lanes], keys)
+        row_max = jnp.max(scores, -1, keepdims=True)
+        weights = jnp.exp((scores - row_max) * score_scale)
+        row_total = jnp.sum(weights, -1, keepdims=True)
+        probs = (weights * (1.0 / row_total)).astype(jnp.bfloat16)
+        total_ref[block, key_lanes] += jnp.dot(
+            probs, values, preferred_element_type=jnp.float32
         )
-        row_max = jnp.max(scores, -1, keepdims=True)
-        weights = jnp.exp(scores - row_max)
-        row_total = jnp.sum(weights, -1, keepdims=True)
-        probs = (weights / row_total).astype(jnp.bfloat16)
-        mixed = jnp.einsum(
-            "lhqk,lkhd->lqhd", probs, values_part, preferred_element_type=jnp.float32
+        log_total = row_max * score_scale + jnp.log(row_total)
+        lane = lax.broadcasted_iota(jnp.int32, (rows, 128), 1)
+        log_ref[block, :] = jnp.where(lane == head, log_total, log_ref[block, :])
+
+    @pl.when(head == pl.num_programs(0) - 1)
+    def _():
+        out_ref[...] = total_ref[...].astype(out_ref.dtype)
+
+
+def attend(query, own, other):
+    length, width = query.shape
+    heads = width // HEAD
+    keys = own.shape[0] + other.shape[0]
+    return pl.pallas_call(
+        attend_kernel,
+        grid=(heads,),
+        out_shape=(
+            jax.ShapeDtypeStruct((length, width), jnp.bfloat16),
+            jax.ShapeDtypeStruct((length, 128), jnp.float32),
+        ),
+        in_specs=[
+            pl.BlockSpec((length, width), lambda head: (0, 0)),
+            pl.BlockSpec(own.shape, lambda head: (0, 0)),
+            pl.BlockSpec(other.shape, lambda head: (0, 0)),
+        ],
+        out_specs=(
+            pl.BlockSpec((length, width), lambda head: (0, 0)),
+            pl.BlockSpec((length, 128), lambda head: (0, 0)),
+        ),
+        scratch_shapes=[pltpu.VMEM((length, width), jnp.float32)],
+        compiler_params=pltpu.CompilerParams(vmem_limit_bytes=48 << 20),
+        cost_estimate=pl.CostEstimate(
+            flops=4 * heads * length * keys * WINDOW,
+            bytes_accessed=4 * length * width * 4,
+            transcendentals=heads * length * keys,
+        ),
+    )(query, own, other)
+
+
+def attend_back_kernel(
+    query_ref, own_ref, other_ref, upstream_ref, log_ref, d_query_ref, d_own_ref, d_other_ref,
+    query_total, pair_total,
+):
+    length, width = query_ref.shape
+    head = pl.program_id(0)
+    key_lanes, value_lanes, mask = head_window(width)
+    score_scale = float(HEAD) ** (-0.5)
+
+    @pl.when(head == 0)
+    def _():
+        query_total[...] = jnp.zeros_like(query_total)
+        pair_total[...] = jnp.zeros_like(pair_total)
+
+    keys = jnp.concatenate([own_ref[:, key_lanes], other_ref[:, key_lanes]]) * mask
+    values = jnp.concatenate([own_ref[:, value_lanes], other_ref[:, value_lanes]]) * mask
+    rows = min(256, length)
+    for at in range(0, length, rows):
+        block = pl.ds(at, rows)
+        query = query_ref[block, key_lanes] * mask
+        upstream = upstream_ref[block, key_lanes] * mask
+        scores = dot_last(keys, query)
+        probs = jnp.exp(scores * score_scale - log_ref[0, :, block])
+        d_probs = dot_last(values, upstream)
+        weighted = probs * d_probs
+        row_sum = jnp.sum(weighted, 0, keepdims=True)
+        d_scores = (weighted - probs * row_sum).astype(jnp.bfloat16)
+        pair_total[:, value_lanes] += jnp.dot(
+            probs.astype(jnp.bfloat16), upstream, preferred_element_type=jnp.float32
         )
-        log_total = row_max[..., 0] + jnp.log(row_total[..., 0])
-        return (mixed.reshape(mixed.shape[0], mixed.shape[1], group_width), log_total)
-
-    mixed_all, log_totals = lax.map(per_group, jnp.arange(groups))
-    return (join_groups(mixed_all), log_totals)
-
-
-def attn_backward(query, keys, values, upstream, log_totals, score_scale):
-    group_width = 4 * HEAD
-    groups = query.shape[2] // group_width
-
-    def per_group(group_item):
-        group_index, log_total = group_item
-        query_part = head_slice(query, group_index, group_width)
-        keys_part = head_slice(keys, group_index, group_width)
-        values_part = head_slice(values, group_index, group_width)
-        upstream_part = head_slice(upstream, group_index, group_width)
-        scores = (
-            jnp.einsum("lqhd,lkhd->lhqk", query_part, keys_part, preferred_element_type=jnp.float32)
-            * score_scale
+        pair_total[:, key_lanes] += score_scale * jnp.dot(
+            d_scores, query, preferred_element_type=jnp.float32
         )
-        probs = jnp.exp(scores - log_total[..., None])
-        d_probs = jnp.einsum(
-            "lqhd,lkhd->lhqk", upstream_part, values_part, preferred_element_type=jnp.float32
-        )
-        d_scores = (probs * (d_probs - jnp.sum(probs * d_probs, -1, keepdims=True))).astype(
-            jnp.bfloat16
-        )
-        d_query = (
-            jnp.einsum("lhqk,lkhd->lqhd", d_scores, keys_part, preferred_element_type=jnp.float32)
-            * score_scale
-        )
-        d_keys = (
-            jnp.einsum("lhqk,lqhd->lkhd", d_scores, query_part, preferred_element_type=jnp.float32)
-            * score_scale
-        )
-        d_values = jnp.einsum(
-            "lhqk,lqhd->lkhd",
-            probs.astype(jnp.bfloat16),
-            upstream_part,
-            preferred_element_type=jnp.float32,
-        )
-        number = d_query.shape[0]
-        return (
-            d_query.reshape(number, d_query.shape[1], group_width),
-            d_keys.reshape(number, d_keys.shape[1], group_width),
-            d_values.reshape(number, d_values.shape[1], group_width),
-        )
-
-    d_query, d_keys, d_values = lax.map(per_group, (jnp.arange(groups), log_totals))
-    return (join_groups(d_query), join_groups(d_keys), join_groups(d_values))
+        query_total[block, key_lanes] += dot_first(d_scores, keys)
+
+    @pl.when(head == pl.num_programs(0) - 1)
+    def _():
+        d_query_ref[...] = (query_total[...] * score_scale).astype(d_query_ref.dtype)
+        d_own_ref[...] = pair_total[: own_ref.shape[0]]
+        d_other_ref[...] = pair_total[own_ref.shape[0] :].astype(d_other_ref.dtype)
+
+
+def attend_back(query, own, other, upstream, log_totals):
+    length, width = query.shape
+    heads = width // HEAD
+    keys = own.shape[0] + other.shape[0]
+    whole = lambda head: (0, 0)
+    return pl.pallas_call(
+        attend_back_kernel,
+        grid=(heads,),
+        out_shape=(
+            jax.ShapeDtypeStruct((length, width), jnp.bfloat16),
+            jax.ShapeDtypeStruct(own.shape, jnp.float32),
+            jax.ShapeDtypeStruct(other.shape, jnp.bfloat16),
+        ),
+        in_specs=[
+            pl.BlockSpec((length, width), whole),
+            pl.BlockSpec(own.shape, whole),
+            pl.BlockSpec(other.shape, whole),
+            pl.BlockSpec((length, width), whole),
+            pl.BlockSpec((1, 1, length), lambda head: (head, 0, 0)),
+        ],
+        out_specs=(
+            pl.BlockSpec((length, width), whole),
+            pl.BlockSpec(own.shape, whole),
+            pl.BlockSpec(other.shape, whole),
+        ),
+        scratch_shapes=[
+            pltpu.VMEM((length, width), jnp.float32),
+            pltpu.VMEM((keys, own.shape[1]), jnp.float32),
+        ],
+        compiler_params=pltpu.CompilerParams(vmem_limit_bytes=56 << 20),
+        cost_estimate=pl.CostEstimate(
+            flops=10 * heads * length * keys * WINDOW,
+            bytes_accessed=12 * length * width * 4,
+            transcendentals=heads * length * keys,
+        ),
+    )(query, own, other, upstream, log_totals)
 
 
 def per_device(
@@ -309,7 +374,6 @@
 ):
     number, length, width = latent_in.shape
     hidden_width = up_weight.shape[1]
-    score_scale = float(HEAD) ** (-0.5)
     place = place_of()
     fsdp_index = lax.axis_index("fsdp")
     held = (place >> 2) * 2 + (place & 1)
@@ -331,8 +395,8 @@
     latent_low = swap_halves(latent_in)
     full_out = gather_weight(out_weight)
     cotangent_low = swap_halves(cotangent)
-    full_up = gather_weight(up_weight)
-    full_down = gather_weight(down_weight)
+    full_up = lax.all_gather(up_weight, GROUP, axis=0, tiled=True)
+    full_down = lax.all_gather(down_weight, GROUP, axis=0, tiled=True)
 
     bounds = [0, width]
     for bias in (qv_bias, out_bias, up_bias, down_bias):
@@ -374,11 +438,8 @@
     query = projected[:, :width]
     pair_own = projected[:, width:]
     pair_other = permute(pair_own, core_rule)
-    pair_all = jnp.concatenate([pair_own, pair_other], axis=0)[None]
-    keys = pair_all[..., :width]
-    values = pair_all[..., width:]
-    attended, log_totals = attn_forward(query[None], keys, values, score_scale)
-    attended_low = attended[0].astype(jnp.bfloat16)
+    attended_low, log_totals = attend(query, pair_own, pair_other)
+    log_rows = log_totals[:, : width // HEAD].T[:, None, :]
     branch_one = matmul(attended_low, full_out) + full_out_bias
     middle = latent + gate_one * branch_one
 
@@ -396,15 +457,16 @@
     d_gate_two = jnp.sum(d_out * branch_two, axis=0)
     d_branch_two = (gate_two * d_out).astype(jnp.bfloat16)
     down_grad = matmul_left(activated_low, d_branch_two).astype(jnp.bfloat16)
-    down_shard = reduce_scatter(down_grad.reshape(SHARDS, hidden_width // SHARDS, width))
-    down_total = reduce_replicas(down_shard, replicas)
+    down_shard = lax.psum_scatter(down_grad, GROUP, scatter_dimension=0, tiled=True)
+    down_total = lax.psum(down_shard, "rep")
     down_bias_grad = jnp.sum(d_branch_two.astype(jnp.float32), axis=0)
     d_activated = matmul_right(d_branch_two, full_down)
     d_preact = gelu_pull(d_activated)[0].astype(jnp.bfloat16)
 
     up_grad = matmul_left(hidden_two, d_preact).astype(jnp.bfloat16)
     up_shard = reduce_scatter(up_grad.reshape(SHARDS, rows, hidden_width))
-    up_total = reduce_replicas(up_shard, replicas)
+    up_shard, down_total = lax.optimization_barrier((up_shard.astype(jnp.bfloat16), down_total))
+    up_total = lax.psum(up_shard, "rep")
     up_bias_grad = jnp.sum(d_preact.astype(jnp.float32), axis=0)
     d_hidden_two = matmul_right(d_preact, full_up)
     d_shift_two = jnp.sum(d_hidden_two, axis=0)
@@ -415,20 +477,20 @@
 
     out_grad = matmul_left(attended_low, d_branch_one).astype(jnp.bfloat16)
     out_shard = reduce_scatter(out_grad.reshape(SHARDS, rows, width))
-    out_total = reduce_replicas(out_shard, replicas)
     out_bias_grad = jnp.sum(d_branch_one.astype(jnp.float32), axis=0)
     d_attended = matmul_right(d_branch_one, full_out).astype(jnp.bfloat16)
-    d_query, d_keys_all, d_values_all = attn_backward(
-        query[None], keys, values, d_attended[None], log_totals, score_scale
-    )
-    d_pair = jnp.concatenate([d_keys_all[0], d_values_all[0]], axis=-1)
-    d_pair_other = permute(d_pair[length:].astype(jnp.bfloat16), core_rule)
-    d_pair = d_pair[:length] + d_pair_other.astype(jnp.float32)
-    d_projected = jnp.concatenate([d_query[0], d_pair], axis=-1).astype(jnp.bfloat16)
+    d_query, d_pair, d_pair_other = attend_back(
+        query, pair_own, pair_other, d_attended, log_rows
+    )
+    d_pair = d_pair + permute(d_pair_other, core_rule).astype(jnp.float32)
+    d_projected = jnp.concatenate([d_query, d_pair.astype(jnp.bfloat16)], axis=-1)
 
     qkv_grad = matmul_left(hidden_one, d_projected).astype(jnp.bfloat16)
     qkv_shard = reduce_scatter(qkv_grad.reshape(SHARDS, rows, 3 * width))
-    qkv_total = reduce_replicas(qkv_shard, replicas)
+    out_shard, qkv_shard, up_total = lax.optimization_barrier(
+        (out_shard.astype(jnp.bfloat16), qkv_shard.astype(jnp.bfloat16), up_total)
+    )
+    out_total, qkv_total = lax.psum((out_shard, qkv_shard), "rep")
     column_sums = jnp.sum(d_projected.astype(jnp.float32), axis=0)
     d_hidden_one = matmul_right(d_projected, full_qkv)
     d_shift_one = jnp.sum(d_hidden_one, axis=0)
@@ -490,13 +552,13 @@
         cond_grad,
         ada_total,
         ada_bias_total,
-        qkv_total,
+        qkv_total.astype(jnp.float32),
         qv_total,
-        out_total,
+        out_total.astype(jnp.float32),
         out_bias_total,
-        up_total,
+        up_total.astype(jnp.float32),
         up_bias_total,
-        down_total,
+        down_total.astype(jnp.float32),
         down_bias_total,
     )
 

time: 873 us -> 702 us (0.80)
  local copies, waits for them, and re-layouts: 146 us -> 48.7 us
  Pallas kernels: 15.7 us -> 77.8 us
  matrix products: 169 us -> 117 us
  starting transfers between devices: 110 us -> 58.6 us
  other arithmetic: 103 us -> 56.2 us
  between operations: 3.06 us -> 16.4 us
  waiting for transfers between devices: 308 us -> 319 us
    psum x0 -> x3, waiting for transfers between devices: none -> 158 us  [the longest x1 57.5 us: per_device(): up_total = lax.psum(up_shard, 'rep')]
    pallas_call x0 -> x2, Pallas kernels: none -> 70.3 us  [the longest x1 43.5 us: attend_back(): pl.pallas_call(attend_back_kernel, grid=(heads,), out_shape=(jax.ShapeDty...]
    ppermute x15 -> x3, waiting for transfers between devices: 58.5 us -> 0.01 us  [gather_replicas(): stacked.append(lax.ppermute(values, 'rep', pairs))]
    ppermute x12 -> x0, waiting for transfers between devices: 52.5 us -> none  [reduce_replicas(): total = total + lax.ppermute(piece, 'rep', pairs).astype(jnp.float32)]
    dot_general x28 -> x0, matrix products: 48.4 us -> none  [the longest x4 11.6 us: per_group(): jnp.einsum('lqhd,lkhd->lhqk', upstream_part, values_part, preferred_eleme...]
    dynamic_slice x36 -> x0, local copies, waits for them, and re-layouts: 28.1 us -> none  [the longest x24 22.2 us: head_slice(): lax.dynamic_slice_in_dim(values, group_index * group_width, group_width, 2)]
    ppermute x54 -> x37, waiting for transfers between devices: 184 us -> 160 us  [permute(): return lax.ppermute(values, GROUP, pairs_by(rule))]
    ppermute x15 -> x3, starting transfers between devices: 24.1 us -> 4.49 us  [gather_replicas(): stacked.append(lax.ppermute(values, 'rep', pairs))]
  transfers between devices with their start and end apart: 85 -> 50, of which waited for: 34 -> 17; matrix products, arithmetic and copies ran while one was open for 36% -> 19% of each run, Pallas kernels for 2% -> 11%
where the time goes in v3:
time: 702 us; the launch traced here: 694 us
  waiting for transfers between devices  319 us (45%)
  matrix products  117 us (17%)
  Pallas kernels  77.8 us (11%)
  starting transfers between devices  58.6 us (8%)
  other arithmetic  56.2 us (8%)
  local copies, waits for them, and re-layouts  48.7 us (7%)
  between operations  16.4 us (2%)
    ppermute x37, waiting for transfers between devices, permute(): return lax.ppermute(values, GROUP, pairs_by(rule))  160 us
    psum x1, waiting for transfers between devices, per_device(): up_total = lax.psum(up_shard, 'rep')  57.5 us
    psum x1, waiting for transfers between devices, per_device(): down_total = lax.psum(down_shard, 'rep')  52 us
    psum x1, waiting for transfers between devices, per_device(): out_total, qkv_total = lax.psum((out_shard, qkv_shard), 'rep')  48.1 us
    pallas_call x1, Pallas kernels, attend_back(): pl.pallas_call(attend_back_kernel, grid=(heads,), out_shape=(jax.ShapeDty...  43.5 us
    ppermute x37, starting transfers between devices, permute(): return lax.ppermute(values, GROUP, pairs_by(rule))  42.9 us
    dot_general x5, matrix products, matmul(): return jnp.dot(left, right, preferred_element_type=jnp.float32)  39.7 us
    dot_general x4, matrix products, matmul_right(): lax.dot_general(left, right, (((1,), (1,)), ((), ())), preferred_element_...  39.2 us
  transfers between devices with their start and end apart: 50, of which 17 were waited for; matrix products, arithmetic and copies ran while one was open for 19% of the time, Pallas kernels for 11%

profile of v3, /device:TPU:9, one launch (start us, length us, event | category | flops | bytes accessed | tf_op | source)
XLA Modules:
  0.0 693.7 jit_solution(6958482119856041170)
XLA Ops:
  19.9 30.8 %collective-permute-done.2 = bf16[4,2432]{1,0:T(4,128)(2,1)S(1)} collective-permute-done((bf16[4,2432]{1,0:T(4,128)(2,1)S(1)}, bf16[4,2432]{1,0:T(4,128)(2,1)S(1)}, u32[]{:S(2)}, u32[]{:S(2)}) %collective-permute-start.2) | collective-permute-done | bytes 19488 | tf_op jit(solution)/shard_map/ppermute | solution.py:72
  55.0 2.9 collective-permute-start.5
  59.4 27.7 %collective-permute-done.5 = f32[1,6912]{1,0:T(1,128)S(1)} collective-permute-done((f32[1,6912]{1,0:T(1,128)S(1)}, f32[1,6912]{1,0:T(1,128)S(1)}, u32[]{:S(2)}, u32[]{:S(2)}) %collective-permute-start.5) | collective-permute-done | bytes 27680 | tf_op jit(solution)/shard_map/ppermute | solution.py:72
  89.0 4.1 collective-permute-done.9.refs_3_
  93.1 12.6 %collective-permute-start.13 = (bf16[144,3456]{1,0:T(8,128)(2,1)S(1)}, bf16[144,3456]{1,0:T(8,128)(2,1)S(1)}, u32[]{:S(2)}, u32[]{:S(2)}) collective-permute-start(bf16[144,3456]{1,0:T(8,128)(2,1)S(1)} %collective-permute-done.9.refs_3_), channel_id=1, source_target_pairs={{0,2},{1,3},{2,0},{3,1},{4,6},{5,7},{6,4},{7,5},{8,10},{9,11},{10,... | collective-permute-start | bytes 2985992 | tf_op jit(solution)/shard_map/ppermute | solution.py:72
  108.0 4.9 shard_map.237
  113.0 5.5 add_convert_fusion
  122.4 15.4 %collective-permute-done.15.refs_1_ = bf16[144,1152]{1,0:T(8,128)(2,1)S(1)} collective-permute-done((bf16[144,1152]{1,0:T(8,128)(2,1)S(1)}, bf16[144,1152]{1,0:T(8,128)(2,1)S(1)}, u32[]{:S(2)}, u32[]{:S(2)}) %collective-permute-start.15) | collective-permute-done | bytes 331808 | tf_op jit(solution)/shard_map/ppermute | solution.py:72
  140.0 5.9 collective-permute-done.17.refs_3_
  147.8 2.5 collective-permute-start.23
  150.4 2.5 shard_map.239
  155.8 26.8 %shard_map.238 = (bf16[512,1152]{1,0:T(8,128)(2,1)S(1)}, f32[512,128]{1,0:T(8,128)S(1)}) custom-call(bf16[512,1152]{1,0:T(8,128)(2,1)S(1)} %slice.162.query_ref, bf16[512,2304]{1,0:T(8,128)(2,1)} %slice.163.own_ref, bf16[512,2304]{1,0:T(8,128)(2,1)} %collective-permute-done.14.other_ref), custom_call_target="tpu_custom_call" | custom-call | flops 8589934592 | bytes 9437184 | tf_op jit(solution)/shard_map/pallas_call | solution.py:253
  184.9 5.4 fusion.61
  192.1 12.4 %fusion.60 = f32[512,4608]{1,0:T(8,128)} fusion(bf16[1152,4608]{1,0:T(8,128)(2,1)} %all-gather.3.cloned.1.call-done, f32[512,1152]{1,0:T(8,128)} %copy-done.11, f32[1152]{0:T(1024)S(1)} %get-tuple-element.46, f32[1152]{0:T(1024)S(1)} %get-tuple-element.47, f32[512]{0:T(512)S(1)} %add_rsqrt_fusion, f32[512]{0:T(512)S(1)} %broadcast_multiply_fusion.4), kind=kOutput, calls=%fused_computation.184 | convolution fusion | flops 5438767104 | bytes 22426624 | tf_op jit(solution)/shard_map/dot_general | solution.py:32
  204.5 16.0 %convert_reduce_fusion.3 = (f32[1152]{0:T(1024)}, f32[1152]{0:T(1024)}, bf16[1,512,1152]{2,1,0:T(8,128)(2,1)S(1)}, bf16[1,512,1152]{2,1,0:T(8,128)(2,1)}) fusion(f32[]{:T(128)} %bitcast.1, f32[1152]{0:T(1024)S(1)} %get-tuple-element.45, bf16[1,512,1152]{2,1,0:T(8,128)(2,1)} %param.27, bf16[1,512,1152]{2,1,0:T(8,128)(2,1)} %collective-permute-done.23, ...), kind=kOutput, calls=%fused_computation.62 | convolution fusion | flops 5467666432 | bytes 27168772 | tf_op jit(solution)/shard_map/dot_general | solution.py:32
  221.5 12.0 %convolution_convert_fusion = bf16[4608,1152]{1,0:T(8,128)(2,1)} fusion(bf16[1,512,1152]{2,1,0:T(8,128)(2,1)S(1)} %get-tuple-element.56, f32[]{:T(128)} %bitcast.1, f32[1152]{0:T(1024)S(1)} %get-tuple-element.45, f32[512,4608]{1,0:T(8,128)S(1)} %copy-done.56, f32[4608]{0:T(1024)S(1)} %reshape.159), kind=kOutput, calls=%fused_computation | convolution fusion | flops 5467078656 | bytes 21256708 | tf_op jit(solution)/shard_map/dot_general | solution.py:36
  233.5 17.5 %convert_reduce_fusion = (f32[4608]{0:T(1024)}, bf16[512,4608]{1,0:T(8,128)(2,1)S(1)}) fusion(f32[512,4608]{1,0:T(8,128)} %fusion.60, f32[4608]{0:T(1024)S(1)} %reshape.159, bf16[4608,1152]{1,0:T(8,128)(2,1)} %all-gather.5.cloned.1.call-done, bf16[1,512,1152]{2,1,0:T(8,128)(2,1)} %copy-done.27, f32[]{:T(128)} %bitcast.1, f32[1152]{0:T(1024)S(1)} %get-tuple-element.45), kind=kOutput, calls=%fused_computation.14 | convolution fusion | flops 5492436480 | bytes 25993732 | tf_op jit(solution)/shard_map/dot_general | solution.py:42
  251.0 13.0 %multiply_reduce_fusion = (f32[1152]{0:T(1024)}, f32[512]{0:T(512)S(1)}, f32[512]{0:T(512)S(1)}, f32[1152]{0:T(1024)}, f32[512,1152]{1,0:T(8,128)S(1)}) fusion(f32[512,1152]{1,0:T(8,128)S(1)} %copy-done.12, f32[512]{0:T(512)S(1)} %add_rsqrt_fusion, f32[512]{0:T(512)S(1)} %broadcast_multiply_fusion.4, f32[1152]{0:T(1024)S(1)} %get-tuple-element.47, ...), kind=kOutput, calls=%fused_computation.64 | convolution fusion | flops 5441123328 | bytes 20076032 | tf_op jit(solution)/shard_map/dot_general | solution.py:42
  264.1 3.4 convert_reduce_fusion.4
  267.4 2.9 convolution_convert_fusion.4.upstream_ref
  270.3 3.2 convolution_convert_fusion.3
  274.8 3.3 collective-permute-start.22
  279.7 43.5 %shard_map.240 = (bf16[512,1152]{1,0:T(8,128)(2,1)}, f32[512,2304]{1,0:T(8,128)}, bf16[512,2304]{1,0:T(8,128)(2,1)}) custom-call(bf16[512,1152]{1,0:T(8,128)(2,1)} %copy-done.4, bf16[512,2304]{1,0:T(8,128)(2,1)} %slice.163.own_ref, bf16[512,2304]{1,0:T(8,128)(2,1)} %collective-permute-done.14.other_ref, ...), custom_call_target="tpu_custom_call" | custom-call | flops 21474836480 | bytes 28311552 | tf_op jit(solution)/shard_map/pallas_call | solution.py:326
  323.2 9.0 %convolution_convert_fusion.1 = bf16[1152,4608]{1,0:T(8,128)(2,1)S(1)} fusion(bf16[512,4608]{1,0:T(8,128)(2,1)} %copy-done.57, f32[512,1152]{1,0:T(8,128)S(1)} %copy-done.13, f32[1152]{0:T(1024)S(1)} %copy-done.40, f32[1152]{0:T(1024)S(1)} %get-tuple-element.47, f32[512]{0:T(512)S(1)} %copy-done.36, f32[512]{0:T(512)S(1)} %broadcast_multiply_fusion.4), kind=kOutput, calls=%fused_computation.1 | convolution fusion | flops 5444075520 | bytes 17708032 | tf_op jit(solution)/shard_map/dot_general | solution.py:36
  332.9 2.9 dynamic-slice_bitcast_fusion
  335.8 3.3 copy-done.8
  339.6 2.9 broadcast_select_fusion.1
  350.8 5.7 fusion.27
  358.3 2.4 multiply_reduce_fusion.1
  364.3 4.8 collective-permute-start.27
  369.1 5.2 convolution_convert_fusion.2
  379.3 4.0 collective-permute-done.28
  395.8 5.5 fusion
  412.2 3.2 collective-permute-start.25
  419.6 4.3 fusion.8
  424.8 27.1 %collective-permute-done.42 = bf16[2,144,4608]{2,1,0:T(8,128)(2,1)} collective-permute-done((bf16[2,144,4608]{2,1,0:T(8,128)(2,1)}, bf16[2,144,4608]{2,1,0:T(8,128)(2,1)}, u32[]{:S(2)}, u32[]{:S(2)}) %collective-permute-start.42) | collective-permute-done | bytes 2654240 | tf_op jit(solution)/shard_map/ppermute | solution.py:72
  451.9 2.5 convert_add_fusion.2
  458.0 36.5 %collective-permute-done.39 = bf16[2,144,3456]{2,1,0:T(8,128)(2,1)S(1)} collective-permute-done((bf16[2,144,3456]{2,1,0:T(8,128)(2,1)S(1)}, bf16[2,144,3456]{2,1,0:T(8,128)(2,1)S(1)}, u32[]{:S(2)}, u32[]{:S(2)}) %collective-permute-start.39) | collective-permute-done | bytes 1990688 | tf_op jit(solution)/shard_map/ppermute | solution.py:72
  494.5 2.4 convert_add_fusion.3
  497.0 2.6 fusion.37
  499.7 3.7 fusion.18
  503.4 52.0 %all-reduce.5.cloned.1.call-done = bf16[576,1152]{1,0:T(8,128)(2,1)} async-done(((bf16[576,1152]{1,0:T(8,128)(2,1)}), bf16[576,1152]{1,0:T(8,128)(2,1)}) %all-reduce.5.cloned.1.call-update) | async-done | bytes 1327120 | tf_op jit(solution)/shard_map/psum | solution.py:461
  558.3 2.9 fusion.32
  561.2 57.5 %all-reduce.7.cloned.1.call-done = bf16[144,4608]{1,0:T(8,128)(2,1)} async-done(((bf16[144,4608]{1,0:T(8,128)(2,1)}), bf16[144,4608]{1,0:T(8,128)(2,1)}) %all-reduce.7.cloned.1.call-update) | async-done | bytes 1327120 | tf_op jit(solution)/shard_map/psum | solution.py:469
  621.1 6.2 fusion.65
  627.4 3.0 select_convert_fusion
  633.9 48.1 %all-reduce.9.cloned.1.call-done = (bf16[144,3456]{1,0:T(8,128)(2,1)}, bf16[144,1152]{1,0:T(8,128)(2,1)}) async-done(((bf16[144,3456]{1,0:T(8,128)(2,1)}, bf16[144,1152]{1,0:T(8,128)(2,1)}), (bf16[144,3456]{1,0:T(8,128)(2,1)}, bf16[144,1152]{1,0:T(8,128)(2,1)})) %all-reduce.9.cloned.1.call-update) | async-done | bytes 1327120 | tf_op jit(solution)/shard_map/psum | solution.py:493
  683.8 2.6 convert_element_type.284
  (329 shorter events, 102.6 us)
Async XLA Ops:
  7.3 184.8 %all-gather.3.cloned.1.call-start = ((), (), s32[]{:S(2)}) async-start(), calls=%async_computation.1 | async-start | bytes 11943936 | tf_op jit(solution)/shard_map/all_gather | solution.py:398
  8.0 196.5 %all-gather.5.cloned.1.call-start = ((), (), s32[]{:S(2)}) async-start(), calls=%async_computation.2 | async-start | bytes 11943936 | tf_op jit(solution)/shard_map/all_gather | solution.py:399
  8.8 488.2 %reduce-scatter.2.cloned.1.call-start = ((), (), s32[]{:S(2)}) async-start(), calls=%async_computation.3 | async-start | bytes 11943936 | tf_op jit(solution)/shard_map/reduce_scatter | solution.py:460
  9.6 2.6 collective-permute-start
  12.3 7.0 %collective-permute-start.1 = (bf16[2,2432]{1,0:T(2,128)(2,1)S(1)}, bf16[2,2432]{1,0:T(2,128)(2,1)S(1)}, u32[]{:S(2)}, u32[]{:S(2)}) collective-permute-start(bf16[2,2432]{1,0:T(2,128)(2,1)S(1)} %broadcast_select_fusion.6), channel_id=1, source_target_pairs={{0,2},{1,3},{2,0},{3,1},{4,6},{5,7},{6,4},{7,5},{8,10},{9,11},{10,... | collective-permute-start | bytes 29192 | tf_op jit(solution)/shard_map/ppermute | solution.py:72
  14.2 74.5 %collective-permute-start.8 = (bf16[144,3456]{1,0:T(8,128)(2,1)S(1)}, bf16[144,3456]{1,0:T(8,128)(2,1)}, u32[]{:S(2)}, u32[]{:S(2)}) collective-permute-start(bf16[144,3456]{1,0:T(8,128)(2,1)S(1)} %copy-done.5), channel_id=1, source_target_pairs={{0,1},{1,0},{2,6},{3,7},{4,5},{5,4},{6,2},{7,3},{8,9},{9,8},{10,14... | collective-permute-start | bytes 2985992 | tf_op jit(solution)/shard_map/ppermute | solution.py:72
  15.4 42.7 %collective-permute-start.7 = (bf16[144,3456]{1,0:T(8,128)(2,1)S(1)}, bf16[144,3456]{1,0:T(8,128)(2,1)}, u32[]{:S(2)}, u32[]{:S(2)}) collective-permute-start(bf16[144,3456]{1,0:T(8,128)(2,1)S(1)} %copy-done.5), channel_id=1, source_target_pairs={{0,4},{1,5},{2,3},{3,2},{4,0},{5,1},{6,7},{7,6},{8,12},{9,13},{10,... | collective-permute-start | bytes 2985992 | tf_op jit(solution)/shard_map/ppermute | solution.py:72
  16.6 91.4 %collective-permute-start.10 = (bf16[144,3456]{1,0:T(8,128)(2,1)S(1)}, bf16[144,3456]{1,0:T(8,128)(2,1)}, u32[]{:S(2)}, u32[]{:S(2)}) collective-permute-start(bf16[144,3456]{1,0:T(8,128)(2,1)S(1)} %copy-done.5), channel_id=1, source_target_pairs={{0,2},{1,3},{2,0},{3,1},{4,6},{5,7},{6,4},{7,5},{8,10},{9,11},{10,... | collective-permute-start | bytes 2985992 | tf_op jit(solution)/shard_map/ppermute | solution.py:72
  17.3 88.5 %collective-permute-start.3 = (bf16[1,512,1152]{2,1,0:T(8,128)(2,1)}, bf16[1,512,1152]{2,1,0:T(8,128)(2,1)}, u32[]{:S(2)}, u32[]{:S(2)}) collective-permute-start(bf16[1,512,1152]{2,1,0:T(8,128)(2,1)} %param.14), channel_id=1, source_target_pairs={{1,2},{2,1},{5,6},{6,5},{9,10},{10,9},{13,14},{14,13},{17,18},{18,... | collective-permute-start | bytes 3538952 | tf_op jit(solution)/shard_map/ppermute | solution.py:78
  19.4 31.3 %collective-permute-start.2 = (bf16[4,2432]{1,0:T(4,128)(2,1)S(1)}, bf16[4,2432]{1,0:T(4,128)(2,1)S(1)}, u32[]{:S(2)}, u32[]{:S(2)}) collective-permute-start(bf16[4,2432]{1,0:T(4,128)(2,1)S(1)} %maximum_select_fusion.4), channel_id=1, source_target_pairs={{0,4},{1,5},{2,6},{3,7},{4,0},{5,1},{6,2},{7,3},{8,12},{9,13},{10,... | collective-permute-start | bytes 58376 | tf_op jit(solution)/shard_map/ppermute | solution.py:72
  51.8 3.1 collective-permute-start.4
  55.0 32.1 %collective-permute-start.5 = (f32[1,6912]{1,0:T(1,128)S(1)}, f32[1,6912]{1,0:T(1,128)S(1)}, u32[]{:S(2)}, u32[]{:S(2)}) collective-permute-start(f32[1,6912]{1,0:T(1,128)S(1)} %broadcast_select_fusion.4), channel_id=1, source_target_pairs={{0,1},{1,0},{2,3},{3,2},{4,5},{5,4},{6,7},{7,6},{8,9},{9,8},{10,11... | collective-permute-start | bytes 82952 | tf_op jit(solution)/shard_map/ppermute | solution.py:72
  58.1 35.0 %collective-permute-start.9 = (bf16[144,3456]{1,0:T(8,128)(2,1)}, bf16[144,3456]{1,0:T(8,128)(2,1)S(1)}, u32[]{:S(2)}, u32[]{:S(2)}) collective-permute-start(bf16[144,3456]{1,0:T(8,128)(2,1)} %collective-permute-done.7.refs_1_), channel_id=1, source_target_pairs={{0,1},{1,0},{2,6},{3,7},{4,5},{5,4},{6,2},{7,3},{8,9},{9,8},{10,14... | collective-permute-start | bytes 2985992 | tf_op jit(solution)/shard_map/ppermute | solution.py:72
  88.5 19.6 %collective-permute-start.11 = (bf16[144,3456]{1,0:T(8,128)(2,1)}, bf16[144,3456]{1,0:T(8,128)(2,1)S(1)}, u32[]{:S(2)}, u32[]{:S(2)}) collective-permute-start(bf16[144,3456]{1,0:T(8,128)(2,1)} %collective-permute-done.7.refs_1_), channel_id=1, source_target_pairs={{0,2},{1,3},{2,0},{3,1},{4,6},{5,7},{6,4},{7,5},{8,10},{9,11},{10,... | collective-permute-start | bytes 2985992 | tf_op jit(solution)/shard_map/ppermute | solution.py:72
  88.7 19.3 %collective-permute-start.12 = (bf16[144,3456]{1,0:T(8,128)(2,1)}, bf16[144,3456]{1,0:T(8,128)(2,1)S(1)}, u32[]{:S(2)}, u32[]{:S(2)}) collective-permute-start(bf16[144,3456]{1,0:T(8,128)(2,1)} %collective-permute-done.8.refs_2_), channel_id=1, source_target_pairs={{0,2},{1,3},{2,0},{3,1},{4,6},{5,7},{6,4},{7,5},{8,10},{9,11},{10,... | collective-permute-start | bytes 2985992 | tf_op jit(solution)/shard_map/ppermute | solution.py:72
  93.1 14.9 %collective-permute-start.13 = (bf16[144,3456]{1,0:T(8,128)(2,1)S(1)}, bf16[144,3456]{1,0:T(8,128)(2,1)S(1)}, u32[]{:S(2)}, u32[]{:S(2)}) collective-permute-start(bf16[144,3456]{1,0:T(8,128)(2,1)S(1)} %collective-permute-done.9.refs_3_), channel_id=1, source_target_pairs={{0,2},{1,3},{2,0},{3,1},{4,6},{5,7},{6,4},{7,5},{8,10},{9,11},{10,... | collective-permute-start | bytes 2985992 | tf_op jit(solution)/shard_map/ppermute | solution.py:72
  121.1 34.6 %collective-permute-start.14 = (bf16[512,2304]{1,0:T(8,128)(2,1)}, bf16[512,2304]{1,0:T(8,128)(2,1)}, u32[]{:S(2)}, u32[]{:S(2)}) collective-permute-start(bf16[512,2304]{1,0:T(8,128)(2,1)} %slice.163.own_ref), channel_id=1, source_target_pairs={{0,2},{1,3},{2,0},{3,1},{4,6},{5,7},{6,4},{7,5},{8,10},{9,11},{10,... | collective-permute-start | bytes 7077896 | tf_op jit(solution)/shard_map/ppermute | solution.py:72
  121.4 16.3 %collective-permute-start.15 = (bf16[144,1152]{1,0:T(8,128)(2,1)S(1)}, bf16[144,1152]{1,0:T(8,128)(2,1)S(1)}, u32[]{:S(2)}, u32[]{:S(2)}) collective-permute-start(bf16[144,1152]{1,0:T(8,128)(2,1)S(1)} %copy-done.6), channel_id=1, source_target_pairs={{0,4},{1,5},{2,3},{3,2},{4,0},{5,1},{6,7},{7,6},{8,12},{9,13},{10,... | collective-permute-start | bytes 995336 | tf_op jit(solution)/shard_map/ppermute | solution.py:72
  121.4 18.0 %collective-permute-start.16 = (bf16[144,1152]{1,0:T(8,128)(2,1)S(1)}, bf16[144,1152]{1,0:T(8,128)(2,1)S(1)}, u32[]{:S(2)}, u32[]{:S(2)}) collective-permute-start(bf16[144,1152]{1,0:T(8,128)(2,1)S(1)} %copy-done.6), channel_id=1, source_target_pairs={{0,1},{1,0},{2,6},{3,7},{4,5},{5,4},{6,2},{7,3},{8,9},{9,8},{10,14... | collective-permute-start | bytes 995336 | tf_op jit(solution)/shard_map/ppermute | solution.py:72
  137.7 8.2 %collective-permute-start.17 = (bf16[144,1152]{1,0:T(8,128)(2,1)S(1)}, bf16[144,1152]{1,0:T(8,128)(2,1)S(1)}, u32[]{:S(2)}, u32[]{:S(2)}) collective-permute-start(bf16[144,1152]{1,0:T(8,128)(2,1)S(1)} %collective-permute-done.15.refs_1_), channel_id=1, source_target_pairs={{0,1},{1,0},{2,6},{3,7},{4,5},{5,4},{6,2},{7,3},{8,9},{9,8},{10,14... | collective-permute-start | bytes 995336 | tf_op jit(solution)/shard_map/ppermute | solution.py:72
  138.9 8.9 %collective-permute-start.18 = (bf16[144,1152]{1,0:T(8,128)(2,1)S(1)}, bf16[144,1152]{1,0:T(8,128)(2,1)}, u32[]{:S(2)}, u32[]{:S(2)}) collective-permute-start(bf16[144,1152]{1,0:T(8,128)(2,1)S(1)} %copy-done.6), channel_id=1, source_target_pairs={{0,2},{1,3},{2,0},{3,1},{4,6},{5,7},{6,4},{7,5},{8,10},{9,11},{10,... | collective-permute-start | bytes 995336 | tf_op jit(solution)/shard_map/ppermute | solution.py:72
  139.2 11.2 %collective-permute-start.19 = (bf16[144,1152]{1,0:T(8,128)(2,1)S(1)}, bf16[144,1152]{1,0:T(8,128)(2,1)}, u32[]{:S(2)}, u32[]{:S(2)}) collective-permute-start(bf16[144,1152]{1,0:T(8,128)(2,1)S(1)} %collective-permute-done.15.refs_1_), channel_id=1, source_target_pairs={{0,2},{1,3},{2,0},{3,1},{4,6},{5,7},{6,4},{7,5},{8,10},{9,11},{10,... | collective-permute-start | bytes 995336 | tf_op jit(solution)/shard_map/ppermute | solution.py:72
  139.4 10.9 %collective-permute-start.20 = (bf16[144,1152]{1,0:T(8,128)(2,1)S(1)}, bf16[144,1152]{1,0:T(8,128)(2,1)}, u32[]{:S(2)}, u32[]{:S(2)}) collective-permute-start(bf16[144,1152]{1,0:T(8,128)(2,1)S(1)} %collective-permute-done.16.refs_2_), channel_id=1, source_target_pairs={{0,2},{1,3},{2,0},{3,1},{4,6},{5,7},{6,4},{7,5},{8,10},{9,11},{10,... | collective-permute-start | bytes 995336 | tf_op jit(solution)/shard_map/ppermute | solution.py:72
  145.9 4.4 collective-permute-start.21
  147.8 56.7 %collective-permute-start.23 = (bf16[1,512,1152]{2,1,0:T(8,128)(2,1)}, bf16[1,512,1152]{2,1,0:T(8,128)(2,1)}, u32[]{:S(2)}, u32[]{:S(2)}) collective-permute-start(bf16[1,512,1152]{2,1,0:T(8,128)(2,1)} %param.27), channel_id=1, source_target_pairs={{1,2},{2,1},{5,6},{6,5},{9,10},{10,9},{13,14},{14,13},{17,18},{18,... | collective-permute-start | bytes 3538952 | tf_op jit(solution)/shard_map/ppermute | solution.py:78
  273.6 281.8 %all-reduce.5.cloned.1.call-start = ((), (), s32[]{:S(2)}) async-start(), calls=%async_computation.4 | async-start | bytes 2654208 | tf_op jit(solution)/shard_map/psum | solution.py:461
  274.8 64.8 %collective-permute-start.22 = (bf16[1,512,1152]{2,1,0:T(8,128)(2,1)S(1)}, bf16[1,512,1152]{2,1,0:T(8,128)(2,1)}, u32[]{:S(2)}, u32[]{:S(2)}) collective-permute-start(bf16[1,512,1152]{2,1,0:T(8,128)(2,1)S(1)} %copy-done.30), channel_id=1, source_target_pairs={{1,2},{2,1},{5,6},{6,5},{9,10},{10,9},{13,14},{14,13},{17,18},{18,... | collective-permute-start | bytes 3538952 | tf_op jit(solution)/shard_map/ppermute | solution.py:78
  279.6 52.6 %collective-permute-start.35 = (bf16[2,2,144,1152]{3,2,1,0:T(8,128)(2,1)S(1)}, bf16[2,2,144,1152]{3,2,1,0:T(8,128)(2,1)S(1)}, u32[]{:S(2)}, u32[]{:S(2)}) collective-permute-start(bf16[2,2,144,1152]{3,2,1,0:T(8,128)(2,1)S(1)} %dynamic-slice_bitcast_fusion.2), channel_id=1, source_target_pairs={{0,2},{1,3},{2,0},{3,1},{4,6},{5,7},{6,4},{7,5},{8,10},{9,11},{10,... | collective-permute-start | bytes 3981320 | tf_op jit(solution)/shard_map/ppermute | solution.py:72
  323.2 22.6 %collective-permute-start.24 = (bf16[512,2304]{1,0:T(8,128)(2,1)}, bf16[512,2304]{1,0:T(8,128)(2,1)S(1)}, u32[]{:S(2)}, u32[]{:S(2)}) collective-permute-start(bf16[512,2304]{1,0:T(8,128)(2,1)} %get-tuple-element.27), channel_id=1, source_target_pairs={{0,2},{1,3},{2,0},{3,1},{4,6},{5,7},{6,4},{7,5},{8,10},{9,11},{10,... | collective-permute-start | bytes 7077896 | tf_op jit(solution)/shard_map/ppermute | solution.py:72
  332.8 11.8 %collective-permute-start.36 = (bf16[2,144,1152]{2,1,0:T(8,128)(2,1)S(1)}, bf16[2,144,1152]{2,1,0:T(8,128)(2,1)S(1)}, u32[]{:S(2)}, u32[]{:S(2)}) collective-permute-start(bf16[2,144,1152]{2,1,0:T(8,128)(2,1)S(1)} %pad_maximum_fusion.5), channel_id=1, source_target_pairs={{0,4},{1,5},{2,3},{3,2},{4,0},{5,1},{6,7},{7,6},{8,12},{9,13},{10,... | collective-permute-start | bytes 1990664 | tf_op jit(solution)/shard_map/ppermute | solution.py:72
  339.1 55.2 %collective-permute-start.41 = (bf16[2,2,144,4608]{3,2,1,0:T(8,128)(2,1)}, bf16[2,2,144,4608]{3,2,1,0:T(8,128)(2,1)}, u32[]{:S(2)}, u32[]{:S(2)}) collective-permute-start(bf16[2,2,144,4608]{3,2,1,0:T(8,128)(2,1)} %dynamic-slice_bitcast_fusion), channel_id=1, source_target_pairs={{0,2},{1,3},{2,0},{3,1},{4,6},{5,7},{6,4},{7,5},{8,10},{9,11},{10,... | collective-permute-start | bytes 15925256 | tf_op jit(solution)/shard_map/ppermute | solution.py:72
  361.0 3.2 collective-permute-start.26
  362.9 41.7 %collective-permute-start.37 = (bf16[144,1152]{1,0:T(8,128)(2,1)}, bf16[144,1152]{1,0:T(8,128)(2,1)}, u32[]{:S(2)}, u32[]{:S(2)}) collective-permute-start(bf16[144,1152]{1,0:T(8,128)(2,1)} %fusion.45), channel_id=1, source_target_pairs={{0,1},{1,0},{2,6},{3,7},{4,5},{5,4},{6,2},{7,3},{8,9},{9,8},{10,14... | collective-permute-start | bytes 995336 | tf_op jit(solution)/shard_map/ppermute | solution.py:72
  364.3 10.0 %collective-permute-start.27 = (f32[2,16128]{1,0:T(2,128)S(1)}, f32[2,16128]{1,0:T(2,128)S(1)}, u32[]{:S(2)}, u32[]{:S(2)}) collective-permute-start(f32[2,16128]{1,0:T(2,128)S(1)} %maximum_select_fusion.2), channel_id=1, source_target_pairs={{0,2},{1,3},{2,0},{3,1},{4,6},{5,7},{6,4},{7,5},{8,10},{9,11},{10,... | collective-permute-start | bytes 387080 | tf_op jit(solution)/shard_map/ppermute | solution.py:72
  374.6 8.8 %collective-permute-start.28 = (f32[4,16128]{1,0:T(4,128)S(1)}, f32[4,16128]{1,0:T(4,128)S(1)}, u32[]{:S(2)}, u32[]{:S(2)}) collective-permute-start(f32[4,16128]{1,0:T(4,128)S(1)} %maximum_select_fusion.1), channel_id=1, source_target_pairs={{0,4},{1,5},{2,6},{3,7},{4,0},{5,1},{6,2},{7,3},{8,12},{9,13},{10,... | collective-permute-start | bytes 774152 | tf_op jit(solution)/shard_map/ppermute | solution.py:72
  379.0 40.6 %collective-permute-start.38 = (bf16[2,2,144,3456]{3,2,1,0:T(8,128)(2,1)}, bf16[2,2,144,3456]{3,2,1,0:T(8,128)(2,1)}, u32[]{:S(2)}, u32[]{:S(2)}) collective-permute-start(bf16[2,2,144,3456]{3,2,1,0:T(8,128)(2,1)} %dynamic-slice_bitcast_fusion.1), channel_id=1, source_target_pairs={{0,2},{1,3},{2,0},{3,1},{4,6},{5,7},{6,4},{7,5},{8,10},{9,11},{10,... | collective-permute-start | bytes 11943944 | tf_op jit(solution)/shard_map/ppermute | solution.py:72
  388.8 3.7 collective-permute-start.30
  391.9 19.7 %collective-permute-start.34 = (f32[29376]{0:T(1024)}, f32[29376]{0:T(1024)S(1)}, u32[]{:S(2)}, u32[]{:S(2)}) collective-permute-start(f32[29376]{0:T(1024)} %concatenate.109), channel_id=1, source_target_pairs={{0,24},{8,0},{16,8},{24,16},{1,25},{9,1},{17,9},{25,17},{2,26},{10... | collective-permute-start | bytes 352520 | tf_op jit(solution)/shard_map/ppermute | solution.py:100
  392.5 23.8 %collective-permute-start.33 = (f32[29376]{0:T(1024)}, f32[29376]{0:T(1024)}, u32[]{:S(2)}, u32[]{:S(2)}) collective-permute-start(f32[29376]{0:T(1024)} %concatenate.109), channel_id=1, source_target_pairs={{0,16},{8,24},{16,0},{24,8},{1,17},{9,25},{17,1},{25,9},{2,18},{10... | collective-permute-start | bytes 352520 | tf_op jit(solution)/shard_map/ppermute | solution.py:100
  394.3 12.4 %collective-permute-start.31 = (f32[4,4,144]{2,1,0:T(4,128)S(1)}, f32[4,4,144]{2,1,0:T(4,128)S(1)}, u32[]{:S(2)}, u32[]{:S(2)}) collective-permute-start(f32[4,4,144]{2,1,0:T(4,128)S(1)} %maximum_select_fusion.5), channel_id=1, source_target_pairs={{0,4},{1,5},{2,6},{3,7},{4,0},{5,1},{6,2},{7,3},{8,12},{9,13},{10,... | collective-permute-start | bytes 27656 | tf_op jit(solution)/shard_map/ppermute | solution.py:72
  404.6 13.4 %collective-permute-start.32 = (f32[29376]{0:T(1024)}, f32[29376]{0:T(1024)}, u32[]{:S(2)}, u32[]{:S(2)}) collective-permute-start(f32[29376]{0:T(1024)} %concatenate.109), channel_id=1, source_target_pairs={{0,8},{8,16},{16,24},{24,0},{1,9},{9,17},{17,25},{25,1},{2,10},{10... | collective-permute-start | bytes 352520 | tf_op jit(solution)/shard_map/ppermute | solution.py:100
  406.7 45.2 %collective-permute-start.42 = (bf16[2,144,4608]{2,1,0:T(8,128)(2,1)}, bf16[2,144,4608]{2,1,0:T(8,128)(2,1)}, u32[]{:S(2)}, u32[]{:S(2)}) collective-permute-start(bf16[2,144,4608]{2,1,0:T(8,128)(2,1)} %pad_maximum_fusion.1), channel_id=1, source_target_pairs={{0,4},{1,5},{2,3},{3,2},{4,0},{5,1},{6,7},{7,6},{8,12},{9,13},{10,... | collective-permute-start | bytes 7962632 | tf_op jit(solution)/shard_map/ppermute | solution.py:72
  412.2 215.2 %collective-permute-start.25 = (bf16[1,512,1152]{2,1,0:T(8,128)(2,1)}, bf16[1,512,1152]{2,1,0:T(8,128)(2,1)}, u32[]{:S(2)}, u32[]{:S(2)}) collective-permute-start(bf16[1,512,1152]{2,1,0:T(8,128)(2,1)} %get-tuple-element.71), channel_id=1, source_target_pairs={{1,2},{2,1},{5,6},{6,5},{9,10},{10,9},{13,14},{14,13},{17,18},{18,... | collective-permute-start | bytes 3538952 | tf_op jit(solution)/shard_map/ppermute | solution.py:78
  424.5 70.0 %collective-permute-start.39 = (bf16[2,144,3456]{2,1,0:T(8,128)(2,1)S(1)}, bf16[2,144,3456]{2,1,0:T(8,128)(2,1)S(1)}, u32[]{:S(2)}, u32[]{:S(2)}) collective-permute-start(bf16[2,144,3456]{2,1,0:T(8,128)(2,1)S(1)} %pad_maximum_fusion.2), channel_id=1, source_target_pairs={{0,4},{1,5},{2,3},{3,2},{4,0},{5,1},{6,7},{7,6},{8,12},{9,13},{10,... | collective-permute-start | bytes 5971976 | tf_op jit(solution)/shard_map/ppermute | solution.py:72
  458.0 41.7 %collective-permute-start.43 = (bf16[144,4608]{1,0:T(8,128)(2,1)}, bf16[144,4608]{1,0:T(8,128)(2,1)}, u32[]{:S(2)}, u32[]{:S(2)}) collective-permute-start(bf16[144,4608]{1,0:T(8,128)(2,1)} %fusion.33), channel_id=1, source_target_pairs={{0,1},{1,0},{2,6},{3,7},{4,5},{5,4},{6,2},{7,3},{8,9},{9,8},{10,14... | collective-permute-start | bytes 3981320 | tf_op jit(solution)/shard_map/ppermute | solution.py:72
  497.0 121.8 %all-reduce.7.cloned.1.call-start = ((), (), s32[]{:S(2)}) async-start(), calls=%async_computation.5 | async-start | bytes 2654208 | tf_op jit(solution)/shard_map/psum | solution.py:469
  499.6 58.7 %collective-permute-start.40 = (bf16[144,3456]{1,0:T(8,128)(2,1)}, bf16[144,3456]{1,0:T(8,128)(2,1)}, u32[]{:S(2)}, u32[]{:S(2)}) collective-permute-start(bf16[144,3456]{1,0:T(8,128)(2,1)} %fusion.37), channel_id=1, source_target_pairs={{0,1},{1,0},{2,6},{3,7},{4,5},{5,4},{6,2},{7,3},{8,9},{9,8},{10,14... | collective-permute-start | bytes 2985992 | tf_op jit(solution)/shard_map/ppermute | solution.py:72
  555.4 126.6 %all-reduce.9.cloned.1.call-start = ((), (), s32[]{:S(2)}) async-start(), calls=%async_computation.6 | async-start | bytes 2654208 | tf_op jit(solution)/shard_map/psum | solution.py:493
  (64 other events, 761.5 us)
Sparse Core Ops, SparseCore 0:
  10.0 94.4 all-gather.2
  106.3 88.6 all-gather.4
  273.7 85.5 reduce-scatter.1
  497.1 58.2 all-reduce.4
  558.1 60.5 all-reduce.6
  621.0 60.9 all-reduce.8

commit v4 on v3

--- a/solution.py
+++ b/solution.py
@@ -1,3 +1,5 @@
+import functools
+
 import jax
 import jax.numpy as jnp
 from jax import lax
@@ -146,7 +148,7 @@
     )(order, *pieces)
 
 
-def gather_weight(shard):
+def gather_pieces(shard):
     place = place_of()
     near = jnp.where((place & 2) == 0, 4, 1)
     far = 5 - near
@@ -158,47 +160,90 @@
     pieces = held + [permute(piece, core_rule) for piece in held]
     order = [place, place ^ near, place ^ far, place ^ 5]
     order += [other, other ^ far, other ^ near, other ^ 5]
-    return assemble(pieces, jnp.stack(order).astype(jnp.int32))
-
-
-def reduce_scatter(partial):
-    low = partial.dtype
-    place = place_of()
-    core = (place >> 1) & 1
-    _, rows, columns = partial.shape
-    spread = partial.reshape(2, 2, 2, rows, columns)
-
-    def core_half(which):
-        return lax.dynamic_index_in_dim(spread, which, 1, keepdims=False)
-
-    received = permute(core_half(1 - core), core_rule)
-    kept = (core_half(core).astype(jnp.float32) + received.astype(jnp.float32)).astype(low)
-    kept = kept.reshape(4, rows, columns)
-    mine = ((place >> 2) << 1) | (place & 1)
-    near = jnp.where(core == 0, 2, 1)
-    far = 3 - near
-
-    def block(which):
-        return lax.dynamic_slice_in_dim(kept, which, 1, 0)
-
-    received = permute(jnp.concatenate([block(mine ^ near), block(mine ^ 3)]), first_rule)
-    halved = jnp.concatenate([block(mine), block(mine ^ far)]).astype(jnp.float32)
-    halved = halved + received.astype(jnp.float32)
-    received = permute(halved[1].astype(low), second_rule)
-    return halved[0] + received.astype(jnp.float32)
+    return pieces, jnp.stack(order).astype(jnp.int32)
+
+
+def tie(*values):
+    return lax.optimization_barrier(values)
+
+
+class Scatter:
+    def __init__(self, partial):
+        _, rows, columns = partial.shape
+        self.place = place_of()
+        self.core = (self.place >> 1) & 1
+        self.partial = partial.reshape(2, 2, 2, rows, columns)
+        self.received = permute(self.half(1 - self.core), core_rule)
+
+    def half(self, core):
+        return lax.dynamic_index_in_dim(self.partial, core, 1, keepdims=False)
+
+    def second(self):
+        _, _, _, rows, columns = self.partial.shape
+        kept = self.half(self.core).astype(jnp.float32) + self.received.astype(jnp.float32)
+        kept = kept.astype(self.partial.dtype).reshape(4, rows, columns)
+        mine = ((self.place >> 2) << 1) | (self.place & 1)
+        near = jnp.where(self.core == 0, 2, 1)
+
+        def pair(which):
+            parts = [which, which ^ 3 ^ near]
+            return jnp.concatenate([lax.dynamic_slice_in_dim(kept, at, 1, 0) for at in parts])
+
+        self.kept = pair(mine)
+        self.received = permute(pair(mine ^ near), first_rule)
+
+    def third(self):
+        kept = self.kept.astype(jnp.float32) + self.received.astype(jnp.float32)
+        self.kept = kept[0]
+        self.received = permute(kept[1].astype(self.partial.dtype), second_rule)
+
+    def result(self):
+        return self.kept + self.received.astype(jnp.float32)
+
+
+def reduce_replicas(partial, replicas):
+    span = partial.shape[1] // replicas
+    own = lax.axis_index("rep")
+
+    def piece(values, which):
+        return lax.dynamic_slice_in_dim(values, which % replicas * span, span, 1)
+
+    low = partial.astype(jnp.bfloat16)
+    total = piece(partial, own)
+    for shift in range(1, replicas):
+        pairs = [(at, (at + shift) % replicas) for at in range(replicas)]
+        received = lax.ppermute(piece(low, own + shift), "rep", pairs)
+        total = total + received.astype(jnp.float32)
+    stacked = gather_replicas(total.astype(jnp.bfloat16), replicas)
+    whole = jnp.zeros(partial.shape, jnp.float32)
+    for shift in range(replicas):
+        whole = lax.dynamic_update_slice_in_dim(
+            whole, stacked[shift].astype(jnp.float32), (own - shift) % replicas * span, 1
+        )
+    return whole
 
 
 WINDOW = 256
-
-
-def head_window(width):
-    first = pl.program_id(0) * HEAD
+SHORT = pl.CostEstimate(flops=1 << 20, bytes_accessed=1 << 20, transcendentals=0)
+GELU_RATE = 0.7978845608028654
+GELU_CUBE = 0.044715
+
+
+def head_lanes(heads, width):
+    low = heads[0] * HEAD // 128 * 128
+    high = -(-(heads[-1] + 1) * HEAD // 128) * 128
+    return min(low, width - WINDOW), high
+
+
+def head_window(first_head, width, base):
+    first = (first_head + pl.program_id(0)) * HEAD
     start = jnp.minimum(first // 128 * 128, width - WINDOW)
     start = pl.multiple_of(start, 128)
     lane = lax.broadcasted_iota(jnp.int32, (1, WINDOW), 1) + start
     inside = (lane >= first) & (lane < first + HEAD)
     mask = jnp.where(inside, 1.0, 0.0).astype(jnp.bfloat16)
-    return pl.ds(start, WINDOW), pl.ds(pl.multiple_of(start + width, 128), WINDOW), mask
+    lanes = [pl.ds(pl.multiple_of(start + at, 128), WINDOW) for at in (0, width, -base)]
+    return (*lanes, mask)
 
 
 def dot_last(left, right):
@@ -213,10 +258,10 @@
     )
 
 
-def attend_kernel(query_ref, own_ref, other_ref, out_ref, log_ref, total_ref):
+def attend_kernel(first_head, base, query_ref, own_ref, other_ref, out_ref, log_ref, total_ref):
     length, width = query_ref.shape
     head = pl.program_id(0)
-    key_lanes, value_lanes, mask = head_window(width)
+    key_lanes, value_lanes, out_lanes, mask = head_window(first_head, width, base)
     score_scale = float(HEAD) ** (-0.5)
 
     @pl.when(head == 0)
@@ -234,27 +279,26 @@
         weights = jnp.exp((scores - row_max) * score_scale)
         row_total = jnp.sum(weights, -1, keepdims=True)
         probs = (weights * (1.0 / row_total)).astype(jnp.bfloat16)
-        total_ref[block, key_lanes] += jnp.dot(
+        total_ref[block, out_lanes] += jnp.dot(
             probs, values, preferred_element_type=jnp.float32
         )
         log_total = row_max * score_scale + jnp.log(row_total)
         lane = lax.broadcasted_iota(jnp.int32, (rows, 128), 1)
-        log_ref[block, :] = jnp.where(lane == head, log_total, log_ref[block, :])
+        log_ref[block, :] = jnp.where(lane == first_head + head, log_total, log_ref[block, :])
 
     @pl.when(head == pl.num_programs(0) - 1)
     def _():
         out_ref[...] = total_ref[...].astype(out_ref.dtype)
 
 
-def attend(query, own, other):
+def attend(query, own, other, heads):
     length, width = query.shape
-    heads = width // HEAD
-    keys = own.shape[0] + other.shape[0]
+    low, high = head_lanes(heads, width)
     return pl.pallas_call(
-        attend_kernel,
-        grid=(heads,),
+        functools.partial(attend_kernel, heads[0], low),
+        grid=(len(heads),),
         out_shape=(
-            jax.ShapeDtypeStruct((length, width), jnp.bfloat16),
+            jax.ShapeDtypeStruct((length, high - low), jnp.bfloat16),
             jax.ShapeDtypeStruct((length, 128), jnp.float32),
         ),
         in_specs=[
@@ -263,32 +307,29 @@
             pl.BlockSpec(other.shape, lambda head: (0, 0)),
         ],
         out_specs=(
-            pl.BlockSpec((length, width), lambda head: (0, 0)),
+            pl.BlockSpec((length, high - low), lambda head: (0, 0)),
             pl.BlockSpec((length, 128), lambda head: (0, 0)),
         ),
-        scratch_shapes=[pltpu.VMEM((length, width), jnp.float32)],
+        scratch_shapes=[pltpu.VMEM((length, high - low), jnp.float32)],
         compiler_params=pltpu.CompilerParams(vmem_limit_bytes=48 << 20),
-        cost_estimate=pl.CostEstimate(
-            flops=4 * heads * length * keys * WINDOW,
-            bytes_accessed=4 * length * width * 4,
-            transcendentals=heads * length * keys,
-        ),
+        cost_estimate=SHORT,
     )(query, own, other)
 
 
 def attend_back_kernel(
-    query_ref, own_ref, other_ref, upstream_ref, log_ref, d_query_ref, d_own_ref, d_other_ref,
-    query_total, pair_total,
+    first_head, base, query_ref, own_ref, other_ref, upstream_ref, log_ref, d_query_ref, d_own_ref, d_other_ref,
+    query_total, key_total, value_total,
 ):
     length, width = query_ref.shape
     head = pl.program_id(0)
-    key_lanes, value_lanes, mask = head_window(width)
+    key_lanes, value_lanes, out_lanes, mask = head_window(first_head, width, base)
     score_scale = float(HEAD) ** (-0.5)
 
     @pl.when(head == 0)
     def _():
         query_total[...] = jnp.zeros_like(query_total)
-        pair_total[...] = jnp.zeros_like(pair_total)
+        key_total[...] = jnp.zeros_like(key_total)
+        value_total[...] = jnp.zeros_like(value_total)
 
     keys = jnp.concatenate([own_ref[:, key_lanes], other_ref[:, key_lanes]]) * mask
     values = jnp.concatenate([own_ref[:, value_lanes], other_ref[:, value_lanes]]) * mask
@@ -303,57 +344,116 @@
         weighted = probs * d_probs
         row_sum = jnp.sum(weighted, 0, keepdims=True)
         d_scores = (weighted - probs * row_sum).astype(jnp.bfloat16)
-        pair_total[:, value_lanes] += jnp.dot(
+        value_total[:, out_lanes] += jnp.dot(
             probs.astype(jnp.bfloat16), upstream, preferred_element_type=jnp.float32
         )
-        pair_total[:, key_lanes] += score_scale * jnp.dot(
+        key_total[:, out_lanes] += score_scale * jnp.dot(
             d_scores, query, preferred_element_type=jnp.float32
         )
-        query_total[block, key_lanes] += dot_first(d_scores, keys)
+        query_total[block, out_lanes] += dot_first(d_scores, keys)
 
     @pl.when(head == pl.num_programs(0) - 1)
     def _():
         d_query_ref[...] = (query_total[...] * score_scale).astype(d_query_ref.dtype)
-        d_own_ref[...] = pair_total[: own_ref.shape[0]]
-        d_other_ref[...] = pair_total[own_ref.shape[0] :].astype(d_other_ref.dtype)
-
-
-def attend_back(query, own, other, upstream, log_totals):
+        for at, total in enumerate((key_total, value_total)):
+            d_own_ref[at] = total[: own_ref.shape[0]]
+            d_other_ref[at] = total[own_ref.shape[0] :].astype(d_other_ref.dtype)
+
+
+def attend_back(query, own, other, upstream, log_totals, heads):
     length, width = query.shape
-    heads = width // HEAD
-    keys = own.shape[0] + other.shape[0]
+    low, high = head_lanes(heads, width)
+    span = high - low
     whole = lambda head: (0, 0)
+    halves = pl.BlockSpec((2, own.shape[0], span), lambda head: (0, 0, 0))
     return pl.pallas_call(
-        attend_back_kernel,
-        grid=(heads,),
+        functools.partial(attend_back_kernel, heads[0], low),
+        grid=(len(heads),),
         out_shape=(
-            jax.ShapeDtypeStruct((length, width), jnp.bfloat16),
-            jax.ShapeDtypeStruct(own.shape, jnp.float32),
-            jax.ShapeDtypeStruct(other.shape, jnp.bfloat16),
+            jax.ShapeDtypeStruct((length, span), jnp.bfloat16),
+            jax.ShapeDtypeStruct((2, own.shape[0], span), jnp.float32),
+            jax.ShapeDtypeStruct((2, other.shape[0], span), jnp.bfloat16),
         ),
         in_specs=[
             pl.BlockSpec((length, width), whole),
             pl.BlockSpec(own.shape, whole),
             pl.BlockSpec(other.shape, whole),
             pl.BlockSpec((length, width), whole),
-            pl.BlockSpec((1, 1, length), lambda head: (head, 0, 0)),
+            pl.BlockSpec((1, 1, length), lambda head: (heads[0] + head, 0, 0)),
         ],
-        out_specs=(
-            pl.BlockSpec((length, width), whole),
-            pl.BlockSpec(own.shape, whole),
-            pl.BlockSpec(other.shape, whole),
-        ),
+        out_specs=(pl.BlockSpec((length, span), whole), halves, halves),
         scratch_shapes=[
-            pltpu.VMEM((length, width), jnp.float32),
-            pltpu.VMEM((keys, own.shape[1]), jnp.float32),
+            pltpu.VMEM((length, span), jnp.float32),
+            pltpu.VMEM((own.shape[0] + other.shape[0], span), jnp.float32),
+            pltpu.VMEM((own.shape[0] + other.shape[0], span), jnp.float32),
         ],
         compiler_params=pltpu.CompilerParams(vmem_limit_bytes=56 << 20),
-        cost_estimate=pl.CostEstimate(
-            flops=10 * heads * length * keys * WINDOW,
-            bytes_accessed=12 * length * width * 4,
-            transcendentals=heads * length * keys,
+        cost_estimate=SHORT,
+    )(query, own, other, upstream, log_totals)
+
+
+def join_heads(left, right, width):
+    shared = left.shape[-1] + right.shape[-1] - width
+    if shared == 0:
+        return jnp.concatenate([left, right], axis=-1)
+    edge = left.shape[-1] - shared
+    middle = left[..., edge:] + right[..., :shared]
+    return jnp.concatenate([left[..., :edge], middle, right[..., shared:]], axis=-1)
+
+
+def mlp_kernel(
+    hidden_ref, upstream_ref, up_ref, bias_ref, down_ref,
+    branch_ref, d_hidden_ref, up_grad_ref, down_grad_ref, bias_grad_ref,
+):
+    @pl.when(pl.program_id(0) == 0)
+    def _():
+        branch_ref[...] = jnp.zeros_like(branch_ref)
+        d_hidden_ref[...] = jnp.zeros_like(d_hidden_ref)
+
+    hidden = hidden_ref[...]
+    upstream = upstream_ref[...]
+    preact = (
+        jnp.dot(hidden, up_ref[...], preferred_element_type=jnp.float32) + bias_ref[...]
+    )
+    square = preact * preact
+    bent = jnp.tanh(GELU_RATE * preact * (1.0 + GELU_CUBE * square))
+    half = 0.5 * (1.0 + bent)
+    slope = half + (0.5 * GELU_RATE) * preact * (1.0 - bent * bent) * (
+        1.0 + (3.0 * GELU_CUBE) * square
+    )
+    activated = (preact * half).astype(jnp.bfloat16)
+    branch_ref[...] += jnp.dot(activated, down_ref[...], preferred_element_type=jnp.float32)
+    d_preact = dot_last(upstream, down_ref[...]) * slope
+    d_preact = d_preact.astype(jnp.bfloat16)
+    bias_grad_ref[...] = jnp.sum(d_preact.astype(jnp.float32), 0, keepdims=True)
+    down_grad_ref[...] = dot_first(activated, upstream).astype(jnp.bfloat16)
+    d_hidden_ref[...] += dot_last(d_preact, up_ref[...])
+    up_grad_ref[...] = dot_first(hidden, d_preact).astype(jnp.bfloat16)
+
+
+def mlp(hidden, upstream, up, bias, down):
+    length, width = hidden.shape
+    units = up.shape[1]
+    block = 512
+    fixed = pl.BlockSpec((length, width), lambda at: (0, 0))
+    columns = pl.BlockSpec((width, block), lambda at: (0, at))
+    lanes = pl.BlockSpec((1, block), lambda at: (0, at))
+    rows = pl.BlockSpec((block, width), lambda at: (at, 0))
+    return pl.pallas_call(
+        mlp_kernel,
+        grid=(units // block,),
+        out_shape=(
+            jax.ShapeDtypeStruct((length, width), jnp.float32),
+            jax.ShapeDtypeStruct((length, width), jnp.float32),
+            jax.ShapeDtypeStruct(up.shape, jnp.bfloat16),
+            jax.ShapeDtypeStruct(down.shape, jnp.bfloat16),
+            jax.ShapeDtypeStruct((1, units), jnp.float32),
         ),
-    )(query, own, other, upstream, log_totals)
+        in_specs=[fixed, fixed, columns, lanes, rows],
+        out_specs=(fixed, fixed, columns, rows, lanes),
+        compiler_params=pltpu.CompilerParams(vmem_limit_bytes=56 << 20),
+        cost_estimate=SHORT,
+    )(hidden, upstream, up, bias, down)
 
 
 def per_device(
@@ -391,12 +491,16 @@
         ]
     )
     small_all = gather_group(small)
-    full_qkv = gather_weight(qkv_weight)
     latent_low = swap_halves(latent_in)
-    full_out = gather_weight(out_weight)
+    qkv_pieces, order = gather_pieces(qkv_weight)
+    qkv_pieces[3], up_weight, out_weight, down_weight, cotangent = tie(
+        qkv_pieces[3], up_weight, out_weight, down_weight, cotangent
+    )
+    full_up = lax.all_gather(up_weight, GROUP, axis=0, tiled=True)
+    out_pieces, _ = gather_pieces(out_weight)
+    down_pieces, _ = gather_pieces(down_weight)
     cotangent_low = swap_halves(cotangent)
-    full_up = lax.all_gather(up_weight, GROUP, axis=0, tiled=True)
-    full_down = lax.all_gather(down_weight, GROUP, axis=0, tiled=True)
+    full_qkv = assemble(qkv_pieces, order)
 
     bounds = [0, width]
     for bias in (qv_bias, out_bias, up_bias, down_bias):
@@ -438,37 +542,36 @@
     query = projected[:, :width]
     pair_own = projected[:, width:]
     pair_other = permute(pair_own, core_rule)
-    attended_low, log_totals = attend(query, pair_own, pair_other)
-    log_rows = log_totals[:, : width // HEAD].T[:, None, :]
+    heads = range(width // HEAD)
+    halves = heads[: len(heads) // 2], heads[len(heads) // 2 :]
+    attended, log_totals = attend(query, pair_own, pair_other, halves[0])
+    attended, query, down_pieces[1], down_pieces[2] = tie(
+        attended, query, down_pieces[1], down_pieces[2]
+    )
+    attended_right, log_right = attend(query, pair_own, pair_other, halves[1])
+    attended_low = join_heads(attended, attended_right, width)
+    log_rows = (log_totals + log_right)[:, : len(heads)].T[:, None, :]
+    full_out = assemble(out_pieces, order)
     branch_one = matmul(attended_low, full_out) + full_out_bias
     middle = latent + gate_one * branch_one
 
     normed_two, inverse_two = normalize(middle)
     hidden_two = (normed_two * (1.0 + scale_two) + shift_two).astype(jnp.bfloat16)
-    preact = matmul(hidden_two, full_up) + full_up_bias
-    activated, gelu_pull = jax.vjp(lambda inner: jax.nn.gelu(inner, approximate=True), preact)
-    activated_low = activated.astype(jnp.bfloat16)
-    branch_two = matmul(activated_low, full_down) + full_down_bias
+    full_down = assemble(down_pieces, order)
     mask_row = slot_mask[0]
+    d_out = cotangent_low[0].astype(jnp.float32) * mask_row
+    d_branch_two = (gate_two * d_out).astype(jnp.bfloat16)
+    branch_two, d_hidden_two, up_grad, down_grad, up_bias_grad = mlp(
+        hidden_two, d_branch_two, full_up, full_up_bias[None], full_down
+    )
+    up_scatter = Scatter(up_grad.reshape(SHARDS, rows, hidden_width))
+    down_shard = lax.psum_scatter(down_grad, GROUP, scatter_dimension=0, tiled=True)
+    branch_two = branch_two + full_down_bias
     block_out = (mask_row * (middle + gate_two * branch_two)).astype(jnp.bfloat16)
     block_out = swap_halves(block_out[None])
-
-    d_out = cotangent_low[0].astype(jnp.float32) * mask_row
     d_gate_two = jnp.sum(d_out * branch_two, axis=0)
-    d_branch_two = (gate_two * d_out).astype(jnp.bfloat16)
-    down_grad = matmul_left(activated_low, d_branch_two).astype(jnp.bfloat16)
-    down_shard = lax.psum_scatter(down_grad, GROUP, scatter_dimension=0, tiled=True)
-    down_total = lax.psum(down_shard, "rep")
     down_bias_grad = jnp.sum(d_branch_two.astype(jnp.float32), axis=0)
-    d_activated = matmul_right(d_branch_two, full_down)
-    d_preact = gelu_pull(d_activated)[0].astype(jnp.bfloat16)
-
-    up_grad = matmul_left(hidden_two, d_preact).astype(jnp.bfloat16)
-    up_shard = reduce_scatter(up_grad.reshape(SHARDS, rows, hidden_width))
-    up_shard, down_total = lax.optimization_barrier((up_shard.astype(jnp.bfloat16), down_total))
-    up_total = lax.psum(up_shard, "rep")
-    up_bias_grad = jnp.sum(d_preact.astype(jnp.float32), axis=0)
-    d_hidden_two = matmul_right(d_preact, full_up)
+    up_bias_grad = up_bias_grad[0]
     d_shift_two = jnp.sum(d_hidden_two, axis=0)
     d_scale_two = jnp.sum(d_hidden_two * normed_two, axis=0)
     d_middle = d_out + norm_back(d_hidden_two * (1.0 + scale_two), normed_two, inverse_two)
@@ -476,27 +579,44 @@
     d_branch_one = (gate_one * d_middle).astype(jnp.bfloat16)
 
     out_grad = matmul_left(attended_low, d_branch_one).astype(jnp.bfloat16)
-    out_shard = reduce_scatter(out_grad.reshape(SHARDS, rows, width))
+    out_scatter = Scatter(out_grad.reshape(SHARDS, rows, width))
     out_bias_grad = jnp.sum(d_branch_one.astype(jnp.float32), axis=0)
     d_attended = matmul_right(d_branch_one, full_out).astype(jnp.bfloat16)
-    d_query, d_pair, d_pair_other = attend_back(
-        query, pair_own, pair_other, d_attended, log_rows
-    )
-    d_pair = d_pair + permute(d_pair_other, core_rule).astype(jnp.float32)
-    d_projected = jnp.concatenate([d_query, d_pair.astype(jnp.bfloat16)], axis=-1)
+    left = attend_back(query, pair_own, pair_other, d_attended, log_rows, halves[0])
+    d_query, d_attended, up_scatter.received, out_scatter.received = tie(
+        left[0], d_attended, up_scatter.received, out_scatter.received
+    )
+    up_scatter.second()
+    out_scatter.second()
+    right = attend_back(query, pair_own, pair_other, d_attended, log_rows, halves[1])
+    d_query = join_heads(d_query, right[0], width)
+    d_own = join_heads(left[1], right[1], width)
+    d_other = permute(join_heads(left[2], right[2], width), core_rule)
+    d_own = (d_own + d_other.astype(jnp.float32)).astype(jnp.bfloat16)
+    d_projected = jnp.concatenate([d_query, d_own[0], d_own[1]], axis=-1)
 
     qkv_grad = matmul_left(hidden_one, d_projected).astype(jnp.bfloat16)
-    qkv_shard = reduce_scatter(qkv_grad.reshape(SHARDS, rows, 3 * width))
-    out_shard, qkv_shard, up_total = lax.optimization_barrier(
-        (out_shard.astype(jnp.bfloat16), qkv_shard.astype(jnp.bfloat16), up_total)
-    )
-    out_total, qkv_total = lax.psum((out_shard, qkv_shard), "rep")
+    qkv_scatter = Scatter(qkv_grad.reshape(SHARDS, rows, 3 * width))
     column_sums = jnp.sum(d_projected.astype(jnp.float32), axis=0)
     d_hidden_one = matmul_right(d_projected, full_qkv)
+    d_hidden_one, up_scatter.received, out_scatter.received, qkv_scatter.received = tie(
+        d_hidden_one, up_scatter.received, out_scatter.received, qkv_scatter.received
+    )
+    up_scatter.third()
+    out_scatter.third()
+    qkv_scatter.second()
     d_shift_one = jnp.sum(d_hidden_one, axis=0)
     d_scale_one = jnp.sum(d_hidden_one * normed_one, axis=0)
     latent_grad = d_middle + norm_back(d_hidden_one * (1.0 + scale_one), normed_one, inverse_one)
     latent_grad = swap_halves(latent_grad.astype(jnp.bfloat16)[None]).astype(jnp.float32)
+
+    down_total = lax.psum(down_shard, "rep")
+    up_shard, down_total = tie(up_scatter.result().astype(jnp.bfloat16), down_total)
+    up_total = lax.psum(up_shard, "rep")
+    qkv_scatter.third()
+    late = jnp.concatenate([out_scatter.result(), qkv_scatter.result()], axis=1)
+    late_total = reduce_replicas(late, replicas)
+    out_total, qkv_total = late_total[:, :width], late_total[:, width:]
 
     bias_grads = (
         jnp.concatenate([column_sums[:width], column_sums[2 * width :]]),

time: 702 us -> 721 us (1.027)
  matrix products: 117 us -> 37.9 us
  Pallas kernels: 77.8 us -> 133 us
  local copies, waits for them, and re-layouts: 48.7 us -> 73.8 us
  starting transfers between devices: 58.6 us -> 76.7 us
  waiting for transfers between devices: 319 us -> 301 us
  other arithmetic: 56.2 us -> 72.9 us
    pallas_call x2 -> x5, Pallas kernels: 70.3 us -> 123 us  [the longest x2 49.3 us: attend_back(): pl.pallas_call(functools.partial(attend_back_kernel, heads[0], low), grid...]
    psum x1 -> x0, waiting for transfers between devices: 48.1 us -> none  [per_device(): out_total, qkv_total = lax.psum((out_shard, qkv_shard), 'rep')]
    psum x1, waiting for transfers between devices: 52 us -> 83.6 us  [per_device(): down_total = lax.psum(down_shard, 'rep')]
    dot_general x5 -> x3, matrix products: 39.7 us -> 9.2 us  [matmul(): return jnp.dot(left, right, preferred_element_type=jnp.float32)]
    dot_general x4 -> x2, matrix products: 39.2 us -> 11.9 us  [matmul_right(): lax.dot_general(left, right, (((1,), (1,)), ((), ())), preferred_element_...]
    dot_general x4 -> x2, matrix products: 29.4 us -> 9.3 us  [matmul_left(): lax.dot_general(left, right, (((0,), (0,)), ((), ())), preferred_element_...]
    ppermute x37 -> x44, waiting for transfers between devices: 160 us -> 146 us  [permute(): return lax.ppermute(values, GROUP, pairs_by(rule))]
    unnamed x134 -> x161, local copies, waits for them, and re-layouts: 17 us -> 29.5 us
  transfers between devices with their start and end apart: 50 -> 61, of which waited for: 17 -> 24; matrix products, arithmetic and copies ran while one was open for 19% -> 21% of each run, Pallas kernels for 11% -> 12%
where the time goes in v4:
time: 721 us; the launch traced here: 712 us
  waiting for transfers between devices  301 us (42%)
  Pallas kernels  133 us (18%)
  starting transfers between devices  76.7 us (11%)
  local copies, waits for them, and re-layouts  73.8 us (10%)
  other arithmetic  72.9 us (10%)
  matrix products  37.9 us (5%)
  between operations  16.1 us (2%)
    ppermute x44, waiting for transfers between devices, permute(): return lax.ppermute(values, GROUP, pairs_by(rule))  146 us
    psum x1, waiting for transfers between devices, per_device(): down_total = lax.psum(down_shard, 'rep')  83.6 us
    psum x1, waiting for transfers between devices, per_device(): up_total = lax.psum(up_shard, 'rep')  56.2 us
    ppermute x44, starting transfers between devices, permute(): return lax.ppermute(values, GROUP, pairs_by(rule))  52.1 us
    pallas_call x2, Pallas kernels, attend_back(): pl.pallas_call(functools.partial(attend_back_kernel, heads[0], low), grid...  49.3 us
    pallas_call x1, Pallas kernels, mlp(): pl.pallas_call(mlp_kernel, grid=(units // block,), out_shape=(jax.ShapeDt...  44.5 us
    unnamed x161, local copies, waits for them, and re-layouts  29.5 us
    pallas_call x2, Pallas kernels, attend(): pl.pallas_call(functools.partial(attend_kernel, heads[0], low), grid=(len...  28.8 us
  transfers between devices with their start and end apart: 61, of which 24 were waited for; matrix products, arithmetic and copies ran while one was open for 21% of the time, Pallas kernels for 12%

profile of v4, /device:TPU:9, one launch (start us, length us, event | category | flops | bytes accessed | tf_op | source)
XLA Modules:
  0.0 712.0 jit_solution(7142743690054013363)
XLA Ops:
  8.5 12.4 %collective-permute-done.7.refs_1_ = bf16[144,3456]{1,0:T(8,128)(2,1)} collective-permute-done((bf16[144,3456]{1,0:T(8,128)(2,1)}, bf16[144,3456]{1,0:T(8,128)(2,1)}, u32[]{:S(2)}, u32[]{:S(2)}) %collective-permute-start.7) | collective-permute-done | bytes 995360 | tf_op jit(solution)/shard_map/ppermute | solution.py:74
  22.2 12.5 %collective-permute-done.9.refs_3_ = bf16[144,3456]{1,0:T(8,128)(2,1)} collective-permute-done((bf16[144,3456]{1,0:T(8,128)(2,1)}, bf16[144,3456]{1,0:T(8,128)(2,1)}, u32[]{:S(2)}, u32[]{:S(2)}) %collective-permute-start.9) | collective-permute-done | bytes 995360 | tf_op jit(solution)/shard_map/ppermute | solution.py:74
  36.1 2.8 concatenate.99
  41.6 3.6 collective-permute-start.1
  46.8 3.1 collective-permute-start.3
  51.2 22.5 %collective-permute-done.2 = bf16[4,2432]{1,0:T(4,128)(2,1)S(1)} collective-permute-done((bf16[4,2432]{1,0:T(4,128)(2,1)S(1)}, bf16[4,2432]{1,0:T(4,128)(2,1)S(1)}, u32[]{:S(2)}, u32[]{:S(2)}) %collective-permute-start.2) | collective-permute-done | bytes 19488 | tf_op jit(solution)/shard_map/ppermute | solution.py:74
  80.3 10.7 %collective-permute-done.5 = f32[1,6912]{1,0:T(1,128)S(1)} collective-permute-done((f32[1,6912]{1,0:T(1,128)S(1)}, f32[1,6912]{1,0:T(1,128)S(1)}, u32[]{:S(2)}, u32[]{:S(2)}) %collective-permute-start.5) | collective-permute-done | bytes 27680 | tf_op jit(solution)/shard_map/ppermute | solution.py:74
  98.7 4.6 shard_map.237
  103.4 5.5 add_convert_fusion
  116.0 20.2 %collective-permute-done.17.refs_1_ = bf16[144,1152]{1,0:T(8,128)(2,1)S(1)} collective-permute-done((bf16[144,1152]{1,0:T(8,128)(2,1)S(1)}, bf16[144,1152]{1,0:T(8,128)(2,1)S(1)}, u32[]{:S(2)}, u32[]{:S(2)}) %collective-permute-start.17) | collective-permute-done | bytes 331808 | tf_op jit(solution)/shard_map/ppermute | solution.py:74
  153.6 2.6 shard_map.240
  158.4 3.5 collective-permute-done.24
  161.9 4.5 convert_reduce_fusion.2
  166.4 3.8 collective-permute-start.28
  170.2 3.3 collective-permute-done.25.refs_3_
  173.4 10.9 %collective-permute-start.29 = (bf16[576,1152]{1,0:T(8,128)(2,1)}, bf16[576,1152]{1,0:T(8,128)(2,1)S(1)}, u32[]{:S(2)}, u32[]{:S(2)}) collective-permute-start(bf16[576,1152]{1,0:T(8,128)(2,1)} %collective-permute-done.25.refs_3_), channel_id=1, source_target_pairs={{0,2},{1,3},{2,0},{3,1},{4,6},{5,7},{6,4},{7,5},{8,10},{9,11},{10,... | collective-permute-start | bytes 3981320 | tf_op jit(solution)/shard_map/ppermute | solution.py:74
  184.4 14.4 %shard_map.238 = (bf16[512,640]{1,0:T(8,128)(2,1)S(1)}, f32[512,128]{1,0:T(8,128)S(1)}) custom-call(bf16[512,1152]{1,0:T(8,128)(2,1)S(1)} %slice.242.query_ref, bf16[512,2304]{1,0:T(8,128)(2,1)} %slice.243.own_ref, bf16[512,2304]{1,0:T(8,128)(2,1)} %collective-permute-done.14.other_ref), custom_call_target="tpu_custom_call" | custom-call | flops 1048576 | bytes 1048576 | tf_op jit(solution)/shard_map/pallas_call | solution.py:297
  199.5 14.5 %shard_map.239 = (bf16[512,640]{1,0:T(8,128)(2,1)S(1)}, f32[512,128]{1,0:T(8,128)S(1)}) custom-call(bf16[512,1152]{1,0:T(8,128)(2,1)S(1)} %slice.242.query_ref, bf16[512,2304]{1,0:T(8,128)(2,1)} %slice.243.own_ref, bf16[512,2304]{1,0:T(8,128)(2,1)} %collective-permute-done.14.other_ref), custom_call_target="tpu_custom_call" | custom-call | flops 1048576 | bytes 1048576 | tf_op jit(solution)/shard_map/pallas_call | solution.py:297
  215.7 3.3 fusion.57
  220.9 3.5 shard_map.241.down_ref
  224.4 4.0 copy-done.1
  228.3 44.5 %shard_map.242 = (f32[512,1152]{1,0:T(8,128)}, f32[512,1152]{1,0:T(8,128)}, bf16[1152,4608]{1,0:T(8,128)(2,1)}, bf16[4608,1152]{1,0:T(8,128)(2,1)}, f32[1,4608]{1,0:T(1,128)}) custom-call(bf16[512,1152]{1,0:T(8,128)(2,1)} %add_convert_fusion.1.hidden_ref, bf16[512,1152]{1,0:T(8,128)(2,1)} %get-tuple-element.100.upstream_ref, ...), custom_call_target="tpu_custom_call" | custom-call | flops 1048576 | bytes 1048576 | tf_op jit(solution)/shard_map/pallas_call | solution.py:442
  272.8 5.3 dynamic-slice_bitcast_fusion
  278.2 4.1 multiply_reduce_fusion
  282.4 6.1 fusion.25
  296.1 5.0 convolution_convert_fusion.2.upstream_ref
  301.0 23.9 %shard_map.243 = (bf16[512,640]{1,0:T(8,128)(2,1)}, f32[2,512,640]{2,1,0:T(8,128)}, bf16[2,512,640]{2,1,0:T(8,128)(2,1)}) custom-call(bf16[512,1152]{1,0:T(8,128)(2,1)} %copy-done.2, bf16[512,2304]{1,0:T(8,128)(2,1)} %slice.243.own_ref, bf16[512,2304]{1,0:T(8,128)(2,1)} %collective-permute-done.14.other_ref, ...), custom_call_target="tpu_custom_call" | custom-call | flops 1048576 | bytes 1048576 | tf_op jit(solution)/shard_map/pallas_call | solution.py:369
  326.3 3.1 slice.203
  333.2 25.4 %shard_map.244 = (bf16[512,640]{1,0:T(8,128)(2,1)}, f32[2,512,640]{2,1,0:T(8,128)}, bf16[2,512,640]{2,1,0:T(8,128)(2,1)}) custom-call(bf16[512,1152]{1,0:T(8,128)(2,1)} %copy-done.2, bf16[512,2304]{1,0:T(8,128)(2,1)} %slice.243.own_ref, bf16[512,2304]{1,0:T(8,128)(2,1)} %collective-permute-done.14.other_ref, ...), custom_call_target="tpu_custom_call" | custom-call | flops 1048576 | bytes 1048576 | tf_op jit(solution)/shard_map/pallas_call | solution.py:369
  367.6 6.0 fusion
  376.6 7.6 %convolution_convert_fusion = bf16[1152,3456]{1,0:T(8,128)(2,1)S(1)} fusion(bf16[512,3456]{1,0:T(8,128)(2,1)} %fusion.30, bf16[1,512,1152]{2,1,0:T(8,128)(2,1)S(1)} %copy-done.25, f32[1152]{0:T(1024)S(1)} %get-tuple-element.94, f32[1152]{0:T(1024)S(1)} %get-tuple-element.95, f32[512]{0:T(512)S(1)} %add_rsqrt_fusion.1, f32[512]{0:T(512)S(1)} %broadcast_multiply_fusion.5), kind=kOutput, calls=%fused_computation | convolution fusion | flops 4084383744 | bytes 12694528 | tf_op jit(solution)/shard_map/dot_general | solution.py:38
  395.2 6.9 fusion.61
  402.1 2.8 convert_reduce_fusion
  404.9 37.2 %collective-permute-done.35 = bf16[2,144,1152]{2,1,0:T(8,128)(2,1)S(1)} collective-permute-done((bf16[2,144,1152]{2,1,0:T(8,128)(2,1)S(1)}, bf16[2,144,1152]{2,1,0:T(8,128)(2,1)S(1)}, u32[]{:S(2)}, u32[]{:S(2)}) %collective-permute-start.35) | collective-permute-done | bytes 663584 | tf_op jit(solution)/shard_map/ppermute | solution.py:74
  442.0 2.9 convert_add_fusion.2
  463.2 4.9 collective-permute-done.40
  472.8 13.5 %collective-permute-done.41 = f32[1,4,144]{2,1,0:T(4,128)S(1)} collective-permute-done((f32[1,4,144]{2,1,0:T(4,128)S(1)}, f32[1,4,144]{2,1,0:T(4,128)S(1)}, u32[]{:S(2)}, u32[]{:S(2)}) %collective-permute-start.41) | collective-permute-done | bytes 2336 | tf_op jit(solution)/shard_map/ppermute | solution.py:74
  495.5 5.5 collective-permute-start.37
  515.1 5.2 fusion.62
  527.6 2.8 select_convert_fusion
  530.5 7.4 %collective-permute-done.50 = bf16[144,1152]{1,0:T(8,128)(2,1)S(1)} collective-permute-done((bf16[144,1152]{1,0:T(8,128)(2,1)}, bf16[144,1152]{1,0:T(8,128)(2,1)S(1)}, u32[]{:S(2)}, u32[]{:S(2)}) %collective-permute-start.50) | collective-permute-done | bytes 331808 | tf_op jit(solution)/shard_map/ppermute | solution.py:215
  537.9 3.6 collective-permute-done.51
  545.5 3.4 fusion.13
  548.9 2.6 collective-permute-start.54
  552.9 83.6 %all-reduce.3.cloned.1.call-done = bf16[576,1152]{1,0:T(8,128)(2,1)} async-done(((bf16[576,1152]{1,0:T(8,128)(2,1)}), bf16[576,1152]{1,0:T(8,128)(2,1)}) %all-reduce.3.cloned.1.call-update) | async-done | bytes 1327120 | tf_op jit(solution)/shard_map/psum | solution.py:613
  639.3 3.1 slice.263
  646.0 56.2 %all-reduce.5.cloned.1.call-done = bf16[144,4608]{1,0:T(8,128)(2,1)} async-done(((bf16[144,4608]{1,0:T(8,128)(2,1)}), bf16[144,4608]{1,0:T(8,128)(2,1)}) %all-reduce.5.cloned.1.call-update) | async-done | bytes 1327120 | tf_op jit(solution)/shard_map/psum | solution.py:615
  702.2 3.1 convert_element_type.289
  (399 shorter events, 154.5 us)
Async XLA Ops:
  7.2 221.2 %all-gather.2.cloned.1.call-start = ((), (), s32[]{:S(2)}) async-start(), calls=%async_computation.1 | async-start | bytes 11943936 | tf_op jit(solution)/shard_map/all_gather | solution.py:499
  7.2 13.8 %collective-permute-start.7 = (bf16[144,3456]{1,0:T(8,128)(2,1)}, bf16[144,3456]{1,0:T(8,128)(2,1)}, u32[]{:S(2)}, u32[]{:S(2)}) collective-permute-start(bf16[144,3456]{1,0:T(8,128)(2,1)} %refs_0_.1), channel_id=1, source_target_pairs={{0,4},{1,5},{2,3},{3,2},{4,0},{5,1},{6,7},{7,6},{8,12},{9,13},{10,... | collective-permute-start | bytes 2985992 | tf_op jit(solution)/shard_map/ppermute | solution.py:74
  21.0 13.7 %collective-permute-start.9 = (bf16[144,3456]{1,0:T(8,128)(2,1)}, bf16[144,3456]{1,0:T(8,128)(2,1)}, u32[]{:S(2)}, u32[]{:S(2)}) collective-permute-start(bf16[144,3456]{1,0:T(8,128)(2,1)} %collective-permute-done.7.refs_1_), channel_id=1, source_target_pairs={{0,1},{1,0},{2,6},{3,7},{4,5},{5,4},{6,2},{7,3},{8,9},{9,8},{10,14... | collective-permute-start | bytes 2985992 | tf_op jit(solution)/shard_map/ppermute | solution.py:74
  34.7 495.7 %reduce-scatter.2.cloned.1.call-start = ((), (), s32[]{:S(2)}) async-start(), calls=%async_computation.2 | async-start | bytes 11943936 | tf_op jit(solution)/shard_map/reduce_scatter | solution.py:568
  41.6 8.4 %collective-permute-start.1 = (bf16[2,2432]{1,0:T(2,128)(2,1)S(1)}, bf16[2,2432]{1,0:T(2,128)(2,1)S(1)}, u32[]{:S(2)}, u32[]{:S(2)}) collective-permute-start(bf16[2,2432]{1,0:T(2,128)(2,1)S(1)} %broadcast_select_fusion.6), channel_id=1, source_target_pairs={{0,2},{1,3},{2,0},{3,1},{4,6},{5,7},{6,4},{7,5},{8,10},{9,11},{10,... | collective-permute-start | bytes 29192 | tf_op jit(solution)/shard_map/ppermute | solution.py:74
  45.2 47.4 %collective-permute-start.8 = (bf16[144,3456]{1,0:T(8,128)(2,1)}, bf16[144,3456]{1,0:T(8,128)(2,1)}, u32[]{:S(2)}, u32[]{:S(2)}) collective-permute-start(bf16[144,3456]{1,0:T(8,128)(2,1)} %refs_0_.1), channel_id=1, source_target_pairs={{0,1},{1,0},{2,6},{3,7},{4,5},{5,4},{6,2},{7,3},{8,9},{9,8},{10,14... | collective-permute-start | bytes 2985992 | tf_op jit(solution)/shard_map/ppermute | solution.py:74
  46.4 51.5 %collective-permute-start.10 = (bf16[144,3456]{1,0:T(8,128)(2,1)}, bf16[144,3456]{1,0:T(8,128)(2,1)}, u32[]{:S(2)}, u32[]{:S(2)}) collective-permute-start(bf16[144,3456]{1,0:T(8,128)(2,1)} %refs_0_.1), channel_id=1, source_target_pairs={{0,2},{1,3},{2,0},{3,1},{4,6},{5,7},{6,4},{7,5},{8,10},{9,11},{10,... | collective-permute-start | bytes 2985992 | tf_op jit(solution)/shard_map/ppermute | solution.py:74
  46.8 46.4 %collective-permute-start.3 = (bf16[1,512,1152]{2,1,0:T(8,128)(2,1)}, bf16[1,512,1152]{2,1,0:T(8,128)(2,1)}, u32[]{:S(2)}, u32[]{:S(2)}) collective-permute-start(bf16[1,512,1152]{2,1,0:T(8,128)(2,1)} %param.14), channel_id=1, source_target_pairs={{1,2},{2,1},{5,6},{6,5},{9,10},{10,9},{13,14},{14,13},{17,18},{18,... | collective-permute-start | bytes 3538952 | tf_op jit(solution)/shard_map/ppermute | solution.py:80
  50.0 23.7 %collective-permute-start.2 = (bf16[4,2432]{1,0:T(4,128)(2,1)S(1)}, bf16[4,2432]{1,0:T(4,128)(2,1)S(1)}, u32[]{:S(2)}, u32[]{:S(2)}) collective-permute-start(bf16[4,2432]{1,0:T(4,128)(2,1)S(1)} %maximum_select_fusion.4), channel_id=1, source_target_pairs={{0,4},{1,5},{2,6},{3,7},{4,0},{5,1},{6,2},{7,3},{8,12},{9,13},{10,... | collective-permute-start | bytes 58376 | tf_op jit(solution)/shard_map/ppermute | solution.py:74
  78.0 12.9 %collective-permute-start.5 = (f32[1,6912]{1,0:T(1,128)S(1)}, f32[1,6912]{1,0:T(1,128)S(1)}, u32[]{:S(2)}, u32[]{:S(2)}) collective-permute-start(f32[1,6912]{1,0:T(1,128)S(1)} %broadcast_select_fusion.4), channel_id=1, source_target_pairs={{0,1},{1,0},{2,3},{3,2},{4,5},{5,4},{6,7},{7,6},{8,9},{9,8},{10,11... | collective-permute-start | bytes 82952 | tf_op jit(solution)/shard_map/ppermute | solution.py:74
  95.5 47.9 %collective-permute-start.15 = (bf16[576,1152]{1,0:T(8,128)(2,1)S(1)}, bf16[576,1152]{1,0:T(8,128)(2,1)}, u32[]{:S(2)}, u32[]{:S(2)}) collective-permute-start(bf16[576,1152]{1,0:T(8,128)(2,1)S(1)} %copy-done.5), channel_id=1, source_target_pairs={{0,4},{1,5},{2,3},{3,2},{4,0},{5,1},{6,7},{7,6},{8,12},{9,13},{10,... | collective-permute-start | bytes 3981320 | tf_op jit(solution)/shard_map/ppermute | solution.py:74
  111.5 72.9 %collective-permute-start.14 = (bf16[512,2304]{1,0:T(8,128)(2,1)}, bf16[512,2304]{1,0:T(8,128)(2,1)}, u32[]{:S(2)}, u32[]{:S(2)}) collective-permute-start(bf16[512,2304]{1,0:T(8,128)(2,1)} %slice.243.own_ref), channel_id=1, source_target_pairs={{0,2},{1,3},{2,0},{3,1},{4,6},{5,7},{6,4},{7,5},{8,10},{9,11},{10,... | collective-permute-start | bytes 7077896 | tf_op jit(solution)/shard_map/ppermute | solution.py:74
  111.7 24.6 %collective-permute-start.17 = (bf16[144,1152]{1,0:T(8,128)(2,1)S(1)}, bf16[144,1152]{1,0:T(8,128)(2,1)S(1)}, u32[]{:S(2)}, u32[]{:S(2)}) collective-permute-start(bf16[144,1152]{1,0:T(8,128)(2,1)S(1)} %copy-done.7), channel_id=1, source_target_pairs={{0,4},{1,5},{2,3},{3,2},{4,0},{5,1},{6,7},{7,6},{8,12},{9,13},{10,... | collective-permute-start | bytes 995336 | tf_op jit(solution)/shard_map/ppermute | solution.py:74
  114.0 23.5 %collective-permute-start.18 = (bf16[144,1152]{1,0:T(8,128)(2,1)S(1)}, bf16[144,1152]{1,0:T(8,128)(2,1)}, u32[]{:S(2)}, u32[]{:S(2)}) collective-permute-start(bf16[144,1152]{1,0:T(8,128)(2,1)S(1)} %copy-done.7), channel_id=1, source_target_pairs={{0,1},{1,0},{2,6},{3,7},{4,5},{5,4},{6,2},{7,3},{8,9},{9,8},{10,14... | collective-permute-start | bytes 995336 | tf_op jit(solution)/shard_map/ppermute | solution.py:74
  115.1 24.5 %collective-permute-start.20 = (bf16[144,1152]{1,0:T(8,128)(2,1)S(1)}, bf16[144,1152]{1,0:T(8,128)(2,1)S(1)}, u32[]{:S(2)}, u32[]{:S(2)}) collective-permute-start(bf16[144,1152]{1,0:T(8,128)(2,1)S(1)} %copy-done.7), channel_id=1, source_target_pairs={{0,2},{1,3},{2,0},{3,1},{4,6},{5,7},{6,4},{7,5},{8,10},{9,11},{10,... | collective-permute-start | bytes 995336 | tf_op jit(solution)/shard_map/ppermute | solution.py:74
  136.2 6.0 collective-permute-start.19
  137.4 24.4 %collective-permute-start.24 = (bf16[1,512,1152]{2,1,0:T(8,128)(2,1)}, bf16[1,512,1152]{2,1,0:T(8,128)(2,1)}, u32[]{:S(2)}, u32[]{:S(2)}) collective-permute-start(bf16[1,512,1152]{2,1,0:T(8,128)(2,1)} %param.27), channel_id=1, source_target_pairs={{1,2},{2,1},{5,6},{6,5},{9,10},{10,9},{13,14},{14,13},{17,18},{18,... | collective-permute-start | bytes 3538952 | tf_op jit(solution)/shard_map/ppermute | solution.py:80
  142.2 24.2 %collective-permute-start.16 = (bf16[576,1152]{1,0:T(8,128)(2,1)S(1)}, bf16[576,1152]{1,0:T(8,128)(2,1)}, u32[]{:S(2)}, u32[]{:S(2)}) collective-permute-start(bf16[576,1152]{1,0:T(8,128)(2,1)S(1)} %copy-done.5), channel_id=1, source_target_pairs={{0,1},{1,0},{2,6},{3,7},{4,5},{5,4},{6,2},{7,3},{8,9},{9,8},{10,14... | collective-permute-start | bytes 3981320 | tf_op jit(solution)/shard_map/ppermute | solution.py:74
  143.4 30.0 %collective-permute-start.25 = (bf16[576,1152]{1,0:T(8,128)(2,1)}, bf16[576,1152]{1,0:T(8,128)(2,1)}, u32[]{:S(2)}, u32[]{:S(2)}) collective-permute-start(bf16[576,1152]{1,0:T(8,128)(2,1)} %collective-permute-done.15.refs_1_), channel_id=1, source_target_pairs={{0,1},{1,0},{2,6},{3,7},{4,5},{5,4},{6,2},{7,3},{8,9},{9,8},{10,14... | collective-permute-start | bytes 3981320 | tf_op jit(solution)/shard_map/ppermute | solution.py:74
  148.4 72.5 %collective-permute-start.26 = (bf16[576,1152]{1,0:T(8,128)(2,1)S(1)}, bf16[576,1152]{1,0:T(8,128)(2,1)S(1)}, u32[]{:S(2)}, u32[]{:S(2)}) collective-permute-start(bf16[576,1152]{1,0:T(8,128)(2,1)S(1)} %copy-done.5), channel_id=1, source_target_pairs={{0,2},{1,3},{2,0},{3,1},{4,6},{5,7},{6,4},{7,5},{8,10},{9,11},{10,... | collective-permute-start | bytes 3981320 | tf_op jit(solution)/shard_map/ppermute | solution.py:74
  166.3 54.5 %collective-permute-start.27 = (bf16[576,1152]{1,0:T(8,128)(2,1)}, bf16[576,1152]{1,0:T(8,128)(2,1)S(1)}, u32[]{:S(2)}, u32[]{:S(2)}) collective-permute-start(bf16[576,1152]{1,0:T(8,128)(2,1)} %collective-permute-done.15.refs_1_), channel_id=1, source_target_pairs={{0,2},{1,3},{2,0},{3,1},{4,6},{5,7},{6,4},{7,5},{8,10},{9,11},{10,... | collective-permute-start | bytes 3981320 | tf_op jit(solution)/shard_map/ppermute | solution.py:74
  166.4 54.5 %collective-permute-start.28 = (bf16[576,1152]{1,0:T(8,128)(2,1)}, bf16[576,1152]{1,0:T(8,128)(2,1)S(1)}, u32[]{:S(2)}, u32[]{:S(2)}) collective-permute-start(bf16[576,1152]{1,0:T(8,128)(2,1)} %collective-permute-done.16.refs_2_), channel_id=1, source_target_pairs={{0,2},{1,3},{2,0},{3,1},{4,6},{5,7},{6,4},{7,5},{8,10},{9,11},{10,... | collective-permute-start | bytes 3981320 | tf_op jit(solution)/shard_map/ppermute | solution.py:74
  173.4 47.4 %collective-permute-start.29 = (bf16[576,1152]{1,0:T(8,128)(2,1)}, bf16[576,1152]{1,0:T(8,128)(2,1)S(1)}, u32[]{:S(2)}, u32[]{:S(2)}) collective-permute-start(bf16[576,1152]{1,0:T(8,128)(2,1)} %collective-permute-done.25.refs_3_), channel_id=1, source_target_pairs={{0,2},{1,3},{2,0},{3,1},{4,6},{5,7},{6,4},{7,5},{8,10},{9,11},{10,... | collective-permute-start | bytes 3981320 | tf_op jit(solution)/shard_map/ppermute | solution.py:74
  278.1 55.1 %collective-permute-start.31 = (bf16[2,2,144,4608]{3,2,1,0:T(8,128)(2,1)}, bf16[2,2,144,4608]{3,2,1,0:T(8,128)(2,1)}, u32[]{:S(2)}, u32[]{:S(2)}) collective-permute-start(bf16[2,2,144,4608]{3,2,1,0:T(8,128)(2,1)} %dynamic-slice_bitcast_fusion), channel_id=1, source_target_pairs={{0,2},{1,3},{2,0},{3,1},{4,6},{5,7},{6,4},{7,5},{8,10},{9,11},{10,... | collective-permute-start | bytes 15925256 | tf_op jit(solution)/shard_map/ppermute | solution.py:74
  288.4 42.3 %collective-permute-start.30 = (bf16[1,512,1152]{2,1,0:T(8,128)(2,1)}, bf16[1,512,1152]{2,1,0:T(8,128)(2,1)}, u32[]{:S(2)}, u32[]{:S(2)}) collective-permute-start(bf16[1,512,1152]{2,1,0:T(8,128)(2,1)} %get-tuple-element.118), channel_id=1, source_target_pairs={{1,2},{2,1},{5,6},{6,5},{9,10},{10,9},{13,14},{14,13},{17,18},{18,... | collective-permute-start | bytes 3538952 | tf_op jit(solution)/shard_map/ppermute | solution.py:80
  295.1 38.0 %collective-permute-start.32 = (bf16[2,2,144,1152]{3,2,1,0:T(8,128)(2,1)}, bf16[2,2,144,1152]{3,2,1,0:T(8,128)(2,1)}, u32[]{:S(2)}, u32[]{:S(2)}) collective-permute-start(bf16[2,2,144,1152]{3,2,1,0:T(8,128)(2,1)} %dynamic-slice_bitcast_fusion.2), channel_id=1, source_target_pairs={{0,2},{1,3},{2,0},{3,1},{4,6},{5,7},{6,4},{7,5},{8,10},{9,11},{10,... | collective-permute-start | bytes 3981320 | tf_op jit(solution)/shard_map/ppermute | solution.py:74
  329.4 307.2 %all-reduce.3.cloned.1.call-start = ((), (), s32[]{:S(2)}) async-start(), calls=%async_computation.3 | async-start | bytes 2654208 | tf_op jit(solution)/shard_map/psum | solution.py:613
  362.5 11.1 %collective-permute-start.33 = (bf16[2,512,1152]{2,1,0:T(8,128)(2,1)}, bf16[2,512,1152]{2,1,0:T(8,128)(2,1)S(1)}, u32[]{:S(2)}, u32[]{:S(2)}) collective-permute-start(bf16[2,512,1152]{2,1,0:T(8,128)(2,1)} %pad_maximum_fusion.2), channel_id=1, source_target_pairs={{0,2},{1,3},{2,0},{3,1},{4,6},{5,7},{6,4},{7,5},{8,10},{9,11},{10,... | collective-permute-start | bytes 7077896 | tf_op jit(solution)/shard_map/ppermute | solution.py:74
  388.6 53.4 %collective-permute-start.36 = (bf16[2,2,144,3456]{3,2,1,0:T(8,128)(2,1)}, bf16[2,2,144,3456]{3,2,1,0:T(8,128)(2,1)S(1)}, u32[]{:S(2)}, u32[]{:S(2)}) collective-permute-start(bf16[2,2,144,3456]{3,2,1,0:T(8,128)(2,1)} %dynamic-slice_bitcast_fusion.1), channel_id=1, source_target_pairs={{0,2},{1,3},{2,0},{3,1},{4,6},{5,7},{6,4},{7,5},{8,10},{9,11},{10,... | collective-permute-start | bytes 11943944 | tf_op jit(solution)/shard_map/ppermute | solution.py:74
  389.5 52.5 %collective-permute-start.34 = (bf16[2,144,4608]{2,1,0:T(8,128)(2,1)S(1)}, bf16[2,144,4608]{2,1,0:T(8,128)(2,1)}, u32[]{:S(2)}, u32[]{:S(2)}) collective-permute-start(bf16[2,144,4608]{2,1,0:T(8,128)(2,1)S(1)} %pad_maximum_fusion.1), channel_id=1, source_target_pairs={{0,4},{1,5},{2,3},{3,2},{4,0},{5,1},{6,7},{7,6},{8,12},{9,13},{10,... | collective-permute-start | bytes 7962632 | tf_op jit(solution)/shard_map/ppermute | solution.py:74
  394.2 47.9 %collective-permute-start.35 = (bf16[2,144,1152]{2,1,0:T(8,128)(2,1)S(1)}, bf16[2,144,1152]{2,1,0:T(8,128)(2,1)S(1)}, u32[]{:S(2)}, u32[]{:S(2)}) collective-permute-start(bf16[2,144,1152]{2,1,0:T(8,128)(2,1)S(1)} %pad_maximum_fusion.5), channel_id=1, source_target_pairs={{0,4},{1,5},{2,3},{3,2},{4,0},{5,1},{6,7},{7,6},{8,12},{9,13},{10,... | collective-permute-start | bytes 1990664 | tf_op jit(solution)/shard_map/ppermute | solution.py:74
  455.2 35.7 %collective-permute-start.47 = (bf16[144,1152]{1,0:T(8,128)(2,1)}, bf16[144,1152]{1,0:T(8,128)(2,1)S(1)}, u32[]{:S(2)}, u32[]{:S(2)}) collective-permute-start(bf16[144,1152]{1,0:T(8,128)(2,1)} %fusion.39), channel_id=1, source_target_pairs={{0,1},{1,0},{2,6},{3,7},{4,5},{5,4},{6,2},{7,3},{8,9},{9,8},{10,14... | collective-permute-start | bytes 995336 | tf_op jit(solution)/shard_map/ppermute | solution.py:74
  460.2 7.9 %collective-permute-start.40 = (f32[4,16128]{1,0:T(4,128)S(1)}, f32[4,16128]{1,0:T(4,128)S(1)}, u32[]{:S(2)}, u32[]{:S(2)}) collective-permute-start(f32[4,16128]{1,0:T(4,128)S(1)} %maximum_select_fusion.1), channel_id=1, source_target_pairs={{0,4},{1,5},{2,6},{3,7},{4,0},{5,1},{6,2},{7,3},{8,12},{9,13},{10,... | collective-permute-start | bytes 774152 | tf_op jit(solution)/shard_map/ppermute | solution.py:74
  461.8 40.4 %collective-permute-start.48 = (bf16[2,144,3456]{2,1,0:T(8,128)(2,1)}, bf16[2,144,3456]{2,1,0:T(8,128)(2,1)}, u32[]{:S(2)}, u32[]{:S(2)}) collective-permute-start(bf16[2,144,3456]{2,1,0:T(8,128)(2,1)} %pad_maximum_fusion.3), channel_id=1, source_target_pairs={{0,4},{1,5},{2,3},{3,2},{4,0},{5,1},{6,7},{7,6},{8,12},{9,13},{10,... | collective-permute-start | bytes 5971976 | tf_op jit(solution)/shard_map/ppermute | solution.py:74
  471.1 15.2 %collective-permute-start.41 = (f32[1,4,144]{2,1,0:T(4,128)S(1)}, f32[1,4,144]{2,1,0:T(4,128)S(1)}, u32[]{:S(2)}, u32[]{:S(2)}) collective-permute-start(f32[1,4,144]{2,1,0:T(4,128)S(1)} %get-tuple-element.134), channel_id=1, source_target_pairs={{0,1},{1,0},{2,3},{3,2},{4,5},{5,4},{6,7},{7,6},{8,9},{9,8},{10,11... | collective-permute-start | bytes 6920 | tf_op jit(solution)/shard_map/ppermute | solution.py:74
  486.8 8.6 %collective-permute-start.44 = (f32[29376]{0:T(1024)S(1)}, f32[29376]{0:T(1024)S(1)}, u32[]{:S(2)}, u32[]{:S(2)}) collective-permute-start(f32[29376]{0:T(1024)S(1)} %concatenate.126), channel_id=1, source_target_pairs={{0,8},{8,16},{16,24},{24,0},{1,9},{9,17},{17,25},{25,1},{2,10},{10... | collective-permute-start | bytes 352520 | tf_op jit(solution)/shard_map/ppermute | solution.py:102
  488.3 12.8 %collective-permute-start.45 = (f32[29376]{0:T(1024)S(1)}, f32[29376]{0:T(1024)S(1)}, u32[]{:S(2)}, u32[]{:S(2)}) collective-permute-start(f32[29376]{0:T(1024)S(1)} %concatenate.126), channel_id=1, source_target_pairs={{0,16},{8,24},{16,0},{24,8},{1,17},{9,25},{17,1},{25,9},{2,18},{10... | collective-permute-start | bytes 352520 | tf_op jit(solution)/shard_map/ppermute | solution.py:102
  489.5 11.7 %collective-permute-start.46 = (f32[29376]{0:T(1024)S(1)}, f32[29376]{0:T(1024)}, u32[]{:S(2)}, u32[]{:S(2)}) collective-permute-start(f32[29376]{0:T(1024)S(1)} %concatenate.126), channel_id=1, source_target_pairs={{0,24},{8,0},{16,8},{24,16},{1,25},{9,1},{17,9},{25,17},{2,26},{10... | collective-permute-start | bytes 352520 | tf_op jit(solution)/shard_map/ppermute | solution.py:102
  493.5 52.0 %collective-permute-start.56 = (bf16[144,4608]{1,0:T(8,128)(2,1)}, bf16[144,4608]{1,0:T(8,128)(2,1)}, u32[]{:S(2)}, u32[]{:S(2)}) collective-permute-start(bf16[144,4608]{1,0:T(8,128)(2,1)} %fusion.27), channel_id=1, source_target_pairs={{0,1},{1,0},{2,6},{3,7},{4,5},{5,4},{6,2},{7,3},{8,9},{9,8},{10,14... | collective-permute-start | bytes 3981320 | tf_op jit(solution)/shard_map/ppermute | solution.py:74
  495.5 32.1 %collective-permute-start.37 = (bf16[1,512,1152]{2,1,0:T(8,128)(2,1)}, bf16[1,512,1152]{2,1,0:T(8,128)(2,1)}, u32[]{:S(2)}, u32[]{:S(2)}) collective-permute-start(bf16[1,512,1152]{2,1,0:T(8,128)(2,1)} %get-tuple-element.123), channel_id=1, source_target_pairs={{1,2},{2,1},{5,6},{6,5},{9,10},{10,9},{13,14},{14,13},{17,18},{18,... | collective-permute-start | bytes 3538952 | tf_op jit(solution)/shard_map/ppermute | solution.py:80
  507.8 13.4 %collective-permute-start.49 = (bf16[144,3456]{1,0:T(8,128)(2,1)}, bf16[144,3456]{1,0:T(8,128)(2,1)}, u32[]{:S(2)}, u32[]{:S(2)}) collective-permute-start(bf16[144,3456]{1,0:T(8,128)(2,1)} %fusion.32), channel_id=1, source_target_pairs={{0,1},{1,0},{2,6},{3,7},{4,5},{5,4},{6,2},{7,3},{8,9},{9,8},{10,14... | collective-permute-start | bytes 2985992 | tf_op jit(solution)/shard_map/ppermute | solution.py:74
  524.2 13.7 %collective-permute-start.50 = (bf16[144,1152]{1,0:T(8,128)(2,1)}, bf16[144,1152]{1,0:T(8,128)(2,1)S(1)}, u32[]{:S(2)}, u32[]{:S(2)}) collective-permute-start(bf16[144,1152]{1,0:T(8,128)(2,1)} %get-tuple-element.124), channel_id=1, source_target_pairs={{0,8},{8,16},{16,24},{24,0},{1,9},{9,17},{17,25},{25,1},{2,10},{10... | collective-permute-start | bytes 995336 | tf_op jit(solution)/shard_map/ppermute | solution.py:215
  526.4 15.0 %collective-permute-start.51 = (bf16[144,1152]{1,0:T(8,128)(2,1)}, bf16[144,1152]{1,0:T(8,128)(2,1)S(1)}, u32[]{:S(2)}, u32[]{:S(2)}) collective-permute-start(bf16[144,1152]{1,0:T(8,128)(2,1)} %get-tuple-element.126), channel_id=1, source_target_pairs={{0,16},{8,24},{16,0},{24,8},{1,17},{9,25},{17,1},{25,9},{2,18},{10... | collective-permute-start | bytes 995336 | tf_op jit(solution)/shard_map/ppermute | solution.py:215
  527.5 14.9 %collective-permute-start.52 = (bf16[144,1152]{1,0:T(8,128)(2,1)}, bf16[144,1152]{1,0:T(8,128)(2,1)}, u32[]{:S(2)}, u32[]{:S(2)}) collective-permute-start(bf16[144,1152]{1,0:T(8,128)(2,1)} %get-tuple-element.125), channel_id=1, source_target_pairs={{0,24},{8,0},{16,8},{24,16},{1,25},{9,1},{17,9},{25,17},{2,26},{10... | collective-permute-start | bytes 995336 | tf_op jit(solution)/shard_map/ppermute | solution.py:215
  530.5 171.7 %all-reduce.5.cloned.1.call-start = ((), (), s32[]{:S(2)}) async-start(), calls=%async_computation.4 | async-start | bytes 2654208 | tf_op jit(solution)/shard_map/psum | solution.py:615
  545.5 91.1 %collective-permute-start.53 = (bf16[144,1152]{1,0:T(8,128)(2,1)S(1)}, bf16[144,1152]{1,0:T(8,128)(2,1)S(1)}, u32[]{:S(2)}, u32[]{:S(2)}) collective-permute-start(bf16[144,1152]{1,0:T(8,128)(2,1)S(1)} %get-tuple-element.98), channel_id=1, source_target_pairs={{0,8},{8,16},{16,24},{24,0},{1,9},{9,17},{17,25},{25,1},{2,10},{10... | collective-permute-start | bytes 995336 | tf_op jit(solution)/shard_map/ppermute | solution.py:102
  548.9 88.6 %collective-permute-start.54 = (bf16[144,1152]{1,0:T(8,128)(2,1)S(1)}, bf16[144,1152]{1,0:T(8,128)(2,1)S(1)}, u32[]{:S(2)}, u32[]{:S(2)}) collective-permute-start(bf16[144,1152]{1,0:T(8,128)(2,1)S(1)} %get-tuple-element.98), channel_id=1, source_target_pairs={{0,16},{8,24},{16,0},{24,8},{1,17},{9,25},{17,1},{25,9},{2,18},{10... | collective-permute-start | bytes 995336 | tf_op jit(solution)/shard_map/ppermute | solution.py:102
  551.5 86.9 %collective-permute-start.55 = (bf16[144,1152]{1,0:T(8,128)(2,1)S(1)}, bf16[144,1152]{1,0:T(8,128)(2,1)S(1)}, u32[]{:S(2)}, u32[]{:S(2)}) collective-permute-start(bf16[144,1152]{1,0:T(8,128)(2,1)S(1)} %get-tuple-element.98), channel_id=1, source_target_pairs={{0,24},{8,0},{16,8},{24,16},{1,25},{9,1},{17,9},{25,17},{2,26},{10... | collective-permute-start | bytes 995336 | tf_op jit(solution)/shard_map/ppermute | solution.py:102
  (87 other events, 1017.5 us)
Sparse Core Ops, SparseCore 0:
  34.8 92.6 all-gather.1
  329.5 89.5 reduce-scatter.1
  530.6 105.9 all-reduce.2
  639.4 62.7 all-reduce.4

commit v5 on v4

--- a/solution.py
+++ b/solution.py
@@ -32,18 +32,6 @@
 
 def matmul(left, right):
     return jnp.dot(left, right, preferred_element_type=jnp.float32)
-
-
-def matmul_left(left, right):
-    return lax.dot_general(
-        left, right, (((0,), (0,)), ((), ())), preferred_element_type=jnp.float32
-    )
-
-
-def matmul_right(left, right):
-    return lax.dot_general(
-        left, right, (((1,), (1,)), ((), ())), preferred_element_type=jnp.float32
-    )
 
 
 def place_of():
@@ -144,7 +132,7 @@
             pltpu.SemaphoreType.DMA((SHARDS,)),
         ],
         compiler_params=pltpu.CompilerParams(vmem_limit_bytes=size + (4 << 20)),
-        cost_estimate=pl.CostEstimate(flops=0, bytes_accessed=2 * size, transcendentals=0),
+        cost_estimate=SHORT,
     )(order, *pieces)
 
 
@@ -168,20 +156,16 @@
 
 
 class Scatter:
-    def __init__(self, partial):
-        _, rows, columns = partial.shape
+    def __init__(self, halves):
         self.place = place_of()
         self.core = (self.place >> 1) & 1
-        self.partial = partial.reshape(2, 2, 2, rows, columns)
-        self.received = permute(self.half(1 - self.core), core_rule)
-
-    def half(self, core):
-        return lax.dynamic_index_in_dim(self.partial, core, 1, keepdims=False)
+        self.kept, sent = halves
+        self.low = sent.dtype
+        self.received = permute(sent, core_rule)
 
     def second(self):
-        _, _, _, rows, columns = self.partial.shape
-        kept = self.half(self.core).astype(jnp.float32) + self.received.astype(jnp.float32)
-        kept = kept.astype(self.partial.dtype).reshape(4, rows, columns)
+        kept = self.kept.astype(jnp.float32) + self.received.astype(jnp.float32)
+        kept = kept.astype(self.low)
         mine = ((self.place >> 2) << 1) | (self.place & 1)
         near = jnp.where(self.core == 0, 2, 1)
 
@@ -195,7 +179,7 @@
     def third(self):
         kept = self.kept.astype(jnp.float32) + self.received.astype(jnp.float32)
         self.kept = kept[0]
-        self.received = permute(kept[1].astype(self.partial.dtype), second_rule)
+        self.received = permute(kept[1].astype(self.low), second_rule)
 
     def result(self):
         return self.kept + self.received.astype(jnp.float32)
@@ -224,9 +208,9 @@
 
 
 WINDOW = 256
-SHORT = pl.CostEstimate(flops=1 << 20, bytes_accessed=1 << 20, transcendentals=0)
 GELU_RATE = 0.7978845608028654
 GELU_CUBE = 0.044715
+SHORT = pl.CostEstimate(flops=1 << 20, bytes_accessed=1 << 20, transcendentals=0)
 
 
 def head_lanes(heads, width):
@@ -401,9 +385,64 @@
     return jnp.concatenate([left[..., :edge], middle, right[..., shared:]], axis=-1)
 
 
+def store_halves(grad, kept_ref, sent_ref):
+    core = lax.axis_index("fsdp") % 2
+    rows = grad.shape[0] // SHARDS
+    low = grad.astype(kept_ref.dtype)
+    for owner in (0, 1):
+        blocks = [at for at in range(SHARDS) if (at >> 1) & 1 == owner]
+
+        @pl.when(core == owner)
+        def _():
+            for slot, at in enumerate(blocks):
+                kept_ref[slot] = low[at * rows : (at + 1) * rows]
+
+        @pl.when(core != owner)
+        def _():
+            for slot, at in enumerate(blocks):
+                sent_ref[slot] = low[at * rows : (at + 1) * rows]
+
+
+def product_back_kernel(left_ref, upstream_ref, weight_ref, d_left_ref, kept_ref, sent_ref):
+    @pl.when(pl.program_id(0) == 0)
+    def _():
+        d_left_ref[...] = jnp.zeros_like(d_left_ref)
+
+    upstream = upstream_ref[...]
+    store_halves(dot_first(left_ref[...], upstream), kept_ref, sent_ref)
+    d_left_ref[...] += dot_last(upstream, weight_ref[...])
+
+
+def product_back(left, upstream, weight):
+    length, width = left.shape
+    columns = weight.shape[1]
+    block = 384
+    fixed = pl.BlockSpec((length, width), lambda at: (0, 0))
+    half = pl.BlockSpec((SHARDS // 2, width // SHARDS, block), lambda at: (0, 0, at))
+    half_shape = jax.ShapeDtypeStruct((SHARDS // 2, width // SHARDS, columns), jnp.bfloat16)
+    d_left, kept, sent = pl.pallas_call(
+        product_back_kernel,
+        grid=(columns // block,),
+        out_shape=(
+            jax.ShapeDtypeStruct((length, width), jnp.float32),
+            half_shape,
+            half_shape,
+        ),
+        in_specs=[
+            fixed,
+            pl.BlockSpec((length, block), lambda at: (0, at)),
+            pl.BlockSpec((width, block), lambda at: (0, at)),
+        ],
+        out_specs=(fixed, half, half),
+        compiler_params=pltpu.CompilerParams(vmem_limit_bytes=32 << 20),
+        cost_estimate=SHORT,
+    )(left, upstream, weight)
+    return d_left, (kept, sent)
+
+
 def mlp_kernel(
     hidden_ref, upstream_ref, up_ref, bias_ref, down_ref,
-    branch_ref, d_hidden_ref, up_grad_ref, down_grad_ref, bias_grad_ref,
+    branch_ref, d_hidden_ref, up_kept_ref, up_sent_ref, down_grad_ref, bias_grad_ref,
 ):
     @pl.when(pl.program_id(0) == 0)
     def _():
@@ -428,7 +467,7 @@
     bias_grad_ref[...] = jnp.sum(d_preact.astype(jnp.float32), 0, keepdims=True)
     down_grad_ref[...] = dot_first(activated, upstream).astype(jnp.bfloat16)
     d_hidden_ref[...] += dot_last(d_preact, up_ref[...])
-    up_grad_ref[...] = dot_first(hidden, d_preact).astype(jnp.bfloat16)
+    store_halves(dot_first(hidden, d_preact), up_kept_ref, up_sent_ref)
 
 
 def mlp(hidden, upstream, up, bias, down):
@@ -439,18 +478,21 @@
     columns = pl.BlockSpec((width, block), lambda at: (0, at))
     lanes = pl.BlockSpec((1, block), lambda at: (0, at))
     rows = pl.BlockSpec((block, width), lambda at: (at, 0))
+    half = pl.BlockSpec((SHARDS // 2, width // SHARDS, block), lambda at: (0, 0, at))
+    half_shape = jax.ShapeDtypeStruct((SHARDS // 2, width // SHARDS, units), jnp.bfloat16)
     return pl.pallas_call(
         mlp_kernel,
         grid=(units // block,),
         out_shape=(
             jax.ShapeDtypeStruct((length, width), jnp.float32),
             jax.ShapeDtypeStruct((length, width), jnp.float32),
-            jax.ShapeDtypeStruct(up.shape, jnp.bfloat16),
+            half_shape,
+            half_shape,
             jax.ShapeDtypeStruct(down.shape, jnp.bfloat16),
             jax.ShapeDtypeStruct((1, units), jnp.float32),
         ),
         in_specs=[fixed, fixed, columns, lanes, rows],
-        out_specs=(fixed, fixed, columns, rows, lanes),
+        out_specs=(fixed, fixed, half, half, rows, lanes),
         compiler_params=pltpu.CompilerParams(vmem_limit_bytes=56 << 20),
         cost_estimate=SHORT,
     )(hidden, upstream, up, bias, down)
@@ -473,7 +515,6 @@
     cotangent,
 ):
     number, length, width = latent_in.shape
-    hidden_width = up_weight.shape[1]
     place = place_of()
     fsdp_index = lax.axis_index("fsdp")
     held = (place >> 2) * 2 + (place & 1)
@@ -493,14 +534,11 @@
     small_all = gather_group(small)
     latent_low = swap_halves(latent_in)
     qkv_pieces, order = gather_pieces(qkv_weight)
-    qkv_pieces[3], up_weight, out_weight, down_weight, cotangent = tie(
-        qkv_pieces[3], up_weight, out_weight, down_weight, cotangent
-    )
     full_up = lax.all_gather(up_weight, GROUP, axis=0, tiled=True)
     out_pieces, _ = gather_pieces(out_weight)
-    down_pieces, _ = gather_pieces(down_weight)
     cotangent_low = swap_halves(cotangent)
     full_qkv = assemble(qkv_pieces, order)
+    full_down = lax.all_gather(down_weight, GROUP, axis=0, tiled=True)
 
     bounds = [0, width]
     for bias in (qv_bias, out_bias, up_bias, down_bias):
@@ -544,27 +582,21 @@
     pair_other = permute(pair_own, core_rule)
     heads = range(width // HEAD)
     halves = heads[: len(heads) // 2], heads[len(heads) // 2 :]
-    attended, log_totals = attend(query, pair_own, pair_other, halves[0])
-    attended, query, down_pieces[1], down_pieces[2] = tie(
-        attended, query, down_pieces[1], down_pieces[2]
-    )
-    attended_right, log_right = attend(query, pair_own, pair_other, halves[1])
-    attended_low = join_heads(attended, attended_right, width)
-    log_rows = (log_totals + log_right)[:, : len(heads)].T[:, None, :]
+    attended_low, log_totals = attend(query, pair_own, pair_other, heads)
+    log_rows = log_totals[:, : len(heads)].T[:, None, :]
     full_out = assemble(out_pieces, order)
     branch_one = matmul(attended_low, full_out) + full_out_bias
     middle = latent + gate_one * branch_one
 
     normed_two, inverse_two = normalize(middle)
     hidden_two = (normed_two * (1.0 + scale_two) + shift_two).astype(jnp.bfloat16)
-    full_down = assemble(down_pieces, order)
     mask_row = slot_mask[0]
     d_out = cotangent_low[0].astype(jnp.float32) * mask_row
     d_branch_two = (gate_two * d_out).astype(jnp.bfloat16)
-    branch_two, d_hidden_two, up_grad, down_grad, up_bias_grad = mlp(
+    branch_two, d_hidden_two, up_kept, up_sent, down_grad, up_bias_grad = mlp(
         hidden_two, d_branch_two, full_up, full_up_bias[None], full_down
     )
-    up_scatter = Scatter(up_grad.reshape(SHARDS, rows, hidden_width))
+    up_scatter = Scatter((up_kept, up_sent))
     down_shard = lax.psum_scatter(down_grad, GROUP, scatter_dimension=0, tiled=True)
     branch_two = branch_two + full_down_bias
     block_out = (mask_row * (middle + gate_two * branch_two)).astype(jnp.bfloat16)
@@ -578,10 +610,10 @@
     d_gate_one = jnp.sum(d_middle * branch_one, axis=0)
     d_branch_one = (gate_one * d_middle).astype(jnp.bfloat16)
 
-    out_grad = matmul_left(attended_low, d_branch_one).astype(jnp.bfloat16)
-    out_scatter = Scatter(out_grad.reshape(SHARDS, rows, width))
+    d_attended, out_halves = product_back(attended_low, d_branch_one, full_out)
+    d_attended = d_attended.astype(jnp.bfloat16)
+    out_scatter = Scatter(out_halves)
     out_bias_grad = jnp.sum(d_branch_one.astype(jnp.float32), axis=0)
-    d_attended = matmul_right(d_branch_one, full_out).astype(jnp.bfloat16)
     left = attend_back(query, pair_own, pair_other, d_attended, log_rows, halves[0])
     d_query, d_attended, up_scatter.received, out_scatter.received = tie(
         left[0], d_attended, up_scatter.received, out_scatter.received
@@ -595,12 +627,12 @@
     d_own = (d_own + d_other.astype(jnp.float32)).astype(jnp.bfloat16)
     d_projected = jnp.concatenate([d_query, d_own[0], d_own[1]], axis=-1)
 
-    qkv_grad = matmul_left(hidden_one, d_projected).astype(jnp.bfloat16)
-    qkv_scatter = Scatter(qkv_grad.reshape(SHARDS, rows, 3 * width))
+    d_projected, up_scatter.received = tie(d_projected, up_scatter.received)
+    d_hidden_one, qkv_halves = product_back(hidden_one, d_projected, full_qkv)
+    qkv_scatter = Scatter(qkv_halves)
     column_sums = jnp.sum(d_projected.astype(jnp.float32), axis=0)
-    d_hidden_one = matmul_right(d_projected, full_qkv)
-    d_hidden_one, up_scatter.received, out_scatter.received, qkv_scatter.received = tie(
-        d_hidden_one, up_scatter.received, out_scatter.received, qkv_scatter.received
+    d_hidden_one, out_scatter.received, down_shard = tie(
+        d_hidden_one, out_scatter.received, down_shard
     )
     up_scatter.third()
     out_scatter.third()
@@ -611,9 +643,11 @@
     latent_grad = swap_halves(latent_grad.astype(jnp.bfloat16)[None]).astype(jnp.float32)
 
     down_total = lax.psum(down_shard, "rep")
-    up_shard, down_total = tie(up_scatter.result().astype(jnp.bfloat16), down_total)
+    qkv_scatter.third()
+    up_shard, down_total, qkv_scatter.received = tie(
+        up_scatter.result().astype(jnp.bfloat16), down_total, qkv_scatter.received
+    )
     up_total = lax.psum(up_shard, "rep")
-    qkv_scatter.third()
     late = jnp.concatenate([out_scatter.result(), qkv_scatter.result()], axis=1)
     late_total = reduce_replicas(late, replicas)
     out_total, qkv_total = late_total[:, :width], late_total[:, width:]

time: 721 us -> 725 us (level)
  waiting for transfers between devices: 301 us -> 340 us
  local copies, waits for them, and re-layouts: 73.8 us -> 49.3 us
  Pallas kernels: 133 us -> 157 us
  matrix products: 37.9 us -> 16.4 us
  starting transfers between devices: 76.7 us -> 55.8 us
  other arithmetic: 72.9 us -> 82.2 us
    ppermute x44 -> x37, waiting for transfers between devices: 146 us -> 210 us  [permute(): return lax.ppermute(values, GROUP, pairs_by(rule))]
    psum x1, waiting for transfers between devices: 83.6 us -> 22.6 us  [per_device(): down_total = lax.psum(down_shard, 'rep')]
    ppermute x6, waiting for transfers between devices: 0.02 us -> 48.4 us  [gather_replicas(): stacked.append(lax.ppermute(values, 'rep', pairs))]
    pallas_call x0 -> x2, Pallas kernels: none -> 26.2 us  [product_back(): pl.pallas_call(product_back_kernel, grid=(columns // block,), out_shape=(...]
    psum x1, waiting for transfers between devices: 56.2 us -> 33.5 us  [per_device(): up_total = lax.psum(up_shard, 'rep')]
    dot_general x4 -> x0, matrix products: 21.2 us -> none  [the longest x2 11.9 us: matmul_right(): lax.dot_general(left, right, (((1,), (1,)), ((), ())), preferred_element_...]
    ppermute x44 -> x37, starting transfers between devices: 52.1 us -> 34.8 us  [permute(): return lax.ppermute(values, GROUP, pairs_by(rule))]
    unnamed x161 -> x137, local copies, waits for them, and re-layouts: 29.5 us -> 16.8 us
  transfers between devices with their start and end apart: 61 -> 55, of which waited for: 24 -> 27; matrix products, arithmetic and copies ran while one was open for 21% -> 17% of each run, Pallas kernels for 12% -> 15%
where the time goes in v5:
time: 725 us; the launch traced here: 717 us
  waiting for transfers between devices  340 us (47%)
  Pallas kernels  157 us (22%)
  other arithmetic  82.2 us (11%)
  starting transfers between devices  55.8 us (8%)
  local copies, waits for them, and re-layouts  49.3 us (7%)
  matrix products  16.4 us (2%)
  between operations  16 us (2%)
    ppermute x37, waiting for transfers between devices, permute(): return lax.ppermute(values, GROUP, pairs_by(rule))  210 us
    pallas_call x2, Pallas kernels, attend_back(): pl.pallas_call(functools.partial(attend_back_kernel, heads[0], low), grid...  49.3 us
    ppermute x6, waiting for transfers between devices, gather_replicas(): stacked.append(lax.ppermute(values, 'rep', pairs))  48.4 us
    pallas_call x1, Pallas kernels, mlp(): pl.pallas_call(mlp_kernel, grid=(units // block,), out_shape=(jax.ShapeDt...  47.4 us
    ppermute x37, starting transfers between devices, permute(): return lax.ppermute(values, GROUP, pairs_by(rule))  34.8 us
    psum x1, waiting for transfers between devices, per_device(): up_total = lax.psum(up_shard, 'rep')  33.5 us
    pallas_call x1, Pallas kernels, attend(): pl.pallas_call(functools.partial(attend_kernel, heads[0], low), grid=(len...  26.8 us
    pallas_call x2, Pallas kernels, product_back(): pl.pallas_call(product_back_kernel, grid=(columns // block,), out_shape=(...  26.2 us
  transfers between devices with their start and end apart: 55, of which 27 were waited for; matrix products, arithmetic and copies ran while one was open for 17% of the time, Pallas kernels for 15%

profile of v5, /device:TPU:9, one launch (start us, length us, event | category | flops | bytes accessed | tf_op | source)
XLA Modules:
  0.0 716.9 jit_solution(16456928839495018618)
XLA Ops:
  19.8 33.4 %collective-permute-done.2 = bf16[4,2432]{1,0:T(4,128)(2,1)S(1)} collective-permute-done((bf16[4,2432]{1,0:T(4,128)(2,1)S(1)}, bf16[4,2432]{1,0:T(4,128)(2,1)S(1)}, u32[]{:S(2)}, u32[]{:S(2)}) %collective-permute-start.2) | collective-permute-done | bytes 19488 | tf_op jit(solution)/shard_map/ppermute | solution.py:62
  60.5 25.0 %collective-permute-done.5 = f32[1,6912]{1,0:T(1,128)S(1)} collective-permute-done((f32[1,6912]{1,0:T(1,128)S(1)}, f32[1,6912]{1,0:T(1,128)S(1)}, u32[]{:S(2)}, u32[]{:S(2)}) %collective-permute-start.5) | collective-permute-done | bytes 27680 | tf_op jit(solution)/shard_map/ppermute | solution.py:62
  89.8 4.5 collective-permute-done.9.refs_3_
  94.3 11.0 %collective-permute-start.13 = (bf16[144,3456]{1,0:T(8,128)(2,1)S(1)}, bf16[144,3456]{1,0:T(8,128)(2,1)S(1)}, u32[]{:S(2)}, u32[]{:S(2)}) collective-permute-start(bf16[144,3456]{1,0:T(8,128)(2,1)S(1)} %collective-permute-done.9.refs_3_), channel_id=1, source_target_pairs={{0,2},{1,3},{2,0},{3,1},{4,6},{5,7},{6,4},{7,5},{8,10},{9,11},{10,... | collective-permute-start | bytes 2985992 | tf_op jit(solution)/shard_map/ppermute | solution.py:62
  107.6 4.6 shard_map.237.weight_ref
  112.2 5.2 add_convert_fusion.2
  126.4 44.0 %collective-permute-done.15.refs_1_ = bf16[144,1152]{1,0:T(8,128)(2,1)} collective-permute-done((bf16[144,1152]{1,0:T(8,128)(2,1)S(1)}, bf16[144,1152]{1,0:T(8,128)(2,1)}, u32[]{:S(2)}, u32[]{:S(2)}) %collective-permute-start.15) | collective-permute-done | bytes 331808 | tf_op jit(solution)/shard_map/ppermute | solution.py:62
  172.1 12.0 %collective-permute-done.17.refs_3_ = bf16[144,1152]{1,0:T(8,128)(2,1)} collective-permute-done((bf16[144,1152]{1,0:T(8,128)(2,1)}, bf16[144,1152]{1,0:T(8,128)(2,1)}, u32[]{:S(2)}, u32[]{:S(2)}) %collective-permute-start.17) | collective-permute-done | bytes 331808 | tf_op jit(solution)/shard_map/ppermute | solution.py:62
  191.3 2.6 shard_map.239.weight_ref
  193.9 4.7 convert_reduce_fusion.2
  200.0 26.8 %shard_map.238 = (bf16[512,1152]{1,0:T(8,128)(2,1)S(1)}, f32[512,128]{1,0:T(8,128)S(1)}) custom-call(bf16[512,1152]{1,0:T(8,128)(2,1)S(1)} %slice.226.query_ref, bf16[512,2304]{1,0:T(8,128)(2,1)} %slice.227.own_ref, bf16[512,2304]{1,0:T(8,128)(2,1)} %collective-permute-done.14.other_ref), custom_call_target="tpu_custom_call" | custom-call | flops 1048576 | bytes 1048576 | tf_op jit(solution)/shard_map/pallas_call | solution.py:281
  226.9 3.3 fusion.49
  233.1 47.4 %shard_map.240 = (f32[512,1152]{1,0:T(8,128)}, f32[512,1152]{1,0:T(8,128)}, bf16[4,144,4608]{2,1,0:T(8,128)(2,1)}, bf16[4,144,4608]{2,1,0:T(8,128)(2,1)}, bf16[4608,1152]{1,0:T(8,128)(2,1)}, /*index=5*/f32[1,4608]{1,0:T(1,128)}) custom-call(bf16[512,1152]{1,0:T(8,128)(2,1)} %add_convert_fusion.4.hidden_ref, ...), custom_call_target="tpu_custom_call" | custom-call | flops 1048576 | bytes 1048576 | tf_op jit(solution)/shard_map/pallas_call | solution.py:483
  281.2 4.1 multiply_reduce_fusion
  285.3 6.6 fusion.22
  291.9 7.3 %shard_map.241 = (f32[512,1152]{1,0:T(8,128)S(1)}, bf16[4,144,1152]{2,1,0:T(8,128)(2,1)S(1)}, bf16[4,144,1152]{2,1,0:T(8,128)(2,1)}) custom-call(bf16[512,1152]{1,0:T(8,128)(2,1)S(1)} %copy-done.16, bf16[512,1152]{1,0:T(8,128)(2,1)S(1)} %get-tuple-element.116.upstream_ref, bf16[1152,1152]{1,0:T(8,128)(2,1)S(1)} %copy-done.7), custom_call_target="tpu_custom_call" | custom-call | flops 1048576 | bytes 1048576 | tf_op jit(solution)/shard_map/pallas_call | solution.py:423
  304.0 2.8 convert_element_type.230.upstream_ref
  306.8 25.0 %shard_map.242 = (bf16[512,640]{1,0:T(8,128)(2,1)}, f32[2,512,640]{2,1,0:T(8,128)}, bf16[2,512,640]{2,1,0:T(8,128)(2,1)}) custom-call(bf16[512,1152]{1,0:T(8,128)(2,1)} %copy-done.3, bf16[512,2304]{1,0:T(8,128)(2,1)} %slice.227.own_ref, bf16[512,2304]{1,0:T(8,128)(2,1)} %collective-permute-done.14.other_ref, ...), custom_call_target="tpu_custom_call" | custom-call | flops 1048576 | bytes 1048576 | tf_op jit(solution)/shard_map/pallas_call | solution.py:353
  334.8 3.6 collective-permute-start.23
  338.5 24.3 %shard_map.243 = (bf16[512,640]{1,0:T(8,128)(2,1)}, f32[2,512,640]{2,1,0:T(8,128)}, bf16[2,512,640]{2,1,0:T(8,128)(2,1)}) custom-call(bf16[512,1152]{1,0:T(8,128)(2,1)} %copy-done.3, bf16[512,2304]{1,0:T(8,128)(2,1)} %slice.227.own_ref, bf16[512,2304]{1,0:T(8,128)(2,1)} %collective-permute-done.14.other_ref, ...), custom_call_target="tpu_custom_call" | custom-call | flops 1048576 | bytes 1048576 | tf_op jit(solution)/shard_map/pallas_call | solution.py:353
  366.7 5.4 add_convert_fusion
  377.9 3.1 fusion
  381.3 38.7 %collective-permute-done.27 = bf16[2,144,4608]{2,1,0:T(8,128)(2,1)} collective-permute-done((bf16[2,144,4608]{2,1,0:T(8,128)(2,1)S(1)}, bf16[2,144,4608]{2,1,0:T(8,128)(2,1)}, u32[]{:S(2)}, u32[]{:S(2)}) %collective-permute-start.27) | collective-permute-done | bytes 2654240 | tf_op jit(solution)/shard_map/ppermute | solution.py:62
  420.0 3.3 copy-done.2
  423.3 19.0 %shard_map.244 = (f32[512,1152]{1,0:T(8,128)S(1)}, bf16[4,144,3456]{2,1,0:T(8,128)(2,1)S(1)}, bf16[4,144,3456]{2,1,0:T(8,128)(2,1)}) custom-call(bf16[512,1152]{1,0:T(8,128)(2,1)S(1)} %fusion.13.left_ref, bf16[512,3456]{1,0:T(8,128)(2,1)S(1)} %fusion.27.upstream_ref, bf16[1152,3456]{1,0:T(8,128)(2,1)S(1)} %copy-done.2), custom_call_target="tpu_custom_call" | custom-call | flops 1048576 | bytes 1048576 | tf_op jit(solution)/shard_map/pallas_call | solution.py:423
  446.9 2.4 broadcast_select_fusion
  451.5 2.6 convert_add_fusion
  454.4 3.2 add_convert_fusion.1
  464.8 13.4 %collective-permute-done.42 = bf16[144,4608]{1,0:T(8,128)(2,1)S(1)} collective-permute-done((bf16[144,4608]{1,0:T(8,128)(2,1)S(1)}, bf16[144,4608]{1,0:T(8,128)(2,1)S(1)}, u32[]{:S(2)}, u32[]{:S(2)}) %collective-permute-start.42) | collective-permute-done | bytes 1327136 | tf_op jit(solution)/shard_map/ppermute | solution.py:62
  479.6 13.7 %collective-permute-done.41 = bf16[2,144,3456]{2,1,0:T(8,128)(2,1)} collective-permute-done((bf16[2,144,3456]{2,1,0:T(8,128)(2,1)}, bf16[2,144,3456]{2,1,0:T(8,128)(2,1)}, u32[]{:S(2)}, u32[]{:S(2)}) %collective-permute-start.41) | collective-permute-done | bytes 1990688 | tf_op jit(solution)/shard_map/ppermute | solution.py:62
  493.3 4.5 convert_add_fusion.1
  500.1 2.9 fusion.19
  503.1 3.8 multiply_reduce_fusion.1
  507.2 2.6 fusion.29
  516.1 13.0 %collective-permute-done.32 = f32[4,16128]{1,0:T(4,128)S(1)} collective-permute-done((f32[4,16128]{1,0:T(4,128)S(1)}, f32[4,16128]{1,0:T(4,128)S(1)}, u32[]{:S(2)}, u32[]{:S(2)}) %collective-permute-start.32) | collective-permute-done | bytes 258080 | tf_op jit(solution)/shard_map/ppermute | solution.py:62
  542.3 5.5 collective-permute-start.29
  548.7 4.4 collective-permute-done.37
  553.1 2.5 collective-permute-done.38
  562.6 22.6 %all-reduce.3.cloned.1.call-done = bf16[576,1152]{1,0:T(8,128)(2,1)} async-done(((bf16[576,1152]{1,0:T(8,128)(2,1)}), bf16[576,1152]{1,0:T(8,128)(2,1)}) %all-reduce.3.cloned.1.call-update) | async-done | bytes 1327120 | tf_op jit(solution)/shard_map/psum | solution.py:645
  590.0 5.2 fusion.53
  595.9 20.6 %collective-permute-done.45 = bf16[144,1152]{1,0:T(8,128)(2,1)S(1)} collective-permute-done((bf16[144,1152]{1,0:T(8,128)(2,1)S(1)}, bf16[144,1152]{1,0:T(8,128)(2,1)S(1)}, u32[]{:S(2)}, u32[]{:S(2)}) %collective-permute-start.45) | collective-permute-done | bytes 331808 | tf_op jit(solution)/shard_map/ppermute | solution.py:199
  616.5 3.1 collective-permute-done.46
  622.4 3.1 select_convert_fusion
  628.6 3.0 collective-permute-done.47
  632.6 34.1 %collective-permute-done.48 = bf16[144,1152]{1,0:T(8,128)(2,1)S(1)} collective-permute-done((bf16[144,1152]{1,0:T(8,128)(2,1)}, bf16[144,1152]{1,0:T(8,128)(2,1)S(1)}, u32[]{:S(2)}, u32[]{:S(2)}) %collective-permute-start.48) | collective-permute-done | bytes 331808 | tf_op jit(solution)/shard_map/ppermute | solution.py:90
  666.7 4.4 collective-permute-done.49
  673.5 33.5 %all-reduce.5.cloned.1.call-done = bf16[144,4608]{1,0:T(8,128)(2,1)} async-done(((bf16[144,4608]{1,0:T(8,128)(2,1)}), bf16[144,4608]{1,0:T(8,128)(2,1)}) %all-reduce.5.cloned.1.call-update) | async-done | bytes 1327120 | tf_op jit(solution)/shard_map/psum | solution.py:650
  707.0 3.1 convert_element_type.269
  (353 shorter events, 126.1 us)
Async XLA Ops:
  7.3 225.8 %all-gather.3.cloned.1.call-start = ((), (), s32[]{:S(2)}) async-start(), calls=%async_computation.1 | async-start | bytes 11943936 | tf_op jit(solution)/shard_map/all_gather | solution.py:537
  8.0 225.1 %all-gather.5.cloned.1.call-start = ((), (), s32[]{:S(2)}) async-start(), calls=%async_computation.2 | async-start | bytes 11943936 | tf_op jit(solution)/shard_map/all_gather | solution.py:541
  8.8 491.3 %reduce-scatter.2.cloned.1.call-start = ((), (), s32[]{:S(2)}) async-start(), calls=%async_computation.3 | async-start | bytes 11943936 | tf_op jit(solution)/shard_map/reduce_scatter | solution.py:600
  12.3 7.0 collective-permute-start.1
  14.2 45.1 %collective-permute-start.7 = (bf16[144,3456]{1,0:T(8,128)(2,1)}, bf16[144,3456]{1,0:T(8,128)(2,1)}, u32[]{:S(2)}, u32[]{:S(2)}) collective-permute-start(bf16[144,3456]{1,0:T(8,128)(2,1)} %refs_0_.2), channel_id=1, source_target_pairs={{0,4},{1,5},{2,3},{3,2},{4,0},{5,1},{6,7},{7,6},{8,12},{9,13},{10,... | collective-permute-start | bytes 2985992 | tf_op jit(solution)/shard_map/ppermute | solution.py:62
  15.4 72.3 %collective-permute-start.8 = (bf16[144,3456]{1,0:T(8,128)(2,1)}, bf16[144,3456]{1,0:T(8,128)(2,1)}, u32[]{:S(2)}, u32[]{:S(2)}) collective-permute-start(bf16[144,3456]{1,0:T(8,128)(2,1)} %refs_0_.2), channel_id=1, source_target_pairs={{0,1},{1,0},{2,6},{3,7},{4,5},{5,4},{6,2},{7,3},{8,9},{9,8},{10,14... | collective-permute-start | bytes 2985992 | tf_op jit(solution)/shard_map/ppermute | solution.py:62
  16.6 89.7 %collective-permute-start.10 = (bf16[144,3456]{1,0:T(8,128)(2,1)}, bf16[144,3456]{1,0:T(8,128)(2,1)}, u32[]{:S(2)}, u32[]{:S(2)}) collective-permute-start(bf16[144,3456]{1,0:T(8,128)(2,1)} %refs_0_.2), channel_id=1, source_target_pairs={{0,2},{1,3},{2,0},{3,1},{4,6},{5,7},{6,4},{7,5},{8,10},{9,11},{10,... | collective-permute-start | bytes 2985992 | tf_op jit(solution)/shard_map/ppermute | solution.py:62
  17.3 70.8 %collective-permute-start.3 = (bf16[1,512,1152]{2,1,0:T(8,128)(2,1)S(1)}, bf16[1,512,1152]{2,1,0:T(8,128)(2,1)}, u32[]{:S(2)}, u32[]{:S(2)}) collective-permute-start(bf16[1,512,1152]{2,1,0:T(8,128)(2,1)S(1)} %copy-done.35), channel_id=1, source_target_pairs={{1,2},{2,1},{5,6},{6,5},{9,10},{10,9},{13,14},{14,13},{17,18},{18,... | collective-permute-start | bytes 3538952 | tf_op jit(solution)/shard_map/ppermute | solution.py:68
  19.3 34.0 %collective-permute-start.2 = (bf16[4,2432]{1,0:T(4,128)(2,1)S(1)}, bf16[4,2432]{1,0:T(4,128)(2,1)S(1)}, u32[]{:S(2)}, u32[]{:S(2)}) collective-permute-start(bf16[4,2432]{1,0:T(4,128)(2,1)S(1)} %maximum_select_fusion.4), channel_id=1, source_target_pairs={{0,4},{1,5},{2,6},{3,7},{4,0},{5,1},{6,2},{7,3},{8,12},{9,13},{10,... | collective-permute-start | bytes 58376 | tf_op jit(solution)/shard_map/ppermute | solution.py:62
  58.1 27.4 %collective-permute-start.5 = (f32[1,6912]{1,0:T(1,128)S(1)}, f32[1,6912]{1,0:T(1,128)S(1)}, u32[]{:S(2)}, u32[]{:S(2)}) collective-permute-start(f32[1,6912]{1,0:T(1,128)S(1)} %broadcast_select_fusion.4), channel_id=1, source_target_pairs={{0,1},{1,0},{2,3},{3,2},{4,5},{5,4},{6,7},{7,6},{8,9},{9,8},{10,11... | collective-permute-start | bytes 82952 | tf_op jit(solution)/shard_map/ppermute | solution.py:62
  59.3 35.0 %collective-permute-start.9 = (bf16[144,3456]{1,0:T(8,128)(2,1)}, bf16[144,3456]{1,0:T(8,128)(2,1)S(1)}, u32[]{:S(2)}, u32[]{:S(2)}) collective-permute-start(bf16[144,3456]{1,0:T(8,128)(2,1)} %collective-permute-done.7.refs_1_), channel_id=1, source_target_pairs={{0,1},{1,0},{2,6},{3,7},{4,5},{5,4},{6,2},{7,3},{8,9},{9,8},{10,14... | collective-permute-start | bytes 2985992 | tf_op jit(solution)/shard_map/ppermute | solution.py:62
  87.5 18.8 %collective-permute-start.11 = (bf16[144,3456]{1,0:T(8,128)(2,1)}, bf16[144,3456]{1,0:T(8,128)(2,1)S(1)}, u32[]{:S(2)}, u32[]{:S(2)}) collective-permute-start(bf16[144,3456]{1,0:T(8,128)(2,1)} %collective-permute-done.7.refs_1_), channel_id=1, source_target_pairs={{0,2},{1,3},{2,0},{3,1},{4,6},{5,7},{6,4},{7,5},{8,10},{9,11},{10,... | collective-permute-start | bytes 2985992 | tf_op jit(solution)/shard_map/ppermute | solution.py:62
  87.7 18.7 %collective-permute-start.12 = (bf16[144,3456]{1,0:T(8,128)(2,1)}, bf16[144,3456]{1,0:T(8,128)(2,1)S(1)}, u32[]{:S(2)}, u32[]{:S(2)}) collective-permute-start(bf16[144,3456]{1,0:T(8,128)(2,1)} %collective-permute-done.8.refs_2_), channel_id=1, source_target_pairs={{0,2},{1,3},{2,0},{3,1},{4,6},{5,7},{6,4},{7,5},{8,10},{9,11},{10,... | collective-permute-start | bytes 2985992 | tf_op jit(solution)/shard_map/ppermute | solution.py:62
  94.3 13.3 %collective-permute-start.13 = (bf16[144,3456]{1,0:T(8,128)(2,1)S(1)}, bf16[144,3456]{1,0:T(8,128)(2,1)S(1)}, u32[]{:S(2)}, u32[]{:S(2)}) collective-permute-start(bf16[144,3456]{1,0:T(8,128)(2,1)S(1)} %collective-permute-done.9.refs_3_), channel_id=1, source_target_pairs={{0,2},{1,3},{2,0},{3,1},{4,6},{5,7},{6,4},{7,5},{8,10},{9,11},{10,... | collective-permute-start | bytes 2985992 | tf_op jit(solution)/shard_map/ppermute | solution.py:62
  120.2 79.8 %collective-permute-start.14 = (bf16[512,2304]{1,0:T(8,128)(2,1)}, bf16[512,2304]{1,0:T(8,128)(2,1)}, u32[]{:S(2)}, u32[]{:S(2)}) collective-permute-start(bf16[512,2304]{1,0:T(8,128)(2,1)} %slice.227.own_ref), channel_id=1, source_target_pairs={{0,2},{1,3},{2,0},{3,1},{4,6},{5,7},{6,4},{7,5},{8,10},{9,11},{10,... | collective-permute-start | bytes 7077896 | tf_op jit(solution)/shard_map/ppermute | solution.py:62
  120.6 73.3 %collective-permute-start.22 = (bf16[1,512,1152]{2,1,0:T(8,128)(2,1)}, bf16[1,512,1152]{2,1,0:T(8,128)(2,1)}, u32[]{:S(2)}, u32[]{:S(2)}) collective-permute-start(bf16[1,512,1152]{2,1,0:T(8,128)(2,1)} %param.27), channel_id=1, source_target_pairs={{1,2},{2,1},{5,6},{6,5},{9,10},{10,9},{13,14},{14,13},{17,18},{18,... | collective-permute-start | bytes 3538952 | tf_op jit(solution)/shard_map/ppermute | solution.py:68
  122.7 47.7 %collective-permute-start.15 = (bf16[144,1152]{1,0:T(8,128)(2,1)S(1)}, bf16[144,1152]{1,0:T(8,128)(2,1)}, u32[]{:S(2)}, u32[]{:S(2)}) collective-permute-start(bf16[144,1152]{1,0:T(8,128)(2,1)S(1)} %copy-done.17), channel_id=1, source_target_pairs={{0,4},{1,5},{2,3},{3,2},{4,0},{5,1},{6,7},{7,6},{8,12},{9,13},{10,... | collective-permute-start | bytes 995336 | tf_op jit(solution)/shard_map/ppermute | solution.py:62
  122.8 48.8 %collective-permute-start.16 = (bf16[144,1152]{1,0:T(8,128)(2,1)S(1)}, bf16[144,1152]{1,0:T(8,128)(2,1)}, u32[]{:S(2)}, u32[]{:S(2)}) collective-permute-start(bf16[144,1152]{1,0:T(8,128)(2,1)S(1)} %copy-done.17), channel_id=1, source_target_pairs={{0,1},{1,0},{2,6},{3,7},{4,5},{5,4},{6,2},{7,3},{8,9},{9,8},{10,14... | collective-permute-start | bytes 995336 | tf_op jit(solution)/shard_map/ppermute | solution.py:62
  124.1 47.5 %collective-permute-start.18 = (bf16[144,1152]{1,0:T(8,128)(2,1)S(1)}, bf16[144,1152]{1,0:T(8,128)(2,1)}, u32[]{:S(2)}, u32[]{:S(2)}) collective-permute-start(bf16[144,1152]{1,0:T(8,128)(2,1)S(1)} %copy-done.17), channel_id=1, source_target_pairs={{0,2},{1,3},{2,0},{3,1},{4,6},{5,7},{6,4},{7,5},{8,10},{9,11},{10,... | collective-permute-start | bytes 995336 | tf_op jit(solution)/shard_map/ppermute | solution.py:62
  170.4 13.7 %collective-permute-start.17 = (bf16[144,1152]{1,0:T(8,128)(2,1)}, bf16[144,1152]{1,0:T(8,128)(2,1)}, u32[]{:S(2)}, u32[]{:S(2)}) collective-permute-start(bf16[144,1152]{1,0:T(8,128)(2,1)} %collective-permute-done.15.refs_1_), channel_id=1, source_target_pairs={{0,1},{1,0},{2,6},{3,7},{4,5},{5,4},{6,2},{7,3},{8,9},{9,8},{10,14... | collective-permute-start | bytes 995336 | tf_op jit(solution)/shard_map/ppermute | solution.py:62
  171.6 19.7 %collective-permute-start.19 = (bf16[144,1152]{1,0:T(8,128)(2,1)}, bf16[144,1152]{1,0:T(8,128)(2,1)}, u32[]{:S(2)}, u32[]{:S(2)}) collective-permute-start(bf16[144,1152]{1,0:T(8,128)(2,1)} %collective-permute-done.15.refs_1_), channel_id=1, source_target_pairs={{0,2},{1,3},{2,0},{3,1},{4,6},{5,7},{6,4},{7,5},{8,10},{9,11},{10,... | collective-permute-start | bytes 995336 | tf_op jit(solution)/shard_map/ppermute | solution.py:62
  171.6 19.7 %collective-permute-start.20 = (bf16[144,1152]{1,0:T(8,128)(2,1)}, bf16[144,1152]{1,0:T(8,128)(2,1)}, u32[]{:S(2)}, u32[]{:S(2)}) collective-permute-start(bf16[144,1152]{1,0:T(8,128)(2,1)} %collective-permute-done.16.refs_2_), channel_id=1, source_target_pairs={{0,2},{1,3},{2,0},{3,1},{4,6},{5,7},{6,4},{7,5},{8,10},{9,11},{10,... | collective-permute-start | bytes 995336 | tf_op jit(solution)/shard_map/ppermute | solution.py:62
  184.1 7.2 %collective-permute-start.21 = (bf16[144,1152]{1,0:T(8,128)(2,1)}, bf16[144,1152]{1,0:T(8,128)(2,1)}, u32[]{:S(2)}, u32[]{:S(2)}) collective-permute-start(bf16[144,1152]{1,0:T(8,128)(2,1)} %collective-permute-done.17.refs_3_), channel_id=1, source_target_pairs={{0,2},{1,3},{2,0},{3,1},{4,6},{5,7},{6,4},{7,5},{8,10},{9,11},{10,... | collective-permute-start | bytes 995336 | tf_op jit(solution)/shard_map/ppermute | solution.py:62
  280.5 58.0 %collective-permute-start.24 = (bf16[4,144,4608]{2,1,0:T(8,128)(2,1)}, bf16[4,144,4608]{2,1,0:T(8,128)(2,1)}, u32[]{:S(2)}, u32[]{:S(2)}) collective-permute-start(bf16[4,144,4608]{2,1,0:T(8,128)(2,1)} %get-tuple-element.51), channel_id=1, source_target_pairs={{0,2},{1,3},{2,0},{3,1},{4,6},{5,7},{6,4},{7,5},{8,10},{9,11},{10,... | collective-permute-start | bytes 15925256 | tf_op jit(solution)/shard_map/ppermute | solution.py:62
  301.6 36.8 %collective-permute-start.25 = (bf16[4,144,1152]{2,1,0:T(8,128)(2,1)}, bf16[4,144,1152]{2,1,0:T(8,128)(2,1)}, u32[]{:S(2)}, u32[]{:S(2)}) collective-permute-start(bf16[4,144,1152]{2,1,0:T(8,128)(2,1)} %get-tuple-element.52), channel_id=1, source_target_pairs={{0,2},{1,3},{2,0},{3,1},{4,6},{5,7},{6,4},{7,5},{8,10},{9,11},{10,... | collective-permute-start | bytes 3981320 | tf_op jit(solution)/shard_map/ppermute | solution.py:62
  302.5 282.7 %all-reduce.3.cloned.1.call-start = ((), (), s32[]{:S(2)}) async-start(), calls=%async_computation.4 | async-start | bytes 2654208 | tf_op jit(solution)/shard_map/psum | solution.py:645
  334.8 112.1 %collective-permute-start.23 = (bf16[1,512,1152]{2,1,0:T(8,128)(2,1)}, bf16[1,512,1152]{2,1,0:T(8,128)(2,1)}, u32[]{:S(2)}, u32[]{:S(2)}) collective-permute-start(bf16[1,512,1152]{2,1,0:T(8,128)(2,1)} %get-tuple-element.114), channel_id=1, source_target_pairs={{1,2},{2,1},{5,6},{6,5},{9,10},{10,9},{13,14},{14,13},{17,18},{18,... | collective-permute-start | bytes 3538952 | tf_op jit(solution)/shard_map/ppermute | solution.py:68
  366.7 11.1 %collective-permute-start.26 = (bf16[2,512,1152]{2,1,0:T(8,128)(2,1)}, bf16[2,512,1152]{2,1,0:T(8,128)(2,1)}, u32[]{:S(2)}, u32[]{:S(2)}) collective-permute-start(bf16[2,512,1152]{2,1,0:T(8,128)(2,1)} %pad_maximum_fusion.2), channel_id=1, source_target_pairs={{0,2},{1,3},{2,0},{3,1},{4,6},{5,7},{6,4},{7,5},{8,10},{9,11},{10,... | collective-permute-start | bytes 7077896 | tf_op jit(solution)/shard_map/ppermute | solution.py:62
  374.5 45.5 %collective-permute-start.27 = (bf16[2,144,4608]{2,1,0:T(8,128)(2,1)S(1)}, bf16[2,144,4608]{2,1,0:T(8,128)(2,1)}, u32[]{:S(2)}, u32[]{:S(2)}) collective-permute-start(bf16[2,144,4608]{2,1,0:T(8,128)(2,1)S(1)} %pad_maximum_fusion.1), channel_id=1, source_target_pairs={{0,4},{1,5},{2,3},{3,2},{4,0},{5,1},{6,7},{7,6},{8,12},{9,13},{10,... | collective-permute-start | bytes 7962632 | tf_op jit(solution)/shard_map/ppermute | solution.py:62
  445.6 8.7 %collective-permute-start.40 = (bf16[4,144,3456]{2,1,0:T(8,128)(2,1)}, bf16[4,144,3456]{2,1,0:T(8,128)(2,1)}, u32[]{:S(2)}, u32[]{:S(2)}) collective-permute-start(bf16[4,144,3456]{2,1,0:T(8,128)(2,1)} %get-tuple-element.71), channel_id=1, source_target_pairs={{0,2},{1,3},{2,0},{3,1},{4,6},{5,7},{6,4},{7,5},{8,10},{9,11},{10,... | collective-permute-start | bytes 11943944 | tf_op jit(solution)/shard_map/ppermute | solution.py:62
  454.3 23.9 %collective-permute-start.42 = (bf16[144,4608]{1,0:T(8,128)(2,1)S(1)}, bf16[144,4608]{1,0:T(8,128)(2,1)S(1)}, u32[]{:S(2)}, u32[]{:S(2)}) collective-permute-start(bf16[144,4608]{1,0:T(8,128)(2,1)S(1)} %fusion.24), channel_id=1, source_target_pairs={{0,1},{1,0},{2,6},{3,7},{4,5},{5,4},{6,2},{7,3},{8,9},{9,8},{10,14... | collective-permute-start | bytes 3981320 | tf_op jit(solution)/shard_map/ppermute | solution.py:62
  460.9 32.4 %collective-permute-start.41 = (bf16[2,144,3456]{2,1,0:T(8,128)(2,1)}, bf16[2,144,3456]{2,1,0:T(8,128)(2,1)}, u32[]{:S(2)}, u32[]{:S(2)}) collective-permute-start(bf16[2,144,3456]{2,1,0:T(8,128)(2,1)} %pad_maximum_fusion.3), channel_id=1, source_target_pairs={{0,4},{1,5},{2,3},{3,2},{4,0},{5,1},{6,7},{7,6},{8,12},{9,13},{10,... | collective-permute-start | bytes 5971976 | tf_op jit(solution)/shard_map/ppermute | solution.py:62
  462.7 37.4 %collective-permute-start.28 = (bf16[2,144,1152]{2,1,0:T(8,128)(2,1)}, bf16[2,144,1152]{2,1,0:T(8,128)(2,1)}, u32[]{:S(2)}, u32[]{:S(2)}) collective-permute-start(bf16[2,144,1152]{2,1,0:T(8,128)(2,1)} %pad_maximum_fusion.4), channel_id=1, source_target_pairs={{0,4},{1,5},{2,3},{3,2},{4,0},{5,1},{6,7},{7,6},{8,12},{9,13},{10,... | collective-permute-start | bytes 1990664 | tf_op jit(solution)/shard_map/ppermute | solution.py:62
  507.1 3.6 collective-permute-start.30
  509.8 52.8 %collective-permute-start.43 = (bf16[144,3456]{1,0:T(8,128)(2,1)}, bf16[144,3456]{1,0:T(8,128)(2,1)}, u32[]{:S(2)}, u32[]{:S(2)}) collective-permute-start(bf16[144,3456]{1,0:T(8,128)(2,1)} %fusion.29), channel_id=1, source_target_pairs={{0,1},{1,0},{2,6},{3,7},{4,5},{5,4},{6,2},{7,3},{8,9},{9,8},{10,14... | collective-permute-start | bytes 2985992 | tf_op jit(solution)/shard_map/ppermute | solution.py:62
  513.7 15.3 %collective-permute-start.32 = (f32[4,16128]{1,0:T(4,128)S(1)}, f32[4,16128]{1,0:T(4,128)S(1)}, u32[]{:S(2)}, u32[]{:S(2)}) collective-permute-start(f32[4,16128]{1,0:T(4,128)S(1)} %maximum_select_fusion.1), channel_id=1, source_target_pairs={{0,4},{1,5},{2,6},{3,7},{4,0},{5,1},{6,2},{7,3},{8,12},{9,13},{10,... | collective-permute-start | bytes 774152 | tf_op jit(solution)/shard_map/ppermute | solution.py:62
  515.3 23.9 %collective-permute-start.39 = (bf16[144,1152]{1,0:T(8,128)(2,1)}, bf16[144,1152]{1,0:T(8,128)(2,1)S(1)}, u32[]{:S(2)}, u32[]{:S(2)}) collective-permute-start(bf16[144,1152]{1,0:T(8,128)(2,1)} %fusion.36), channel_id=1, source_target_pairs={{0,1},{1,0},{2,6},{3,7},{4,5},{5,4},{6,2},{7,3},{8,9},{9,8},{10,14... | collective-permute-start | bytes 995336 | tf_op jit(solution)/shard_map/ppermute | solution.py:62
  516.0 191.0 %all-reduce.5.cloned.1.call-start = ((), (), s32[]{:S(2)}) async-start(), calls=%async_computation.5 | async-start | bytes 2654208 | tf_op jit(solution)/shard_map/psum | solution.py:650
  535.6 13.0 %collective-permute-start.36 = (f32[29376]{0:T(1024)S(1)}, f32[29376]{0:T(1024)S(1)}, u32[]{:S(2)}, u32[]{:S(2)}) collective-permute-start(f32[29376]{0:T(1024)S(1)} %concatenate.122), channel_id=1, source_target_pairs={{0,8},{8,16},{16,24},{24,0},{1,9},{9,17},{17,25},{25,1},{2,10},{10... | collective-permute-start | bytes 352520 | tf_op jit(solution)/shard_map/ppermute | solution.py:90
  536.6 16.4 %collective-permute-start.37 = (f32[29376]{0:T(1024)S(1)}, f32[29376]{0:T(1024)S(1)}, u32[]{:S(2)}, u32[]{:S(2)}) collective-permute-start(f32[29376]{0:T(1024)S(1)} %concatenate.122), channel_id=1, source_target_pairs={{0,16},{8,24},{16,0},{24,8},{1,17},{9,25},{17,1},{25,9},{2,18},{10... | collective-permute-start | bytes 352520 | tf_op jit(solution)/shard_map/ppermute | solution.py:90
  537.9 17.7 %collective-permute-start.38 = (f32[29376]{0:T(1024)S(1)}, f32[29376]{0:T(1024)}, u32[]{:S(2)}, u32[]{:S(2)}) collective-permute-start(f32[29376]{0:T(1024)S(1)} %concatenate.122), channel_id=1, source_target_pairs={{0,24},{8,0},{16,8},{24,16},{1,25},{9,1},{17,9},{25,17},{2,26},{10... | collective-permute-start | bytes 352520 | tf_op jit(solution)/shard_map/ppermute | solution.py:90
  542.3 80.0 %collective-permute-start.29 = (bf16[1,512,1152]{2,1,0:T(8,128)(2,1)}, bf16[1,512,1152]{2,1,0:T(8,128)(2,1)}, u32[]{:S(2)}, u32[]{:S(2)}) collective-permute-start(bf16[1,512,1152]{2,1,0:T(8,128)(2,1)} %get-tuple-element.119), channel_id=1, source_target_pairs={{1,2},{2,1},{5,6},{6,5},{9,10},{10,9},{13,14},{14,13},{17,18},{18,... | collective-permute-start | bytes 3538952 | tf_op jit(solution)/shard_map/ppermute | solution.py:68
  587.5 8.5 %collective-permute-start.44 = (bf16[144,1152]{1,0:T(8,128)(2,1)S(1)}, bf16[144,1152]{1,0:T(8,128)(2,1)S(1)}, u32[]{:S(2)}, u32[]{:S(2)}) collective-permute-start(bf16[144,1152]{1,0:T(8,128)(2,1)S(1)} %get-tuple-element.120), channel_id=1, source_target_pairs={{0,8},{8,16},{16,24},{24,0},{1,9},{9,17},{17,25},{25,1},{2,10},{10... | collective-permute-start | bytes 995336 | tf_op jit(solution)/shard_map/ppermute | solution.py:199
  588.7 27.8 %collective-permute-start.45 = (bf16[144,1152]{1,0:T(8,128)(2,1)S(1)}, bf16[144,1152]{1,0:T(8,128)(2,1)S(1)}, u32[]{:S(2)}, u32[]{:S(2)}) collective-permute-start(bf16[144,1152]{1,0:T(8,128)(2,1)S(1)} %get-tuple-element.122), channel_id=1, source_target_pairs={{0,16},{8,24},{16,0},{24,8},{1,17},{9,25},{17,1},{25,9},{2,18},{10... | collective-permute-start | bytes 995336 | tf_op jit(solution)/shard_map/ppermute | solution.py:199
  589.9 29.6 %collective-permute-start.46 = (bf16[144,1152]{1,0:T(8,128)(2,1)S(1)}, bf16[144,1152]{1,0:T(8,128)(2,1)S(1)}, u32[]{:S(2)}, u32[]{:S(2)}) collective-permute-start(bf16[144,1152]{1,0:T(8,128)(2,1)S(1)} %get-tuple-element.121), channel_id=1, source_target_pairs={{0,24},{8,0},{16,8},{24,16},{1,25},{9,1},{17,9},{25,17},{2,26},{10... | collective-permute-start | bytes 995336 | tf_op jit(solution)/shard_map/ppermute | solution.py:199
  622.3 9.2 %collective-permute-start.47 = (bf16[144,1152]{1,0:T(8,128)(2,1)}, bf16[144,1152]{1,0:T(8,128)(2,1)}, u32[]{:S(2)}, u32[]{:S(2)}) collective-permute-start(bf16[144,1152]{1,0:T(8,128)(2,1)} %get-tuple-element.94), channel_id=1, source_target_pairs={{0,8},{8,16},{16,24},{24,0},{1,9},{9,17},{17,25},{25,1},{2,10},{10... | collective-permute-start | bytes 995336 | tf_op jit(solution)/shard_map/ppermute | solution.py:90
  627.2 39.5 %collective-permute-start.48 = (bf16[144,1152]{1,0:T(8,128)(2,1)}, bf16[144,1152]{1,0:T(8,128)(2,1)S(1)}, u32[]{:S(2)}, u32[]{:S(2)}) collective-permute-start(bf16[144,1152]{1,0:T(8,128)(2,1)} %get-tuple-element.94), channel_id=1, source_target_pairs={{0,16},{8,24},{16,0},{24,8},{1,17},{9,25},{17,1},{25,9},{2,18},{10... | collective-permute-start | bytes 995336 | tf_op jit(solution)/shard_map/ppermute | solution.py:90
  627.2 43.9 %collective-permute-start.49 = (bf16[144,1152]{1,0:T(8,128)(2,1)}, bf16[144,1152]{1,0:T(8,128)(2,1)S(1)}, u32[]{:S(2)}, u32[]{:S(2)}) collective-permute-start(bf16[144,1152]{1,0:T(8,128)(2,1)} %get-tuple-element.94), channel_id=1, source_target_pairs={{0,24},{8,0},{16,8},{24,16},{1,25},{9,1},{17,9},{25,17},{2,26},{10... | collective-permute-start | bytes 995336 | tf_op jit(solution)/shard_map/ppermute | solution.py:90
  (69 other events, 543.9 us)
Sparse Core Ops, SparseCore 0:
  10.0 94.3 all-gather.2
  106.2 83.5 all-gather.4
  302.6 100.4 reduce-scatter.1
  516.1 69.0 all-reduce.2
  625.6 81.4 all-reduce.4

commit v6 on v5

--- a/solution.py
+++ b/solution.py
@@ -185,26 +185,38 @@
         return self.kept + self.received.astype(jnp.float32)
 
 
-def reduce_replicas(partial, replicas):
-    span = partial.shape[1] // replicas
-    own = lax.axis_index("rep")
-
-    def piece(values, which):
-        return lax.dynamic_slice_in_dim(values, which % replicas * span, span, 1)
-
-    low = partial.astype(jnp.bfloat16)
-    total = piece(partial, own)
-    for shift in range(1, replicas):
-        pairs = [(at, (at + shift) % replicas) for at in range(replicas)]
-        received = lax.ppermute(piece(low, own + shift), "rep", pairs)
-        total = total + received.astype(jnp.float32)
-    stacked = gather_replicas(total.astype(jnp.bfloat16), replicas)
-    whole = jnp.zeros(partial.shape, jnp.float32)
-    for shift in range(replicas):
-        whole = lax.dynamic_update_slice_in_dim(
-            whole, stacked[shift].astype(jnp.float32), (own - shift) % replicas * span, 1
-        )
-    return whole
+class ReplicaSum:
+    def __init__(self, partial, replicas):
+        self.replicas = replicas
+        self.own = lax.axis_index("rep")
+        self.shape = partial.shape
+        self.span = partial.shape[1] // replicas
+        low = partial.astype(jnp.bfloat16)
+        self.kept = self.piece(partial, self.own)
+        self.received = [
+            self.send(self.piece(low, self.own + shift), shift) for shift in range(1, replicas)
+        ]
+
+    def piece(self, values, which):
+        return lax.dynamic_slice_in_dim(values, which % self.replicas * self.span, self.span, 1)
+
+    def send(self, values, shift):
+        pairs = [(at, (at + shift) % self.replicas) for at in range(self.replicas)]
+        return lax.ppermute(values, "rep", pairs)
+
+    def second(self):
+        total = self.kept
+        for received in self.received:
+            total = total + received.astype(jnp.float32)
+        low = total.astype(jnp.bfloat16)
+        self.received = [low] + [self.send(low, shift) for shift in range(1, self.replicas)]
+
+    def result(self):
+        whole = jnp.zeros(self.shape, jnp.float32)
+        for shift, received in enumerate(self.received):
+            start = (self.own - shift) % self.replicas * self.span
+            whole = lax.dynamic_update_slice_in_dim(whole, received.astype(jnp.float32), start, 1)
+        return whole
 
 
 WINDOW = 256
@@ -535,7 +547,7 @@
     latent_low = swap_halves(latent_in)
     qkv_pieces, order = gather_pieces(qkv_weight)
     full_up = lax.all_gather(up_weight, GROUP, axis=0, tiled=True)
-    out_pieces, _ = gather_pieces(out_weight)
+    full_out = lax.all_gather(out_weight, GROUP, axis=0, tiled=True)
     cotangent_low = swap_halves(cotangent)
     full_qkv = assemble(qkv_pieces, order)
     full_down = lax.all_gather(down_weight, GROUP, axis=0, tiled=True)
@@ -584,7 +596,6 @@
     halves = heads[: len(heads) // 2], heads[len(heads) // 2 :]
     attended_low, log_totals = attend(query, pair_own, pair_other, heads)
     log_rows = log_totals[:, : len(heads)].T[:, None, :]
-    full_out = assemble(out_pieces, order)
     branch_one = matmul(attended_low, full_out) + full_out_bias
     middle = latent + gate_one * branch_one
 
@@ -614,42 +625,47 @@
     d_attended = d_attended.astype(jnp.bfloat16)
     out_scatter = Scatter(out_halves)
     out_bias_grad = jnp.sum(d_branch_one.astype(jnp.float32), axis=0)
+    d_attended, up_scatter.received = tie(d_attended, up_scatter.received)
+    up_scatter.second()
     left = attend_back(query, pair_own, pair_other, d_attended, log_rows, halves[0])
     d_query, d_attended, up_scatter.received, out_scatter.received = tie(
         left[0], d_attended, up_scatter.received, out_scatter.received
     )
-    up_scatter.second()
+    up_scatter.third()
     out_scatter.second()
     right = attend_back(query, pair_own, pair_other, d_attended, log_rows, halves[1])
+    *right, up_scatter.received, out_scatter.received = tie(
+        *right, up_scatter.received, out_scatter.received
+    )
     d_query = join_heads(d_query, right[0], width)
     d_own = join_heads(left[1], right[1], width)
     d_other = permute(join_heads(left[2], right[2], width), core_rule)
     d_own = (d_own + d_other.astype(jnp.float32)).astype(jnp.bfloat16)
     d_projected = jnp.concatenate([d_query, d_own[0], d_own[1]], axis=-1)
 
-    d_projected, up_scatter.received = tie(d_projected, up_scatter.received)
+    up_sum = ReplicaSum(up_scatter.result(), replicas)
+    out_scatter.third()
     d_hidden_one, qkv_halves = product_back(hidden_one, d_projected, full_qkv)
     qkv_scatter = Scatter(qkv_halves)
     column_sums = jnp.sum(d_projected.astype(jnp.float32), axis=0)
-    d_hidden_one, out_scatter.received, down_shard = tie(
-        d_hidden_one, out_scatter.received, down_shard
-    )
-    up_scatter.third()
-    out_scatter.third()
+    d_hidden_one, down_shard, qkv_scatter.received, *up_sum.received = tie(
+        d_hidden_one, down_shard, qkv_scatter.received, *up_sum.received
+    )
     qkv_scatter.second()
+    up_sum.second()
+    down_total = lax.psum(down_shard, "rep")
     d_shift_one = jnp.sum(d_hidden_one, axis=0)
     d_scale_one = jnp.sum(d_hidden_one * normed_one, axis=0)
     latent_grad = d_middle + norm_back(d_hidden_one * (1.0 + scale_one), normed_one, inverse_one)
     latent_grad = swap_halves(latent_grad.astype(jnp.bfloat16)[None]).astype(jnp.float32)
 
-    down_total = lax.psum(down_shard, "rep")
     qkv_scatter.third()
-    up_shard, down_total, qkv_scatter.received = tie(
-        up_scatter.result().astype(jnp.bfloat16), down_total, qkv_scatter.received
-    )
-    up_total = lax.psum(up_shard, "rep")
     late = jnp.concatenate([out_scatter.result(), qkv_scatter.result()], axis=1)
-    late_total = reduce_replicas(late, replicas)
+    late_sum = ReplicaSum(late, replicas)
+    down_total, *late_sum.received = tie(down_total, *late_sum.received)
+    late_sum.second()
+    up_total = up_sum.result()
+    late_total = late_sum.result()
     out_total, qkv_total = late_total[:, :width], late_total[:, width:]
 
     bias_grads = (

time: 725 us -> 644 us (0.89)
  waiting for transfers between devices: 340 us -> 256 us
  starting transfers between devices: 55.8 us -> 67.9 us
    ppermute x37 -> x30, waiting for transfers between devices: 210 us -> 96 us  [permute(): return lax.ppermute(values, GROUP, pairs_by(rule))]
    ppermute x3 -> x12, waiting for transfers between devices: 24.4 us -> 94.4 us  [send(): return lax.ppermute(values, 'rep', pairs)]
    psum x1 -> x0, waiting for transfers between devices: 33.5 us -> none  [per_device(): up_total = lax.psum(up_shard, 'rep')]
    ppermute x6 -> x3, waiting for transfers between devices: 48.4 us -> 15.8 us  [gather_replicas(): stacked.append(lax.ppermute(values, 'rep', pairs))]
    ppermute x4, waiting for transfers between devices: 0.01 us -> 28.5 us  [swap_halves(): received = lax.ppermute(values, GROUP, pairs)]
    psum x1, waiting for transfers between devices: 22.6 us -> 0.01 us  [per_device(): down_total = lax.psum(down_shard, 'rep')]
    all_gather x1, waiting for transfers between devices: 0.01 us -> 19.7 us  [per_device(): full_down = lax.all_gather(down_weight, GROUP, axis=0, tiled=True)]
    ppermute x3 -> x12, starting transfers between devices: 2.49 us -> 12 us  [send(): return lax.ppermute(values, 'rep', pairs)]
  transfers between devices with their start and end apart: 55 -> 54, of which waited for: 27 -> 24; matrix products, arithmetic and copies ran while one was open for 17% -> 19% of each run, Pallas kernels for 15% -> 17%
where the time goes in v6:
time: 644 us; the launch traced here: 637 us
  waiting for transfers between devices  256 us (40%)
  Pallas kernels  155 us (24%)
  other arithmetic  77.8 us (12%)
  starting transfers between devices  67.9 us (11%)
  local copies, waits for them, and re-layouts  45.7 us (7%)
  matrix products  18.1 us (3%)
  between operations  16.2 us (3%)
    ppermute x30, waiting for transfers between devices, permute(): return lax.ppermute(values, GROUP, pairs_by(rule))  96 us
    ppermute x12, waiting for transfers between devices, send(): return lax.ppermute(values, 'rep', pairs)  94.4 us
    pallas_call x2, Pallas kernels, attend_back(): pl.pallas_call(functools.partial(attend_back_kernel, heads[0], low), grid...  49.3 us
    pallas_call x1, Pallas kernels, mlp(): pl.pallas_call(mlp_kernel, grid=(units // block,), out_shape=(jax.ShapeDt...  47.4 us
    ppermute x30, starting transfers between devices, permute(): return lax.ppermute(values, GROUP, pairs_by(rule))  40.4 us
    ppermute x4, waiting for transfers between devices, swap_halves(): received = lax.ppermute(values, GROUP, pairs)  28.5 us
    pallas_call x1, Pallas kernels, attend(): pl.pallas_call(functools.partial(attend_kernel, heads[0], low), grid=(len...  27.5 us
    pallas_call x2, Pallas kernels, product_back(): pl.pallas_call(product_back_kernel, grid=(columns // block,), out_shape=(...  25.5 us
  transfers between devices with their start and end apart: 54, of which 24 were waited for; matrix products, arithmetic and copies ran while one was open for 19% of the time, Pallas kernels for 17%

profile of v6, /device:TPU:9, one launch (start us, length us, event | category | flops | bytes accessed | tf_op | source)
XLA Modules:
  0.0 636.8 jit_solution(14200085022489912382)
XLA Ops:
  20.6 30.1 %collective-permute-done.2 = bf16[4,2432]{1,0:T(4,128)(2,1)S(1)} collective-permute-done((bf16[4,2432]{1,0:T(4,128)(2,1)S(1)}, bf16[4,2432]{1,0:T(4,128)(2,1)S(1)}, u32[]{:S(2)}, u32[]{:S(2)}) %collective-permute-start.2) | collective-permute-done | bytes 19488 | tf_op jit(solution)/shard_map/ppermute | solution.py:62
  52.1 2.2 collective-permute-done.4
  56.8 10.4 %collective-permute-done.5 = f32[1,6912]{1,0:T(1,128)S(1)} collective-permute-done((f32[1,6912]{1,0:T(1,128)S(1)}, f32[1,6912]{1,0:T(1,128)S(1)}, u32[]{:S(2)}, u32[]{:S(2)}) %collective-permute-start.5) | collective-permute-done | bytes 27680 | tf_op jit(solution)/shard_map/ppermute | solution.py:62
  71.0 6.8 %collective-permute-done.9.refs_3_ = bf16[144,3456]{1,0:T(8,128)(2,1)S(1)} collective-permute-done((bf16[144,3456]{1,0:T(8,128)(2,1)}, bf16[144,3456]{1,0:T(8,128)(2,1)S(1)}, u32[]{:S(2)}, u32[]{:S(2)}) %collective-permute-start.9) | collective-permute-done | bytes 995360 | tf_op jit(solution)/shard_map/ppermute | solution.py:62
  77.8 10.3 %collective-permute-start.13 = (bf16[144,3456]{1,0:T(8,128)(2,1)S(1)}, bf16[144,3456]{1,0:T(8,128)(2,1)S(1)}, u32[]{:S(2)}, u32[]{:S(2)}) collective-permute-start(bf16[144,3456]{1,0:T(8,128)(2,1)S(1)} %collective-permute-done.9.refs_3_), channel_id=1, source_target_pairs={{0,2},{1,3},{2,0},{3,1},{4,6},{5,7},{6,4},{7,5},{8,10},{9,11},{10,... | collective-permute-start | bytes 2985992 | tf_op jit(solution)/shard_map/ppermute | solution.py:62
  90.3 4.9 shard_map.237.weight_ref
  95.3 5.1 add_convert_fusion.2
  103.4 3.2 collective-permute-start.15
  108.0 28.5 %collective-permute-done.15 = bf16[1,512,1152]{2,1,0:T(8,128)(2,1)} collective-permute-done((bf16[1,512,1152]{2,1,0:T(8,128)(2,1)S(1)}, bf16[1,512,1152]{2,1,0:T(8,128)(2,1)}, u32[]{:S(2)}, u32[]{:S(2)}) %collective-permute-start.15) | collective-permute-done | bytes 1179680 | tf_op jit(solution)/shard_map/ppermute | solution.py:68
  136.5 4.5 convert_reduce_fusion.2
  142.4 27.5 %shard_map.238 = (bf16[512,1152]{1,0:T(8,128)(2,1)S(1)}, f32[512,128]{1,0:T(8,128)S(1)}) custom-call(bf16[512,1152]{1,0:T(8,128)(2,1)S(1)} %slice.226.query_ref, bf16[512,2304]{1,0:T(8,128)(2,1)} %slice.227.own_ref, bf16[512,2304]{1,0:T(8,128)(2,1)} %collective-permute-done.14.other_ref), custom_call_target="tpu_custom_call" | custom-call | flops 1048576 | bytes 1048576 | tf_op jit(solution)/shard_map/pallas_call | solution.py:293
  171.6 5.7 fusion.50
  180.2 19.7 %all-gather.8.cloned.1.call-done.down_ref = bf16[4608,1152]{1,0:T(8,128)(2,1)} async-done(((bf16[576,1152]{1,0:T(8,128)(2,1)}), bf16[4608,1152]{1,0:T(8,128)(2,1)}) %all-gather.8.cloned.1.call-update) | async-done | bytes 10616848 | tf_op jit(solution)/shard_map/all_gather | solution.py:553
  199.9 47.4 %shard_map.239 = (f32[512,1152]{1,0:T(8,128)}, f32[512,1152]{1,0:T(8,128)}, bf16[4,144,4608]{2,1,0:T(8,128)(2,1)}, bf16[4,144,4608]{2,1,0:T(8,128)(2,1)}, bf16[4608,1152]{1,0:T(8,128)(2,1)}, /*index=5*/f32[1,4608]{1,0:T(1,128)}) custom-call(bf16[512,1152]{1,0:T(8,128)(2,1)} %add_convert_fusion.4.hidden_ref, ...), custom_call_target="tpu_custom_call" | custom-call | flops 1048576 | bytes 1048576 | tf_op jit(solution)/shard_map/pallas_call | solution.py:495
  247.7 4.1 multiply_reduce_fusion
  251.8 6.5 %fusion.21 = (f32[1152]{0:T(1024)}, bf16[1,512,1152]{2,1,0:T(8,128)(2,1)}, f32[1152]{0:T(1024)}, bf16[512,1152]{1,0:T(8,128)(2,1)S(1)}, f32[512,1152]{1,0:T(8,128)}) fusion(bf16[1,512,1152]{2,1,0:T(8,128)(2,1)S(1)} %copy-done.28, f32[512,1152]{1,0:T(8,128)} %get-tuple-element.55, f32[1152]{0:T(1024)S(1)} %reshape.147, f32[]{:T(128)} %bitcast.1, ...), kind=kLoop, calls=%fused_computation.43 | loop fusion | flops 12384000 | bytes 13011972 | tf_op jit(solution)/shard_map/reduce_sum | solution.py:615
  258.3 7.0 %shard_map.240 = (f32[512,1152]{1,0:T(8,128)S(1)}, bf16[4,144,1152]{2,1,0:T(8,128)(2,1)S(1)}, bf16[4,144,1152]{2,1,0:T(8,128)(2,1)}) custom-call(bf16[512,1152]{1,0:T(8,128)(2,1)S(1)} %copy-done.12, bf16[512,1152]{1,0:T(8,128)(2,1)S(1)} %get-tuple-element.138.upstream_ref, bf16[1152,1152]{1,0:T(8,128)(2,1)S(1)} %copy-done.10), custom_call_target="tpu_custom_call" | custom-call | flops 1048576 | bytes 1048576 | tf_op jit(solution)/shard_map/pallas_call | solution.py:435
  266.6 5.4 add_convert_fusion
  280.6 25.2 %shard_map.241 = (bf16[512,640]{1,0:T(8,128)(2,1)}, f32[2,512,640]{2,1,0:T(8,128)}, bf16[2,512,640]{2,1,0:T(8,128)(2,1)}) custom-call(bf16[512,1152]{1,0:T(8,128)(2,1)} %copy-done.3, bf16[512,2304]{1,0:T(8,128)(2,1)} %slice.227.own_ref, bf16[512,2304]{1,0:T(8,128)(2,1)} %collective-permute-done.14.other_ref, ...), custom_call_target="tpu_custom_call" | custom-call | flops 1048576 | bytes 1048576 | tf_op jit(solution)/shard_map/pallas_call | solution.py:365
  305.8 22.6 %collective-permute-done.18 = bf16[2,144,4608]{2,1,0:T(8,128)(2,1)} collective-permute-done((bf16[2,144,4608]{2,1,0:T(8,128)(2,1)}, bf16[2,144,4608]{2,1,0:T(8,128)(2,1)}, u32[]{:S(2)}, u32[]{:S(2)}) %collective-permute-start.18) | collective-permute-done | bytes 2654240 | tf_op jit(solution)/shard_map/ppermute | solution.py:62
  328.4 2.6 convert_add_fusion
  336.6 24.1 %shard_map.242 = (bf16[512,640]{1,0:T(8,128)(2,1)}, f32[2,512,640]{2,1,0:T(8,128)}, bf16[2,512,640]{2,1,0:T(8,128)(2,1)}) custom-call(bf16[512,1152]{1,0:T(8,128)(2,1)} %copy-done.3, bf16[512,2304]{1,0:T(8,128)(2,1)} %slice.227.own_ref, bf16[512,2304]{1,0:T(8,128)(2,1)} %collective-permute-done.14.other_ref, ...), custom_call_target="tpu_custom_call" | custom-call | flops 1048576 | bytes 1048576 | tf_op jit(solution)/shard_map/pallas_call | solution.py:365
  360.6 9.7 %collective-permute-done.20 = bf16[144,4608]{1,0:T(8,128)(2,1)S(1)} collective-permute-done((bf16[144,4608]{1,0:T(8,128)(2,1)S(1)}, bf16[144,4608]{1,0:T(8,128)(2,1)S(1)}, u32[]{:S(2)}, u32[]{:S(2)}) %collective-permute-start.20) | collective-permute-done | bytes 1327136 | tf_op jit(solution)/shard_map/ppermute | solution.py:62
  374.7 3.0 collective-permute-start.22
  385.6 2.6 fusion
  389.4 3.3 copy-done.2
  392.7 18.4 %shard_map.243 = (f32[512,1152]{1,0:T(8,128)S(1)}, bf16[4,144,3456]{2,1,0:T(8,128)(2,1)S(1)}, bf16[4,144,3456]{2,1,0:T(8,128)(2,1)S(1)}) custom-call(bf16[512,1152]{1,0:T(8,128)(2,1)S(1)} %copy-done.7, bf16[512,3456]{1,0:T(8,128)(2,1)S(1)} %fusion.26.upstream_ref, bf16[1152,3456]{1,0:T(8,128)(2,1)S(1)} %copy-done.2), custom_call_target="tpu_custom_call" | custom-call | flops 1048576 | bytes 1048576 | tf_op jit(solution)/shard_map/pallas_call | solution.py:435
  413.1 3.4 broadcast_select_fusion
  426.2 4.8 collective-permute-done.24
  431.0 20.4 %collective-permute-done.25 = bf16[144,1152]{1,0:T(8,128)(2,1)S(1)} collective-permute-done((bf16[144,1152]{1,0:T(8,128)(2,1)S(1)}, bf16[144,1152]{1,0:T(8,128)(2,1)S(1)}, u32[]{:S(2)}, u32[]{:S(2)}) %collective-permute-start.25) | collective-permute-done | bytes 331808 | tf_op jit(solution)/shard_map/ppermute | solution.py:205
  451.3 2.7 collective-permute-done.26
  456.6 2.5 convert_dynamic-update-slice_fusion.3
  465.0 3.2 add_convert_fusion.1
  477.3 22.6 %collective-permute-done.47 = bf16[144,1152]{1,0:T(8,128)(2,1)S(1)} collective-permute-done((bf16[144,1152]{1,0:T(8,128)(2,1)}, bf16[144,1152]{1,0:T(8,128)(2,1)S(1)}, u32[]{:S(2)}, u32[]{:S(2)}) %collective-permute-start.47) | collective-permute-done | bytes 331808 | tf_op jit(solution)/shard_map/ppermute | solution.py:205
  504.8 2.8 collective-permute-done.31
  507.6 5.5 collective-permute-start.32
  513.8 3.5 collective-permute-start.35
  521.7 3.1 collective-permute-start.27
  525.7 6.1 collective-permute-done.35
  531.8 9.8 %collective-permute-done.36 = f32[29376]{0:T(1024)} collective-permute-done((f32[29376]{0:T(1024)S(1)}, f32[29376]{0:T(1024)}, u32[]{:S(2)}, u32[]{:S(2)}) %collective-permute-start.36) | collective-permute-done | bytes 117536 | tf_op jit(solution)/shard_map/ppermute | solution.py:90
  542.6 2.5 convert_add_fusion.1
  554.7 7.1 %collective-permute-done.39 = bf16[144,3456]{1,0:T(8,128)(2,1)} collective-permute-done((bf16[144,3456]{1,0:T(8,128)(2,1)}, bf16[144,3456]{1,0:T(8,128)(2,1)}, u32[]{:S(2)}, u32[]{:S(2)}) %collective-permute-start.39) | collective-permute-done | bytes 995360 | tf_op jit(solution)/shard_map/ppermute | solution.py:62
  567.2 5.2 fusion.54
  573.5 19.4 %collective-permute-done.41 = bf16[144,1152]{1,0:T(8,128)(2,1)} collective-permute-done((bf16[144,1152]{1,0:T(8,128)(2,1)}, bf16[144,1152]{1,0:T(8,128)(2,1)}, u32[]{:S(2)}, u32[]{:S(2)}) %collective-permute-start.41) | collective-permute-done | bytes 331808 | tf_op jit(solution)/shard_map/ppermute | solution.py:205
  594.7 2.9 select_convert_fusion
  597.7 3.1 collective-permute-start.44
  603.9 18.8 %collective-permute-done.44 = bf16[144,1152]{1,0:T(8,128)(2,1)S(1)} collective-permute-done((bf16[144,1152]{1,0:T(8,128)(2,1)S(1)}, bf16[144,1152]{1,0:T(8,128)(2,1)S(1)}, u32[]{:S(2)}, u32[]{:S(2)}) %collective-permute-start.44) | collective-permute-done | bytes 331808 | tf_op jit(solution)/shard_map/ppermute | solution.py:205
  622.7 4.7 collective-permute-done.45
  (352 shorter events, 125.8 us)
Async XLA Ops:
  7.3 164.3 %all-gather.4.cloned.1.call-start = ((), (), s32[]{:S(2)}) async-start(), calls=%async_computation.1 | async-start | bytes 2985984 | tf_op jit(solution)/shard_map/all_gather | solution.py:550
  8.0 172.2 %all-gather.6.cloned.1.call-start = ((), (), s32[]{:S(2)}) async-start(), calls=%async_computation.2 | async-start | bytes 11943936 | tf_op jit(solution)/shard_map/all_gather | solution.py:549
  8.8 191.1 %all-gather.8.cloned.1.call-start = ((), (), s32[]{:S(2)}) async-start(), calls=%async_computation.3 | async-start | bytes 11943936 | tf_op jit(solution)/shard_map/all_gather | solution.py:553
  9.5 445.3 %reduce-scatter.2.cloned.1.call-start = ((), (), s32[]{:S(2)}) async-start(), calls=%async_computation.4 | async-start | bytes 11943936 | tf_op jit(solution)/shard_map/reduce_scatter | solution.py:611
  13.0 7.0 %collective-permute-start.1 = (bf16[2,2432]{1,0:T(2,128)(2,1)S(1)}, bf16[2,2432]{1,0:T(2,128)(2,1)S(1)}, u32[]{:S(2)}, u32[]{:S(2)}) collective-permute-start(bf16[2,2432]{1,0:T(2,128)(2,1)S(1)} %broadcast_select_fusion.6), channel_id=1, source_target_pairs={{0,2},{1,3},{2,0},{3,1},{4,6},{5,7},{6,4},{7,5},{8,10},{9,11},{10,... | collective-permute-start | bytes 29192 | tf_op jit(solution)/shard_map/ppermute | solution.py:62
  14.9 40.4 %collective-permute-start.7 = (bf16[144,3456]{1,0:T(8,128)(2,1)S(1)}, bf16[144,3456]{1,0:T(8,128)(2,1)}, u32[]{:S(2)}, u32[]{:S(2)}) collective-permute-start(bf16[144,3456]{1,0:T(8,128)(2,1)S(1)} %copy-done.13), channel_id=1, source_target_pairs={{0,4},{1,5},{2,3},{3,2},{4,0},{5,1},{6,7},{7,6},{8,12},{9,13},{10,... | collective-permute-start | bytes 2985992 | tf_op jit(solution)/shard_map/ppermute | solution.py:62
  16.1 52.8 %collective-permute-start.8 = (bf16[144,3456]{1,0:T(8,128)(2,1)S(1)}, bf16[144,3456]{1,0:T(8,128)(2,1)}, u32[]{:S(2)}, u32[]{:S(2)}) collective-permute-start(bf16[144,3456]{1,0:T(8,128)(2,1)S(1)} %copy-done.13), channel_id=1, source_target_pairs={{0,1},{1,0},{2,6},{3,7},{4,5},{5,4},{6,2},{7,3},{8,9},{9,8},{10,14... | collective-permute-start | bytes 2985992 | tf_op jit(solution)/shard_map/ppermute | solution.py:62
  17.4 71.8 %collective-permute-start.10 = (bf16[144,3456]{1,0:T(8,128)(2,1)S(1)}, bf16[144,3456]{1,0:T(8,128)(2,1)}, u32[]{:S(2)}, u32[]{:S(2)}) collective-permute-start(bf16[144,3456]{1,0:T(8,128)(2,1)S(1)} %copy-done.13), channel_id=1, source_target_pairs={{0,2},{1,3},{2,0},{3,1},{4,6},{5,7},{6,4},{7,5},{8,10},{9,11},{10,... | collective-permute-start | bytes 2985992 | tf_op jit(solution)/shard_map/ppermute | solution.py:62
  18.0 51.3 %collective-permute-start.3 = (bf16[1,512,1152]{2,1,0:T(8,128)(2,1)}, bf16[1,512,1152]{2,1,0:T(8,128)(2,1)}, u32[]{:S(2)}, u32[]{:S(2)}) collective-permute-start(bf16[1,512,1152]{2,1,0:T(8,128)(2,1)} %param.14), channel_id=1, source_target_pairs={{1,2},{2,1},{5,6},{6,5},{9,10},{10,9},{13,14},{14,13},{17,18},{18,... | collective-permute-start | bytes 3538952 | tf_op jit(solution)/shard_map/ppermute | solution.py:68
  20.1 30.6 %collective-permute-start.2 = (bf16[4,2432]{1,0:T(4,128)(2,1)S(1)}, bf16[4,2432]{1,0:T(4,128)(2,1)S(1)}, u32[]{:S(2)}, u32[]{:S(2)}) collective-permute-start(bf16[4,2432]{1,0:T(4,128)(2,1)S(1)} %maximum_select_fusion.4), channel_id=1, source_target_pairs={{0,4},{1,5},{2,6},{3,7},{4,0},{5,1},{6,2},{7,3},{8,12},{9,13},{10,... | collective-permute-start | bytes 58376 | tf_op jit(solution)/shard_map/ppermute | solution.py:62
  54.4 12.8 %collective-permute-start.5 = (f32[1,6912]{1,0:T(1,128)S(1)}, f32[1,6912]{1,0:T(1,128)S(1)}, u32[]{:S(2)}, u32[]{:S(2)}) collective-permute-start(f32[1,6912]{1,0:T(1,128)S(1)} %broadcast_select_fusion.4), channel_id=1, source_target_pairs={{0,1},{1,0},{2,3},{3,2},{4,5},{5,4},{6,7},{7,6},{8,9},{9,8},{10,11... | collective-permute-start | bytes 82952 | tf_op jit(solution)/shard_map/ppermute | solution.py:62
  55.3 22.5 %collective-permute-start.9 = (bf16[144,3456]{1,0:T(8,128)(2,1)}, bf16[144,3456]{1,0:T(8,128)(2,1)S(1)}, u32[]{:S(2)}, u32[]{:S(2)}) collective-permute-start(bf16[144,3456]{1,0:T(8,128)(2,1)} %collective-permute-done.7.refs_1_), channel_id=1, source_target_pairs={{0,1},{1,0},{2,6},{3,7},{4,5},{5,4},{6,2},{7,3},{8,9},{9,8},{10,14... | collective-permute-start | bytes 2985992 | tf_op jit(solution)/shard_map/ppermute | solution.py:62
  68.7 20.4 %collective-permute-start.11 = (bf16[144,3456]{1,0:T(8,128)(2,1)}, bf16[144,3456]{1,0:T(8,128)(2,1)S(1)}, u32[]{:S(2)}, u32[]{:S(2)}) collective-permute-start(bf16[144,3456]{1,0:T(8,128)(2,1)} %collective-permute-done.7.refs_1_), channel_id=1, source_target_pairs={{0,2},{1,3},{2,0},{3,1},{4,6},{5,7},{6,4},{7,5},{8,10},{9,11},{10,... | collective-permute-start | bytes 2985992 | tf_op jit(solution)/shard_map/ppermute | solution.py:62
  68.9 20.2 %collective-permute-start.12 = (bf16[144,3456]{1,0:T(8,128)(2,1)}, bf16[144,3456]{1,0:T(8,128)(2,1)S(1)}, u32[]{:S(2)}, u32[]{:S(2)}) collective-permute-start(bf16[144,3456]{1,0:T(8,128)(2,1)} %collective-permute-done.8.refs_2_), channel_id=1, source_target_pairs={{0,2},{1,3},{2,0},{3,1},{4,6},{5,7},{6,4},{7,5},{8,10},{9,11},{10,... | collective-permute-start | bytes 2985992 | tf_op jit(solution)/shard_map/ppermute | solution.py:62
  77.8 12.5 %collective-permute-start.13 = (bf16[144,3456]{1,0:T(8,128)(2,1)S(1)}, bf16[144,3456]{1,0:T(8,128)(2,1)S(1)}, u32[]{:S(2)}, u32[]{:S(2)}) collective-permute-start(bf16[144,3456]{1,0:T(8,128)(2,1)S(1)} %collective-permute-done.9.refs_3_), channel_id=1, source_target_pairs={{0,2},{1,3},{2,0},{3,1},{4,6},{5,7},{6,4},{7,5},{8,10},{9,11},{10,... | collective-permute-start | bytes 2985992 | tf_op jit(solution)/shard_map/ppermute | solution.py:62
  103.0 39.4 %collective-permute-start.14 = (bf16[512,2304]{1,0:T(8,128)(2,1)}, bf16[512,2304]{1,0:T(8,128)(2,1)}, u32[]{:S(2)}, u32[]{:S(2)}) collective-permute-start(bf16[512,2304]{1,0:T(8,128)(2,1)} %slice.227.own_ref), channel_id=1, source_target_pairs={{0,2},{1,3},{2,0},{3,1},{4,6},{5,7},{6,4},{7,5},{8,10},{9,11},{10,... | collective-permute-start | bytes 7077896 | tf_op jit(solution)/shard_map/ppermute | solution.py:62
  103.4 33.1 %collective-permute-start.15 = (bf16[1,512,1152]{2,1,0:T(8,128)(2,1)S(1)}, bf16[1,512,1152]{2,1,0:T(8,128)(2,1)}, u32[]{:S(2)}, u32[]{:S(2)}) collective-permute-start(bf16[1,512,1152]{2,1,0:T(8,128)(2,1)S(1)} %copy-done.39), channel_id=1, source_target_pairs={{1,2},{2,1},{5,6},{6,5},{9,10},{10,9},{13,14},{14,13},{17,18},{18,... | collective-permute-start | bytes 3538952 | tf_op jit(solution)/shard_map/ppermute | solution.py:68
  247.2 19.4 %collective-permute-start.17 = (bf16[4,144,4608]{2,1,0:T(8,128)(2,1)}, bf16[4,144,4608]{2,1,0:T(8,128)(2,1)}, u32[]{:S(2)}, u32[]{:S(2)}) collective-permute-start(bf16[4,144,4608]{2,1,0:T(8,128)(2,1)} %get-tuple-element.58), channel_id=1, source_target_pairs={{0,2},{1,3},{2,0},{3,1},{4,6},{5,7},{6,4},{7,5},{8,10},{9,11},{10,... | collective-permute-start | bytes 15925256 | tf_op jit(solution)/shard_map/ppermute | solution.py:62
  266.5 305.9 %all-reduce.2.cloned.1.call-start = ((), (), s32[]{:S(2)}) async-start(), calls=%async_computation.5 | async-start | bytes 2654208 | tf_op jit(solution)/shard_map/psum | solution.py:656
  275.9 52.6 %collective-permute-start.18 = (bf16[2,144,4608]{2,1,0:T(8,128)(2,1)}, bf16[2,144,4608]{2,1,0:T(8,128)(2,1)}, u32[]{:S(2)}, u32[]{:S(2)}) collective-permute-start(bf16[2,144,4608]{2,1,0:T(8,128)(2,1)} %pad_maximum_fusion.1), channel_id=1, source_target_pairs={{0,4},{1,5},{2,3},{3,2},{4,0},{5,1},{6,7},{7,6},{8,12},{9,13},{10,... | collective-permute-start | bytes 7962632 | tf_op jit(solution)/shard_map/ppermute | solution.py:62
  276.4 29.4 %collective-permute-start.19 = (bf16[4,144,1152]{2,1,0:T(8,128)(2,1)}, bf16[4,144,1152]{2,1,0:T(8,128)(2,1)}, u32[]{:S(2)}, u32[]{:S(2)}) collective-permute-start(bf16[4,144,1152]{2,1,0:T(8,128)(2,1)} %get-tuple-element.64), channel_id=1, source_target_pairs={{0,2},{1,3},{2,0},{3,1},{4,6},{5,7},{6,4},{7,5},{8,10},{9,11},{10,... | collective-permute-start | bytes 3981320 | tf_op jit(solution)/shard_map/ppermute | solution.py:62
  331.2 39.1 %collective-permute-start.20 = (bf16[144,4608]{1,0:T(8,128)(2,1)S(1)}, bf16[144,4608]{1,0:T(8,128)(2,1)S(1)}, u32[]{:S(2)}, u32[]{:S(2)}) collective-permute-start(bf16[144,4608]{1,0:T(8,128)(2,1)S(1)} %fusion.23), channel_id=1, source_target_pairs={{0,1},{1,0},{2,6},{3,7},{4,5},{5,4},{6,2},{7,3},{8,9},{9,8},{10,14... | collective-permute-start | bytes 3981320 | tf_op jit(solution)/shard_map/ppermute | solution.py:62
  335.6 25.1 %collective-permute-start.21 = (bf16[2,144,1152]{2,1,0:T(8,128)(2,1)S(1)}, bf16[2,144,1152]{2,1,0:T(8,128)(2,1)}, u32[]{:S(2)}, u32[]{:S(2)}) collective-permute-start(bf16[2,144,1152]{2,1,0:T(8,128)(2,1)S(1)} %pad_maximum_fusion.4), channel_id=1, source_target_pairs={{0,4},{1,5},{2,3},{3,2},{4,0},{5,1},{6,7},{7,6},{8,12},{9,13},{10,... | collective-permute-start | bytes 1990664 | tf_op jit(solution)/shard_map/ppermute | solution.py:62
  374.7 10.8 %collective-permute-start.22 = (bf16[2,512,1152]{2,1,0:T(8,128)(2,1)}, bf16[2,512,1152]{2,1,0:T(8,128)(2,1)}, u32[]{:S(2)}, u32[]{:S(2)}) collective-permute-start(bf16[2,512,1152]{2,1,0:T(8,128)(2,1)} %pad_maximum_fusion.2), channel_id=1, source_target_pairs={{0,2},{1,3},{2,0},{3,1},{4,6},{5,7},{6,4},{7,5},{8,10},{9,11},{10,... | collective-permute-start | bytes 7077896 | tf_op jit(solution)/shard_map/ppermute | solution.py:62
  377.7 35.4 %collective-permute-start.16 = (bf16[1,512,1152]{2,1,0:T(8,128)(2,1)S(1)}, bf16[1,512,1152]{2,1,0:T(8,128)(2,1)}, u32[]{:S(2)}, u32[]{:S(2)}) collective-permute-start(bf16[1,512,1152]{2,1,0:T(8,128)(2,1)S(1)} %copy-done.27), channel_id=1, source_target_pairs={{1,2},{2,1},{5,6},{6,5},{9,10},{10,9},{13,14},{14,13},{17,18},{18,... | collective-permute-start | bytes 3538952 | tf_op jit(solution)/shard_map/ppermute | solution.py:68
  413.1 41.7 %collective-permute-start.23 = (bf16[4,144,3456]{2,1,0:T(8,128)(2,1)S(1)}, bf16[4,144,3456]{2,1,0:T(8,128)(2,1)}, u32[]{:S(2)}, u32[]{:S(2)}) collective-permute-start(bf16[4,144,3456]{2,1,0:T(8,128)(2,1)S(1)} %get-tuple-element.80), channel_id=1, source_target_pairs={{0,2},{1,3},{2,0},{3,1},{4,6},{5,7},{6,4},{7,5},{8,10},{9,11},{10,... | collective-permute-start | bytes 11943944 | tf_op jit(solution)/shard_map/ppermute | solution.py:62
  417.9 7.5 %collective-permute-start.37 = (bf16[144,1152]{1,0:T(8,128)(2,1)S(1)}, bf16[144,1152]{1,0:T(8,128)(2,1)S(1)}, u32[]{:S(2)}, u32[]{:S(2)}) collective-permute-start(bf16[144,1152]{1,0:T(8,128)(2,1)S(1)} %fusion.35), channel_id=1, source_target_pairs={{0,1},{1,0},{2,6},{3,7},{4,5},{5,4},{6,2},{7,3},{8,9},{9,8},{10,14... | collective-permute-start | bytes 995336 | tf_op jit(solution)/shard_map/ppermute | solution.py:62
  421.8 9.1 %collective-permute-start.24 = (bf16[144,1152]{1,0:T(8,128)(2,1)S(1)}, bf16[144,1152]{1,0:T(8,128)(2,1)S(1)}, u32[]{:S(2)}, u32[]{:S(2)}) collective-permute-start(bf16[144,1152]{1,0:T(8,128)(2,1)S(1)} %get-tuple-element.151), channel_id=1, source_target_pairs={{0,8},{8,16},{16,24},{24,0},{1,9},{9,17},{17,25},{25,1},{2,10},{10... | collective-permute-start | bytes 995336 | tf_op jit(solution)/shard_map/ppermute | solution.py:205
  423.1 28.2 %collective-permute-start.25 = (bf16[144,1152]{1,0:T(8,128)(2,1)S(1)}, bf16[144,1152]{1,0:T(8,128)(2,1)S(1)}, u32[]{:S(2)}, u32[]{:S(2)}) collective-permute-start(bf16[144,1152]{1,0:T(8,128)(2,1)S(1)} %get-tuple-element.150), channel_id=1, source_target_pairs={{0,16},{8,24},{16,0},{24,8},{1,17},{9,25},{17,1},{25,9},{2,18},{10... | collective-permute-start | bytes 995336 | tf_op jit(solution)/shard_map/ppermute | solution.py:205
  424.7 29.3 %collective-permute-start.26 = (bf16[144,1152]{1,0:T(8,128)(2,1)S(1)}, bf16[144,1152]{1,0:T(8,128)(2,1)S(1)}, u32[]{:S(2)}, u32[]{:S(2)}) collective-permute-start(bf16[144,1152]{1,0:T(8,128)(2,1)S(1)} %get-tuple-element.149), channel_id=1, source_target_pairs={{0,24},{8,0},{16,8},{24,16},{1,25},{9,1},{17,9},{25,17},{2,26},{10... | collective-permute-start | bytes 995336 | tf_op jit(solution)/shard_map/ppermute | solution.py:205
  459.1 17.4 %collective-permute-start.46 = (bf16[144,1152]{1,0:T(8,128)(2,1)}, bf16[144,1152]{1,0:T(8,128)(2,1)S(1)}, u32[]{:S(2)}, u32[]{:S(2)}) collective-permute-start(bf16[144,1152]{1,0:T(8,128)(2,1)} %get-tuple-element.112), channel_id=1, source_target_pairs={{0,8},{8,16},{16,24},{24,0},{1,9},{9,17},{17,25},{25,1},{2,10},{10... | collective-permute-start | bytes 995336 | tf_op jit(solution)/shard_map/ppermute | solution.py:205
  459.1 40.8 %collective-permute-start.47 = (bf16[144,1152]{1,0:T(8,128)(2,1)}, bf16[144,1152]{1,0:T(8,128)(2,1)S(1)}, u32[]{:S(2)}, u32[]{:S(2)}) collective-permute-start(bf16[144,1152]{1,0:T(8,128)(2,1)} %get-tuple-element.112), channel_id=1, source_target_pairs={{0,16},{8,24},{16,0},{24,8},{1,17},{9,25},{17,1},{25,9},{2,18},{10... | collective-permute-start | bytes 995336 | tf_op jit(solution)/shard_map/ppermute | solution.py:205
  459.6 59.1 %collective-permute-start.48 = (bf16[144,1152]{1,0:T(8,128)(2,1)}, bf16[144,1152]{1,0:T(8,128)(2,1)}, u32[]{:S(2)}, u32[]{:S(2)}) collective-permute-start(bf16[144,1152]{1,0:T(8,128)(2,1)} %get-tuple-element.112), channel_id=1, source_target_pairs={{0,24},{8,0},{16,8},{24,16},{1,25},{9,1},{17,9},{25,17},{2,26},{10... | collective-permute-start | bytes 995336 | tf_op jit(solution)/shard_map/ppermute | solution.py:205
  464.8 5.2 collective-permute-start.28
  473.6 69.0 %collective-permute-start.38 = (bf16[2,144,3456]{2,1,0:T(8,128)(2,1)}, bf16[2,144,3456]{2,1,0:T(8,128)(2,1)}, u32[]{:S(2)}, u32[]{:S(2)}) collective-permute-start(bf16[2,144,3456]{2,1,0:T(8,128)(2,1)} %pad_maximum_fusion.3), channel_id=1, source_target_pairs={{0,4},{1,5},{2,3},{3,2},{4,0},{5,1},{6,7},{7,6},{8,12},{9,13},{10,... | collective-permute-start | bytes 5971976 | tf_op jit(solution)/shard_map/ppermute | solution.py:62
  476.3 24.5 %collective-permute-start.30 = (f32[4,16128]{1,0:T(4,128)S(1)}, f32[4,16128]{1,0:T(4,128)S(1)}, u32[]{:S(2)}, u32[]{:S(2)}) collective-permute-start(f32[4,16128]{1,0:T(4,128)S(1)} %maximum_select_fusion.1), channel_id=1, source_target_pairs={{0,4},{1,5},{2,6},{3,7},{4,0},{5,1},{6,2},{7,3},{8,12},{9,13},{10,... | collective-permute-start | bytes 774152 | tf_op jit(solution)/shard_map/ppermute | solution.py:62
  507.6 9.7 %collective-permute-start.32 = (f32[2,4,144]{2,1,0:T(4,128)S(1)}, f32[2,4,144]{2,1,0:T(4,128)S(1)}, u32[]{:S(2)}, u32[]{:S(2)}) collective-permute-start(f32[2,4,144]{2,1,0:T(4,128)S(1)} %maximum_select_fusion.6), channel_id=1, source_target_pairs={{0,2},{1,3},{2,0},{3,1},{4,6},{5,7},{6,4},{7,5},{8,10},{9,11},{10,... | collective-permute-start | bytes 13832 | tf_op jit(solution)/shard_map/ppermute | solution.py:62
  513.7 11.9 %collective-permute-start.34 = (f32[29376]{0:T(1024)S(1)}, f32[29376]{0:T(1024)S(1)}, u32[]{:S(2)}, u32[]{:S(2)}) collective-permute-start(f32[29376]{0:T(1024)S(1)} %concatenate.123), channel_id=1, source_target_pairs={{0,8},{8,16},{16,24},{24,0},{1,9},{9,17},{17,25},{25,1},{2,10},{10... | collective-permute-start | bytes 352520 | tf_op jit(solution)/shard_map/ppermute | solution.py:90
  513.8 18.0 %collective-permute-start.35 = (f32[29376]{0:T(1024)S(1)}, f32[29376]{0:T(1024)S(1)}, u32[]{:S(2)}, u32[]{:S(2)}) collective-permute-start(f32[29376]{0:T(1024)S(1)} %concatenate.123), channel_id=1, source_target_pairs={{0,16},{8,24},{16,0},{24,8},{1,17},{9,25},{17,1},{25,9},{2,18},{10... | collective-permute-start | bytes 352520 | tf_op jit(solution)/shard_map/ppermute | solution.py:90
  517.3 24.3 %collective-permute-start.36 = (f32[29376]{0:T(1024)S(1)}, f32[29376]{0:T(1024)}, u32[]{:S(2)}, u32[]{:S(2)}) collective-permute-start(f32[29376]{0:T(1024)S(1)} %concatenate.123), channel_id=1, source_target_pairs={{0,24},{8,0},{16,8},{24,16},{1,25},{9,1},{17,9},{25,17},{2,26},{10... | collective-permute-start | bytes 352520 | tf_op jit(solution)/shard_map/ppermute | solution.py:90
  521.7 73.0 %collective-permute-start.27 = (bf16[1,512,1152]{2,1,0:T(8,128)(2,1)}, bf16[1,512,1152]{2,1,0:T(8,128)(2,1)}, u32[]{:S(2)}, u32[]{:S(2)}) collective-permute-start(bf16[1,512,1152]{2,1,0:T(8,128)(2,1)} %get-tuple-element.141), channel_id=1, source_target_pairs={{1,2},{2,1},{5,6},{6,5},{9,10},{10,9},{13,14},{14,13},{17,18},{18,... | collective-permute-start | bytes 3538952 | tf_op jit(solution)/shard_map/ppermute | solution.py:68
  548.1 13.7 %collective-permute-start.39 = (bf16[144,3456]{1,0:T(8,128)(2,1)}, bf16[144,3456]{1,0:T(8,128)(2,1)}, u32[]{:S(2)}, u32[]{:S(2)}) collective-permute-start(bf16[144,3456]{1,0:T(8,128)(2,1)} %fusion.28), channel_id=1, source_target_pairs={{0,1},{1,0},{2,6},{3,7},{4,5},{5,4},{6,2},{7,3},{8,9},{9,8},{10,14... | collective-permute-start | bytes 2985992 | tf_op jit(solution)/shard_map/ppermute | solution.py:62
  565.4 8.1 %collective-permute-start.40 = (bf16[144,1152]{1,0:T(8,128)(2,1)}, bf16[144,1152]{1,0:T(8,128)(2,1)S(1)}, u32[]{:S(2)}, u32[]{:S(2)}) collective-permute-start(bf16[144,1152]{1,0:T(8,128)(2,1)} %get-tuple-element.144), channel_id=1, source_target_pairs={{0,8},{8,16},{16,24},{24,0},{1,9},{9,17},{17,25},{25,1},{2,10},{10... | collective-permute-start | bytes 995336 | tf_op jit(solution)/shard_map/ppermute | solution.py:205
  565.4 27.5 %collective-permute-start.41 = (bf16[144,1152]{1,0:T(8,128)(2,1)}, bf16[144,1152]{1,0:T(8,128)(2,1)}, u32[]{:S(2)}, u32[]{:S(2)}) collective-permute-start(bf16[144,1152]{1,0:T(8,128)(2,1)} %get-tuple-element.143), channel_id=1, source_target_pairs={{0,16},{8,24},{16,0},{24,8},{1,17},{9,25},{17,1},{25,9},{2,18},{10... | collective-permute-start | bytes 995336 | tf_op jit(solution)/shard_map/ppermute | solution.py:205
  565.4 27.5 %collective-permute-start.42 = (bf16[144,1152]{1,0:T(8,128)(2,1)}, bf16[144,1152]{1,0:T(8,128)(2,1)}, u32[]{:S(2)}, u32[]{:S(2)}) collective-permute-start(bf16[144,1152]{1,0:T(8,128)(2,1)} %get-tuple-element.142), channel_id=1, source_target_pairs={{0,24},{8,0},{16,8},{24,16},{1,25},{9,1},{17,9},{25,17},{2,26},{10... | collective-permute-start | bytes 995336 | tf_op jit(solution)/shard_map/ppermute | solution.py:205
  594.7 9.2 %collective-permute-start.43 = (bf16[144,1152]{1,0:T(8,128)(2,1)S(1)}, bf16[144,1152]{1,0:T(8,128)(2,1)S(1)}, u32[]{:S(2)}, u32[]{:S(2)}) collective-permute-start(bf16[144,1152]{1,0:T(8,128)(2,1)S(1)} %get-tuple-element.114), channel_id=1, source_target_pairs={{0,8},{8,16},{16,24},{24,0},{1,9},{9,17},{17,25},{25,1},{2,10},{10... | collective-permute-start | bytes 995336 | tf_op jit(solution)/shard_map/ppermute | solution.py:205
  597.7 25.0 %collective-permute-start.44 = (bf16[144,1152]{1,0:T(8,128)(2,1)S(1)}, bf16[144,1152]{1,0:T(8,128)(2,1)S(1)}, u32[]{:S(2)}, u32[]{:S(2)}) collective-permute-start(bf16[144,1152]{1,0:T(8,128)(2,1)S(1)} %get-tuple-element.114), channel_id=1, source_target_pairs={{0,16},{8,24},{16,0},{24,8},{1,17},{9,25},{17,1},{25,9},{2,18},{10... | collective-permute-start | bytes 995336 | tf_op jit(solution)/shard_map/ppermute | solution.py:205
  600.8 26.6 %collective-permute-start.45 = (bf16[144,1152]{1,0:T(8,128)(2,1)S(1)}, bf16[144,1152]{1,0:T(8,128)(2,1)S(1)}, u32[]{:S(2)}, u32[]{:S(2)}) collective-permute-start(bf16[144,1152]{1,0:T(8,128)(2,1)S(1)} %get-tuple-element.114), channel_id=1, source_target_pairs={{0,24},{8,0},{16,8},{24,16},{1,25},{9,1},{17,9},{25,17},{2,26},{10... | collective-permute-start | bytes 995336 | tf_op jit(solution)/shard_map/ppermute | solution.py:205
  (66 other events, 527.1 us)
Sparse Core Ops, SparseCore 0:
  10.0 42.0 all-gather.3
  54.0 80.2 all-gather.5
  136.1 63.6 all-gather.7
  266.6 106.6 reduce-scatter.1
  475.3 73.7 all-reduce.1

commit v7 on v6

--- a/solution.py
+++ b/solution.py
@@ -91,14 +91,9 @@
     return jnp.stack(stacked)
 
 
-def assemble_kernel(order_ref, *refs):
-    pieces, whole, buffer, load_sems, store_sems = (
-        refs[:SHARDS],
-        refs[SHARDS],
-        refs[SHARDS + 1],
-        refs[SHARDS + 2],
-        refs[SHARDS + 3],
-    )
+def assemble_kernel(widths, order_ref, *refs):
+    pieces, wholes = refs[:SHARDS], refs[SHARDS : SHARDS + len(widths)]
+    buffer, load_sems, store_sems = refs[SHARDS + len(widths) :]
     rows = buffer.shape[1]
     loads = [
         pltpu.make_async_copy(piece, buffer.at[at], load_sems.at[at])
@@ -110,26 +105,35 @@
     for at, load in enumerate(loads):
         load.wait()
         target = pl.ds(pl.multiple_of(order_ref[at] * rows, 16), rows)
-        store = pltpu.make_async_copy(buffer.at[at], whole.at[target], store_sems.at[at])
-        store.start()
-        stores.append(store)
+        start = 0
+        for which, width in enumerate(widths):
+            store = pltpu.make_async_copy(
+                buffer.at[at, :, pl.ds(start, width)],
+                wholes[which].at[target],
+                store_sems.at[which, at],
+            )
+            store.start()
+            stores.append(store)
+            start += width
     for store in stores:
         store.wait()
 
 
-def assemble(pieces, order):
+def assemble(pieces, order, widths):
     rows, columns = pieces[0].shape
     size = SHARDS * rows * columns * 2
     return pl.pallas_call(
-        assemble_kernel,
-        out_shape=jax.ShapeDtypeStruct((SHARDS * rows, columns), pieces[0].dtype),
+        functools.partial(assemble_kernel, widths),
+        out_shape=[
+            jax.ShapeDtypeStruct((SHARDS * rows, width), pieces[0].dtype) for width in widths
+        ],
         in_specs=[pl.BlockSpec(memory_space=pltpu.SMEM)]
         + [pl.BlockSpec(memory_space=pl.ANY)] * SHARDS,
-        out_specs=pl.BlockSpec(memory_space=pl.ANY),
+        out_specs=[pl.BlockSpec(memory_space=pl.ANY)] * len(widths),
         scratch_shapes=[
             pltpu.VMEM((SHARDS, rows, columns), pieces[0].dtype),
             pltpu.SemaphoreType.DMA((SHARDS,)),
-            pltpu.SemaphoreType.DMA((SHARDS,)),
+            pltpu.SemaphoreType.DMA((len(widths), SHARDS)),
         ],
         compiler_params=pltpu.CompilerParams(vmem_limit_bytes=size + (4 << 20)),
         cost_estimate=SHORT,
@@ -415,13 +419,17 @@
                 sent_ref[slot] = low[at * rows : (at + 1) * rows]
 
 
-def product_back_kernel(left_ref, upstream_ref, weight_ref, d_left_ref, kept_ref, sent_ref):
+def product_back_kernel(
+    left_ref, upstream_ref, weight_ref, d_left_ref, kept_ref, sent_ref, turned_ref
+):
     @pl.when(pl.program_id(0) == 0)
     def _():
+        turned_ref[...] = left_ref[...].T
         d_left_ref[...] = jnp.zeros_like(d_left_ref)
 
     upstream = upstream_ref[...]
-    store_halves(dot_first(left_ref[...], upstream), kept_ref, sent_ref)
+    grad = jnp.dot(turned_ref[...], upstream, preferred_element_type=jnp.float32)
+    store_halves(grad, kept_ref, sent_ref)
     d_left_ref[...] += dot_last(upstream, weight_ref[...])
 
 
@@ -446,6 +454,7 @@
             pl.BlockSpec((width, block), lambda at: (0, at)),
         ],
         out_specs=(fixed, half, half),
+        scratch_shapes=[pltpu.VMEM((width, length), jnp.bfloat16)],
         compiler_params=pltpu.CompilerParams(vmem_limit_bytes=32 << 20),
         cost_estimate=SHORT,
     )(left, upstream, weight)
@@ -455,9 +464,11 @@
 def mlp_kernel(
     hidden_ref, upstream_ref, up_ref, bias_ref, down_ref,
     branch_ref, d_hidden_ref, up_kept_ref, up_sent_ref, down_grad_ref, bias_grad_ref,
+    turned_ref,
 ):
     @pl.when(pl.program_id(0) == 0)
     def _():
+        turned_ref[...] = hidden_ref[...].T
         branch_ref[...] = jnp.zeros_like(branch_ref)
         d_hidden_ref[...] = jnp.zeros_like(d_hidden_ref)
 
@@ -479,7 +490,8 @@
     bias_grad_ref[...] = jnp.sum(d_preact.astype(jnp.float32), 0, keepdims=True)
     down_grad_ref[...] = dot_first(activated, upstream).astype(jnp.bfloat16)
     d_hidden_ref[...] += dot_last(d_preact, up_ref[...])
-    store_halves(dot_first(hidden, d_preact), up_kept_ref, up_sent_ref)
+    up_grad = jnp.dot(turned_ref[...], d_preact, preferred_element_type=jnp.float32)
+    store_halves(up_grad, up_kept_ref, up_sent_ref)
 
 
 def mlp(hidden, upstream, up, bias, down):
@@ -505,6 +517,7 @@
         ),
         in_specs=[fixed, fixed, columns, lanes, rows],
         out_specs=(fixed, fixed, half, half, rows, lanes),
+        scratch_shapes=[pltpu.VMEM((width, length), jnp.bfloat16)],
         compiler_params=pltpu.CompilerParams(vmem_limit_bytes=56 << 20),
         cost_estimate=SHORT,
     )(hidden, upstream, up, bias, down)
@@ -545,11 +558,10 @@
     )
     small_all = gather_group(small)
     latent_low = swap_halves(latent_in)
-    qkv_pieces, order = gather_pieces(qkv_weight)
+    pieces, order = gather_pieces(jnp.concatenate([qkv_weight, out_weight], axis=1))
     full_up = lax.all_gather(up_weight, GROUP, axis=0, tiled=True)
-    full_out = lax.all_gather(out_weight, GROUP, axis=0, tiled=True)
     cotangent_low = swap_halves(cotangent)
-    full_qkv = assemble(qkv_pieces, order)
+    full_qkv, full_out = assemble(pieces, order, (3 * width, width))
     full_down = lax.all_gather(down_weight, GROUP, axis=0, tiled=True)
 
     bounds = [0, width]
@@ -611,7 +623,6 @@
     down_shard = lax.psum_scatter(down_grad, GROUP, scatter_dimension=0, tiled=True)
     branch_two = branch_two + full_down_bias
     block_out = (mask_row * (middle + gate_two * branch_two)).astype(jnp.bfloat16)
-    block_out = swap_halves(block_out[None])
     d_gate_two = jnp.sum(d_out * branch_two, axis=0)
     down_bias_grad = jnp.sum(d_branch_two.astype(jnp.float32), axis=0)
     up_bias_grad = up_bias_grad[0]
@@ -628,55 +639,65 @@
     d_attended, up_scatter.received = tie(d_attended, up_scatter.received)
     up_scatter.second()
     left = attend_back(query, pair_own, pair_other, d_attended, log_rows, halves[0])
-    d_query, d_attended, up_scatter.received, out_scatter.received = tie(
-        left[0], d_attended, up_scatter.received, out_scatter.received
-    )
-    up_scatter.third()
+    d_query, d_attended, out_scatter.received = tie(left[0], d_attended, out_scatter.received)
     out_scatter.second()
     right = attend_back(query, pair_own, pair_other, d_attended, log_rows, halves[1])
-    *right, up_scatter.received, out_scatter.received = tie(
-        *right, up_scatter.received, out_scatter.received
-    )
+    *right, up_scatter.received = tie(*right, up_scatter.received)
+    up_scatter.third()
     d_query = join_heads(d_query, right[0], width)
     d_own = join_heads(left[1], right[1], width)
     d_other = permute(join_heads(left[2], right[2], width), core_rule)
     d_own = (d_own + d_other.astype(jnp.float32)).astype(jnp.bfloat16)
     d_projected = jnp.concatenate([d_query, d_own[0], d_own[1]], axis=-1)
 
-    up_sum = ReplicaSum(up_scatter.result(), replicas)
-    out_scatter.third()
+    d_projected, down_shard = tie(d_projected, down_shard)
     d_hidden_one, qkv_halves = product_back(hidden_one, d_projected, full_qkv)
     qkv_scatter = Scatter(qkv_halves)
     column_sums = jnp.sum(d_projected.astype(jnp.float32), axis=0)
-    d_hidden_one, down_shard, qkv_scatter.received, *up_sum.received = tie(
-        d_hidden_one, down_shard, qkv_scatter.received, *up_sum.received
-    )
+    d_hidden_one, *arrived = tie(
+        d_hidden_one,
+        qkv_scatter.received,
+        up_scatter.received,
+        out_scatter.received,
+    )
+    qkv_scatter.received, up_scatter.received, out_scatter.received = arrived
     qkv_scatter.second()
-    up_sum.second()
     down_total = lax.psum(down_shard, "rep")
+    up_sum = ReplicaSum(up_scatter.result(), replicas)
+    out_scatter.third()
     d_shift_one = jnp.sum(d_hidden_one, axis=0)
     d_scale_one = jnp.sum(d_hidden_one * normed_one, axis=0)
     latent_grad = d_middle + norm_back(d_hidden_one * (1.0 + scale_one), normed_one, inverse_one)
-    latent_grad = swap_halves(latent_grad.astype(jnp.bfloat16)[None]).astype(jnp.float32)
-
+    bias_grads = (
+        jnp.concatenate([column_sums[:width], column_sums[2 * width :]]),
+        out_bias_grad,
+        up_bias_grad,
+        down_bias_grad,
+    )
+    sums = [d_shift_one, d_scale_one, d_gate_one, d_shift_two, d_scale_two, d_gate_two]
+    ada_width = 6 * width
+    small_sums = jnp.concatenate(sums + list(bias_grads))
+    qkv_scatter.received, out_scatter.received, *up_sum.received = tie(
+        qkv_scatter.received, out_scatter.received, *up_sum.received
+    )
     qkv_scatter.third()
-    late = jnp.concatenate([out_scatter.result(), qkv_scatter.result()], axis=1)
-    late_sum = ReplicaSum(late, replicas)
+    up_sum.second()
+    qkv_shard = qkv_scatter.result()
+    qkv_shard, latent_grad, block_out, small_sums = tie(
+        qkv_shard, latent_grad.astype(jnp.bfloat16), block_out, small_sums
+    )
+    late_sum = ReplicaSum(
+        jnp.concatenate([out_scatter.result(), qkv_shard], axis=1), replicas
+    )
+    latent_grad = swap_halves(latent_grad[None]).astype(jnp.float32)
+    block_out = swap_halves(block_out[None])
+    sums_all = gather_group(small_sums)
     down_total, *late_sum.received = tie(down_total, *late_sum.received)
     late_sum.second()
     up_total = up_sum.result()
     late_total = late_sum.result()
     out_total, qkv_total = late_total[:, :width], late_total[:, width:]
 
-    bias_grads = (
-        jnp.concatenate([column_sums[:width], column_sums[2 * width :]]),
-        out_bias_grad,
-        up_bias_grad,
-        down_bias_grad,
-    )
-    sums = [d_shift_one, d_scale_one, d_gate_one, d_shift_two, d_scale_two, d_gate_two]
-    ada_width = 6 * width
-    sums_all = gather_group(jnp.concatenate(sums + list(bias_grads)))
     d_group = sums_all[:, :ada_width].reshape(2, 2, 2, ada_width).sum(1).reshape(4, ada_width)
     bias_mine = []
     start = ada_width

time: 644 us -> 615 us (0.955)
  waiting for transfers between devices: 256 us -> 236 us
    ppermute x30, waiting for transfers between devices: 96 us -> 118 us  [permute(): return lax.ppermute(values, GROUP, pairs_by(rule))]
    all_gather x1, waiting for transfers between devices: 19.7 us -> 0.01 us  [per_device(): full_down = lax.all_gather(down_weight, GROUP, axis=0, tiled=True)]
    ppermute x3, waiting for transfers between devices: 15.8 us -> 0.01 us  [gather_replicas(): stacked.append(lax.ppermute(values, 'rep', pairs))]
    unnamed x133 -> x122, local copies, waits for them, and re-layouts: 14.7 us -> 21.4 us
  transfers between devices with their start and end apart: 54 -> 53, of which waited for: 24 -> 18; matrix products, arithmetic and copies ran while one was open for 19% -> 19% of each run, Pallas kernels for 17% -> 14%
where the time goes in v7:
time: 615 us; the launch traced here: 608 us
  waiting for transfers between devices  236 us (38%)
  Pallas kernels  153 us (25%)
  other arithmetic  71.8 us (12%)
  starting transfers between devices  63.9 us (10%)
  local copies, waits for them, and re-layouts  50.7 us (8%)
  matrix products  16.7 us (3%)
  between operations  16.2 us (3%)
    ppermute x30, waiting for transfers between devices, permute(): return lax.ppermute(values, GROUP, pairs_by(rule))  118 us
    ppermute x12, waiting for transfers between devices, send(): return lax.ppermute(values, 'rep', pairs)  94 us
    pallas_call x2, Pallas kernels, attend_back(): pl.pallas_call(functools.partial(attend_back_kernel, heads[0], low), grid...  48.3 us
    pallas_call x1, Pallas kernels, mlp(): pl.pallas_call(mlp_kernel, grid=(units // block,), out_shape=(jax.ShapeDt...  47.6 us
    ppermute x30, starting transfers between devices, permute(): return lax.ppermute(values, GROUP, pairs_by(rule))  34.3 us
    pallas_call x1, Pallas kernels, attend(): pl.pallas_call(functools.partial(attend_kernel, heads[0], low), grid=(len...  26.8 us
    pallas_call x2, Pallas kernels, product_back(): pl.pallas_call(product_back_kernel, grid=(columns // block,), out_shape=(...  26.1 us
    ppermute x4, waiting for transfers between devices, swap_halves(): received = lax.ppermute(values, GROUP, pairs)  22.9 us
  transfers between devices with their start and end apart: 53, of which 18 were waited for; matrix products, arithmetic and copies ran while one was open for 19% of the time, Pallas kernels for 14%

profile of v7, /device:TPU:9, one launch (start us, length us, event | category | flops | bytes accessed | tf_op | source)
XLA Modules:
  0.0 608.3 jit_solution(4445949235247019281)
XLA Ops:
  11.0 2.2 constant_dynamic-update-slice_fusion.1
  18.0 2.1 collective-permute-start
  20.6 43.9 %collective-permute-done.3 = bf16[4,2432]{1,0:T(4,128)(2,1)S(1)} collective-permute-done((bf16[4,2432]{1,0:T(4,128)(2,1)S(1)}, bf16[4,2432]{1,0:T(4,128)(2,1)S(1)}, u32[]{:S(2)}, u32[]{:S(2)}) %collective-permute-start.3) | collective-permute-done | bytes 19488 | tf_op jit(solution)/shard_map/ppermute | solution.py:62
  65.2 2.2 collective-permute-start.4
  67.4 3.2 collective-permute-done.4
  72.5 34.7 %collective-permute-done.5 = f32[1,6912]{1,0:T(1,128)S(1)} collective-permute-done((f32[1,6912]{1,0:T(1,128)S(1)}, f32[1,6912]{1,0:T(1,128)S(1)}, u32[]{:S(2)}, u32[]{:S(2)}) %collective-permute-start.5) | collective-permute-done | bytes 27680 | tf_op jit(solution)/shard_map/ppermute | solution.py:62
  109.3 7.6 %collective-permute-start.13 = (bf16[144,4608]{1,0:T(8,128)(2,1)S(1)}, bf16[144,4608]{1,0:T(8,128)(2,1)S(1)}, u32[]{:S(2)}, u32[]{:S(2)}) collective-permute-start(bf16[144,4608]{1,0:T(8,128)(2,1)S(1)} %collective-permute-done.9.refs_3_), channel_id=1, source_target_pairs={{0,2},{1,3},{2,0},{3,1},{4,6},{5,7},{6,4},{7,5},{8,10},{9,11},{10,... | collective-permute-start | bytes 3981320 | tf_op jit(solution)/shard_map/ppermute | solution.py:62
  119.7 3.7 shard_map.237
  124.9 5.1 add_convert_fusion.2
  132.9 3.5 collective-permute-start.15
  138.0 22.9 %collective-permute-done.15 = bf16[1,512,1152]{2,1,0:T(8,128)(2,1)} collective-permute-done((bf16[1,512,1152]{2,1,0:T(8,128)(2,1)}, bf16[1,512,1152]{2,1,0:T(8,128)(2,1)}, u32[]{:S(2)}, u32[]{:S(2)}) %collective-permute-start.15) | collective-permute-done | bytes 1179680 | tf_op jit(solution)/shard_map/ppermute | solution.py:68
  160.9 3.9 convert_reduce_fusion.2
  166.1 26.8 %shard_map.238 = (bf16[512,1152]{1,0:T(8,128)(2,1)S(1)}, f32[512,128]{1,0:T(8,128)S(1)}) custom-call(bf16[512,1152]{1,0:T(8,128)(2,1)S(1)} %slice.226.query_ref, bf16[512,2304]{1,0:T(8,128)(2,1)} %slice.227.own_ref, bf16[512,2304]{1,0:T(8,128)(2,1)} %collective-permute-done.14.other_ref), custom_call_target="tpu_custom_call" | custom-call | flops 1048576 | bytes 1048576 | tf_op jit(solution)/shard_map/pallas_call | solution.py:297
  193.0 3.3 fusion.48
  199.1 47.6 %shard_map.239 = (f32[512,1152]{1,0:T(8,128)}, f32[512,1152]{1,0:T(8,128)}, bf16[4,144,4608]{2,1,0:T(8,128)(2,1)}, bf16[4,144,4608]{2,1,0:T(8,128)(2,1)}, bf16[4608,1152]{1,0:T(8,128)(2,1)}, /*index=5*/f32[1,4608]{1,0:T(1,128)}) custom-call(bf16[512,1152]{1,0:T(8,128)(2,1)} %add_convert_fusion.4.hidden_ref, ...), custom_call_target="tpu_custom_call" | custom-call | flops 1048576 | bytes 1048576 | tf_op jit(solution)/shard_map/pallas_call | solution.py:507
  247.1 3.5 multiply_reduce_fusion
  250.9 7.3 %fusion.21 = (f32[1152]{0:T(1024)S(1)}, bf16[512,1152]{1,0:T(8,128)(2,1)}, f32[1152]{0:T(1024)S(1)}, bf16[512,1152]{1,0:T(8,128)(2,1)S(1)}, f32[512,1152]{1,0:T(8,128)}) fusion(bf16[1,512,1152]{2,1,0:T(8,128)(2,1)} %get-tuple-element.135, f32[512,1152]{1,0:T(8,128)} %get-tuple-element.98, f32[1152]{0:T(1024)S(1)} %reshape.147, f32[]{:T(128)} %bitcast.10, ...), kind=kLoop, calls=%fused_computation.43 | loop fusion | flops 12384000 | bytes 13011972 | tf_op jit(solution)/shard_map/reduce_sum | solution.py:626
  258.2 7.2 %shard_map.240 = (f32[512,1152]{1,0:T(8,128)S(1)}, bf16[4,144,1152]{2,1,0:T(8,128)(2,1)S(1)}, bf16[4,144,1152]{2,1,0:T(8,128)(2,1)}) custom-call(bf16[512,1152]{1,0:T(8,128)(2,1)S(1)} %copy-done.16, bf16[512,1152]{1,0:T(8,128)(2,1)S(1)} %get-tuple-element.156.upstream_ref, bf16[1152,1152]{1,0:T(8,128)(2,1)S(1)} %copy-done.12), custom_call_target="tpu_custom_call" | custom-call | flops 1048576 | bytes 1048576 | tf_op jit(solution)/shard_map/pallas_call | solution.py:443
  266.9 4.1 add_convert_fusion
  278.7 24.0 %shard_map.241 = (bf16[512,640]{1,0:T(8,128)(2,1)}, f32[2,512,640]{2,1,0:T(8,128)}, bf16[2,512,640]{2,1,0:T(8,128)(2,1)}) custom-call(bf16[512,1152]{1,0:T(8,128)(2,1)} %copy-done.1, bf16[512,2304]{1,0:T(8,128)(2,1)} %slice.227.own_ref, bf16[512,2304]{1,0:T(8,128)(2,1)} %collective-permute-done.14.other_ref, ...), custom_call_target="tpu_custom_call" | custom-call | flops 1048576 | bytes 1048576 | tf_op jit(solution)/shard_map/pallas_call | solution.py:369
  304.0 24.3 %shard_map.242 = (bf16[512,640]{1,0:T(8,128)(2,1)}, f32[2,512,640]{2,1,0:T(8,128)}, bf16[2,512,640]{2,1,0:T(8,128)(2,1)}) custom-call(bf16[512,1152]{1,0:T(8,128)(2,1)} %copy-done.1, bf16[512,2304]{1,0:T(8,128)(2,1)} %slice.227.own_ref, bf16[512,2304]{1,0:T(8,128)(2,1)} %collective-permute-done.14.other_ref, ...), custom_call_target="tpu_custom_call" | custom-call | flops 1048576 | bytes 1048576 | tf_op jit(solution)/shard_map/pallas_call | solution.py:369
  328.3 16.4 %collective-permute-done.18 = bf16[2,144,4608]{2,1,0:T(8,128)(2,1)} collective-permute-done((bf16[2,144,4608]{2,1,0:T(8,128)(2,1)}, bf16[2,144,4608]{2,1,0:T(8,128)(2,1)}, u32[]{:S(2)}, u32[]{:S(2)}) %collective-permute-start.18) | collective-permute-done | bytes 2654240 | tf_op jit(solution)/shard_map/ppermute | solution.py:62
  356.8 3.3 copy-done.7
  360.1 19.0 %shard_map.243 = (f32[512,1152]{1,0:T(8,128)S(1)}, bf16[4,144,3456]{2,1,0:T(8,128)(2,1)S(1)}, bf16[4,144,3456]{2,1,0:T(8,128)(2,1)}) custom-call(bf16[512,1152]{1,0:T(8,128)(2,1)S(1)} %fusion.12.left_ref, bf16[512,3456]{1,0:T(8,128)(2,1)S(1)} %copy-done.3, bf16[1152,3456]{1,0:T(8,128)(2,1)S(1)} %copy-done.7), custom_call_target="tpu_custom_call" | custom-call | flops 1048576 | bytes 1048576 | tf_op jit(solution)/shard_map/pallas_call | solution.py:443
  379.4 4.6 convert_add_fusion
  389.9 2.7 convert_reduce_fusion
  392.6 14.6 %collective-permute-done.22 = bf16[2,144,1152]{2,1,0:T(8,128)(2,1)} collective-permute-done((bf16[2,144,1152]{2,1,0:T(8,128)(2,1)}, bf16[2,144,1152]{2,1,0:T(8,128)(2,1)}, u32[]{:S(2)}, u32[]{:S(2)}) %collective-permute-start.22) | collective-permute-done | bytes 663584 | tf_op jit(solution)/shard_map/ppermute | solution.py:62
  408.4 2.6 fusion.46
  417.2 3.2 add_convert_fusion.1
  424.2 2.2 multiply_reduce_fusion.1
  426.5 22.8 %collective-permute-done.26 = bf16[144,1152]{1,0:T(8,128)(2,1)S(1)} collective-permute-done((bf16[144,1152]{1,0:T(8,128)(2,1)S(1)}, bf16[144,1152]{1,0:T(8,128)(2,1)S(1)}, u32[]{:S(2)}, u32[]{:S(2)}) %collective-permute-start.26) | collective-permute-done | bytes 331808 | tf_op jit(solution)/shard_map/ppermute | solution.py:209
  449.3 5.0 collective-permute-done.27
  459.3 2.2 collective-permute-start.28
  461.6 23.2 %collective-permute-done.46 = bf16[144,1152]{1,0:T(8,128)(2,1)S(1)} collective-permute-done((bf16[144,1152]{1,0:T(8,128)(2,1)S(1)}, bf16[144,1152]{1,0:T(8,128)(2,1)S(1)}, u32[]{:S(2)}, u32[]{:S(2)}) %collective-permute-start.46) | collective-permute-done | bytes 331808 | tf_op jit(solution)/shard_map/ppermute | solution.py:209
  485.7 9.7 %collective-permute-done.47 = bf16[144,1152]{1,0:T(8,128)(2,1)S(1)} collective-permute-done((bf16[144,1152]{1,0:T(8,128)(2,1)S(1)}, bf16[144,1152]{1,0:T(8,128)(2,1)S(1)}, u32[]{:S(2)}, u32[]{:S(2)}) %collective-permute-start.47) | collective-permute-done | bytes 331808 | tf_op jit(solution)/shard_map/ppermute | solution.py:209
  502.8 3.1 collective-permute-start.41
  509.9 4.1 collective-permute-start.30
  514.1 17.7 %collective-permute-done.41 = bf16[144,1152]{1,0:T(8,128)(2,1)} collective-permute-done((bf16[144,1152]{1,0:T(8,128)(2,1)}, bf16[144,1152]{1,0:T(8,128)(2,1)}, u32[]{:S(2)}, u32[]{:S(2)}) %collective-permute-start.41) | collective-permute-done | bytes 331808 | tf_op jit(solution)/shard_map/ppermute | solution.py:209
  531.8 4.0 collective-permute-done.42
  548.9 2.2 convert_dynamic-update-slice_fusion.7
  554.4 3.8 collective-permute-start.29
  561.1 3.1 collective-permute-start.44
  568.7 2.0 reshape.144
  572.4 6.2 %fusion.52 = f32[144,6912]{1,0:T(8,128)} fusion(f32[16,144]{1,0:T(8,128)S(1)} %reshape.143, f32[16,6912]{1,0:T(8,128)} %reshape.144), kind=kOutput, calls=%fused_computation.192 | convolution fusion | flops 191102976 | bytes 4432896 | tf_op jit(solution)/shard_map/dot_general | solution.py:727
  579.7 8.8 %collective-permute-done.44 = bf16[144,1152]{1,0:T(8,128)(2,1)} collective-permute-done((bf16[144,1152]{1,0:T(8,128)(2,1)}, bf16[144,1152]{1,0:T(8,128)(2,1)}, u32[]{:S(2)}, u32[]{:S(2)}) %collective-permute-start.44) | collective-permute-done | bytes 331808 | tf_op jit(solution)/shard_map/ppermute | solution.py:209
  589.6 2.7 collective-permute-done.45
  595.7 3.2 select_convert_fusion
  598.8 2.5 broadcast_select_fusion
  (339 shorter events, 113.8 us)
Async XLA Ops:
  7.3 191.9 %all-gather.3.cloned.1.call-start = ((), (), s32[]{:S(2)}) async-start(), calls=%async_computation.1 | async-start | bytes 11943936 | tf_op jit(solution)/shard_map/all_gather | solution.py:562
  8.0 191.1 %all-gather.5.cloned.1.call-start = ((), (), s32[]{:S(2)}) async-start(), calls=%async_computation.2 | async-start | bytes 11943936 | tf_op jit(solution)/shard_map/all_gather | solution.py:565
  8.8 346.1 %reduce-scatter.2.cloned.1.call-start = ((), (), s32[]{:S(2)}) async-start(), calls=%async_computation.3 | async-start | bytes 11943936 | tf_op jit(solution)/shard_map/reduce_scatter | solution.py:623
  13.2 6.8 %collective-permute-start.2 = (bf16[2,2432]{1,0:T(2,128)(2,1)S(1)}, bf16[2,2432]{1,0:T(2,128)(2,1)S(1)}, u32[]{:S(2)}, u32[]{:S(2)}) collective-permute-start(bf16[2,2432]{1,0:T(2,128)(2,1)S(1)} %broadcast_select_fusion.6), channel_id=1, source_target_pairs={{0,2},{1,3},{2,0},{3,1},{4,6},{5,7},{6,4},{7,5},{8,10},{9,11},{10,... | collective-permute-start | bytes 29192 | tf_op jit(solution)/shard_map/ppermute | solution.py:62
  15.0 55.9 %collective-permute-start.7 = (bf16[144,4608]{1,0:T(8,128)(2,1)}, bf16[144,4608]{1,0:T(8,128)(2,1)}, u32[]{:S(2)}, u32[]{:S(2)}) collective-permute-start(bf16[144,4608]{1,0:T(8,128)(2,1)} %constant_dynamic-update-slice_fusion.refs_0_), channel_id=1, source_target_pairs={{0,4},{1,5},{2,3},{3,2},{4,0},{5,1},{6,7},{7,6},{8,12},{9,13},{10,... | collective-permute-start | bytes 3981320 | tf_op jit(solution)/shard_map/ppermute | solution.py:62
  16.2 92.8 %collective-permute-start.8 = (bf16[144,4608]{1,0:T(8,128)(2,1)}, bf16[144,4608]{1,0:T(8,128)(2,1)}, u32[]{:S(2)}, u32[]{:S(2)}) collective-permute-start(bf16[144,4608]{1,0:T(8,128)(2,1)} %constant_dynamic-update-slice_fusion.refs_0_), channel_id=1, source_target_pairs={{0,1},{1,0},{2,6},{3,7},{4,5},{5,4},{6,2},{7,3},{8,9},{9,8},{10,14... | collective-permute-start | bytes 3981320 | tf_op jit(solution)/shard_map/ppermute | solution.py:62
  17.4 102.2 %collective-permute-start.10 = (bf16[144,4608]{1,0:T(8,128)(2,1)}, bf16[144,4608]{1,0:T(8,128)(2,1)}, u32[]{:S(2)}, u32[]{:S(2)}) collective-permute-start(bf16[144,4608]{1,0:T(8,128)(2,1)} %constant_dynamic-update-slice_fusion.refs_0_), channel_id=1, source_target_pairs={{0,2},{1,3},{2,0},{3,1},{4,6},{5,7},{6,4},{7,5},{8,10},{9,11},{10,... | collective-permute-start | bytes 3981320 | tf_op jit(solution)/shard_map/ppermute | solution.py:62
  18.0 98.9 %collective-permute-start = (bf16[1,512,1152]{2,1,0:T(8,128)(2,1)S(1)}, bf16[1,512,1152]{2,1,0:T(8,128)(2,1)}, u32[]{:S(2)}, u32[]{:S(2)}) collective-permute-start(bf16[1,512,1152]{2,1,0:T(8,128)(2,1)S(1)} %copy-done.39), channel_id=1, source_target_pairs={{1,2},{2,1},{5,6},{6,5},{9,10},{10,9},{13,14},{14,13},{17,18},{18,... | collective-permute-start | bytes 3538952 | tf_op jit(solution)/shard_map/ppermute | solution.py:68
  20.1 44.4 %collective-permute-start.3 = (bf16[4,2432]{1,0:T(4,128)(2,1)S(1)}, bf16[4,2432]{1,0:T(4,128)(2,1)S(1)}, u32[]{:S(2)}, u32[]{:S(2)}) collective-permute-start(bf16[4,2432]{1,0:T(4,128)(2,1)S(1)} %maximum_select_fusion.4), channel_id=1, source_target_pairs={{0,4},{1,5},{2,6},{3,7},{4,0},{5,1},{6,2},{7,3},{8,12},{9,13},{10,... | collective-permute-start | bytes 58376 | tf_op jit(solution)/shard_map/ppermute | solution.py:62
  65.2 5.4 collective-permute-start.4
  70.7 36.6 %collective-permute-start.5 = (f32[1,6912]{1,0:T(1,128)S(1)}, f32[1,6912]{1,0:T(1,128)S(1)}, u32[]{:S(2)}, u32[]{:S(2)}) collective-permute-start(f32[1,6912]{1,0:T(1,128)S(1)} %broadcast_select_fusion.4), channel_id=1, source_target_pairs={{0,1},{1,0},{2,3},{3,2},{4,5},{5,4},{6,7},{7,6},{8,9},{9,8},{10,11... | collective-permute-start | bytes 82952 | tf_op jit(solution)/shard_map/ppermute | solution.py:62
  70.9 38.4 %collective-permute-start.9 = (bf16[144,4608]{1,0:T(8,128)(2,1)}, bf16[144,4608]{1,0:T(8,128)(2,1)S(1)}, u32[]{:S(2)}, u32[]{:S(2)}) collective-permute-start(bf16[144,4608]{1,0:T(8,128)(2,1)} %collective-permute-done.7.refs_1_), channel_id=1, source_target_pairs={{0,1},{1,0},{2,6},{3,7},{4,5},{5,4},{6,2},{7,3},{8,9},{9,8},{10,14... | collective-permute-start | bytes 3981320 | tf_op jit(solution)/shard_map/ppermute | solution.py:62
  108.7 10.9 %collective-permute-start.11 = (bf16[144,4608]{1,0:T(8,128)(2,1)}, bf16[144,4608]{1,0:T(8,128)(2,1)S(1)}, u32[]{:S(2)}, u32[]{:S(2)}) collective-permute-start(bf16[144,4608]{1,0:T(8,128)(2,1)} %collective-permute-done.7.refs_1_), channel_id=1, source_target_pairs={{0,2},{1,3},{2,0},{3,1},{4,6},{5,7},{6,4},{7,5},{8,10},{9,11},{10,... | collective-permute-start | bytes 3981320 | tf_op jit(solution)/shard_map/ppermute | solution.py:62
  108.9 10.7 %collective-permute-start.12 = (bf16[144,4608]{1,0:T(8,128)(2,1)}, bf16[144,4608]{1,0:T(8,128)(2,1)S(1)}, u32[]{:S(2)}, u32[]{:S(2)}) collective-permute-start(bf16[144,4608]{1,0:T(8,128)(2,1)} %collective-permute-done.8.refs_2_), channel_id=1, source_target_pairs={{0,2},{1,3},{2,0},{3,1},{4,6},{5,7},{6,4},{7,5},{8,10},{9,11},{10,... | collective-permute-start | bytes 3981320 | tf_op jit(solution)/shard_map/ppermute | solution.py:62
  109.3 10.4 %collective-permute-start.13 = (bf16[144,4608]{1,0:T(8,128)(2,1)S(1)}, bf16[144,4608]{1,0:T(8,128)(2,1)S(1)}, u32[]{:S(2)}, u32[]{:S(2)}) collective-permute-start(bf16[144,4608]{1,0:T(8,128)(2,1)S(1)} %collective-permute-done.9.refs_3_), channel_id=1, source_target_pairs={{0,2},{1,3},{2,0},{3,1},{4,6},{5,7},{6,4},{7,5},{8,10},{9,11},{10,... | collective-permute-start | bytes 3981320 | tf_op jit(solution)/shard_map/ppermute | solution.py:62
  132.7 33.5 %collective-permute-start.14 = (bf16[512,2304]{1,0:T(8,128)(2,1)}, bf16[512,2304]{1,0:T(8,128)(2,1)}, u32[]{:S(2)}, u32[]{:S(2)}) collective-permute-start(bf16[512,2304]{1,0:T(8,128)(2,1)} %slice.227.own_ref), channel_id=1, source_target_pairs={{0,2},{1,3},{2,0},{3,1},{4,6},{5,7},{6,4},{7,5},{8,10},{9,11},{10,... | collective-permute-start | bytes 7077896 | tf_op jit(solution)/shard_map/ppermute | solution.py:62
  132.9 27.9 %collective-permute-start.15 = (bf16[1,512,1152]{2,1,0:T(8,128)(2,1)}, bf16[1,512,1152]{2,1,0:T(8,128)(2,1)}, u32[]{:S(2)}, u32[]{:S(2)}) collective-permute-start(bf16[1,512,1152]{2,1,0:T(8,128)(2,1)} %param.27), channel_id=1, source_target_pairs={{1,2},{2,1},{5,6},{6,5},{9,10},{10,9},{13,14},{14,13},{17,18},{18,... | collective-permute-start | bytes 3538952 | tf_op jit(solution)/shard_map/ppermute | solution.py:68
  246.8 267.2 %all-reduce.2.cloned.1.call-start = ((), (), s32[]{:S(2)}) async-start(), calls=%async_computation.4 | async-start | bytes 2654208 | tf_op jit(solution)/shard_map/psum | solution.py:665
  246.9 20.0 %collective-permute-start.16 = (bf16[4,144,4608]{2,1,0:T(8,128)(2,1)}, bf16[4,144,4608]{2,1,0:T(8,128)(2,1)}, u32[]{:S(2)}, u32[]{:S(2)}) collective-permute-start(bf16[4,144,4608]{2,1,0:T(8,128)(2,1)} %get-tuple-element.68), channel_id=1, source_target_pairs={{0,2},{1,3},{2,0},{3,1},{4,6},{5,7},{6,4},{7,5},{8,10},{9,11},{10,... | collective-permute-start | bytes 15925256 | tf_op jit(solution)/shard_map/ppermute | solution.py:62
  274.7 70.1 %collective-permute-start.18 = (bf16[2,144,4608]{2,1,0:T(8,128)(2,1)}, bf16[2,144,4608]{2,1,0:T(8,128)(2,1)}, u32[]{:S(2)}, u32[]{:S(2)}) collective-permute-start(bf16[2,144,4608]{2,1,0:T(8,128)(2,1)} %pad_maximum_fusion.1), channel_id=1, source_target_pairs={{0,4},{1,5},{2,3},{3,2},{4,0},{5,1},{6,7},{7,6},{8,12},{9,13},{10,... | collective-permute-start | bytes 7962632 | tf_op jit(solution)/shard_map/ppermute | solution.py:62
  274.7 28.0 %collective-permute-start.17 = (bf16[4,144,1152]{2,1,0:T(8,128)(2,1)}, bf16[4,144,1152]{2,1,0:T(8,128)(2,1)}, u32[]{:S(2)}, u32[]{:S(2)}) collective-permute-start(bf16[4,144,1152]{2,1,0:T(8,128)(2,1)} %get-tuple-element.72), channel_id=1, source_target_pairs={{0,2},{1,3},{2,0},{3,1},{4,6},{5,7},{6,4},{7,5},{8,10},{9,11},{10,... | collective-permute-start | bytes 3981320 | tf_op jit(solution)/shard_map/ppermute | solution.py:62
  347.4 4.6 collective-permute-start.19
  379.1 29.3 %collective-permute-start.20 = (bf16[4,144,3456]{2,1,0:T(8,128)(2,1)}, bf16[4,144,3456]{2,1,0:T(8,128)(2,1)}, u32[]{:S(2)}, u32[]{:S(2)}) collective-permute-start(bf16[4,144,3456]{2,1,0:T(8,128)(2,1)} %get-tuple-element.89), channel_id=1, source_target_pairs={{0,2},{1,3},{2,0},{3,1},{4,6},{5,7},{6,4},{7,5},{8,10},{9,11},{10,... | collective-permute-start | bytes 11943944 | tf_op jit(solution)/shard_map/ppermute | solution.py:62
  384.1 24.2 %collective-permute-start.21 = (bf16[144,4608]{1,0:T(8,128)(2,1)S(1)}, bf16[144,4608]{1,0:T(8,128)(2,1)}, u32[]{:S(2)}, u32[]{:S(2)}) collective-permute-start(bf16[144,4608]{1,0:T(8,128)(2,1)S(1)} %fusion.23), channel_id=1, source_target_pairs={{0,1},{1,0},{2,6},{3,7},{4,5},{5,4},{6,2},{7,3},{8,9},{9,8},{10,14... | collective-permute-start | bytes 3981320 | tf_op jit(solution)/shard_map/ppermute | solution.py:62
  389.8 17.3 %collective-permute-start.22 = (bf16[2,144,1152]{2,1,0:T(8,128)(2,1)}, bf16[2,144,1152]{2,1,0:T(8,128)(2,1)}, u32[]{:S(2)}, u32[]{:S(2)}) collective-permute-start(bf16[2,144,1152]{2,1,0:T(8,128)(2,1)} %pad_maximum_fusion.4), channel_id=1, source_target_pairs={{0,4},{1,5},{2,3},{3,2},{4,0},{5,1},{6,7},{7,6},{8,12},{9,13},{10,... | collective-permute-start | bytes 1990664 | tf_op jit(solution)/shard_map/ppermute | solution.py:62
  411.1 15.3 %collective-permute-start.25 = (bf16[144,1152]{1,0:T(8,128)(2,1)S(1)}, bf16[144,1152]{1,0:T(8,128)(2,1)S(1)}, u32[]{:S(2)}, u32[]{:S(2)}) collective-permute-start(bf16[144,1152]{1,0:T(8,128)(2,1)S(1)} %get-tuple-element.165), channel_id=1, source_target_pairs={{0,8},{8,16},{16,24},{24,0},{1,9},{9,17},{17,25},{25,1},{2,10},{10... | collective-permute-start | bytes 995336 | tf_op jit(solution)/shard_map/ppermute | solution.py:209
  412.4 36.9 %collective-permute-start.26 = (bf16[144,1152]{1,0:T(8,128)(2,1)S(1)}, bf16[144,1152]{1,0:T(8,128)(2,1)S(1)}, u32[]{:S(2)}, u32[]{:S(2)}) collective-permute-start(bf16[144,1152]{1,0:T(8,128)(2,1)S(1)} %get-tuple-element.164), channel_id=1, source_target_pairs={{0,16},{8,24},{16,0},{24,8},{1,17},{9,25},{17,1},{25,9},{2,18},{10... | collective-permute-start | bytes 995336 | tf_op jit(solution)/shard_map/ppermute | solution.py:209
  413.5 40.7 %collective-permute-start.27 = (bf16[144,1152]{1,0:T(8,128)(2,1)S(1)}, bf16[144,1152]{1,0:T(8,128)(2,1)S(1)}, u32[]{:S(2)}, u32[]{:S(2)}) collective-permute-start(bf16[144,1152]{1,0:T(8,128)(2,1)S(1)} %get-tuple-element.163), channel_id=1, source_target_pairs={{0,24},{8,0},{16,8},{24,16},{1,25},{9,1},{17,9},{25,17},{2,26},{10... | collective-permute-start | bytes 995336 | tf_op jit(solution)/shard_map/ppermute | solution.py:209
  416.1 38.1 %collective-permute-start.24 = (bf16[144,1152]{1,0:T(8,128)(2,1)S(1)}, bf16[144,1152]{1,0:T(8,128)(2,1)S(1)}, u32[]{:S(2)}, u32[]{:S(2)}) collective-permute-start(bf16[144,1152]{1,0:T(8,128)(2,1)S(1)} %fusion.33), channel_id=1, source_target_pairs={{0,1},{1,0},{2,6},{3,7},{4,5},{5,4},{6,2},{7,3},{8,9},{9,8},{10,14... | collective-permute-start | bytes 995336 | tf_op jit(solution)/shard_map/ppermute | solution.py:62
  421.1 33.1 %collective-permute-start.23 = (bf16[2,144,3456]{2,1,0:T(8,128)(2,1)S(1)}, bf16[2,144,3456]{2,1,0:T(8,128)(2,1)S(1)}, u32[]{:S(2)}, u32[]{:S(2)}) collective-permute-start(bf16[2,144,3456]{2,1,0:T(8,128)(2,1)S(1)} %pad_maximum_fusion.3), channel_id=1, source_target_pairs={{0,4},{1,5},{2,3},{3,2},{4,0},{5,1},{6,7},{7,6},{8,12},{9,13},{10,... | collective-permute-start | bytes 5971976 | tf_op jit(solution)/shard_map/ppermute | solution.py:62
  457.0 27.8 %collective-permute-start.46 = (bf16[144,1152]{1,0:T(8,128)(2,1)S(1)}, bf16[144,1152]{1,0:T(8,128)(2,1)S(1)}, u32[]{:S(2)}, u32[]{:S(2)}) collective-permute-start(bf16[144,1152]{1,0:T(8,128)(2,1)S(1)} %get-tuple-element.130), channel_id=1, source_target_pairs={{0,8},{8,16},{16,24},{24,0},{1,9},{9,17},{17,25},{25,1},{2,10},{10... | collective-permute-start | bytes 995336 | tf_op jit(solution)/shard_map/ppermute | solution.py:209
  457.0 38.3 %collective-permute-start.47 = (bf16[144,1152]{1,0:T(8,128)(2,1)S(1)}, bf16[144,1152]{1,0:T(8,128)(2,1)S(1)}, u32[]{:S(2)}, u32[]{:S(2)}) collective-permute-start(bf16[144,1152]{1,0:T(8,128)(2,1)S(1)} %get-tuple-element.130), channel_id=1, source_target_pairs={{0,16},{8,24},{16,0},{24,8},{1,17},{9,25},{17,1},{25,9},{2,18},{10... | collective-permute-start | bytes 995336 | tf_op jit(solution)/shard_map/ppermute | solution.py:209
  457.0 52.0 %collective-permute-start.48 = (bf16[144,1152]{1,0:T(8,128)(2,1)S(1)}, bf16[144,1152]{1,0:T(8,128)(2,1)S(1)}, u32[]{:S(2)}, u32[]{:S(2)}) collective-permute-start(bf16[144,1152]{1,0:T(8,128)(2,1)S(1)} %get-tuple-element.130), channel_id=1, source_target_pairs={{0,24},{8,0},{16,8},{24,16},{1,25},{9,1},{17,9},{25,17},{2,26},{10... | collective-permute-start | bytes 995336 | tf_op jit(solution)/shard_map/ppermute | solution.py:209
  459.3 37.0 %collective-permute-start.28 = (bf16[144,3456]{1,0:T(8,128)(2,1)S(1)}, bf16[144,3456]{1,0:T(8,128)(2,1)S(1)}, u32[]{:S(2)}, u32[]{:S(2)}) collective-permute-start(bf16[144,3456]{1,0:T(8,128)(2,1)S(1)} %fusion.26), channel_id=1, source_target_pairs={{0,1},{1,0},{2,6},{3,7},{4,5},{5,4},{6,2},{7,3},{8,9},{9,8},{10,14... | collective-permute-start | bytes 2985992 | tf_op jit(solution)/shard_map/ppermute | solution.py:62
  499.9 7.4 %collective-permute-start.32 = (f32[2,16128]{1,0:T(2,128)S(1)}, f32[2,16128]{1,0:T(2,128)S(1)}, u32[]{:S(2)}, u32[]{:S(2)}) collective-permute-start(f32[2,16128]{1,0:T(2,128)S(1)} %maximum_select_fusion.2), channel_id=1, source_target_pairs={{0,2},{1,3},{2,0},{3,1},{4,6},{5,7},{6,4},{7,5},{8,10},{9,11},{10,... | collective-permute-start | bytes 387080 | tf_op jit(solution)/shard_map/ppermute | solution.py:62
  502.8 11.3 %collective-permute-start.40 = (bf16[144,1152]{1,0:T(8,128)(2,1)}, bf16[144,1152]{1,0:T(8,128)(2,1)S(1)}, u32[]{:S(2)}, u32[]{:S(2)}) collective-permute-start(bf16[144,1152]{1,0:T(8,128)(2,1)} %get-tuple-element.162), channel_id=1, source_target_pairs={{0,8},{8,16},{16,24},{24,0},{1,9},{9,17},{17,25},{25,1},{2,10},{10... | collective-permute-start | bytes 995336 | tf_op jit(solution)/shard_map/ppermute | solution.py:209
  502.8 29.1 %collective-permute-start.41 = (bf16[144,1152]{1,0:T(8,128)(2,1)}, bf16[144,1152]{1,0:T(8,128)(2,1)}, u32[]{:S(2)}, u32[]{:S(2)}) collective-permute-start(bf16[144,1152]{1,0:T(8,128)(2,1)} %get-tuple-element.161), channel_id=1, source_target_pairs={{0,16},{8,24},{16,0},{24,8},{1,17},{9,25},{17,1},{25,9},{2,18},{10... | collective-permute-start | bytes 995336 | tf_op jit(solution)/shard_map/ppermute | solution.py:209
  505.9 30.0 %collective-permute-start.42 = (bf16[144,1152]{1,0:T(8,128)(2,1)}, bf16[144,1152]{1,0:T(8,128)(2,1)}, u32[]{:S(2)}, u32[]{:S(2)}) collective-permute-start(bf16[144,1152]{1,0:T(8,128)(2,1)} %get-tuple-element.160), channel_id=1, source_target_pairs={{0,24},{8,0},{16,8},{24,16},{1,25},{9,1},{17,9},{25,17},{2,26},{10... | collective-permute-start | bytes 995336 | tf_op jit(solution)/shard_map/ppermute | solution.py:209
  507.5 28.3 %collective-permute-start.33 = (f32[4,16128]{1,0:T(4,128)S(1)}, f32[4,16128]{1,0:T(4,128)}, u32[]{:S(2)}, u32[]{:S(2)}) collective-permute-start(f32[4,16128]{1,0:T(4,128)S(1)} %maximum_select_fusion.1), channel_id=1, source_target_pairs={{0,4},{1,5},{2,6},{3,7},{4,0},{5,1},{6,2},{7,3},{8,12},{9,13},{10,... | collective-permute-start | bytes 774152 | tf_op jit(solution)/shard_map/ppermute | solution.py:62
  509.9 85.8 %collective-permute-start.30 = (bf16[1,512,1152]{2,1,0:T(8,128)(2,1)}, bf16[1,512,1152]{2,1,0:T(8,128)(2,1)}, u32[]{:S(2)}, u32[]{:S(2)}) collective-permute-start(bf16[1,512,1152]{2,1,0:T(8,128)(2,1)} %bitcast.21), channel_id=1, source_target_pairs={{1,2},{2,1},{5,6},{6,5},{9,10},{10,9},{13,14},{14,13},{17,18},{18,... | collective-permute-start | bytes 3538952 | tf_op jit(solution)/shard_map/ppermute | solution.py:68
  545.6 13.4 %collective-permute-start.37 = (f32[29376]{0:T(1024)S(1)}, f32[29376]{0:T(1024)}, u32[]{:S(2)}, u32[]{:S(2)}) collective-permute-start(f32[29376]{0:T(1024)S(1)} %concatenate.130), channel_id=1, source_target_pairs={{0,8},{8,16},{16,24},{24,0},{1,9},{9,17},{17,25},{25,1},{2,10},{10... | collective-permute-start | bytes 352520 | tf_op jit(solution)/shard_map/ppermute | solution.py:90
  545.7 15.5 %collective-permute-start.38 = (f32[29376]{0:T(1024)S(1)}, f32[29376]{0:T(1024)}, u32[]{:S(2)}, u32[]{:S(2)}) collective-permute-start(f32[29376]{0:T(1024)S(1)} %concatenate.130), channel_id=1, source_target_pairs={{0,16},{8,24},{16,0},{24,8},{1,17},{9,25},{17,1},{25,9},{2,18},{10... | collective-permute-start | bytes 352520 | tf_op jit(solution)/shard_map/ppermute | solution.py:90
  545.7 19.5 %collective-permute-start.39 = (f32[29376]{0:T(1024)S(1)}, f32[29376]{0:T(1024)S(1)}, u32[]{:S(2)}, u32[]{:S(2)}) collective-permute-start(f32[29376]{0:T(1024)S(1)} %concatenate.130), channel_id=1, source_target_pairs={{0,24},{8,0},{16,8},{24,16},{1,25},{9,1},{17,9},{25,17},{2,26},{10... | collective-permute-start | bytes 352520 | tf_op jit(solution)/shard_map/ppermute | solution.py:90
  547.1 7.2 %collective-permute-start.36 = (f32[4,4,144]{2,1,0:T(4,128)S(1)}, f32[4,4,144]{2,1,0:T(4,128)S(1)}, u32[]{:S(2)}, u32[]{:S(2)}) collective-permute-start(f32[4,4,144]{2,1,0:T(4,128)S(1)} %maximum_select_fusion.5), channel_id=1, source_target_pairs={{0,4},{1,5},{2,6},{3,7},{4,0},{5,1},{6,2},{7,3},{8,12},{9,13},{10,... | collective-permute-start | bytes 27656 | tf_op jit(solution)/shard_map/ppermute | solution.py:62
  554.4 44.5 %collective-permute-start.29 = (bf16[1,512,1152]{2,1,0:T(8,128)(2,1)S(1)}, bf16[1,512,1152]{2,1,0:T(8,128)(2,1)}, u32[]{:S(2)}, u32[]{:S(2)}) collective-permute-start(bf16[1,512,1152]{2,1,0:T(8,128)(2,1)S(1)} %bitcast.103), channel_id=1, source_target_pairs={{1,2},{2,1},{5,6},{6,5},{9,10},{10,9},{13,14},{14,13},{17,18},{18,... | collective-permute-start | bytes 3538952 | tf_op jit(solution)/shard_map/ppermute | solution.py:68
  558.9 19.7 %collective-permute-start.43 = (bf16[144,1152]{1,0:T(8,128)(2,1)}, bf16[144,1152]{1,0:T(8,128)(2,1)}, u32[]{:S(2)}, u32[]{:S(2)}) collective-permute-start(bf16[144,1152]{1,0:T(8,128)(2,1)} %get-tuple-element.132), channel_id=1, source_target_pairs={{0,8},{8,16},{16,24},{24,0},{1,9},{9,17},{17,25},{25,1},{2,10},{10... | collective-permute-start | bytes 995336 | tf_op jit(solution)/shard_map/ppermute | solution.py:209
  561.1 27.4 %collective-permute-start.44 = (bf16[144,1152]{1,0:T(8,128)(2,1)}, bf16[144,1152]{1,0:T(8,128)(2,1)}, u32[]{:S(2)}, u32[]{:S(2)}) collective-permute-start(bf16[144,1152]{1,0:T(8,128)(2,1)} %get-tuple-element.132), channel_id=1, source_target_pairs={{0,16},{8,24},{16,0},{24,8},{1,17},{9,25},{17,1},{25,9},{2,18},{10... | collective-permute-start | bytes 995336 | tf_op jit(solution)/shard_map/ppermute | solution.py:209
  565.2 27.1 %collective-permute-start.45 = (bf16[144,1152]{1,0:T(8,128)(2,1)}, bf16[144,1152]{1,0:T(8,128)(2,1)}, u32[]{:S(2)}, u32[]{:S(2)}) collective-permute-start(bf16[144,1152]{1,0:T(8,128)(2,1)} %get-tuple-element.132), channel_id=1, source_target_pairs={{0,24},{8,0},{16,8},{24,16},{1,25},{9,1},{17,9},{25,17},{2,26},{10... | collective-permute-start | bytes 995336 | tf_op jit(solution)/shard_map/ppermute | solution.py:209
  (59 other events, 414.1 us)
Sparse Core Ops, SparseCore 0:
  10.0 100.7 all-gather.2
  112.6 75.0 all-gather.4
  246.9 103.3 reduce-scatter.1
  390.0 96.6 all-reduce.1

commit v8 on v7

--- a/solution.py
+++ b/solution.py
@@ -140,19 +140,28 @@
     )(order, *pieces)
 
 
-def gather_pieces(shard):
+def gather_first(shard):
     place = place_of()
     near = jnp.where((place & 2) == 0, 4, 1)
     far = 5 - near
     other = place ^ 2
-    first = permute(shard, first_rule)
-    second = permute(shard, second_rule)
-    both = permute(first, second_rule)
-    held = [shard, first, second, both]
-    pieces = held + [permute(piece, core_rule) for piece in held]
     order = [place, place ^ near, place ^ far, place ^ 5]
     order += [other, other ^ far, other ^ near, other ^ 5]
+    pieces = [shard, permute(shard, first_rule), permute(shard, second_rule)]
     return pieces, jnp.stack(order).astype(jnp.int32)
+
+
+def gather_second(pieces):
+    return pieces + [permute(pieces[1], second_rule)]
+
+
+def gather_third(pieces):
+    return pieces + [permute(piece, core_rule) for piece in pieces]
+
+
+def gather_pieces(shard):
+    pieces, order = gather_first(shard)
+    return gather_third(gather_second(pieces)), order
 
 
 def tie(*values):
@@ -494,10 +503,22 @@
     store_halves(up_grad, up_kept_ref, up_sent_ref)
 
 
+def split_units(values, axis):
+    span = values.shape[axis] // SHARDS // 2
+    cuts = [lax.slice_in_dim(values, at * span, at * span + span, axis=axis) for at in range(16)]
+    return [jnp.concatenate(cuts[half::2], axis=axis) for half in (0, 1)]
+
+
+def join_units(halves):
+    span = halves[0].shape[-1] // SHARDS
+    cuts = [half[..., at * span : at * span + span] for at in range(SHARDS) for half in halves]
+    return jnp.concatenate(cuts, axis=-1)
+
+
 def mlp(hidden, upstream, up, bias, down):
     length, width = hidden.shape
     units = up.shape[1]
-    block = 512
+    block = 768
     fixed = pl.BlockSpec((length, width), lambda at: (0, 0))
     columns = pl.BlockSpec((width, block), lambda at: (0, at))
     lanes = pl.BlockSpec((1, block), lambda at: (0, at))
@@ -518,7 +539,7 @@
         in_specs=[fixed, fixed, columns, lanes, rows],
         out_specs=(fixed, fixed, half, half, rows, lanes),
         scratch_shapes=[pltpu.VMEM((width, length), jnp.bfloat16)],
-        compiler_params=pltpu.CompilerParams(vmem_limit_bytes=56 << 20),
+        compiler_params=pltpu.CompilerParams(vmem_limit_bytes=58 << 20),
         cost_estimate=SHORT,
     )(hidden, upstream, up, bias, down)
 
@@ -557,12 +578,19 @@
         ]
     )
     small_all = gather_group(small)
+    up_halves = split_units(up_weight, 1)
+    down_rows = down_weight.shape[0] // 2
+    full_up = [lax.all_gather(half, GROUP, axis=0, tiled=True) for half in up_halves]
+    full_down = [lax.all_gather(down_weight[:down_rows], GROUP, axis=0, tiled=True)]
+    late_down = down_weight[down_rows:]
+    side_by_side = jnp.concatenate([qkv_weight, out_weight], axis=1)
+    small_all, side_by_side, latent_in = tie(small_all, side_by_side, latent_in)
     latent_low = swap_halves(latent_in)
-    pieces, order = gather_pieces(jnp.concatenate([qkv_weight, out_weight], axis=1))
-    full_up = lax.all_gather(up_weight, GROUP, axis=0, tiled=True)
+    pieces, order = gather_pieces(side_by_side)
+    pieces[3], late_down, cotangent = tie(pieces[3], late_down, cotangent)
+    down_pieces, _ = gather_first(late_down)
     cotangent_low = swap_halves(cotangent)
     full_qkv, full_out = assemble(pieces, order, (3 * width, width))
-    full_down = lax.all_gather(down_weight, GROUP, axis=0, tiled=True)
 
     bounds = [0, width]
     for bias in (qv_bias, out_bias, up_bias, down_bias):
@@ -584,6 +612,7 @@
         0,
     )
     modulation = matmul(silu_mine, ada_weight) + ada_bias_row
+    modulation, pieces[3] = tie(modulation, pieces[3])
     for bit, count in ((4, 2), (1, 1)):
         upper = (place & bit) != 0
         sent = jnp.where(upper, modulation[:count], modulation[count:])
@@ -606,7 +635,11 @@
     pair_other = permute(pair_own, core_rule)
     heads = range(width // HEAD)
     halves = heads[: len(heads) // 2], heads[len(heads) // 2 :]
+    query, down_pieces[1], down_pieces[2] = tie(query, down_pieces[1], down_pieces[2])
+    down_pieces = gather_second(down_pieces)
     attended_low, log_totals = attend(query, pair_own, pair_other, heads)
+    attended_low, down_pieces[3] = tie(attended_low, down_pieces[3])
+    down_pieces = gather_third(down_pieces)
     log_rows = log_totals[:, : len(heads)].T[:, None, :]
     branch_one = matmul(attended_low, full_out) + full_out_bias
     middle = latent + gate_one * branch_one
@@ -616,16 +649,27 @@
     mask_row = slot_mask[0]
     d_out = cotangent_low[0].astype(jnp.float32) * mask_row
     d_branch_two = (gate_two * d_out).astype(jnp.bfloat16)
-    branch_two, d_hidden_two, up_kept, up_sent, down_grad, up_bias_grad = mlp(
-        hidden_two, d_branch_two, full_up, full_up_bias[None], full_down
-    )
-    up_scatter = Scatter((up_kept, up_sent))
-    down_shard = lax.psum_scatter(down_grad, GROUP, scatter_dimension=0, tiled=True)
-    branch_two = branch_two + full_down_bias
+    full_down += assemble(down_pieces, order, (width,))
+    bias_halves = split_units(full_up_bias[None], 1)
+    parts, up_scatters, down_shards = [], [], []
+    for half in (0, 1):
+        branch, d_hidden, kept, sent, down_grad, bias_grad = mlp(
+            hidden_two, d_branch_two, full_up[half], bias_halves[half], full_down[half]
+        )
+        if half == 1:
+            branch, up_scatters[0].received = tie(branch, up_scatters[0].received)
+            up_scatters[0].second()
+        up_scatters.append(Scatter((kept, sent)))
+        down_shards.append(
+            lax.psum_scatter(down_grad, GROUP, scatter_dimension=0, tiled=True)
+        )
+        parts.append((branch, d_hidden, bias_grad))
+    branch_two = parts[0][0] + parts[1][0] + full_down_bias
+    d_hidden_two = parts[0][1] + parts[1][1]
     block_out = (mask_row * (middle + gate_two * branch_two)).astype(jnp.bfloat16)
     d_gate_two = jnp.sum(d_out * branch_two, axis=0)
     down_bias_grad = jnp.sum(d_branch_two.astype(jnp.float32), axis=0)
-    up_bias_grad = up_bias_grad[0]
+    up_bias_grad = join_units([part[2] for part in parts])[0]
     d_shift_two = jnp.sum(d_hidden_two, axis=0)
     d_scale_two = jnp.sum(d_hidden_two * normed_two, axis=0)
     d_middle = d_out + norm_back(d_hidden_two * (1.0 + scale_two), normed_two, inverse_two)
@@ -636,34 +680,44 @@
     d_attended = d_attended.astype(jnp.bfloat16)
     out_scatter = Scatter(out_halves)
     out_bias_grad = jnp.sum(d_branch_one.astype(jnp.float32), axis=0)
-    d_attended, up_scatter.received = tie(d_attended, up_scatter.received)
-    up_scatter.second()
+    d_attended, up_scatters[0].received, up_scatters[1].received = tie(
+        d_attended, up_scatters[0].received, up_scatters[1].received
+    )
+    up_scatters[1].second()
+    up_scatters[0].third()
     left = attend_back(query, pair_own, pair_other, d_attended, log_rows, halves[0])
-    d_query, d_attended, out_scatter.received = tie(left[0], d_attended, out_scatter.received)
+    d_query, d_attended, out_scatter.received, down_shards[0] = tie(
+        left[0], d_attended, out_scatter.received, down_shards[0]
+    )
     out_scatter.second()
     right = attend_back(query, pair_own, pair_other, d_attended, log_rows, halves[1])
-    *right, up_scatter.received = tie(*right, up_scatter.received)
-    up_scatter.third()
+    *right, up_scatters[1].received, down_shards[1] = tie(
+        *right, up_scatters[1].received, down_shards[1]
+    )
+    up_scatters[1].third()
     d_query = join_heads(d_query, right[0], width)
     d_own = join_heads(left[1], right[1], width)
     d_other = permute(join_heads(left[2], right[2], width), core_rule)
     d_own = (d_own + d_other.astype(jnp.float32)).astype(jnp.bfloat16)
     d_projected = jnp.concatenate([d_query, d_own[0], d_own[1]], axis=-1)
 
-    d_projected, down_shard = tie(d_projected, down_shard)
+    down_total = lax.psum(jnp.concatenate(down_shards), "rep")
     d_hidden_one, qkv_halves = product_back(hidden_one, d_projected, full_qkv)
     qkv_scatter = Scatter(qkv_halves)
     column_sums = jnp.sum(d_projected.astype(jnp.float32), axis=0)
     d_hidden_one, *arrived = tie(
         d_hidden_one,
         qkv_scatter.received,
-        up_scatter.received,
+        up_scatters[0].received,
+        up_scatters[1].received,
         out_scatter.received,
     )
-    qkv_scatter.received, up_scatter.received, out_scatter.received = arrived
+    for scatter, received in zip((qkv_scatter, *up_scatters, out_scatter), arrived):
+        scatter.received = received
     qkv_scatter.second()
-    down_total = lax.psum(down_shard, "rep")
-    up_sum = ReplicaSum(up_scatter.result(), replicas)
+    up_sum = ReplicaSum(
+        jnp.concatenate([scatter.result() for scatter in up_scatters], axis=1), replicas
+    )
     out_scatter.third()
     d_shift_one = jnp.sum(d_hidden_one, axis=0)
     d_scale_one = jnp.sum(d_hidden_one * normed_one, axis=0)
@@ -677,12 +731,11 @@
     sums = [d_shift_one, d_scale_one, d_gate_one, d_shift_two, d_scale_two, d_gate_two]
     ada_width = 6 * width
     small_sums = jnp.concatenate(sums + list(bias_grads))
-    qkv_scatter.received, out_scatter.received, *up_sum.received = tie(
-        qkv_scatter.received, out_scatter.received, *up_sum.received
+    qkv_scatter.received, out_scatter.received = tie(
+        qkv_scatter.received, out_scatter.received
     )
     qkv_scatter.third()
-    up_sum.second()
-    qkv_shard = qkv_scatter.result()
+    qkv_shard, *up_sum.received = tie(qkv_scatter.result(), *up_sum.received)
     qkv_shard, latent_grad, block_out, small_sums = tie(
         qkv_shard, latent_grad.astype(jnp.bfloat16), block_out, small_sums
     )
@@ -692,9 +745,12 @@
     latent_grad = swap_halves(latent_grad[None]).astype(jnp.float32)
     block_out = swap_halves(block_out[None])
     sums_all = gather_group(small_sums)
+    up_sum.second()
     down_total, *late_sum.received = tie(down_total, *late_sum.received)
     late_sum.second()
+    *up_sum.received, late_sum.received[0] = tie(*up_sum.received, late_sum.received[0])
     up_total = up_sum.result()
+    up_total = join_units(jnp.split(up_total, 2, axis=1))
     late_total = late_sum.result()
     out_total, qkv_total = late_total[:, :width], late_total[:, width:]
 

time: 615 us -> 677 us (1.10)
  local copies, waits for them, and re-layouts: 50.7 us -> 75 us
  waiting for transfers between devices: 236 us -> 253 us
  Pallas kernels: 153 us -> 167 us
    ppermute x30 -> x40, waiting for transfers between devices: 118 us -> 177 us  [permute(): return lax.ppermute(values, GROUP, pairs_by(rule))]
    ppermute x12, waiting for transfers between devices: 94 us -> 69.3 us  [send(): return lax.ppermute(values, 'rep', pairs)]
    ppermute x4, waiting for transfers between devices: 22.9 us -> 6.06 us  [swap_halves(): received = lax.ppermute(values, GROUP, pairs)]
    concatenate x1 -> x6, local copies, waits for them, and re-layouts: 0.75 us -> 11.4 us  [the longest x4 5.76 us: split_units(): return [jnp.concatenate(cuts[half::2], axis=axis) for half in (0, 1)]]
    slice x0 -> x6, local copies, waits for them, and re-layouts: none -> 10.2 us  [the longest x3 5.4 us: join_units(): half[..., at * span:at * span + span]]
    pallas_call x1 -> x2, Pallas kernels: 47.6 us -> 57.2 us  [mlp(): pl.pallas_call(mlp_kernel, grid=(units // block,), out_shape=(jax.ShapeDt...]
    ppermute x30 -> x40, starting transfers between devices: 34.3 us -> 29.9 us  [permute(): return lax.ppermute(values, GROUP, pairs_by(rule))]
    unnamed x122 -> x139, local copies, waits for them, and re-layouts: 21.4 us -> 17.6 us
  transfers between devices with their start and end apart: 53 -> 65, of which waited for: 18 -> 27; matrix products, arithmetic and copies ran while one was open for 19% -> 20% of each run, Pallas kernels for 14% -> 22%
where the time goes in v8:
time: 677 us; the launch traced here: 668 us
  waiting for transfers between devices  253 us (37%)
  Pallas kernels  167 us (25%)
  other arithmetic  76.3 us (11%)
  local copies, waits for them, and re-layouts  75 us (11%)
  starting transfers between devices  63.5 us (9%)
  matrix products  16.7 us (2%)
  between operations  16.7 us (2%)
    ppermute x40, waiting for transfers between devices, permute(): return lax.ppermute(values, GROUP, pairs_by(rule))  177 us
    ppermute x12, waiting for transfers between devices, send(): return lax.ppermute(values, 'rep', pairs)  69.3 us
    pallas_call x2, Pallas kernels, mlp(): pl.pallas_call(mlp_kernel, grid=(units // block,), out_shape=(jax.ShapeDt...  57.2 us
    pallas_call x2, Pallas kernels, attend_back(): pl.pallas_call(functools.partial(attend_back_kernel, heads[0], low), grid...  48.4 us
    ppermute x40, starting transfers between devices, permute(): return lax.ppermute(values, GROUP, pairs_by(rule))  29.9 us
    pallas_call x1, Pallas kernels, attend(): pl.pallas_call(functools.partial(attend_kernel, heads[0], low), grid=(len...  26.8 us
    pallas_call x2, Pallas kernels, product_back(): pl.pallas_call(product_back_kernel, grid=(columns // block,), out_shape=(...  26.1 us
    unnamed x139, local copies, waits for them, and re-layouts  17.6 us
  transfers between devices with their start and end apart: 65, of which 27 were waited for; matrix products, arithmetic and copies ran while one was open for 20% of the time, Pallas kernels for 22%

profile of v8, /device:TPU:9, one launch (start us, length us, event | category | flops | bytes accessed | tf_op | source)
XLA Modules:
  0.0 667.8 jit_solution(8586180769044592181)
XLA Ops:
  7.2 3.5 fusion.56
  28.5 4.8 collective-permute-start.3
  35.6 36.4 %collective-permute-done.4.refs_1_ = bf16[144,4608]{1,0:T(8,128)(2,1)} collective-permute-done((bf16[144,4608]{1,0:T(8,128)(2,1)S(1)}, bf16[144,4608]{1,0:T(8,128)(2,1)}, u32[]{:S(2)}, u32[]{:S(2)}) %collective-permute-start.4) | collective-permute-done | bytes 1327136 | tf_op jit(solution)/shard_map/ppermute | solution.py:62
  76.5 6.1 collective-permute-done.3
  84.4 12.7 %collective-permute-done.5.refs_3_ = bf16[144,4608]{1,0:T(8,128)(2,1)} collective-permute-done((bf16[144,4608]{1,0:T(8,128)(2,1)}, bf16[144,4608]{1,0:T(8,128)(2,1)}, u32[]{:S(2)}, u32[]{:S(2)}) %collective-permute-start.5) | collective-permute-done | bytes 1327136 | tf_op jit(solution)/shard_map/ppermute | solution.py:62
  98.6 27.7 %collective-permute-done.6 = f32[2,6912]{1,0:T(2,128)S(1)} collective-permute-done((f32[2,6912]{1,0:T(2,128)S(1)}, f32[2,6912]{1,0:T(2,128)S(1)}, u32[]{:S(2)}, u32[]{:S(2)}) %collective-permute-start.6) | collective-permute-done | bytes 55328 | tf_op jit(solution)/shard_map/ppermute | solution.py:62
  129.3 2.7 collective-permute-done.8
  134.1 4.3 shard_map.237
  139.9 5.1 add_convert_fusion.1
  147.6 3.6 collective-permute-start.18
  154.4 38.1 %collective-permute-done.14.refs_1_ = bf16[288,1152]{1,0:T(8,128)(2,1)} collective-permute-done((bf16[288,1152]{1,0:T(8,128)(2,1)}, bf16[288,1152]{1,0:T(8,128)(2,1)}, u32[]{:S(2)}, u32[]{:S(2)}) %collective-permute-start.14) | collective-permute-done | bytes 663584 | tf_op jit(solution)/shard_map/ppermute | solution.py:62
  195.2 3.9 convert_reduce_fusion.2
  199.1 26.8 %shard_map.238 = (bf16[512,1152]{1,0:T(8,128)(2,1)S(1)}, f32[512,128]{1,0:T(8,128)S(1)}) custom-call(bf16[512,1152]{1,0:T(8,128)(2,1)S(1)} %slice.512.query_ref, bf16[512,2304]{1,0:T(8,128)(2,1)} %slice.513.own_ref, bf16[512,2304]{1,0:T(8,128)(2,1)} %collective-permute-done.16.other_ref), custom_call_target="tpu_custom_call" | custom-call | flops 1048576 | bytes 1048576 | tf_op jit(solution)/shard_map/pallas_call | solution.py:306
  225.9 3.3 fusion.53
  232.1 28.5 %shard_map.239 = (f32[512,1152]{1,0:T(8,128)}, f32[512,1152]{1,0:T(8,128)}, bf16[4,144,2304]{2,1,0:T(8,128)(2,1)}, bf16[4,144,2304]{2,1,0:T(8,128)(2,1)}, bf16[2304,1152]{1,0:T(8,128)(2,1)}, /*index=5*/f32[1,2304]{1,0:T(1,128)}) custom-call(bf16[512,1152]{1,0:T(8,128)(2,1)} %add_convert_fusion.5.hidden_ref, ...), custom_call_target="tpu_custom_call" | custom-call | flops 1048576 | bytes 1048576 | tf_op jit(solution)/shard_map/pallas_call | solution.py:528
  263.4 4.8 collective-permute-done.19.refs_4_
  271.3 3.8 shard_map.240.down_ref
  277.6 28.7 %shard_map.241 = (f32[512,1152]{1,0:T(8,128)}, f32[512,1152]{1,0:T(8,128)}, bf16[4,144,2304]{2,1,0:T(8,128)(2,1)}, bf16[4,144,2304]{2,1,0:T(8,128)(2,1)}, bf16[2304,1152]{1,0:T(8,128)(2,1)}, /*index=5*/f32[1,2304]{1,0:T(1,128)}) custom-call(bf16[512,1152]{1,0:T(8,128)(2,1)} %add_convert_fusion.5.hidden_ref, ...), custom_call_target="tpu_custom_call" | custom-call | flops 1048576 | bytes 1048576 | tf_op jit(solution)/shard_map/pallas_call | solution.py:528
  306.8 3.2 add_convert_fusion.3
  316.8 4.6 fusion.21
  321.4 7.2 %shard_map.242 = (f32[512,1152]{1,0:T(8,128)S(1)}, bf16[4,144,1152]{2,1,0:T(8,128)(2,1)S(1)}, bf16[4,144,1152]{2,1,0:T(8,128)(2,1)}) custom-call(bf16[512,1152]{1,0:T(8,128)(2,1)S(1)} %copy-done.15, bf16[512,1152]{1,0:T(8,128)(2,1)S(1)} %get-tuple-element.203.upstream_ref, bf16[1152,1152]{1,0:T(8,128)(2,1)S(1)} %copy-done.13), custom_call_target="tpu_custom_call" | custom-call | flops 1048576 | bytes 1048576 | tf_op jit(solution)/shard_map/pallas_call | solution.py:452
  329.9 4.4 collective-permute-done.24
  341.3 24.3 %shard_map.243 = (bf16[512,640]{1,0:T(8,128)(2,1)}, f32[2,512,640]{2,1,0:T(8,128)}, bf16[2,512,640]{2,1,0:T(8,128)(2,1)}) custom-call(bf16[512,1152]{1,0:T(8,128)(2,1)} %copy-done.2, bf16[512,2304]{1,0:T(8,128)(2,1)} %slice.513.own_ref, bf16[512,2304]{1,0:T(8,128)(2,1)} %collective-permute-done.16.other_ref, ...), custom_call_target="tpu_custom_call" | custom-call | flops 1048576 | bytes 1048576 | tf_op jit(solution)/shard_map/pallas_call | solution.py:378
  367.9 24.1 %shard_map.244 = (bf16[512,640]{1,0:T(8,128)(2,1)}, f32[2,512,640]{2,1,0:T(8,128)}, bf16[2,512,640]{2,1,0:T(8,128)(2,1)}) custom-call(bf16[512,1152]{1,0:T(8,128)(2,1)} %copy-done.2, bf16[512,2304]{1,0:T(8,128)(2,1)} %slice.513.own_ref, bf16[512,2304]{1,0:T(8,128)(2,1)} %collective-permute-done.16.other_ref, ...), custom_call_target="tpu_custom_call" | custom-call | flops 1048576 | bytes 1048576 | tf_op jit(solution)/shard_map/pallas_call | solution.py:378
  408.0 3.3 copy-done.7
  411.3 19.0 %shard_map.245 = (f32[512,1152]{1,0:T(8,128)S(1)}, bf16[4,144,3456]{2,1,0:T(8,128)(2,1)S(1)}, bf16[4,144,3456]{2,1,0:T(8,128)(2,1)}) custom-call(bf16[512,1152]{1,0:T(8,128)(2,1)S(1)} %copy-done.9, bf16[512,3456]{1,0:T(8,128)(2,1)S(1)} %fusion.25.upstream_ref, bf16[1152,3456]{1,0:T(8,128)(2,1)S(1)} %copy-done.7), custom_call_target="tpu_custom_call" | custom-call | flops 1048576 | bytes 1048576 | tf_op jit(solution)/shard_map/pallas_call | solution.py:452
  441.0 2.5 pad_maximum_fusion.7
  443.6 2.7 convert_reduce_fusion
  446.2 8.6 %collective-permute-done.31 = bf16[144,2304]{1,0:T(8,128)(2,1)} collective-permute-done((bf16[144,2304]{1,0:T(8,128)(2,1)}, bf16[144,2304]{1,0:T(8,128)(2,1)}, u32[]{:S(2)}, u32[]{:S(2)}) %collective-permute-start.31) | collective-permute-done | bytes 663584 | tf_op jit(solution)/shard_map/ppermute | solution.py:62
  455.5 4.3 add_convert_fusion
  471.4 2.5 multiply_reduce_fusion.1
  474.0 14.2 %collective-permute-done.33 = bf16[2,144,3456]{2,1,0:T(8,128)(2,1)S(1)} collective-permute-done((bf16[2,144,3456]{2,1,0:T(8,128)(2,1)S(1)}, bf16[2,144,3456]{2,1,0:T(8,128)(2,1)S(1)}, u32[]{:S(2)}, u32[]{:S(2)}) %collective-permute-start.33) | collective-permute-done | bytes 1990688 | tf_op jit(solution)/shard_map/ppermute | solution.py:62
  489.5 12.7 %collective-permute-done.35 = bf16[144,3456]{1,0:T(8,128)(2,1)S(1)} collective-permute-done((bf16[144,3456]{1,0:T(8,128)(2,1)S(1)}, bf16[144,3456]{1,0:T(8,128)(2,1)S(1)}, u32[]{:S(2)}, u32[]{:S(2)}) %collective-permute-start.35) | collective-permute-done | bytes 995360 | tf_op jit(solution)/shard_map/ppermute | solution.py:62
  504.7 7.2 %collective-permute-done.38 = bf16[144,1152]{1,0:T(8,128)(2,1)S(1)} collective-permute-done((bf16[144,1152]{1,0:T(8,128)(2,1)S(1)}, bf16[144,1152]{1,0:T(8,128)(2,1)S(1)}, u32[]{:S(2)}, u32[]{:S(2)}) %collective-permute-start.38) | collective-permute-done | bytes 331808 | tf_op jit(solution)/shard_map/ppermute | solution.py:218
  512.7 3.2 collective-permute-done.41
  516.1 3.7 collective-permute-start.42
  519.9 3.2 collective-permute-start.53
  524.5 45.0 %collective-permute-done.53 = bf16[144,1152]{1,0:T(8,128)(2,1)S(1)} collective-permute-done((bf16[144,1152]{1,0:T(8,128)(2,1)S(1)}, bf16[144,1152]{1,0:T(8,128)(2,1)S(1)}, u32[]{:S(2)}, u32[]{:S(2)}) %collective-permute-start.53) | collective-permute-done | bytes 331808 | tf_op jit(solution)/shard_map/ppermute | solution.py:218
  569.5 7.1 %collective-permute-done.54 = bf16[144,1152]{1,0:T(8,128)(2,1)S(1)} collective-permute-done((bf16[144,1152]{1,0:T(8,128)(2,1)S(1)}, bf16[144,1152]{1,0:T(8,128)(2,1)S(1)}, u32[]{:S(2)}, u32[]{:S(2)}) %collective-permute-start.54) | collective-permute-done | bytes 331808 | tf_op jit(solution)/shard_map/ppermute | solution.py:218
  576.6 4.4 collective-permute-start.39
  599.0 3.2 collective-permute-start.48
  604.7 4.7 fusion.55
  611.2 4.8 concatenate.171
  616.1 4.3 collective-permute-start.40
  635.5 6.2 fusion.63
  642.8 6.7 %collective-permute-done.57 = bf16[144,1152]{1,0:T(8,128)(2,1)} collective-permute-done((bf16[144,1152]{1,0:T(8,128)(2,1)}, bf16[144,1152]{1,0:T(8,128)(2,1)}, u32[]{:S(2)}, u32[]{:S(2)}) %collective-permute-start.57) | collective-permute-done | bytes 331808 | tf_op jit(solution)/shard_map/ppermute | solution.py:218
  654.9 2.8 broadcast_select_fusion
  657.6 2.8 select_convert_fusion
  (405 shorter events, 159.6 us)
Async XLA Ops:
  7.2 224.9 %all-gather.4.cloned.1.call-start = ((), (), s32[]{:S(2)}) async-start(), calls=%async_computation.2 | async-start | bytes 5971968 | tf_op jit(solution)/shard_map/all_gather | solution.py:583
  13.0 219.1 %all-gather.6.cloned.1.call-start = ((), (), s32[]{:S(2)}) async-start(), calls=%async_computation.3 | async-start | bytes 5971968 | tf_op jit(solution)/shard_map/all_gather | solution.py:584
  14.3 263.4 %all-gather.8.cloned.1.call-start = ((), (), s32[]{:S(2)}) async-start(), calls=%async_computation.4 | async-start | bytes 5971968 | tf_op jit(solution)/shard_map/all_gather | solution.py:583
  27.3 44.8 %collective-permute-start.4 = (bf16[144,4608]{1,0:T(8,128)(2,1)S(1)}, bf16[144,4608]{1,0:T(8,128)(2,1)}, u32[]{:S(2)}, u32[]{:S(2)}) collective-permute-start(bf16[144,4608]{1,0:T(8,128)(2,1)S(1)} %pad_maximum_fusion.4.refs_0_), channel_id=1, source_target_pairs={{0,4},{1,5},{2,3},{3,2},{4,0},{5,1},{6,7},{7,6},{8,12},{9,13},{10,... | collective-permute-start | bytes 3981320 | tf_op jit(solution)/shard_map/ppermute | solution.py:62
  28.5 54.1 %collective-permute-start.3 = (bf16[1,512,1152]{2,1,0:T(8,128)(2,1)}, bf16[1,512,1152]{2,1,0:T(8,128)(2,1)}, u32[]{:S(2)}, u32[]{:S(2)}) collective-permute-start(bf16[1,512,1152]{2,1,0:T(8,128)(2,1)} %param.14), channel_id=1, source_target_pairs={{1,2},{2,1},{5,6},{6,5},{9,10},{10,9},{13,14},{14,13},{17,18},{18,... | collective-permute-start | bytes 3538952 | tf_op jit(solution)/shard_map/ppermute | solution.py:68
  35.4 332.4 %reduce-scatter.3.cloned.1.call-start = ((), (), s32[]{:S(2)}) async-start(), calls=%async_computation.5 | async-start | bytes 5971968 | tf_op jit(solution)/shard_map/reduce_scatter | solution.py:664
  72.0 25.0 %collective-permute-start.5 = (bf16[144,4608]{1,0:T(8,128)(2,1)}, bf16[144,4608]{1,0:T(8,128)(2,1)}, u32[]{:S(2)}, u32[]{:S(2)}) collective-permute-start(bf16[144,4608]{1,0:T(8,128)(2,1)} %collective-permute-done.4.refs_1_), channel_id=1, source_target_pairs={{0,1},{1,0},{2,6},{3,7},{4,5},{5,4},{6,2},{7,3},{8,9},{9,8},{10,14... | collective-permute-start | bytes 3981320 | tf_op jit(solution)/shard_map/ppermute | solution.py:62
  74.3 52.7 %collective-permute-start.9 = (bf16[144,4608]{1,0:T(8,128)(2,1)S(1)}, bf16[144,4608]{1,0:T(8,128)(2,1)}, u32[]{:S(2)}, u32[]{:S(2)}) collective-permute-start(bf16[144,4608]{1,0:T(8,128)(2,1)S(1)} %pad_maximum_fusion.4.refs_0_), channel_id=1, source_target_pairs={{0,1},{1,0},{2,6},{3,7},{4,5},{5,4},{6,2},{7,3},{8,9},{9,8},{10,14... | collective-permute-start | bytes 3981320 | tf_op jit(solution)/shard_map/ppermute | solution.py:62
  74.3 58.3 %collective-permute-start.10 = (bf16[144,4608]{1,0:T(8,128)(2,1)S(1)}, bf16[144,4608]{1,0:T(8,128)(2,1)}, u32[]{:S(2)}, u32[]{:S(2)}) collective-permute-start(bf16[144,4608]{1,0:T(8,128)(2,1)S(1)} %pad_maximum_fusion.4.refs_0_), channel_id=1, source_target_pairs={{0,2},{1,3},{2,0},{3,1},{4,6},{5,7},{6,4},{7,5},{8,10},{9,11},{10,... | collective-permute-start | bytes 3981320 | tf_op jit(solution)/shard_map/ppermute | solution.py:62
  97.1 29.2 %collective-permute-start.6 = (f32[2,6912]{1,0:T(2,128)S(1)}, f32[2,6912]{1,0:T(2,128)S(1)}, u32[]{:S(2)}, u32[]{:S(2)}) collective-permute-start(f32[2,6912]{1,0:T(2,128)S(1)} %broadcast_select_fusion.3), channel_id=1, source_target_pairs={{0,4},{1,5},{2,6},{3,7},{4,0},{5,1},{6,2},{7,3},{8,12},{9,13},{10,... | collective-permute-start | bytes 165896 | tf_op jit(solution)/shard_map/ppermute | solution.py:62
  147.5 51.5 %collective-permute-start.16 = (bf16[512,2304]{1,0:T(8,128)(2,1)}, bf16[512,2304]{1,0:T(8,128)(2,1)}, u32[]{:S(2)}, u32[]{:S(2)}) collective-permute-start(bf16[512,2304]{1,0:T(8,128)(2,1)} %slice.513.own_ref), channel_id=1, source_target_pairs={{0,2},{1,3},{2,0},{3,1},{4,6},{5,7},{6,4},{7,5},{8,10},{9,11},{10,... | collective-permute-start | bytes 7077896 | tf_op jit(solution)/shard_map/ppermute | solution.py:62
  147.6 47.5 %collective-permute-start.18 = (bf16[1,512,1152]{2,1,0:T(8,128)(2,1)}, bf16[1,512,1152]{2,1,0:T(8,128)(2,1)}, u32[]{:S(2)}, u32[]{:S(2)}) collective-permute-start(bf16[1,512,1152]{2,1,0:T(8,128)(2,1)} %param.27), channel_id=1, source_target_pairs={{1,2},{2,1},{5,6},{6,5},{9,10},{10,9},{13,14},{14,13},{17,18},{18,... | collective-permute-start | bytes 3538952 | tf_op jit(solution)/shard_map/ppermute | solution.py:68
  151.2 41.2 %collective-permute-start.14 = (bf16[288,1152]{1,0:T(8,128)(2,1)}, bf16[288,1152]{1,0:T(8,128)(2,1)}, u32[]{:S(2)}, u32[]{:S(2)}) collective-permute-start(bf16[288,1152]{1,0:T(8,128)(2,1)} %get-tuple-element.97.refs_0_), channel_id=1, source_target_pairs={{0,4},{1,5},{2,3},{3,2},{4,0},{5,1},{6,7},{7,6},{8,12},{9,13},{10,... | collective-permute-start | bytes 1990664 | tf_op jit(solution)/shard_map/ppermute | solution.py:62
  151.3 41.1 %collective-permute-start.15 = (bf16[288,1152]{1,0:T(8,128)(2,1)}, bf16[288,1152]{1,0:T(8,128)(2,1)}, u32[]{:S(2)}, u32[]{:S(2)}) collective-permute-start(bf16[288,1152]{1,0:T(8,128)(2,1)} %get-tuple-element.97.refs_0_), channel_id=1, source_target_pairs={{0,1},{1,0},{2,6},{3,7},{4,5},{5,4},{6,2},{7,3},{8,9},{9,8},{10,14... | collective-permute-start | bytes 1990664 | tf_op jit(solution)/shard_map/ppermute | solution.py:62
  192.5 33.4 %collective-permute-start.17 = (bf16[288,1152]{1,0:T(8,128)(2,1)}, bf16[288,1152]{1,0:T(8,128)(2,1)}, u32[]{:S(2)}, u32[]{:S(2)}) collective-permute-start(bf16[288,1152]{1,0:T(8,128)(2,1)} %collective-permute-done.14.refs_1_), channel_id=1, source_target_pairs={{0,1},{1,0},{2,6},{3,7},{4,5},{5,4},{6,2},{7,3},{8,9},{9,8},{10,14... | collective-permute-start | bytes 1990664 | tf_op jit(solution)/shard_map/ppermute | solution.py:62
  260.6 131.4 %reduce-scatter.5.cloned.1.call-start = ((), (), s32[]{:S(2)}) async-start(), calls=%async_computation.6 | async-start | bytes 5971968 | tf_op jit(solution)/shard_map/reduce_scatter | solution.py:664
  260.6 46.2 %collective-permute-start.23 = (bf16[4,144,2304]{2,1,0:T(8,128)(2,1)}, bf16[4,144,2304]{2,1,0:T(8,128)(2,1)}, u32[]{:S(2)}, u32[]{:S(2)}) collective-permute-start(bf16[4,144,2304]{2,1,0:T(8,128)(2,1)} %get-tuple-element.111), channel_id=1, source_target_pairs={{0,2},{1,3},{2,0},{3,1},{4,6},{5,7},{6,4},{7,5},{8,10},{9,11},{10,... | collective-permute-start | bytes 7962632 | tf_op jit(solution)/shard_map/ppermute | solution.py:62
  306.4 276.6 %all-reduce.2.cloned.1.call-start = ((), (), s32[]{:S(2)}) async-start(), calls=%async_computation.7 | async-start | bytes 2654208 | tf_op jit(solution)/shard_map/psum | solution.py:704
  306.5 23.4 %collective-permute-start.25 = (bf16[4,144,2304]{2,1,0:T(8,128)(2,1)}, bf16[4,144,2304]{2,1,0:T(8,128)(2,1)S(1)}, u32[]{:S(2)}, u32[]{:S(2)}) collective-permute-start(bf16[4,144,2304]{2,1,0:T(8,128)(2,1)} %get-tuple-element.113), channel_id=1, source_target_pairs={{0,2},{1,3},{2,0},{3,1},{4,6},{5,7},{6,4},{7,5},{8,10},{9,11},{10,... | collective-permute-start | bytes 7962632 | tf_op jit(solution)/shard_map/ppermute | solution.py:62
  311.4 23.0 %collective-permute-start.24 = (bf16[2,144,2304]{2,1,0:T(8,128)(2,1)S(1)}, bf16[2,144,2304]{2,1,0:T(8,128)(2,1)S(1)}, u32[]{:S(2)}, u32[]{:S(2)}) collective-permute-start(bf16[2,144,2304]{2,1,0:T(8,128)(2,1)S(1)} %pad_maximum_fusion.5), channel_id=1, source_target_pairs={{0,4},{1,5},{2,3},{3,2},{4,0},{5,1},{6,7},{7,6},{8,12},{9,13},{10,... | collective-permute-start | bytes 3981320 | tf_op jit(solution)/shard_map/ppermute | solution.py:62
  329.7 38.2 %collective-permute-start.26 = (bf16[4,144,1152]{2,1,0:T(8,128)(2,1)}, bf16[4,144,1152]{2,1,0:T(8,128)(2,1)}, u32[]{:S(2)}, u32[]{:S(2)}) collective-permute-start(bf16[4,144,1152]{2,1,0:T(8,128)(2,1)} %get-tuple-element.117), channel_id=1, source_target_pairs={{0,2},{1,3},{2,0},{3,1},{4,6},{5,7},{6,4},{7,5},{8,10},{9,11},{10,... | collective-permute-start | bytes 3981320 | tf_op jit(solution)/shard_map/ppermute | solution.py:62
  337.8 54.1 %collective-permute-start.27 = (bf16[2,144,2304]{2,1,0:T(8,128)(2,1)}, bf16[2,144,2304]{2,1,0:T(8,128)(2,1)}, u32[]{:S(2)}, u32[]{:S(2)}) collective-permute-start(bf16[2,144,2304]{2,1,0:T(8,128)(2,1)} %pad_maximum_fusion.6), channel_id=1, source_target_pairs={{0,4},{1,5},{2,3},{3,2},{4,0},{5,1},{6,7},{7,6},{8,12},{9,13},{10,... | collective-permute-start | bytes 3981320 | tf_op jit(solution)/shard_map/ppermute | solution.py:62
  430.2 25.3 %collective-permute-start.29 = (bf16[4,144,3456]{2,1,0:T(8,128)(2,1)}, bf16[4,144,3456]{2,1,0:T(8,128)(2,1)}, u32[]{:S(2)}, u32[]{:S(2)}) collective-permute-start(bf16[4,144,3456]{2,1,0:T(8,128)(2,1)} %get-tuple-element.134), channel_id=1, source_target_pairs={{0,2},{1,3},{2,0},{3,1},{4,6},{5,7},{6,4},{7,5},{8,10},{9,11},{10,... | collective-permute-start | bytes 11943944 | tf_op jit(solution)/shard_map/ppermute | solution.py:62
  431.3 15.0 %collective-permute-start.30 = (bf16[144,2304]{1,0:T(8,128)(2,1)}, bf16[144,2304]{1,0:T(8,128)(2,1)}, u32[]{:S(2)}, u32[]{:S(2)}) collective-permute-start(bf16[144,2304]{1,0:T(8,128)(2,1)} %fusion.28), channel_id=1, source_target_pairs={{0,1},{1,0},{2,6},{3,7},{4,5},{5,4},{6,2},{7,3},{8,9},{9,8},{10,14... | collective-permute-start | bytes 1990664 | tf_op jit(solution)/shard_map/ppermute | solution.py:62
  435.2 19.6 %collective-permute-start.31 = (bf16[144,2304]{1,0:T(8,128)(2,1)}, bf16[144,2304]{1,0:T(8,128)(2,1)}, u32[]{:S(2)}, u32[]{:S(2)}) collective-permute-start(bf16[144,2304]{1,0:T(8,128)(2,1)} %fusion.29), channel_id=1, source_target_pairs={{0,1},{1,0},{2,6},{3,7},{4,5},{5,4},{6,2},{7,3},{8,9},{9,8},{10,14... | collective-permute-start | bytes 1990664 | tf_op jit(solution)/shard_map/ppermute | solution.py:62
  438.4 17.2 %collective-permute-start.32 = (bf16[2,144,1152]{2,1,0:T(8,128)(2,1)S(1)}, bf16[2,144,1152]{2,1,0:T(8,128)(2,1)}, u32[]{:S(2)}, u32[]{:S(2)}) collective-permute-start(bf16[2,144,1152]{2,1,0:T(8,128)(2,1)S(1)} %pad_maximum_fusion.8), channel_id=1, source_target_pairs={{0,4},{1,5},{2,3},{3,2},{4,0},{5,1},{6,7},{7,6},{8,12},{9,13},{10,... | collective-permute-start | bytes 1990664 | tf_op jit(solution)/shard_map/ppermute | solution.py:62
  460.5 27.7 %collective-permute-start.33 = (bf16[2,144,3456]{2,1,0:T(8,128)(2,1)S(1)}, bf16[2,144,3456]{2,1,0:T(8,128)(2,1)S(1)}, u32[]{:S(2)}, u32[]{:S(2)}) collective-permute-start(bf16[2,144,3456]{2,1,0:T(8,128)(2,1)S(1)} %pad_maximum_fusion.3), channel_id=1, source_target_pairs={{0,4},{1,5},{2,3},{3,2},{4,0},{5,1},{6,7},{7,6},{8,12},{9,13},{10,... | collective-permute-start | bytes 5971976 | tf_op jit(solution)/shard_map/ppermute | solution.py:62
  463.1 10.9 %collective-permute-start.34 = (bf16[144,1152]{1,0:T(8,128)(2,1)S(1)}, bf16[144,1152]{1,0:T(8,128)(2,1)S(1)}, u32[]{:S(2)}, u32[]{:S(2)}) collective-permute-start(bf16[144,1152]{1,0:T(8,128)(2,1)S(1)} %fusion.41), channel_id=1, source_target_pairs={{0,1},{1,0},{2,6},{3,7},{4,5},{5,4},{6,2},{7,3},{8,9},{9,8},{10,14... | collective-permute-start | bytes 995336 | tf_op jit(solution)/shard_map/ppermute | solution.py:62
  466.6 35.8 %collective-permute-start.36 = (bf16[144,1152]{1,0:T(8,128)(2,1)S(1)}, bf16[144,1152]{1,0:T(8,128)(2,1)S(1)}, u32[]{:S(2)}, u32[]{:S(2)}) collective-permute-start(bf16[144,1152]{1,0:T(8,128)(2,1)S(1)} %get-tuple-element.236), channel_id=1, source_target_pairs={{0,8},{8,16},{16,24},{24,0},{1,9},{9,17},{17,25},{25,1},{2,10},{10... | collective-permute-start | bytes 995336 | tf_op jit(solution)/shard_map/ppermute | solution.py:218
  467.8 36.8 %collective-permute-start.37 = (bf16[144,1152]{1,0:T(8,128)(2,1)S(1)}, bf16[144,1152]{1,0:T(8,128)(2,1)S(1)}, u32[]{:S(2)}, u32[]{:S(2)}) collective-permute-start(bf16[144,1152]{1,0:T(8,128)(2,1)S(1)} %get-tuple-element.235), channel_id=1, source_target_pairs={{0,16},{8,24},{16,0},{24,8},{1,17},{9,25},{17,1},{25,9},{2,18},{10... | collective-permute-start | bytes 995336 | tf_op jit(solution)/shard_map/ppermute | solution.py:218
  469.0 42.9 %collective-permute-start.38 = (bf16[144,1152]{1,0:T(8,128)(2,1)S(1)}, bf16[144,1152]{1,0:T(8,128)(2,1)S(1)}, u32[]{:S(2)}, u32[]{:S(2)}) collective-permute-start(bf16[144,1152]{1,0:T(8,128)(2,1)S(1)} %get-tuple-element.234), channel_id=1, source_target_pairs={{0,24},{8,0},{16,8},{24,16},{1,25},{9,1},{17,9},{25,17},{2,26},{10... | collective-permute-start | bytes 995336 | tf_op jit(solution)/shard_map/ppermute | solution.py:218
  488.7 13.4 %collective-permute-start.35 = (bf16[144,3456]{1,0:T(8,128)(2,1)S(1)}, bf16[144,3456]{1,0:T(8,128)(2,1)S(1)}, u32[]{:S(2)}, u32[]{:S(2)}) collective-permute-start(bf16[144,3456]{1,0:T(8,128)(2,1)S(1)} %fusion.27), channel_id=1, source_target_pairs={{0,1},{1,0},{2,6},{3,7},{4,5},{5,4},{6,2},{7,3},{8,9},{9,8},{10,14... | collective-permute-start | bytes 2985992 | tf_op jit(solution)/shard_map/ppermute | solution.py:62
  512.1 72.5 %collective-permute-start.50 = (bf16[144,1152]{1,0:T(8,128)(2,1)S(1)}, bf16[144,1152]{1,0:T(8,128)(2,1)}, u32[]{:S(2)}, u32[]{:S(2)}) collective-permute-start(bf16[144,1152]{1,0:T(8,128)(2,1)S(1)} %fusion.39), channel_id=1, source_target_pairs={{0,8},{8,16},{16,24},{24,0},{1,9},{9,17},{17,25},{25,1},{2,10},{10... | collective-permute-start | bytes 995336 | tf_op jit(solution)/shard_map/ppermute | solution.py:218
  512.2 72.4 %collective-permute-start.51 = (bf16[144,1152]{1,0:T(8,128)(2,1)S(1)}, bf16[144,1152]{1,0:T(8,128)(2,1)}, u32[]{:S(2)}, u32[]{:S(2)}) collective-permute-start(bf16[144,1152]{1,0:T(8,128)(2,1)S(1)} %fusion.39), channel_id=1, source_target_pairs={{0,16},{8,24},{16,0},{24,8},{1,17},{9,25},{17,1},{25,9},{2,18},{10... | collective-permute-start | bytes 995336 | tf_op jit(solution)/shard_map/ppermute | solution.py:218
  519.9 49.6 %collective-permute-start.53 = (bf16[144,1152]{1,0:T(8,128)(2,1)S(1)}, bf16[144,1152]{1,0:T(8,128)(2,1)S(1)}, u32[]{:S(2)}, u32[]{:S(2)}) collective-permute-start(bf16[144,1152]{1,0:T(8,128)(2,1)S(1)} %get-tuple-element.233), channel_id=1, source_target_pairs={{0,8},{8,16},{16,24},{24,0},{1,9},{9,17},{17,25},{25,1},{2,10},{10... | collective-permute-start | bytes 995336 | tf_op jit(solution)/shard_map/ppermute | solution.py:218
  523.0 53.6 %collective-permute-start.54 = (bf16[144,1152]{1,0:T(8,128)(2,1)S(1)}, bf16[144,1152]{1,0:T(8,128)(2,1)S(1)}, u32[]{:S(2)}, u32[]{:S(2)}) collective-permute-start(bf16[144,1152]{1,0:T(8,128)(2,1)S(1)} %get-tuple-element.232), channel_id=1, source_target_pairs={{0,16},{8,24},{16,0},{24,8},{1,17},{9,25},{17,1},{25,9},{2,18},{10... | collective-permute-start | bytes 995336 | tf_op jit(solution)/shard_map/ppermute | solution.py:218
  523.7 57.4 %collective-permute-start.55 = (bf16[144,1152]{1,0:T(8,128)(2,1)S(1)}, bf16[144,1152]{1,0:T(8,128)(2,1)S(1)}, u32[]{:S(2)}, u32[]{:S(2)}) collective-permute-start(bf16[144,1152]{1,0:T(8,128)(2,1)S(1)} %get-tuple-element.231), channel_id=1, source_target_pairs={{0,24},{8,0},{16,8},{24,16},{1,25},{9,1},{17,9},{25,17},{2,26},{10... | collective-permute-start | bytes 995336 | tf_op jit(solution)/shard_map/ppermute | solution.py:218
  569.5 15.1 %collective-permute-start.52 = (bf16[144,1152]{1,0:T(8,128)(2,1)S(1)}, bf16[144,1152]{1,0:T(8,128)(2,1)}, u32[]{:S(2)}, u32[]{:S(2)}) collective-permute-start(bf16[144,1152]{1,0:T(8,128)(2,1)S(1)} %fusion.39), channel_id=1, source_target_pairs={{0,24},{8,0},{16,8},{24,16},{1,25},{9,1},{17,9},{25,17},{2,26},{10... | collective-permute-start | bytes 995336 | tf_op jit(solution)/shard_map/ppermute | solution.py:218
  576.6 78.2 %collective-permute-start.39 = (bf16[1,512,1152]{2,1,0:T(8,128)(2,1)}, bf16[1,512,1152]{2,1,0:T(8,128)(2,1)}, u32[]{:S(2)}, u32[]{:S(2)}) collective-permute-start(bf16[1,512,1152]{2,1,0:T(8,128)(2,1)} %bitcast.22), channel_id=1, source_target_pairs={{1,2},{2,1},{5,6},{6,5},{9,10},{10,9},{13,14},{14,13},{17,18},{18,... | collective-permute-start | bytes 3538952 | tf_op jit(solution)/shard_map/ppermute | solution.py:68
  581.8 11.6 %collective-permute-start.43 = (f32[4,16128]{1,0:T(4,128)S(1)}, f32[4,16128]{1,0:T(4,128)S(1)}, u32[]{:S(2)}, u32[]{:S(2)}) collective-permute-start(f32[4,16128]{1,0:T(4,128)S(1)} %maximum_select_fusion.1), channel_id=1, source_target_pairs={{0,4},{1,5},{2,6},{3,7},{4,0},{5,1},{6,2},{7,3},{8,12},{9,13},{10,... | collective-permute-start | bytes 774152 | tf_op jit(solution)/shard_map/ppermute | solution.py:62
  598.9 22.3 %collective-permute-start.49 = (f32[29376]{0:T(1024)S(1)}, f32[29376]{0:T(1024)}, u32[]{:S(2)}, u32[]{:S(2)}) collective-permute-start(f32[29376]{0:T(1024)S(1)} %concatenate.168), channel_id=1, source_target_pairs={{0,24},{8,0},{16,8},{24,16},{1,25},{9,1},{17,9},{25,17},{2,26},{10... | collective-permute-start | bytes 352520 | tf_op jit(solution)/shard_map/ppermute | solution.py:90
  599.0 23.2 %collective-permute-start.48 = (f32[29376]{0:T(1024)S(1)}, f32[29376]{0:T(1024)}, u32[]{:S(2)}, u32[]{:S(2)}) collective-permute-start(f32[29376]{0:T(1024)S(1)} %concatenate.168), channel_id=1, source_target_pairs={{0,16},{8,24},{16,0},{24,8},{1,17},{9,25},{17,1},{25,9},{2,18},{10... | collective-permute-start | bytes 352520 | tf_op jit(solution)/shard_map/ppermute | solution.py:90
  602.1 22.1 %collective-permute-start.47 = (f32[29376]{0:T(1024)S(1)}, f32[29376]{0:T(1024)}, u32[]{:S(2)}, u32[]{:S(2)}) collective-permute-start(f32[29376]{0:T(1024)S(1)} %concatenate.168), channel_id=1, source_target_pairs={{0,8},{8,16},{16,24},{24,0},{1,9},{9,17},{17,25},{25,1},{2,10},{10... | collective-permute-start | bytes 352520 | tf_op jit(solution)/shard_map/ppermute | solution.py:90
  604.4 11.7 %collective-permute-start.46 = (f32[4,4,144]{2,1,0:T(4,128)S(1)}, f32[4,4,144]{2,1,0:T(4,128)S(1)}, u32[]{:S(2)}, u32[]{:S(2)}) collective-permute-start(f32[4,4,144]{2,1,0:T(4,128)S(1)} %maximum_select_fusion.5), channel_id=1, source_target_pairs={{0,4},{1,5},{2,6},{3,7},{4,0},{5,1},{6,2},{7,3},{8,12},{9,13},{10,... | collective-permute-start | bytes 27656 | tf_op jit(solution)/shard_map/ppermute | solution.py:62
  616.1 41.5 %collective-permute-start.40 = (bf16[1,512,1152]{2,1,0:T(8,128)(2,1)S(1)}, bf16[1,512,1152]{2,1,0:T(8,128)(2,1)}, u32[]{:S(2)}, u32[]{:S(2)}) collective-permute-start(bf16[1,512,1152]{2,1,0:T(8,128)(2,1)S(1)} %bitcast.106), channel_id=1, source_target_pairs={{1,2},{2,1},{5,6},{6,5},{9,10},{10,9},{13,14},{14,13},{17,18},{18,... | collective-permute-start | bytes 3538952 | tf_op jit(solution)/shard_map/ppermute | solution.py:68
  621.2 20.5 %collective-permute-start.56 = (bf16[144,1152]{1,0:T(8,128)(2,1)}, bf16[144,1152]{1,0:T(8,128)(2,1)}, u32[]{:S(2)}, u32[]{:S(2)}) collective-permute-start(bf16[144,1152]{1,0:T(8,128)(2,1)} %copy-done.49), channel_id=1, source_target_pairs={{0,8},{8,16},{16,24},{24,0},{1,9},{9,17},{17,25},{25,1},{2,10},{10... | collective-permute-start | bytes 995336 | tf_op jit(solution)/shard_map/ppermute | solution.py:218
  622.2 27.3 %collective-permute-start.57 = (bf16[144,1152]{1,0:T(8,128)(2,1)}, bf16[144,1152]{1,0:T(8,128)(2,1)}, u32[]{:S(2)}, u32[]{:S(2)}) collective-permute-start(bf16[144,1152]{1,0:T(8,128)(2,1)} %copy-done.49), channel_id=1, source_target_pairs={{0,16},{8,24},{16,0},{24,8},{1,17},{9,25},{17,1},{25,9},{2,18},{10... | collective-permute-start | bytes 995336 | tf_op jit(solution)/shard_map/ppermute | solution.py:218
  624.2 27.3 %collective-permute-start.58 = (bf16[144,1152]{1,0:T(8,128)(2,1)}, bf16[144,1152]{1,0:T(8,128)(2,1)}, u32[]{:S(2)}, u32[]{:S(2)}) collective-permute-start(bf16[144,1152]{1,0:T(8,128)(2,1)} %copy-done.49), channel_id=1, source_target_pairs={{0,24},{8,0},{16,8},{24,16},{1,25},{9,1},{17,9},{25,17},{2,26},{10... | collective-permute-start | bytes 995336 | tf_op jit(solution)/shard_map/ppermute | solution.py:218
  (80 other events, 646.2 us)
Sparse Core Ops, SparseCore 0:
  13.1 58.4 all-gather.3
  74.0 51.9 all-gather.5
  127.9 55.4 all-gather.7
  260.7 63.2 reduce-scatter.2
  327.6 59.4 reduce-scatter.4
  443.7 111.5 all-reduce.1

commit v9 on v7

--- a/solution.py
+++ b/solution.py
@@ -650,20 +650,18 @@
     d_own = (d_own + d_other.astype(jnp.float32)).astype(jnp.bfloat16)
     d_projected = jnp.concatenate([d_query, d_own[0], d_own[1]], axis=-1)
 
-    d_projected, down_shard = tie(d_projected, down_shard)
+    d_projected, down_shard, up_scatter.received = tie(
+        d_projected, down_shard, up_scatter.received
+    )
+    down_total = lax.psum(down_shard, "rep")
+    up_sum = ReplicaSum(up_scatter.result(), replicas)
     d_hidden_one, qkv_halves = product_back(hidden_one, d_projected, full_qkv)
     qkv_scatter = Scatter(qkv_halves)
     column_sums = jnp.sum(d_projected.astype(jnp.float32), axis=0)
-    d_hidden_one, *arrived = tie(
-        d_hidden_one,
-        qkv_scatter.received,
-        up_scatter.received,
-        out_scatter.received,
-    )
-    qkv_scatter.received, up_scatter.received, out_scatter.received = arrived
+    d_hidden_one, qkv_scatter.received, out_scatter.received = tie(
+        d_hidden_one, qkv_scatter.received, out_scatter.received
+    )
     qkv_scatter.second()
-    down_total = lax.psum(down_shard, "rep")
-    up_sum = ReplicaSum(up_scatter.result(), replicas)
     out_scatter.third()
     d_shift_one = jnp.sum(d_hidden_one, axis=0)
     d_scale_one = jnp.sum(d_hidden_one * normed_one, axis=0)
@@ -677,14 +675,13 @@
     sums = [d_shift_one, d_scale_one, d_gate_one, d_shift_two, d_scale_two, d_gate_two]
     ada_width = 6 * width
     small_sums = jnp.concatenate(sums + list(bias_grads))
-    qkv_scatter.received, out_scatter.received, *up_sum.received = tie(
-        qkv_scatter.received, out_scatter.received, *up_sum.received
+    qkv_scatter.received, out_scatter.received, down_total, *up_sum.received = tie(
+        qkv_scatter.received, out_scatter.received, down_total, *up_sum.received
     )
     qkv_scatter.third()
-    up_sum.second()
     qkv_shard = qkv_scatter.result()
-    qkv_shard, latent_grad, block_out, small_sums = tie(
-        qkv_shard, latent_grad.astype(jnp.bfloat16), block_out, small_sums
+    qkv_shard, latent_grad, block_out, small_sums, *up_sum.received = tie(
+        qkv_shard, latent_grad.astype(jnp.bfloat16), block_out, small_sums, *up_sum.received
     )
     late_sum = ReplicaSum(
         jnp.concatenate([out_scatter.result(), qkv_shard], axis=1), replicas
@@ -692,8 +689,10 @@
     latent_grad = swap_halves(latent_grad[None]).astype(jnp.float32)
     block_out = swap_halves(block_out[None])
     sums_all = gather_group(small_sums)
-    down_total, *late_sum.received = tie(down_total, *late_sum.received)
+    up_sum.second()
+    *late_sum.received, sums_all = tie(*late_sum.received, sums_all)
     late_sum.second()
+    late_sum.received[0], *up_sum.received = tie(late_sum.received[0], *up_sum.received)
     up_total = up_sum.result()
     late_total = late_sum.result()
     out_total, qkv_total = late_total[:, :width], late_total[:, width:]

time: 615 us -> 665 us (1.081)
  waiting for transfers between devices: 236 us -> 260 us
  local copies, waits for them, and re-layouts: 50.7 us -> 64.9 us
  other arithmetic: 71.8 us -> 80.3 us
    psum x1, waiting for transfers between devices: 0.02 us -> 31.2 us  [per_device(): down_total = lax.psum(down_shard, 'rep')]
    ppermute x12, waiting for transfers between devices: 94 us -> 84.4 us  [send(): return lax.ppermute(values, 'rep', pairs)]
    unnamed x122 -> x120, local copies, waits for them, and re-layouts: 21.4 us -> 21 us
  transfers between devices with their start and end apart: 53 -> 53, of which waited for: 18 -> 17; matrix products, arithmetic and copies ran while one was open for 19% -> 21% of each run, Pallas kernels for 14% -> 13%
where the time goes in v9:
time: 665 us; the launch traced here: 658 us
  waiting for transfers between devices  260 us (39%)
  Pallas kernels  153 us (23%)
  other arithmetic  80.3 us (12%)
  starting transfers between devices  65.1 us (10%)
  local copies, waits for them, and re-layouts  64.9 us (10%)
  matrix products  18.3 us (3%)
  between operations  16.2 us (2%)
    ppermute x30, waiting for transfers between devices, permute(): return lax.ppermute(values, GROUP, pairs_by(rule))  121 us
    ppermute x12, waiting for transfers between devices, send(): return lax.ppermute(values, 'rep', pairs)  84.4 us
    pallas_call x2, Pallas kernels, attend_back(): pl.pallas_call(functools.partial(attend_back_kernel, heads[0], low), grid...  48.1 us
    pallas_call x1, Pallas kernels, mlp(): pl.pallas_call(mlp_kernel, grid=(units // block,), out_shape=(jax.ShapeDt...  47.6 us
    ppermute x30, starting transfers between devices, permute(): return lax.ppermute(values, GROUP, pairs_by(rule))  36.1 us
    psum x1, waiting for transfers between devices, per_device(): down_total = lax.psum(down_shard, 'rep')  31.2 us
    pallas_call x1, Pallas kernels, attend(): pl.pallas_call(functools.partial(attend_kernel, heads[0], low), grid=(len...  26.8 us
    pallas_call x2, Pallas kernels, product_back(): pl.pallas_call(product_back_kernel, grid=(columns // block,), out_shape=(...  26.2 us
  transfers between devices with their start and end apart: 53, of which 17 were waited for; matrix products, arithmetic and copies ran while one was open for 21% of the time, Pallas kernels for 13%

profile of v9, /device:TPU:9, one launch (start us, length us, event | category | flops | bytes accessed | tf_op | source)
XLA Modules:
  0.0 657.8 jit_solution(4553572920020633571)
XLA Ops:
  11.0 2.2 constant_dynamic-update-slice_fusion.1
  20.6 43.9 %collective-permute-done.3 = bf16[4,2432]{1,0:T(4,128)(2,1)S(1)} collective-permute-done((bf16[4,2432]{1,0:T(4,128)(2,1)S(1)}, bf16[4,2432]{1,0:T(4,128)(2,1)S(1)}, u32[]{:S(2)}, u32[]{:S(2)}) %collective-permute-start.3) | collective-permute-done | bytes 19488 | tf_op jit(solution)/shard_map/ppermute | solution.py:62
  67.4 3.2 collective-permute-done.4
  72.5 34.7 %collective-permute-done.5 = f32[1,6912]{1,0:T(1,128)S(1)} collective-permute-done((f32[1,6912]{1,0:T(1,128)S(1)}, f32[1,6912]{1,0:T(1,128)S(1)}, u32[]{:S(2)}, u32[]{:S(2)}) %collective-permute-start.5) | collective-permute-done | bytes 27680 | tf_op jit(solution)/shard_map/ppermute | solution.py:62
  109.3 7.6 %collective-permute-start.13 = (bf16[144,4608]{1,0:T(8,128)(2,1)S(1)}, bf16[144,4608]{1,0:T(8,128)(2,1)S(1)}, u32[]{:S(2)}, u32[]{:S(2)}) collective-permute-start(bf16[144,4608]{1,0:T(8,128)(2,1)S(1)} %collective-permute-done.9.refs_3_), channel_id=1, source_target_pairs={{0,2},{1,3},{2,0},{3,1},{4,6},{5,7},{6,4},{7,5},{8,10},{9,11},{10,... | collective-permute-start | bytes 3981320 | tf_op jit(solution)/shard_map/ppermute | solution.py:62
  119.7 3.7 shard_map.237
  124.9 5.1 add_convert_fusion.2
  132.9 3.6 collective-permute-start.15
  138.0 22.8 %collective-permute-done.15 = bf16[1,512,1152]{2,1,0:T(8,128)(2,1)} collective-permute-done((bf16[1,512,1152]{2,1,0:T(8,128)(2,1)}, bf16[1,512,1152]{2,1,0:T(8,128)(2,1)}, u32[]{:S(2)}, u32[]{:S(2)}) %collective-permute-start.15) | collective-permute-done | bytes 1179680 | tf_op jit(solution)/shard_map/ppermute | solution.py:68
  160.8 3.9 convert_reduce_fusion.2
  166.1 26.8 %shard_map.238 = (bf16[512,1152]{1,0:T(8,128)(2,1)S(1)}, f32[512,128]{1,0:T(8,128)S(1)}) custom-call(bf16[512,1152]{1,0:T(8,128)(2,1)S(1)} %slice.226.query_ref, bf16[512,2304]{1,0:T(8,128)(2,1)} %slice.227.own_ref, bf16[512,2304]{1,0:T(8,128)(2,1)} %collective-permute-done.14.other_ref), custom_call_target="tpu_custom_call" | custom-call | flops 1048576 | bytes 1048576 | tf_op jit(solution)/shard_map/pallas_call | solution.py:297
  193.0 3.3 fusion.47
  199.1 47.6 %shard_map.239 = (f32[512,1152]{1,0:T(8,128)}, f32[512,1152]{1,0:T(8,128)}, bf16[4,144,4608]{2,1,0:T(8,128)(2,1)}, bf16[4,144,4608]{2,1,0:T(8,128)(2,1)}, bf16[4608,1152]{1,0:T(8,128)(2,1)}, /*index=5*/f32[1,4608]{1,0:T(1,128)}) custom-call(bf16[512,1152]{1,0:T(8,128)(2,1)} %add_convert_fusion.4.hidden_ref, ...), custom_call_target="tpu_custom_call" | custom-call | flops 1048576 | bytes 1048576 | tf_op jit(solution)/shard_map/pallas_call | solution.py:507
  247.1 3.5 multiply_reduce_fusion
  250.9 6.8 %fusion.21 = (f32[1152]{0:T(1024)S(1)}, bf16[512,1152]{1,0:T(8,128)(2,1)}, f32[1152]{0:T(1024)S(1)}, bf16[512,1152]{1,0:T(8,128)(2,1)S(1)}, f32[512,1152]{1,0:T(8,128)}) fusion(bf16[1,512,1152]{2,1,0:T(8,128)(2,1)} %get-tuple-element.149, f32[512,1152]{1,0:T(8,128)} %get-tuple-element.108, f32[1152]{0:T(1024)S(1)} %reshape.147, f32[]{:T(128)} %bitcast.10, ...), kind=kLoop, calls=%fused_computation.43 | loop fusion | flops 12384000 | bytes 13011972 | tf_op jit(solution)/shard_map/reduce_sum | solution.py:626
  257.7 7.2 %shard_map.240 = (f32[512,1152]{1,0:T(8,128)S(1)}, bf16[4,144,1152]{2,1,0:T(8,128)(2,1)S(1)}, bf16[4,144,1152]{2,1,0:T(8,128)(2,1)}) custom-call(bf16[512,1152]{1,0:T(8,128)(2,1)S(1)} %copy-done.15, bf16[512,1152]{1,0:T(8,128)(2,1)S(1)} %get-tuple-element.170.upstream_ref, bf16[1152,1152]{1,0:T(8,128)(2,1)S(1)} %copy-done.12), custom_call_target="tpu_custom_call" | custom-call | flops 1048576 | bytes 1048576 | tf_op jit(solution)/shard_map/pallas_call | solution.py:443
  266.4 4.1 add_convert_fusion
  278.4 24.0 %shard_map.241 = (bf16[512,640]{1,0:T(8,128)(2,1)}, f32[2,512,640]{2,1,0:T(8,128)}, bf16[2,512,640]{2,1,0:T(8,128)(2,1)}) custom-call(bf16[512,1152]{1,0:T(8,128)(2,1)} %copy-done.1, bf16[512,2304]{1,0:T(8,128)(2,1)} %slice.227.own_ref, bf16[512,2304]{1,0:T(8,128)(2,1)} %collective-permute-done.14.other_ref, ...), custom_call_target="tpu_custom_call" | custom-call | flops 1048576 | bytes 1048576 | tf_op jit(solution)/shard_map/pallas_call | solution.py:369
  305.5 24.2 %shard_map.242 = (bf16[512,640]{1,0:T(8,128)(2,1)}, f32[2,512,640]{2,1,0:T(8,128)}, bf16[2,512,640]{2,1,0:T(8,128)(2,1)}) custom-call(bf16[512,1152]{1,0:T(8,128)(2,1)} %copy-done.1, bf16[512,2304]{1,0:T(8,128)(2,1)} %slice.227.own_ref, bf16[512,2304]{1,0:T(8,128)(2,1)} %collective-permute-done.14.other_ref, ...), custom_call_target="tpu_custom_call" | custom-call | flops 1048576 | bytes 1048576 | tf_op jit(solution)/shard_map/pallas_call | solution.py:369
  329.7 13.6 %collective-permute-done.18 = bf16[2,144,4608]{2,1,0:T(8,128)(2,1)} collective-permute-done((bf16[2,144,4608]{2,1,0:T(8,128)(2,1)}, bf16[2,144,4608]{2,1,0:T(8,128)(2,1)}, u32[]{:S(2)}, u32[]{:S(2)}) %collective-permute-start.18) | collective-permute-done | bytes 2654240 | tf_op jit(solution)/shard_map/ppermute | solution.py:62
  347.8 2.5 convert_add_fusion
  351.5 2.6 copy-done.32
  359.3 8.3 %collective-permute-done.20 = bf16[144,4608]{1,0:T(8,128)(2,1)} collective-permute-done((bf16[144,4608]{1,0:T(8,128)(2,1)S(1)}, bf16[144,4608]{1,0:T(8,128)(2,1)}, u32[]{:S(2)}, u32[]{:S(2)}) %collective-permute-start.20) | collective-permute-done | bytes 1327136 | tf_op jit(solution)/shard_map/ppermute | solution.py:62
  369.6 3.3 copy-done.7
  372.9 19.0 %shard_map.243 = (f32[512,1152]{1,0:T(8,128)S(1)}, bf16[4,144,3456]{2,1,0:T(8,128)(2,1)S(1)}, bf16[4,144,3456]{2,1,0:T(8,128)(2,1)}) custom-call(bf16[512,1152]{1,0:T(8,128)(2,1)S(1)} %fusion.12.left_ref, bf16[512,3456]{1,0:T(8,128)(2,1)S(1)} %copy-done.3, bf16[1152,3456]{1,0:T(8,128)(2,1)S(1)} %copy-done.7), custom_call_target="tpu_custom_call" | custom-call | flops 1048576 | bytes 1048576 | tf_op jit(solution)/shard_map/pallas_call | solution.py:443
  395.2 2.3 collective-permute-start.21
  399.9 4.0 fusion.45
  408.6 2.8 convert_reduce_fusion
  413.9 3.3 add_convert_fusion.1
  423.1 2.5 multiply_reduce_fusion.1
  425.7 26.6 %collective-permute-done.26 = bf16[144,1152]{1,0:T(8,128)(2,1)} collective-permute-done((bf16[144,1152]{1,0:T(8,128)(2,1)}, bf16[144,1152]{1,0:T(8,128)(2,1)}, u32[]{:S(2)}, u32[]{:S(2)}) %collective-permute-start.26) | collective-permute-done | bytes 331808 | tf_op jit(solution)/shard_map/ppermute | solution.py:209
  452.2 6.6 %collective-permute-done.27 = bf16[144,1152]{1,0:T(8,128)(2,1)} collective-permute-done((bf16[144,1152]{1,0:T(8,128)(2,1)}, bf16[144,1152]{1,0:T(8,128)(2,1)}, u32[]{:S(2)}, u32[]{:S(2)}) %collective-permute-start.27) | collective-permute-done | bytes 331808 | tf_op jit(solution)/shard_map/ppermute | solution.py:209
  458.8 31.2 %all-reduce.2.cloned.1.call-done = bf16[576,1152]{1,0:T(8,128)(2,1)} async-done(((bf16[576,1152]{1,0:T(8,128)(2,1)}), bf16[576,1152]{1,0:T(8,128)(2,1)}) %all-reduce.2.cloned.1.call-update) | async-done | bytes 1327120 | tf_op jit(solution)/shard_map/psum | solution.py:656
  490.1 2.2 convert_add_fusion.1
  495.5 10.4 %collective-permute-done.28 = bf16[144,3456]{1,0:T(8,128)(2,1)S(1)} collective-permute-done((bf16[144,3456]{1,0:T(8,128)(2,1)S(1)}, bf16[144,3456]{1,0:T(8,128)(2,1)S(1)}, u32[]{:S(2)}, u32[]{:S(2)}) %collective-permute-start.28) | collective-permute-done | bytes 995360 | tf_op jit(solution)/shard_map/ppermute | solution.py:62
  511.6 2.6 collective-permute-start.35
  518.7 4.3 collective-permute-done.36
  523.2 34.9 %collective-permute-done.31 = bf16[144,1152]{1,0:T(8,128)(2,1)S(1)} collective-permute-done((bf16[144,1152]{1,0:T(8,128)(2,1)S(1)}, bf16[144,1152]{1,0:T(8,128)(2,1)S(1)}, u32[]{:S(2)}, u32[]{:S(2)}) %collective-permute-start.31) | collective-permute-done | bytes 331808 | tf_op jit(solution)/shard_map/ppermute | solution.py:209
  558.1 7.1 %collective-permute-done.32 = bf16[144,1152]{1,0:T(8,128)(2,1)S(1)} collective-permute-done((bf16[144,1152]{1,0:T(8,128)(2,1)S(1)}, bf16[144,1152]{1,0:T(8,128)(2,1)S(1)}, u32[]{:S(2)}, u32[]{:S(2)}) %collective-permute-start.32) | collective-permute-done | bytes 331808 | tf_op jit(solution)/shard_map/ppermute | solution.py:209
  565.2 5.1 collective-permute-start.30
  579.2 3.2 fusion.43
  587.3 3.2 collective-permute-start.41
  603.0 2.9 collective-permute-start.29
  618.9 6.2 fusion.51
  627.0 8.2 %collective-permute-done.47 = bf16[144,1152]{1,0:T(8,128)(2,1)} collective-permute-done((bf16[144,1152]{1,0:T(8,128)(2,1)}, bf16[144,1152]{1,0:T(8,128)(2,1)}, u32[]{:S(2)}, u32[]{:S(2)}) %collective-permute-start.47) | collective-permute-done | bytes 331808 | tf_op jit(solution)/shard_map/ppermute | solution.py:209
  640.1 3.0 slice.243
  645.0 3.2 select_convert_fusion
  648.2 2.5 broadcast_select_fusion
  (339 shorter events, 135.5 us)
Async XLA Ops:
  7.3 191.9 %all-gather.3.cloned.1.call-start = ((), (), s32[]{:S(2)}) async-start(), calls=%async_computation.1 | async-start | bytes 11943936 | tf_op jit(solution)/shard_map/all_gather | solution.py:562
  8.0 191.1 %all-gather.5.cloned.1.call-start = ((), (), s32[]{:S(2)}) async-start(), calls=%async_computation.2 | async-start | bytes 11943936 | tf_op jit(solution)/shard_map/all_gather | solution.py:565
  8.8 358.9 %reduce-scatter.2.cloned.1.call-start = ((), (), s32[]{:S(2)}) async-start(), calls=%async_computation.3 | async-start | bytes 11943936 | tf_op jit(solution)/shard_map/reduce_scatter | solution.py:623
  13.2 6.8 %collective-permute-start.2 = (bf16[2,2432]{1,0:T(2,128)(2,1)S(1)}, bf16[2,2432]{1,0:T(2,128)(2,1)S(1)}, u32[]{:S(2)}, u32[]{:S(2)}) collective-permute-start(bf16[2,2432]{1,0:T(2,128)(2,1)S(1)} %broadcast_select_fusion.6), channel_id=1, source_target_pairs={{0,2},{1,3},{2,0},{3,1},{4,6},{5,7},{6,4},{7,5},{8,10},{9,11},{10,... | collective-permute-start | bytes 29192 | tf_op jit(solution)/shard_map/ppermute | solution.py:62
  15.0 55.9 %collective-permute-start.7 = (bf16[144,4608]{1,0:T(8,128)(2,1)}, bf16[144,4608]{1,0:T(8,128)(2,1)}, u32[]{:S(2)}, u32[]{:S(2)}) collective-permute-start(bf16[144,4608]{1,0:T(8,128)(2,1)} %constant_dynamic-update-slice_fusion.refs_0_), channel_id=1, source_target_pairs={{0,4},{1,5},{2,3},{3,2},{4,0},{5,1},{6,7},{7,6},{8,12},{9,13},{10,... | collective-permute-start | bytes 3981320 | tf_op jit(solution)/shard_map/ppermute | solution.py:62
  16.2 92.8 %collective-permute-start.8 = (bf16[144,4608]{1,0:T(8,128)(2,1)}, bf16[144,4608]{1,0:T(8,128)(2,1)}, u32[]{:S(2)}, u32[]{:S(2)}) collective-permute-start(bf16[144,4608]{1,0:T(8,128)(2,1)} %constant_dynamic-update-slice_fusion.refs_0_), channel_id=1, source_target_pairs={{0,1},{1,0},{2,6},{3,7},{4,5},{5,4},{6,2},{7,3},{8,9},{9,8},{10,14... | collective-permute-start | bytes 3981320 | tf_op jit(solution)/shard_map/ppermute | solution.py:62
  17.4 102.2 %collective-permute-start.10 = (bf16[144,4608]{1,0:T(8,128)(2,1)}, bf16[144,4608]{1,0:T(8,128)(2,1)}, u32[]{:S(2)}, u32[]{:S(2)}) collective-permute-start(bf16[144,4608]{1,0:T(8,128)(2,1)} %constant_dynamic-update-slice_fusion.refs_0_), channel_id=1, source_target_pairs={{0,2},{1,3},{2,0},{3,1},{4,6},{5,7},{6,4},{7,5},{8,10},{9,11},{10,... | collective-permute-start | bytes 3981320 | tf_op jit(solution)/shard_map/ppermute | solution.py:62
  18.0 98.9 %collective-permute-start = (bf16[1,512,1152]{2,1,0:T(8,128)(2,1)S(1)}, bf16[1,512,1152]{2,1,0:T(8,128)(2,1)}, u32[]{:S(2)}, u32[]{:S(2)}) collective-permute-start(bf16[1,512,1152]{2,1,0:T(8,128)(2,1)S(1)} %copy-done.36), channel_id=1, source_target_pairs={{1,2},{2,1},{5,6},{6,5},{9,10},{10,9},{13,14},{14,13},{17,18},{18,... | collective-permute-start | bytes 3538952 | tf_op jit(solution)/shard_map/ppermute | solution.py:68
  20.1 44.4 %collective-permute-start.3 = (bf16[4,2432]{1,0:T(4,128)(2,1)S(1)}, bf16[4,2432]{1,0:T(4,128)(2,1)S(1)}, u32[]{:S(2)}, u32[]{:S(2)}) collective-permute-start(bf16[4,2432]{1,0:T(4,128)(2,1)S(1)} %maximum_select_fusion.4), channel_id=1, source_target_pairs={{0,4},{1,5},{2,6},{3,7},{4,0},{5,1},{6,2},{7,3},{8,12},{9,13},{10,... | collective-permute-start | bytes 58376 | tf_op jit(solution)/shard_map/ppermute | solution.py:62
  65.2 5.4 collective-permute-start.4
  70.7 36.6 %collective-permute-start.5 = (f32[1,6912]{1,0:T(1,128)S(1)}, f32[1,6912]{1,0:T(1,128)S(1)}, u32[]{:S(2)}, u32[]{:S(2)}) collective-permute-start(f32[1,6912]{1,0:T(1,128)S(1)} %broadcast_select_fusion.4), channel_id=1, source_target_pairs={{0,1},{1,0},{2,3},{3,2},{4,5},{5,4},{6,7},{7,6},{8,9},{9,8},{10,11... | collective-permute-start | bytes 82952 | tf_op jit(solution)/shard_map/ppermute | solution.py:62
  70.9 38.4 %collective-permute-start.9 = (bf16[144,4608]{1,0:T(8,128)(2,1)}, bf16[144,4608]{1,0:T(8,128)(2,1)S(1)}, u32[]{:S(2)}, u32[]{:S(2)}) collective-permute-start(bf16[144,4608]{1,0:T(8,128)(2,1)} %collective-permute-done.7.refs_1_), channel_id=1, source_target_pairs={{0,1},{1,0},{2,6},{3,7},{4,5},{5,4},{6,2},{7,3},{8,9},{9,8},{10,14... | collective-permute-start | bytes 3981320 | tf_op jit(solution)/shard_map/ppermute | solution.py:62
  108.7 10.9 %collective-permute-start.11 = (bf16[144,4608]{1,0:T(8,128)(2,1)}, bf16[144,4608]{1,0:T(8,128)(2,1)S(1)}, u32[]{:S(2)}, u32[]{:S(2)}) collective-permute-start(bf16[144,4608]{1,0:T(8,128)(2,1)} %collective-permute-done.7.refs_1_), channel_id=1, source_target_pairs={{0,2},{1,3},{2,0},{3,1},{4,6},{5,7},{6,4},{7,5},{8,10},{9,11},{10,... | collective-permute-start | bytes 3981320 | tf_op jit(solution)/shard_map/ppermute | solution.py:62
  108.9 10.7 %collective-permute-start.12 = (bf16[144,4608]{1,0:T(8,128)(2,1)}, bf16[144,4608]{1,0:T(8,128)(2,1)S(1)}, u32[]{:S(2)}, u32[]{:S(2)}) collective-permute-start(bf16[144,4608]{1,0:T(8,128)(2,1)} %collective-permute-done.8.refs_2_), channel_id=1, source_target_pairs={{0,2},{1,3},{2,0},{3,1},{4,6},{5,7},{6,4},{7,5},{8,10},{9,11},{10,... | collective-permute-start | bytes 3981320 | tf_op jit(solution)/shard_map/ppermute | solution.py:62
  109.3 10.4 %collective-permute-start.13 = (bf16[144,4608]{1,0:T(8,128)(2,1)S(1)}, bf16[144,4608]{1,0:T(8,128)(2,1)S(1)}, u32[]{:S(2)}, u32[]{:S(2)}) collective-permute-start(bf16[144,4608]{1,0:T(8,128)(2,1)S(1)} %collective-permute-done.9.refs_3_), channel_id=1, source_target_pairs={{0,2},{1,3},{2,0},{3,1},{4,6},{5,7},{6,4},{7,5},{8,10},{9,11},{10,... | collective-permute-start | bytes 3981320 | tf_op jit(solution)/shard_map/ppermute | solution.py:62
  132.7 33.4 %collective-permute-start.14 = (bf16[512,2304]{1,0:T(8,128)(2,1)}, bf16[512,2304]{1,0:T(8,128)(2,1)}, u32[]{:S(2)}, u32[]{:S(2)}) collective-permute-start(bf16[512,2304]{1,0:T(8,128)(2,1)} %slice.227.own_ref), channel_id=1, source_target_pairs={{0,2},{1,3},{2,0},{3,1},{4,6},{5,7},{6,4},{7,5},{8,10},{9,11},{10,... | collective-permute-start | bytes 7077896 | tf_op jit(solution)/shard_map/ppermute | solution.py:62
  132.9 27.9 %collective-permute-start.15 = (bf16[1,512,1152]{2,1,0:T(8,128)(2,1)}, bf16[1,512,1152]{2,1,0:T(8,128)(2,1)}, u32[]{:S(2)}, u32[]{:S(2)}) collective-permute-start(bf16[1,512,1152]{2,1,0:T(8,128)(2,1)} %param.27), channel_id=1, source_target_pairs={{1,2},{2,1},{5,6},{6,5},{9,10},{10,9},{13,14},{14,13},{17,18},{18,... | collective-permute-start | bytes 3538952 | tf_op jit(solution)/shard_map/ppermute | solution.py:68
  246.8 19.6 %collective-permute-start.16 = (bf16[4,144,4608]{2,1,0:T(8,128)(2,1)}, bf16[4,144,4608]{2,1,0:T(8,128)(2,1)}, u32[]{:S(2)}, u32[]{:S(2)}) collective-permute-start(bf16[4,144,4608]{2,1,0:T(8,128)(2,1)} %get-tuple-element.77), channel_id=1, source_target_pairs={{0,2},{1,3},{2,0},{3,1},{4,6},{5,7},{6,4},{7,5},{8,10},{9,11},{10,... | collective-permute-start | bytes 15925256 | tf_op jit(solution)/shard_map/ppermute | solution.py:62
  246.9 243.2 %all-reduce.2.cloned.1.call-start = ((), (), s32[]{:S(2)}) async-start(), calls=%async_computation.4 | async-start | bytes 2654208 | tf_op jit(solution)/shard_map/psum | solution.py:656
  274.2 69.2 %collective-permute-start.18 = (bf16[2,144,4608]{2,1,0:T(8,128)(2,1)}, bf16[2,144,4608]{2,1,0:T(8,128)(2,1)}, u32[]{:S(2)}, u32[]{:S(2)}) collective-permute-start(bf16[2,144,4608]{2,1,0:T(8,128)(2,1)} %pad_maximum_fusion.1), channel_id=1, source_target_pairs={{0,4},{1,5},{2,3},{3,2},{4,0},{5,1},{6,7},{7,6},{8,12},{9,13},{10,... | collective-permute-start | bytes 7962632 | tf_op jit(solution)/shard_map/ppermute | solution.py:62
  274.4 28.0 %collective-permute-start.17 = (bf16[4,144,1152]{2,1,0:T(8,128)(2,1)}, bf16[4,144,1152]{2,1,0:T(8,128)(2,1)}, u32[]{:S(2)}, u32[]{:S(2)}) collective-permute-start(bf16[4,144,1152]{2,1,0:T(8,128)(2,1)} %get-tuple-element.81), channel_id=1, source_target_pairs={{0,2},{1,3},{2,0},{3,1},{4,6},{5,7},{6,4},{7,5},{8,10},{9,11},{10,... | collective-permute-start | bytes 3981320 | tf_op jit(solution)/shard_map/ppermute | solution.py:62
  345.9 10.5 %collective-permute-start.19 = (bf16[2,512,1152]{2,1,0:T(8,128)(2,1)S(1)}, bf16[2,512,1152]{2,1,0:T(8,128)(2,1)S(1)}, u32[]{:S(2)}, u32[]{:S(2)}) collective-permute-start(bf16[2,512,1152]{2,1,0:T(8,128)(2,1)S(1)} %pad_maximum_fusion.2), channel_id=1, source_target_pairs={{0,2},{1,3},{2,0},{3,1},{4,6},{5,7},{6,4},{7,5},{8,10},{9,11},{10,... | collective-permute-start | bytes 7077896 | tf_op jit(solution)/shard_map/ppermute | solution.py:62
  350.5 17.1 %collective-permute-start.20 = (bf16[144,4608]{1,0:T(8,128)(2,1)S(1)}, bf16[144,4608]{1,0:T(8,128)(2,1)}, u32[]{:S(2)}, u32[]{:S(2)}) collective-permute-start(bf16[144,4608]{1,0:T(8,128)(2,1)S(1)} %fusion.23), channel_id=1, source_target_pairs={{0,1},{1,0},{2,6},{3,7},{4,5},{5,4},{6,2},{7,3},{8,9},{9,8},{10,14... | collective-permute-start | bytes 3981320 | tf_op jit(solution)/shard_map/ppermute | solution.py:62
  395.2 16.2 %collective-permute-start.21 = (bf16[4,144,3456]{2,1,0:T(8,128)(2,1)}, bf16[4,144,3456]{2,1,0:T(8,128)(2,1)}, u32[]{:S(2)}, u32[]{:S(2)}) collective-permute-start(bf16[4,144,3456]{2,1,0:T(8,128)(2,1)} %get-tuple-element.99), channel_id=1, source_target_pairs={{0,2},{1,3},{2,0},{3,1},{4,6},{5,7},{6,4},{7,5},{8,10},{9,11},{10,... | collective-permute-start | bytes 11943944 | tf_op jit(solution)/shard_map/ppermute | solution.py:62
  399.8 11.6 %collective-permute-start.22 = (bf16[2,144,1152]{2,1,0:T(8,128)(2,1)S(1)}, bf16[2,144,1152]{2,1,0:T(8,128)(2,1)}, u32[]{:S(2)}, u32[]{:S(2)}) collective-permute-start(bf16[2,144,1152]{2,1,0:T(8,128)(2,1)S(1)} %pad_maximum_fusion.4), channel_id=1, source_target_pairs={{0,4},{1,5},{2,3},{3,2},{4,0},{5,1},{6,7},{7,6},{8,12},{9,13},{10,... | collective-permute-start | bytes 1990664 | tf_op jit(solution)/shard_map/ppermute | solution.py:62
  405.0 20.7 %collective-permute-start.25 = (bf16[144,1152]{1,0:T(8,128)(2,1)}, bf16[144,1152]{1,0:T(8,128)(2,1)}, u32[]{:S(2)}, u32[]{:S(2)}) collective-permute-start(bf16[144,1152]{1,0:T(8,128)(2,1)} %get-tuple-element.179), channel_id=1, source_target_pairs={{0,8},{8,16},{16,24},{24,0},{1,9},{9,17},{17,25},{25,1},{2,10},{10... | collective-permute-start | bytes 995336 | tf_op jit(solution)/shard_map/ppermute | solution.py:209
  406.2 46.0 %collective-permute-start.26 = (bf16[144,1152]{1,0:T(8,128)(2,1)}, bf16[144,1152]{1,0:T(8,128)(2,1)}, u32[]{:S(2)}, u32[]{:S(2)}) collective-permute-start(bf16[144,1152]{1,0:T(8,128)(2,1)} %get-tuple-element.178), channel_id=1, source_target_pairs={{0,16},{8,24},{16,0},{24,8},{1,17},{9,25},{17,1},{25,9},{2,18},{10... | collective-permute-start | bytes 995336 | tf_op jit(solution)/shard_map/ppermute | solution.py:209
  407.3 51.5 %collective-permute-start.27 = (bf16[144,1152]{1,0:T(8,128)(2,1)}, bf16[144,1152]{1,0:T(8,128)(2,1)}, u32[]{:S(2)}, u32[]{:S(2)}) collective-permute-start(bf16[144,1152]{1,0:T(8,128)(2,1)} %get-tuple-element.177), channel_id=1, source_target_pairs={{0,24},{8,0},{16,8},{24,16},{1,25},{9,1},{17,9},{25,17},{2,26},{10... | collective-permute-start | bytes 995336 | tf_op jit(solution)/shard_map/ppermute | solution.py:209
  420.1 70.0 %collective-permute-start.23 = (bf16[2,144,3456]{2,1,0:T(8,128)(2,1)}, bf16[2,144,3456]{2,1,0:T(8,128)(2,1)}, u32[]{:S(2)}, u32[]{:S(2)}) collective-permute-start(bf16[2,144,3456]{2,1,0:T(8,128)(2,1)} %pad_maximum_fusion.3), channel_id=1, source_target_pairs={{0,4},{1,5},{2,3},{3,2},{4,0},{5,1},{6,7},{7,6},{8,12},{9,13},{10,... | collective-permute-start | bytes 5971976 | tf_op jit(solution)/shard_map/ppermute | solution.py:62
  422.5 67.5 %collective-permute-start.24 = (bf16[144,1152]{1,0:T(8,128)(2,1)}, bf16[144,1152]{1,0:T(8,128)(2,1)S(1)}, u32[]{:S(2)}, u32[]{:S(2)}) collective-permute-start(bf16[144,1152]{1,0:T(8,128)(2,1)} %fusion.33), channel_id=1, source_target_pairs={{0,1},{1,0},{2,6},{3,7},{4,5},{5,4},{6,2},{7,3},{8,9},{9,8},{10,14... | collective-permute-start | bytes 995336 | tf_op jit(solution)/shard_map/ppermute | solution.py:62
  492.4 13.4 %collective-permute-start.28 = (bf16[144,3456]{1,0:T(8,128)(2,1)S(1)}, bf16[144,3456]{1,0:T(8,128)(2,1)S(1)}, u32[]{:S(2)}, u32[]{:S(2)}) collective-permute-start(bf16[144,3456]{1,0:T(8,128)(2,1)S(1)} %fusion.26), channel_id=1, source_target_pairs={{0,1},{1,0},{2,6},{3,7},{4,5},{5,4},{6,2},{7,3},{8,9},{9,8},{10,14... | collective-permute-start | bytes 2985992 | tf_op jit(solution)/shard_map/ppermute | solution.py:62
  506.1 5.3 collective-permute-start.34
  508.9 78.4 %collective-permute-start.43 = (bf16[144,1152]{1,0:T(8,128)(2,1)S(1)}, bf16[144,1152]{1,0:T(8,128)(2,1)}, u32[]{:S(2)}, u32[]{:S(2)}) collective-permute-start(bf16[144,1152]{1,0:T(8,128)(2,1)S(1)} %add_convert_fusion.5), channel_id=1, source_target_pairs={{0,8},{8,16},{16,24},{24,0},{1,9},{9,17},{17,25},{25,1},{2,10},{10... | collective-permute-start | bytes 995336 | tf_op jit(solution)/shard_map/ppermute | solution.py:209
  510.1 80.4 %collective-permute-start.44 = (bf16[144,1152]{1,0:T(8,128)(2,1)S(1)}, bf16[144,1152]{1,0:T(8,128)(2,1)}, u32[]{:S(2)}, u32[]{:S(2)}) collective-permute-start(bf16[144,1152]{1,0:T(8,128)(2,1)S(1)} %add_convert_fusion.5), channel_id=1, source_target_pairs={{0,16},{8,24},{16,0},{24,8},{1,17},{9,25},{17,1},{25,9},{2,18},{10... | collective-permute-start | bytes 995336 | tf_op jit(solution)/shard_map/ppermute | solution.py:209
  515.4 7.6 %collective-permute-start.36 = (f32[4,16128]{1,0:T(4,128)S(1)}, f32[4,16128]{1,0:T(4,128)S(1)}, u32[]{:S(2)}, u32[]{:S(2)}) collective-permute-start(f32[4,16128]{1,0:T(4,128)S(1)} %maximum_select_fusion.1), channel_id=1, source_target_pairs={{0,4},{1,5},{2,6},{3,7},{4,0},{5,1},{6,2},{7,3},{8,12},{9,13},{10,... | collective-permute-start | bytes 774152 | tf_op jit(solution)/shard_map/ppermute | solution.py:62
  516.7 41.3 %collective-permute-start.31 = (bf16[144,1152]{1,0:T(8,128)(2,1)S(1)}, bf16[144,1152]{1,0:T(8,128)(2,1)S(1)}, u32[]{:S(2)}, u32[]{:S(2)}) collective-permute-start(bf16[144,1152]{1,0:T(8,128)(2,1)S(1)} %get-tuple-element.176), channel_id=1, source_target_pairs={{0,8},{8,16},{16,24},{24,0},{1,9},{9,17},{17,25},{25,1},{2,10},{10... | collective-permute-start | bytes 995336 | tf_op jit(solution)/shard_map/ppermute | solution.py:209
  517.0 48.1 %collective-permute-start.32 = (bf16[144,1152]{1,0:T(8,128)(2,1)S(1)}, bf16[144,1152]{1,0:T(8,128)(2,1)S(1)}, u32[]{:S(2)}, u32[]{:S(2)}) collective-permute-start(bf16[144,1152]{1,0:T(8,128)(2,1)S(1)} %get-tuple-element.175), channel_id=1, source_target_pairs={{0,16},{8,24},{16,0},{24,8},{1,17},{9,25},{17,1},{25,9},{2,18},{10... | collective-permute-start | bytes 995336 | tf_op jit(solution)/shard_map/ppermute | solution.py:209
  523.0 47.3 %collective-permute-start.33 = (bf16[144,1152]{1,0:T(8,128)(2,1)S(1)}, bf16[144,1152]{1,0:T(8,128)(2,1)S(1)}, u32[]{:S(2)}, u32[]{:S(2)}) collective-permute-start(bf16[144,1152]{1,0:T(8,128)(2,1)S(1)} %get-tuple-element.174), channel_id=1, source_target_pairs={{0,24},{8,0},{16,8},{24,16},{1,25},{9,1},{17,9},{25,17},{2,26},{10... | collective-permute-start | bytes 995336 | tf_op jit(solution)/shard_map/ppermute | solution.py:209
  558.1 33.9 %collective-permute-start.45 = (bf16[144,1152]{1,0:T(8,128)(2,1)S(1)}, bf16[144,1152]{1,0:T(8,128)(2,1)}, u32[]{:S(2)}, u32[]{:S(2)}) collective-permute-start(bf16[144,1152]{1,0:T(8,128)(2,1)S(1)} %add_convert_fusion.5), channel_id=1, source_target_pairs={{0,24},{8,0},{16,8},{24,16},{1,25},{9,1},{17,9},{25,17},{2,26},{10... | collective-permute-start | bytes 995336 | tf_op jit(solution)/shard_map/ppermute | solution.py:209
  565.2 79.8 %collective-permute-start.30 = (bf16[1,512,1152]{2,1,0:T(8,128)(2,1)}, bf16[1,512,1152]{2,1,0:T(8,128)(2,1)}, u32[]{:S(2)}, u32[]{:S(2)}) collective-permute-start(bf16[1,512,1152]{2,1,0:T(8,128)(2,1)} %bitcast.21), channel_id=1, source_target_pairs={{1,2},{2,1},{5,6},{6,5},{9,10},{10,9},{13,14},{14,13},{17,18},{18,... | collective-permute-start | bytes 3538952 | tf_op jit(solution)/shard_map/ppermute | solution.py:68
  585.8 20.8 %collective-permute-start.40 = (f32[29376]{0:T(1024)}, f32[29376]{0:T(1024)}, u32[]{:S(2)}, u32[]{:S(2)}) collective-permute-start(f32[29376]{0:T(1024)} %concatenate.131), channel_id=1, source_target_pairs={{0,8},{8,16},{16,24},{24,0},{1,9},{9,17},{17,25},{25,1},{2,10},{10... | collective-permute-start | bytes 352520 | tf_op jit(solution)/shard_map/ppermute | solution.py:90
  587.3 20.2 %collective-permute-start.41 = (f32[29376]{0:T(1024)}, f32[29376]{0:T(1024)}, u32[]{:S(2)}, u32[]{:S(2)}) collective-permute-start(f32[29376]{0:T(1024)} %concatenate.131), channel_id=1, source_target_pairs={{0,16},{8,24},{16,0},{24,8},{1,17},{9,25},{17,1},{25,9},{2,18},{10... | collective-permute-start | bytes 352520 | tf_op jit(solution)/shard_map/ppermute | solution.py:90
  590.5 20.2 %collective-permute-start.42 = (f32[29376]{0:T(1024)}, f32[29376]{0:T(1024)}, u32[]{:S(2)}, u32[]{:S(2)}) collective-permute-start(f32[29376]{0:T(1024)} %concatenate.131), channel_id=1, source_target_pairs={{0,24},{8,0},{16,8},{24,16},{1,25},{9,1},{17,9},{25,17},{2,26},{10... | collective-permute-start | bytes 352520 | tf_op jit(solution)/shard_map/ppermute | solution.py:90
  592.0 4.1 collective-permute-start.37
  603.0 45.3 %collective-permute-start.29 = (bf16[1,512,1152]{2,1,0:T(8,128)(2,1)S(1)}, bf16[1,512,1152]{2,1,0:T(8,128)(2,1)}, u32[]{:S(2)}, u32[]{:S(2)}) collective-permute-start(bf16[1,512,1152]{2,1,0:T(8,128)(2,1)S(1)} %bitcast.103), channel_id=1, source_target_pairs={{1,2},{2,1},{5,6},{6,5},{9,10},{10,9},{13,14},{14,13},{17,18},{18,... | collective-permute-start | bytes 3538952 | tf_op jit(solution)/shard_map/ppermute | solution.py:68
  606.6 18.6 %collective-permute-start.46 = (bf16[144,1152]{1,0:T(8,128)(2,1)}, bf16[144,1152]{1,0:T(8,128)(2,1)}, u32[]{:S(2)}, u32[]{:S(2)}) collective-permute-start(bf16[144,1152]{1,0:T(8,128)(2,1)} %copy-done.35), channel_id=1, source_target_pairs={{0,8},{8,16},{16,24},{24,0},{1,9},{9,17},{17,25},{25,1},{2,10},{10... | collective-permute-start | bytes 995336 | tf_op jit(solution)/shard_map/ppermute | solution.py:209
  607.6 27.7 %collective-permute-start.47 = (bf16[144,1152]{1,0:T(8,128)(2,1)}, bf16[144,1152]{1,0:T(8,128)(2,1)}, u32[]{:S(2)}, u32[]{:S(2)}) collective-permute-start(bf16[144,1152]{1,0:T(8,128)(2,1)} %copy-done.35), channel_id=1, source_target_pairs={{0,16},{8,24},{16,0},{24,8},{1,17},{9,25},{17,1},{25,9},{2,18},{10... | collective-permute-start | bytes 995336 | tf_op jit(solution)/shard_map/ppermute | solution.py:209
  610.7 27.5 %collective-permute-start.48 = (bf16[144,1152]{1,0:T(8,128)(2,1)}, bf16[144,1152]{1,0:T(8,128)(2,1)}, u32[]{:S(2)}, u32[]{:S(2)}) collective-permute-start(bf16[144,1152]{1,0:T(8,128)(2,1)} %copy-done.35), channel_id=1, source_target_pairs={{0,24},{8,0},{16,8},{24,16},{1,25},{9,1},{17,9},{25,17},{2,26},{10... | collective-permute-start | bytes 995336 | tf_op jit(solution)/shard_map/ppermute | solution.py:209
  (58 other events, 412.6 us)
Sparse Core Ops, SparseCore 0:
  10.0 100.7 all-gather.2
  112.6 75.0 all-gather.4
  247.0 103.1 reduce-scatter.1
  408.7 81.2 all-reduce.1

commit v10 on v7

--- a/solution.py
+++ b/solution.py
@@ -436,7 +436,7 @@
 def product_back(left, upstream, weight):
     length, width = left.shape
     columns = weight.shape[1]
-    block = 384
+    block = width
     fixed = pl.BlockSpec((length, width), lambda at: (0, 0))
     half = pl.BlockSpec((SHARDS // 2, width // SHARDS, block), lambda at: (0, 0, at))
     half_shape = jax.ShapeDtypeStruct((SHARDS // 2, width // SHARDS, columns), jnp.bfloat16)
@@ -455,7 +455,7 @@
         ],
         out_specs=(fixed, half, half),
         scratch_shapes=[pltpu.VMEM((width, length), jnp.bfloat16)],
-        compiler_params=pltpu.CompilerParams(vmem_limit_bytes=32 << 20),
+        compiler_params=pltpu.CompilerParams(vmem_limit_bytes=52 << 20),
         cost_estimate=SHORT,
     )(left, upstream, weight)
     return d_left, (kept, sent)
@@ -677,14 +677,13 @@
     sums = [d_shift_one, d_scale_one, d_gate_one, d_shift_two, d_scale_two, d_gate_two]
     ada_width = 6 * width
     small_sums = jnp.concatenate(sums + list(bias_grads))
-    qkv_scatter.received, out_scatter.received, *up_sum.received = tie(
-        qkv_scatter.received, out_scatter.received, *up_sum.received
+    qkv_scatter.received, out_scatter.received = tie(
+        qkv_scatter.received, out_scatter.received
     )
     qkv_scatter.third()
-    up_sum.second()
     qkv_shard = qkv_scatter.result()
-    qkv_shard, latent_grad, block_out, small_sums = tie(
-        qkv_shard, latent_grad.astype(jnp.bfloat16), block_out, small_sums
+    qkv_shard, latent_grad, block_out, small_sums, *up_sum.received = tie(
+        qkv_shard, latent_grad.astype(jnp.bfloat16), block_out, small_sums, *up_sum.received
     )
     late_sum = ReplicaSum(
         jnp.concatenate([out_scatter.result(), qkv_shard], axis=1), replicas
@@ -692,11 +691,9 @@
     latent_grad = swap_halves(latent_grad[None]).astype(jnp.float32)
     block_out = swap_halves(block_out[None])
     sums_all = gather_group(small_sums)
-    down_total, *late_sum.received = tie(down_total, *late_sum.received)
+    up_sum.second()
+    down_total, sums_all, *late_sum.received = tie(down_total, sums_all, *late_sum.received)
     late_sum.second()
-    up_total = up_sum.result()
-    late_total = late_sum.result()
-    out_total, qkv_total = late_total[:, :width], late_total[:, width:]
 
     d_group = sums_all[:, :ada_width].reshape(2, 2, 2, ada_width).sum(1).reshape(4, ada_width)
     bias_mine = []
@@ -722,6 +719,12 @@
         [d_group.reshape(-1), silu_mine.astype(jnp.float32).reshape(-1)] + bias_mine
     )
     packed_all = gather_replicas(packed, replicas)
+    packed_all, *late_sum.received = tie(packed_all, *late_sum.received)
+    late_sum.received[0], *up_sum.received = tie(late_sum.received[0], *up_sum.received)
+    up_total = up_sum.result()
+    late_total = late_sum.result()
+    out_total, qkv_total = late_total[:, :width], late_total[:, width:]
+
     d_all = packed_all[:, : 4 * ada_width].reshape(-1, ada_width)
     silu_all = packed_all[:, 4 * ada_width : 4 * ada_width + 4 * rows].reshape(-1, rows)
     ada_total = lax.dot_general(

time: 615 us -> 620 us (level)
  waiting for transfers between devices: 236 us -> 249 us
  local copies, waits for them, and re-layouts: 50.7 us -> 42.3 us
    ppermute x30, waiting for transfers between devices: 118 us -> 154 us  [permute(): return lax.ppermute(values, GROUP, pairs_by(rule))]
    ppermute x12, waiting for transfers between devices: 94 us -> 68.5 us  [send(): return lax.ppermute(values, 'rep', pairs)]
    unnamed x122 -> x124, local copies, waits for them, and re-layouts: 21.4 us -> 11.8 us
  transfers between devices with their start and end apart: 53 -> 53, of which waited for: 18 -> 19; matrix products, arithmetic and copies ran while one was open for 19% -> 19% of each run, Pallas kernels for 14% -> 14%
where the time goes in v10:
time: 620 us; the launch traced here: 613 us
  waiting for transfers between devices  249 us (40%)
  Pallas kernels  154 us (25%)
  other arithmetic  71.8 us (12%)
  starting transfers between devices  64.3 us (10%)
  local copies, waits for them, and re-layouts  42.3 us (7%)
  between operations  16.3 us (3%)
  matrix products  15.7 us (3%)
    ppermute x30, waiting for transfers between devices, permute(): return lax.ppermute(values, GROUP, pairs_by(rule))  154 us
    ppermute x12, waiting for transfers between devices, send(): return lax.ppermute(values, 'rep', pairs)  68.5 us
    pallas_call x2, Pallas kernels, attend_back(): pl.pallas_call(functools.partial(attend_back_kernel, heads[0], low), grid...  48.4 us
    pallas_call x1, Pallas kernels, mlp(): pl.pallas_call(mlp_kernel, grid=(units // block,), out_shape=(jax.ShapeDt...  47.6 us
    ppermute x30, starting transfers between devices, permute(): return lax.ppermute(values, GROUP, pairs_by(rule))  36.7 us
    pallas_call x2, Pallas kernels, product_back(): pl.pallas_call(product_back_kernel, grid=(columns // block,), out_shape=(...  27.3 us
    pallas_call x1, Pallas kernels, attend(): pl.pallas_call(functools.partial(attend_kernel, heads[0], low), grid=(len...  26.9 us
    ppermute x4, waiting for transfers between devices, swap_halves(): received = lax.ppermute(values, GROUP, pairs)  24.7 us
  transfers between devices with their start and end apart: 53, of which 19 were waited for; matrix products, arithmetic and copies ran while one was open for 19% of the time, Pallas kernels for 14%

profile of v10, /device:TPU:9, one launch (start us, length us, event | category | flops | bytes accessed | tf_op | source)
XLA Modules:
  0.0 612.9 jit_solution(16984937174355005986)
XLA Ops:
  18.3 2.0 collective-permute-start
  20.8 43.8 %collective-permute-done.3 = bf16[4,2432]{1,0:T(4,128)(2,1)S(1)} collective-permute-done((bf16[4,2432]{1,0:T(4,128)(2,1)S(1)}, bf16[4,2432]{1,0:T(4,128)(2,1)S(1)}, u32[]{:S(2)}, u32[]{:S(2)}) %collective-permute-start.3) | collective-permute-done | bytes 19488 | tf_op jit(solution)/shard_map/ppermute | solution.py:62
  65.3 2.2 collective-permute-start.4
  67.5 3.1 collective-permute-done.4
  72.5 35.0 %collective-permute-done.5 = f32[1,6912]{1,0:T(1,128)S(1)} collective-permute-done((f32[1,6912]{1,0:T(1,128)S(1)}, f32[1,6912]{1,0:T(1,128)S(1)}, u32[]{:S(2)}, u32[]{:S(2)}) %collective-permute-start.5) | collective-permute-done | bytes 27680 | tf_op jit(solution)/shard_map/ppermute | solution.py:62
  109.5 7.4 %collective-permute-start.13 = (bf16[144,4608]{1,0:T(8,128)(2,1)S(1)}, bf16[144,4608]{1,0:T(8,128)(2,1)S(1)}, u32[]{:S(2)}, u32[]{:S(2)}) collective-permute-start(bf16[144,4608]{1,0:T(8,128)(2,1)S(1)} %collective-permute-done.9.refs_3_), channel_id=1, source_target_pairs={{0,2},{1,3},{2,0},{3,1},{4,6},{5,7},{6,4},{7,5},{8,10},{9,11},{10,... | collective-permute-start | bytes 3981320 | tf_op jit(solution)/shard_map/ppermute | solution.py:62
  119.7 3.5 shard_map.237
  123.2 5.1 add_convert_fusion.2
  131.1 3.5 collective-permute-start.15
  136.1 22.8 %collective-permute-done.15 = bf16[1,512,1152]{2,1,0:T(8,128)(2,1)} collective-permute-done((bf16[1,512,1152]{2,1,0:T(8,128)(2,1)S(1)}, bf16[1,512,1152]{2,1,0:T(8,128)(2,1)}, u32[]{:S(2)}, u32[]{:S(2)}) %collective-permute-start.15) | collective-permute-done | bytes 1179680 | tf_op jit(solution)/shard_map/ppermute | solution.py:68
  158.8 3.5 convert_reduce_fusion.2
  163.7 26.9 %shard_map.238 = (bf16[512,1152]{1,0:T(8,128)(2,1)S(1)}, f32[512,128]{1,0:T(8,128)S(1)}) custom-call(bf16[512,1152]{1,0:T(8,128)(2,1)S(1)} %slice.226.query_ref, bf16[512,2304]{1,0:T(8,128)(2,1)} %slice.227.own_ref, bf16[512,2304]{1,0:T(8,128)(2,1)} %collective-permute-done.14.other_ref), custom_call_target="tpu_custom_call" | custom-call | flops 1048576 | bytes 1048576 | tf_op jit(solution)/shard_map/pallas_call | solution.py:297
  190.7 3.3 fusion.47
  196.8 47.6 %shard_map.239 = (f32[512,1152]{1,0:T(8,128)}, f32[512,1152]{1,0:T(8,128)}, bf16[4,144,4608]{2,1,0:T(8,128)(2,1)}, bf16[4,144,4608]{2,1,0:T(8,128)(2,1)}, bf16[4608,1152]{1,0:T(8,128)(2,1)}, /*index=5*/f32[1,4608]{1,0:T(1,128)}) custom-call(bf16[512,1152]{1,0:T(8,128)(2,1)} %add_convert_fusion.4.hidden_ref, ...), custom_call_target="tpu_custom_call" | custom-call | flops 1048576 | bytes 1048576 | tf_op jit(solution)/shard_map/pallas_call | solution.py:507
  245.1 3.5 multiply_reduce_fusion
  248.9 7.1 %fusion.21 = (f32[1152]{0:T(1024)S(1)}, bf16[512,1152]{1,0:T(8,128)(2,1)}, f32[1152]{0:T(1024)S(1)}, bf16[512,1152]{1,0:T(8,128)(2,1)}, f32[512,1152]{1,0:T(8,128)}) fusion(bf16[1,512,1152]{2,1,0:T(8,128)(2,1)S(1)} %get-tuple-element.155, f32[512,1152]{1,0:T(8,128)} %get-tuple-element.108, f32[1152]{0:T(1024)S(1)} %reshape.147, f32[]{:T(128)} %bitcast.10, ...), kind=kLoop, calls=%fused_computation.43 | loop fusion | flops 12384000 | bytes 13011972 | tf_op jit(solution)/shard_map/reduce_sum | solution.py:626
  256.0 9.1 %shard_map.240 = (f32[512,1152]{1,0:T(8,128)}, bf16[4,144,1152]{2,1,0:T(8,128)(2,1)}, bf16[4,144,1152]{2,1,0:T(8,128)(2,1)}) custom-call(bf16[512,1152]{1,0:T(8,128)(2,1)S(1)} %copy-done.8, bf16[512,1152]{1,0:T(8,128)(2,1)} %get-tuple-element.174.upstream_ref, bf16[1152,1152]{1,0:T(8,128)(2,1)} %copy-done.5), custom_call_target="tpu_custom_call" | custom-call | flops 1048576 | bytes 1048576 | tf_op jit(solution)/shard_map/pallas_call | solution.py:443
  265.1 2.9 convert_element_type.248.upstream_ref
  268.1 3.8 add_convert_fusion
  271.9 2.1 constant_dynamic-slice_fusion.15
  278.2 24.4 %shard_map.241 = (bf16[512,640]{1,0:T(8,128)(2,1)}, f32[2,512,640]{2,1,0:T(8,128)}, bf16[2,512,640]{2,1,0:T(8,128)(2,1)}) custom-call(bf16[512,1152]{1,0:T(8,128)(2,1)} %copy-done.1, bf16[512,2304]{1,0:T(8,128)(2,1)} %slice.227.own_ref, bf16[512,2304]{1,0:T(8,128)(2,1)} %collective-permute-done.14.other_ref, ...), custom_call_target="tpu_custom_call" | custom-call | flops 1048576 | bytes 1048576 | tf_op jit(solution)/shard_map/pallas_call | solution.py:369
  303.9 24.0 %shard_map.242 = (bf16[512,640]{1,0:T(8,128)(2,1)}, f32[2,512,640]{2,1,0:T(8,128)}, bf16[2,512,640]{2,1,0:T(8,128)(2,1)}) custom-call(bf16[512,1152]{1,0:T(8,128)(2,1)} %copy-done.1, bf16[512,2304]{1,0:T(8,128)(2,1)} %slice.227.own_ref, bf16[512,2304]{1,0:T(8,128)(2,1)} %collective-permute-done.14.other_ref, ...), custom_call_target="tpu_custom_call" | custom-call | flops 1048576 | bytes 1048576 | tf_op jit(solution)/shard_map/pallas_call | solution.py:369
  327.9 17.4 %collective-permute-done.18 = bf16[2,144,4608]{2,1,0:T(8,128)(2,1)} collective-permute-done((bf16[2,144,4608]{2,1,0:T(8,128)(2,1)}, bf16[2,144,4608]{2,1,0:T(8,128)(2,1)}, u32[]{:S(2)}, u32[]{:S(2)}) %collective-permute-start.18) | collective-permute-done | bytes 2654240 | tf_op jit(solution)/shard_map/ppermute | solution.py:62
  357.3 18.2 %shard_map.243 = (f32[512,1152]{1,0:T(8,128)}, bf16[4,144,3456]{2,1,0:T(8,128)(2,1)}, bf16[4,144,3456]{2,1,0:T(8,128)(2,1)}) custom-call(bf16[512,1152]{1,0:T(8,128)(2,1)S(1)} %copy-done.4, bf16[512,3456]{1,0:T(8,128)(2,1)} %fusion.24.upstream_ref, bf16[1152,3456]{1,0:T(8,128)(2,1)} %copy-done.2), custom_call_target="tpu_custom_call" | custom-call | flops 1048576 | bytes 1048576 | tf_op jit(solution)/shard_map/pallas_call | solution.py:443
  375.9 2.6 convert_add_fusion
  385.6 2.7 convert_reduce_fusion
  388.3 13.4 %collective-permute-done.22 = bf16[2,144,1152]{2,1,0:T(8,128)(2,1)} collective-permute-done((bf16[2,144,1152]{2,1,0:T(8,128)(2,1)}, bf16[2,144,1152]{2,1,0:T(8,128)(2,1)}, u32[]{:S(2)}, u32[]{:S(2)}) %collective-permute-start.22) | collective-permute-done | bytes 663584 | tf_op jit(solution)/shard_map/ppermute | solution.py:62
  402.9 4.2 fusion.44
  410.9 3.3 add_convert_fusion.1
  419.3 2.1 multiply_reduce_fusion.1
  421.4 5.9 collective-permute-done.24
  427.4 15.1 %collective-permute-done.23 = bf16[2,144,3456]{2,1,0:T(8,128)(2,1)S(1)} collective-permute-done((bf16[2,144,3456]{2,1,0:T(8,128)(2,1)S(1)}, bf16[2,144,3456]{2,1,0:T(8,128)(2,1)S(1)}, u32[]{:S(2)}, u32[]{:S(2)}) %collective-permute-start.23) | collective-permute-done | bytes 1990688 | tf_op jit(solution)/shard_map/ppermute | solution.py:62
  444.2 12.4 %collective-permute-done.25 = bf16[144,3456]{1,0:T(8,128)(2,1)S(1)} collective-permute-done((bf16[144,3456]{1,0:T(8,128)(2,1)S(1)}, bf16[144,3456]{1,0:T(8,128)(2,1)S(1)}, u32[]{:S(2)}, u32[]{:S(2)}) %collective-permute-start.25) | collective-permute-done | bytes 995360 | tf_op jit(solution)/shard_map/ppermute | solution.py:62
  458.4 2.2 collective-permute-done.31
  460.7 4.3 collective-permute-start.32
  468.1 3.1 collective-permute-start.35
  471.2 2.6 collective-permute-done.33
  474.0 3.0 collective-permute-done.34
  477.0 19.3 %collective-permute-done.35 = bf16[144,1152]{1,0:T(8,128)(2,1)} collective-permute-done((bf16[144,1152]{1,0:T(8,128)(2,1)}, bf16[144,1152]{1,0:T(8,128)(2,1)}, u32[]{:S(2)}, u32[]{:S(2)}) %collective-permute-start.35) | collective-permute-done | bytes 331808 | tf_op jit(solution)/shard_map/ppermute | solution.py:209
  496.3 3.6 collective-permute-done.36
  507.2 2.1 collective-permute-start.38
  509.3 2.3 fusion.31
  518.7 2.0 collective-permute-start.46
  529.7 42.6 %collective-permute-done.44 = bf16[144,1152]{1,0:T(8,128)(2,1)S(1)} collective-permute-done((bf16[144,1152]{1,0:T(8,128)(2,1)}, bf16[144,1152]{1,0:T(8,128)(2,1)S(1)}, u32[]{:S(2)}, u32[]{:S(2)}) %collective-permute-start.44) | collective-permute-done | bytes 331808 | tf_op jit(solution)/shard_map/ppermute | solution.py:209
  572.3 4.2 collective-permute-start.30
  586.3 5.2 fusion.51
  597.5 3.9 select_convert_fusion
  603.4 2.5 broadcast_select_fusion
  (343 shorter events, 109.8 us)
Async XLA Ops:
  7.2 189.5 %all-gather.3.cloned.1.call-start = ((), (), s32[]{:S(2)}) async-start(), calls=%async_computation.1 | async-start | bytes 11943936 | tf_op jit(solution)/shard_map/all_gather | solution.py:562
  8.0 188.8 %all-gather.5.cloned.1.call-start = ((), (), s32[]{:S(2)}) async-start(), calls=%async_computation.2 | async-start | bytes 11943936 | tf_op jit(solution)/shard_map/all_gather | solution.py:565
  8.7 348.6 %reduce-scatter.2.cloned.1.call-start = ((), (), s32[]{:S(2)}) async-start(), calls=%async_computation.3 | async-start | bytes 11943936 | tf_op jit(solution)/shard_map/reduce_scatter | solution.py:623
  12.3 8.0 %collective-permute-start.2 = (bf16[2,2432]{1,0:T(2,128)(2,1)S(1)}, bf16[2,2432]{1,0:T(2,128)(2,1)S(1)}, u32[]{:S(2)}, u32[]{:S(2)}) collective-permute-start(bf16[2,2432]{1,0:T(2,128)(2,1)S(1)} %broadcast_select_fusion.6), channel_id=1, source_target_pairs={{0,2},{1,3},{2,0},{3,1},{4,6},{5,7},{6,4},{7,5},{8,10},{9,11},{10,... | collective-permute-start | bytes 29192 | tf_op jit(solution)/shard_map/ppermute | solution.py:62
  15.2 55.8 %collective-permute-start.7 = (bf16[144,4608]{1,0:T(8,128)(2,1)S(1)}, bf16[144,4608]{1,0:T(8,128)(2,1)}, u32[]{:S(2)}, u32[]{:S(2)}) collective-permute-start(bf16[144,4608]{1,0:T(8,128)(2,1)S(1)} %constant_dynamic-update-slice_fusion.refs_0_), channel_id=1, source_target_pairs={{0,4},{1,5},{2,3},{3,2},{4,0},{5,1},{6,7},{7,6},{8,12},{9,13},{10,... | collective-permute-start | bytes 3981320 | tf_op jit(solution)/shard_map/ppermute | solution.py:62
  16.5 92.7 %collective-permute-start.8 = (bf16[144,4608]{1,0:T(8,128)(2,1)S(1)}, bf16[144,4608]{1,0:T(8,128)(2,1)}, u32[]{:S(2)}, u32[]{:S(2)}) collective-permute-start(bf16[144,4608]{1,0:T(8,128)(2,1)S(1)} %constant_dynamic-update-slice_fusion.refs_0_), channel_id=1, source_target_pairs={{0,1},{1,0},{2,6},{3,7},{4,5},{5,4},{6,2},{7,3},{8,9},{9,8},{10,14... | collective-permute-start | bytes 3981320 | tf_op jit(solution)/shard_map/ppermute | solution.py:62
  17.7 101.9 %collective-permute-start.10 = (bf16[144,4608]{1,0:T(8,128)(2,1)S(1)}, bf16[144,4608]{1,0:T(8,128)(2,1)}, u32[]{:S(2)}, u32[]{:S(2)}) collective-permute-start(bf16[144,4608]{1,0:T(8,128)(2,1)S(1)} %constant_dynamic-update-slice_fusion.refs_0_), channel_id=1, source_target_pairs={{0,2},{1,3},{2,0},{3,1},{4,6},{5,7},{6,4},{7,5},{8,10},{9,11},{10,... | collective-permute-start | bytes 3981320 | tf_op jit(solution)/shard_map/ppermute | solution.py:62
  18.3 98.6 %collective-permute-start = (bf16[1,512,1152]{2,1,0:T(8,128)(2,1)}, bf16[1,512,1152]{2,1,0:T(8,128)(2,1)}, u32[]{:S(2)}, u32[]{:S(2)}) collective-permute-start(bf16[1,512,1152]{2,1,0:T(8,128)(2,1)} %param.14), channel_id=1, source_target_pairs={{1,2},{2,1},{5,6},{6,5},{9,10},{10,9},{13,14},{14,13},{17,18},{18,... | collective-permute-start | bytes 3538952 | tf_op jit(solution)/shard_map/ppermute | solution.py:68
  20.3 44.3 %collective-permute-start.3 = (bf16[4,2432]{1,0:T(4,128)(2,1)S(1)}, bf16[4,2432]{1,0:T(4,128)(2,1)S(1)}, u32[]{:S(2)}, u32[]{:S(2)}) collective-permute-start(bf16[4,2432]{1,0:T(4,128)(2,1)S(1)} %maximum_select_fusion.4), channel_id=1, source_target_pairs={{0,4},{1,5},{2,6},{3,7},{4,0},{5,1},{6,2},{7,3},{8,12},{9,13},{10,... | collective-permute-start | bytes 58376 | tf_op jit(solution)/shard_map/ppermute | solution.py:62
  65.3 5.3 collective-permute-start.4
  70.7 36.8 %collective-permute-start.5 = (f32[1,6912]{1,0:T(1,128)S(1)}, f32[1,6912]{1,0:T(1,128)S(1)}, u32[]{:S(2)}, u32[]{:S(2)}) collective-permute-start(f32[1,6912]{1,0:T(1,128)S(1)} %broadcast_select_fusion.4), channel_id=1, source_target_pairs={{0,1},{1,0},{2,3},{3,2},{4,5},{5,4},{6,7},{7,6},{8,9},{9,8},{10,11... | collective-permute-start | bytes 82952 | tf_op jit(solution)/shard_map/ppermute | solution.py:62
  70.9 38.6 %collective-permute-start.9 = (bf16[144,4608]{1,0:T(8,128)(2,1)}, bf16[144,4608]{1,0:T(8,128)(2,1)S(1)}, u32[]{:S(2)}, u32[]{:S(2)}) collective-permute-start(bf16[144,4608]{1,0:T(8,128)(2,1)} %collective-permute-done.7.refs_1_), channel_id=1, source_target_pairs={{0,1},{1,0},{2,6},{3,7},{4,5},{5,4},{6,2},{7,3},{8,9},{9,8},{10,14... | collective-permute-start | bytes 3981320 | tf_op jit(solution)/shard_map/ppermute | solution.py:62
  108.9 10.7 %collective-permute-start.11 = (bf16[144,4608]{1,0:T(8,128)(2,1)}, bf16[144,4608]{1,0:T(8,128)(2,1)S(1)}, u32[]{:S(2)}, u32[]{:S(2)}) collective-permute-start(bf16[144,4608]{1,0:T(8,128)(2,1)} %collective-permute-done.7.refs_1_), channel_id=1, source_target_pairs={{0,2},{1,3},{2,0},{3,1},{4,6},{5,7},{6,4},{7,5},{8,10},{9,11},{10,... | collective-permute-start | bytes 3981320 | tf_op jit(solution)/shard_map/ppermute | solution.py:62
  109.2 10.4 %collective-permute-start.12 = (bf16[144,4608]{1,0:T(8,128)(2,1)}, bf16[144,4608]{1,0:T(8,128)(2,1)S(1)}, u32[]{:S(2)}, u32[]{:S(2)}) collective-permute-start(bf16[144,4608]{1,0:T(8,128)(2,1)} %collective-permute-done.8.refs_2_), channel_id=1, source_target_pairs={{0,2},{1,3},{2,0},{3,1},{4,6},{5,7},{6,4},{7,5},{8,10},{9,11},{10,... | collective-permute-start | bytes 3981320 | tf_op jit(solution)/shard_map/ppermute | solution.py:62
  109.5 10.1 %collective-permute-start.13 = (bf16[144,4608]{1,0:T(8,128)(2,1)S(1)}, bf16[144,4608]{1,0:T(8,128)(2,1)S(1)}, u32[]{:S(2)}, u32[]{:S(2)}) collective-permute-start(bf16[144,4608]{1,0:T(8,128)(2,1)S(1)} %collective-permute-done.9.refs_3_), channel_id=1, source_target_pairs={{0,2},{1,3},{2,0},{3,1},{4,6},{5,7},{6,4},{7,5},{8,10},{9,11},{10,... | collective-permute-start | bytes 3981320 | tf_op jit(solution)/shard_map/ppermute | solution.py:62
  130.8 32.9 %collective-permute-start.14 = (bf16[512,2304]{1,0:T(8,128)(2,1)}, bf16[512,2304]{1,0:T(8,128)(2,1)}, u32[]{:S(2)}, u32[]{:S(2)}) collective-permute-start(bf16[512,2304]{1,0:T(8,128)(2,1)} %slice.227.own_ref), channel_id=1, source_target_pairs={{0,2},{1,3},{2,0},{3,1},{4,6},{5,7},{6,4},{7,5},{8,10},{9,11},{10,... | collective-permute-start | bytes 7077896 | tf_op jit(solution)/shard_map/ppermute | solution.py:62
  131.1 27.7 %collective-permute-start.15 = (bf16[1,512,1152]{2,1,0:T(8,128)(2,1)S(1)}, bf16[1,512,1152]{2,1,0:T(8,128)(2,1)}, u32[]{:S(2)}, u32[]{:S(2)}) collective-permute-start(bf16[1,512,1152]{2,1,0:T(8,128)(2,1)S(1)} %copy-done.34), channel_id=1, source_target_pairs={{1,2},{2,1},{5,6},{6,5},{9,10},{10,9},{13,14},{14,13},{17,18},{18,... | collective-permute-start | bytes 3538952 | tf_op jit(solution)/shard_map/ppermute | solution.py:68
  244.4 229.6 %all-reduce.2.cloned.1.call-start = ((), (), s32[]{:S(2)}) async-start(), calls=%async_computation.4 | async-start | bytes 2654208 | tf_op jit(solution)/shard_map/psum | solution.py:665
  244.9 23.2 %collective-permute-start.16 = (bf16[4,144,4608]{2,1,0:T(8,128)(2,1)}, bf16[4,144,4608]{2,1,0:T(8,128)(2,1)}, u32[]{:S(2)}, u32[]{:S(2)}) collective-permute-start(bf16[4,144,4608]{2,1,0:T(8,128)(2,1)} %get-tuple-element.79), channel_id=1, source_target_pairs={{0,2},{1,3},{2,0},{3,1},{4,6},{5,7},{6,4},{7,5},{8,10},{9,11},{10,... | collective-permute-start | bytes 15925256 | tf_op jit(solution)/shard_map/ppermute | solution.py:62
  275.7 69.6 %collective-permute-start.18 = (bf16[2,144,4608]{2,1,0:T(8,128)(2,1)}, bf16[2,144,4608]{2,1,0:T(8,128)(2,1)}, u32[]{:S(2)}, u32[]{:S(2)}) collective-permute-start(bf16[2,144,4608]{2,1,0:T(8,128)(2,1)} %pad_maximum_fusion.1), channel_id=1, source_target_pairs={{0,4},{1,5},{2,3},{3,2},{4,0},{5,1},{6,7},{7,6},{8,12},{9,13},{10,... | collective-permute-start | bytes 7962632 | tf_op jit(solution)/shard_map/ppermute | solution.py:62
  276.1 26.5 %collective-permute-start.17 = (bf16[4,144,1152]{2,1,0:T(8,128)(2,1)}, bf16[4,144,1152]{2,1,0:T(8,128)(2,1)}, u32[]{:S(2)}, u32[]{:S(2)}) collective-permute-start(bf16[4,144,1152]{2,1,0:T(8,128)(2,1)} %get-tuple-element.83), channel_id=1, source_target_pairs={{0,2},{1,3},{2,0},{3,1},{4,6},{5,7},{6,4},{7,5},{8,10},{9,11},{10,... | collective-permute-start | bytes 3981320 | tf_op jit(solution)/shard_map/ppermute | solution.py:62
  347.9 6.3 %collective-permute-start.19 = (bf16[2,512,1152]{2,1,0:T(8,128)(2,1)S(1)}, bf16[2,512,1152]{2,1,0:T(8,128)(2,1)S(1)}, u32[]{:S(2)}, u32[]{:S(2)}) collective-permute-start(bf16[2,512,1152]{2,1,0:T(8,128)(2,1)S(1)} %pad_maximum_fusion.2), channel_id=1, source_target_pairs={{0,2},{1,3},{2,0},{3,1},{4,6},{5,7},{6,4},{7,5},{8,10},{9,11},{10,... | collective-permute-start | bytes 7077896 | tf_op jit(solution)/shard_map/ppermute | solution.py:62
  375.5 27.4 %collective-permute-start.20 = (bf16[4,144,3456]{2,1,0:T(8,128)(2,1)}, bf16[4,144,3456]{2,1,0:T(8,128)(2,1)}, u32[]{:S(2)}, u32[]{:S(2)}) collective-permute-start(bf16[4,144,3456]{2,1,0:T(8,128)(2,1)} %get-tuple-element.100), channel_id=1, source_target_pairs={{0,2},{1,3},{2,0},{3,1},{4,6},{5,7},{6,4},{7,5},{8,10},{9,11},{10,... | collective-permute-start | bytes 11943944 | tf_op jit(solution)/shard_map/ppermute | solution.py:62
  378.7 24.2 %collective-permute-start.21 = (bf16[144,4608]{1,0:T(8,128)(2,1)S(1)}, bf16[144,4608]{1,0:T(8,128)(2,1)}, u32[]{:S(2)}, u32[]{:S(2)}) collective-permute-start(bf16[144,4608]{1,0:T(8,128)(2,1)S(1)} %fusion.23), channel_id=1, source_target_pairs={{0,1},{1,0},{2,6},{3,7},{4,5},{5,4},{6,2},{7,3},{8,9},{9,8},{10,14... | collective-permute-start | bytes 3981320 | tf_op jit(solution)/shard_map/ppermute | solution.py:62
  384.4 17.3 %collective-permute-start.22 = (bf16[2,144,1152]{2,1,0:T(8,128)(2,1)}, bf16[2,144,1152]{2,1,0:T(8,128)(2,1)}, u32[]{:S(2)}, u32[]{:S(2)}) collective-permute-start(bf16[2,144,1152]{2,1,0:T(8,128)(2,1)} %pad_maximum_fusion.4), channel_id=1, source_target_pairs={{0,4},{1,5},{2,3},{3,2},{4,0},{5,1},{6,7},{7,6},{8,12},{9,13},{10,... | collective-permute-start | bytes 1990664 | tf_op jit(solution)/shard_map/ppermute | solution.py:62
  407.2 49.6 %collective-permute-start.26 = (bf16[144,1152]{1,0:T(8,128)(2,1)S(1)}, bf16[144,1152]{1,0:T(8,128)(2,1)S(1)}, u32[]{:S(2)}, u32[]{:S(2)}) collective-permute-start(bf16[144,1152]{1,0:T(8,128)(2,1)S(1)} %get-tuple-element.183), channel_id=1, source_target_pairs={{0,8},{8,16},{16,24},{24,0},{1,9},{9,17},{17,25},{25,1},{2,10},{10... | collective-permute-start | bytes 995336 | tf_op jit(solution)/shard_map/ppermute | solution.py:209
  408.5 48.4 %collective-permute-start.27 = (bf16[144,1152]{1,0:T(8,128)(2,1)S(1)}, bf16[144,1152]{1,0:T(8,128)(2,1)S(1)}, u32[]{:S(2)}, u32[]{:S(2)}) collective-permute-start(bf16[144,1152]{1,0:T(8,128)(2,1)S(1)} %get-tuple-element.182), channel_id=1, source_target_pairs={{0,16},{8,24},{16,0},{24,8},{1,17},{9,25},{17,1},{25,9},{2,18},{10... | collective-permute-start | bytes 995336 | tf_op jit(solution)/shard_map/ppermute | solution.py:209
  409.6 47.3 %collective-permute-start.28 = (bf16[144,1152]{1,0:T(8,128)(2,1)S(1)}, bf16[144,1152]{1,0:T(8,128)(2,1)S(1)}, u32[]{:S(2)}, u32[]{:S(2)}) collective-permute-start(bf16[144,1152]{1,0:T(8,128)(2,1)S(1)} %get-tuple-element.181), channel_id=1, source_target_pairs={{0,24},{8,0},{16,8},{24,16},{1,25},{9,1},{17,9},{25,17},{2,26},{10... | collective-permute-start | bytes 995336 | tf_op jit(solution)/shard_map/ppermute | solution.py:209
  414.8 27.7 %collective-permute-start.23 = (bf16[2,144,3456]{2,1,0:T(8,128)(2,1)S(1)}, bf16[2,144,3456]{2,1,0:T(8,128)(2,1)S(1)}, u32[]{:S(2)}, u32[]{:S(2)}) collective-permute-start(bf16[2,144,3456]{2,1,0:T(8,128)(2,1)S(1)} %pad_maximum_fusion.3), channel_id=1, source_target_pairs={{0,4},{1,5},{2,3},{3,2},{4,0},{5,1},{6,7},{7,6},{8,12},{9,13},{10,... | collective-permute-start | bytes 5971976 | tf_op jit(solution)/shard_map/ppermute | solution.py:62
  417.5 9.9 %collective-permute-start.24 = (bf16[144,1152]{1,0:T(8,128)(2,1)S(1)}, bf16[144,1152]{1,0:T(8,128)(2,1)S(1)}, u32[]{:S(2)}, u32[]{:S(2)}) collective-permute-start(bf16[144,1152]{1,0:T(8,128)(2,1)S(1)} %fusion.33), channel_id=1, source_target_pairs={{0,1},{1,0},{2,6},{3,7},{4,5},{5,4},{6,2},{7,3},{8,9},{9,8},{10,14... | collective-permute-start | bytes 995336 | tf_op jit(solution)/shard_map/ppermute | solution.py:62
  443.1 13.5 %collective-permute-start.25 = (bf16[144,3456]{1,0:T(8,128)(2,1)S(1)}, bf16[144,3456]{1,0:T(8,128)(2,1)S(1)}, u32[]{:S(2)}, u32[]{:S(2)}) collective-permute-start(bf16[144,3456]{1,0:T(8,128)(2,1)S(1)} %fusion.26), channel_id=1, source_target_pairs={{0,1},{1,0},{2,6},{3,7},{4,5},{5,4},{6,2},{7,3},{8,9},{9,8},{10,14... | collective-permute-start | bytes 2985992 | tf_op jit(solution)/shard_map/ppermute | solution.py:62
  466.2 7.6 %collective-permute-start.33 = (f32[4,16128]{1,0:T(4,128)S(1)}, f32[4,16128]{1,0:T(4,128)S(1)}, u32[]{:S(2)}, u32[]{:S(2)}) collective-permute-start(f32[4,16128]{1,0:T(4,128)S(1)} %maximum_select_fusion.1), channel_id=1, source_target_pairs={{0,4},{1,5},{2,6},{3,7},{4,0},{5,1},{6,2},{7,3},{8,12},{9,13},{10,... | collective-permute-start | bytes 774152 | tf_op jit(solution)/shard_map/ppermute | solution.py:62
  468.0 9.0 %collective-permute-start.34 = (bf16[144,1152]{1,0:T(8,128)(2,1)}, bf16[144,1152]{1,0:T(8,128)(2,1)}, u32[]{:S(2)}, u32[]{:S(2)}) collective-permute-start(bf16[144,1152]{1,0:T(8,128)(2,1)} %get-tuple-element.180), channel_id=1, source_target_pairs={{0,8},{8,16},{16,24},{24,0},{1,9},{9,17},{17,25},{25,1},{2,10},{10... | collective-permute-start | bytes 995336 | tf_op jit(solution)/shard_map/ppermute | solution.py:209
  468.1 28.1 %collective-permute-start.35 = (bf16[144,1152]{1,0:T(8,128)(2,1)}, bf16[144,1152]{1,0:T(8,128)(2,1)}, u32[]{:S(2)}, u32[]{:S(2)}) collective-permute-start(bf16[144,1152]{1,0:T(8,128)(2,1)} %get-tuple-element.179), channel_id=1, source_target_pairs={{0,16},{8,24},{16,0},{24,8},{1,17},{9,25},{17,1},{25,9},{2,18},{10... | collective-permute-start | bytes 995336 | tf_op jit(solution)/shard_map/ppermute | solution.py:209
  471.2 28.7 %collective-permute-start.36 = (bf16[144,1152]{1,0:T(8,128)(2,1)S(1)}, bf16[144,1152]{1,0:T(8,128)(2,1)}, u32[]{:S(2)}, u32[]{:S(2)}) collective-permute-start(bf16[144,1152]{1,0:T(8,128)(2,1)S(1)} %get-tuple-element.178), channel_id=1, source_target_pairs={{0,24},{8,0},{16,8},{24,16},{1,25},{9,1},{17,9},{25,17},{2,26},{10... | collective-permute-start | bytes 995336 | tf_op jit(solution)/shard_map/ppermute | solution.py:209
  505.7 15.8 %collective-permute-start.40 = (f32[29376]{0:T(1024)}, f32[29376]{0:T(1024)}, u32[]{:S(2)}, u32[]{:S(2)}) collective-permute-start(f32[29376]{0:T(1024)} %concatenate.131), channel_id=1, source_target_pairs={{0,8},{8,16},{16,24},{24,0},{1,9},{9,17},{17,25},{25,1},{2,10},{10... | collective-permute-start | bytes 352520 | tf_op jit(solution)/shard_map/ppermute | solution.py:90
  505.7 17.9 %collective-permute-start.41 = (f32[29376]{0:T(1024)}, f32[29376]{0:T(1024)}, u32[]{:S(2)}, u32[]{:S(2)}) collective-permute-start(f32[29376]{0:T(1024)} %concatenate.131), channel_id=1, source_target_pairs={{0,16},{8,24},{16,0},{24,8},{1,17},{9,25},{17,1},{25,9},{2,18},{10... | collective-permute-start | bytes 352520 | tf_op jit(solution)/shard_map/ppermute | solution.py:90
  505.7 20.3 %collective-permute-start.42 = (f32[29376]{0:T(1024)}, f32[29376]{0:T(1024)}, u32[]{:S(2)}, u32[]{:S(2)}) collective-permute-start(f32[29376]{0:T(1024)} %concatenate.131), channel_id=1, source_target_pairs={{0,24},{8,0},{16,8},{24,16},{1,25},{9,1},{17,9},{25,17},{2,26},{10... | collective-permute-start | bytes 352520 | tf_op jit(solution)/shard_map/ppermute | solution.py:90
  507.2 5.5 collective-permute-start.38
  511.6 15.5 %collective-permute-start.43 = (bf16[144,1152]{1,0:T(8,128)(2,1)}, bf16[144,1152]{1,0:T(8,128)(2,1)}, u32[]{:S(2)}, u32[]{:S(2)}) collective-permute-start(bf16[144,1152]{1,0:T(8,128)(2,1)} %fusion.31), channel_id=1, source_target_pairs={{0,8},{8,16},{16,24},{24,0},{1,9},{9,17},{17,25},{25,1},{2,10},{10... | collective-permute-start | bytes 995336 | tf_op jit(solution)/shard_map/ppermute | solution.py:209
  512.7 6.0 collective-permute-start.39
  518.7 60.7 %collective-permute-start.46 = (bf16[144,1152]{1,0:T(8,128)(2,1)S(1)}, bf16[144,1152]{1,0:T(8,128)(2,1)}, u32[]{:S(2)}, u32[]{:S(2)}) collective-permute-start(bf16[144,1152]{1,0:T(8,128)(2,1)S(1)} %add_convert_fusion.5), channel_id=1, source_target_pairs={{0,8},{8,16},{16,24},{24,0},{1,9},{9,17},{17,25},{25,1},{2,10},{10... | collective-permute-start | bytes 995336 | tf_op jit(solution)/shard_map/ppermute | solution.py:209
  521.5 57.9 %collective-permute-start.47 = (bf16[144,1152]{1,0:T(8,128)(2,1)S(1)}, bf16[144,1152]{1,0:T(8,128)(2,1)S(1)}, u32[]{:S(2)}, u32[]{:S(2)}) collective-permute-start(bf16[144,1152]{1,0:T(8,128)(2,1)S(1)} %add_convert_fusion.5), channel_id=1, source_target_pairs={{0,16},{8,24},{16,0},{24,8},{1,17},{9,25},{17,1},{25,9},{2,18},{10... | collective-permute-start | bytes 995336 | tf_op jit(solution)/shard_map/ppermute | solution.py:209
  523.6 56.6 %collective-permute-start.48 = (bf16[144,1152]{1,0:T(8,128)(2,1)S(1)}, bf16[144,1152]{1,0:T(8,128)(2,1)}, u32[]{:S(2)}, u32[]{:S(2)}) collective-permute-start(bf16[144,1152]{1,0:T(8,128)(2,1)S(1)} %add_convert_fusion.5), channel_id=1, source_target_pairs={{0,24},{8,0},{16,8},{24,16},{1,25},{9,1},{17,9},{25,17},{2,26},{10... | collective-permute-start | bytes 995336 | tf_op jit(solution)/shard_map/ppermute | solution.py:209
  526.1 46.3 %collective-permute-start.44 = (bf16[144,1152]{1,0:T(8,128)(2,1)}, bf16[144,1152]{1,0:T(8,128)(2,1)S(1)}, u32[]{:S(2)}, u32[]{:S(2)}) collective-permute-start(bf16[144,1152]{1,0:T(8,128)(2,1)} %fusion.31), channel_id=1, source_target_pairs={{0,16},{8,24},{16,0},{24,8},{1,17},{9,25},{17,1},{25,9},{2,18},{10... | collective-permute-start | bytes 995336 | tf_op jit(solution)/shard_map/ppermute | solution.py:209
  527.1 49.4 %collective-permute-start.45 = (bf16[144,1152]{1,0:T(8,128)(2,1)}, bf16[144,1152]{1,0:T(8,128)(2,1)S(1)}, u32[]{:S(2)}, u32[]{:S(2)}) collective-permute-start(bf16[144,1152]{1,0:T(8,128)(2,1)} %fusion.31), channel_id=1, source_target_pairs={{0,24},{8,0},{16,8},{24,16},{1,25},{9,1},{17,9},{25,17},{2,26},{10... | collective-permute-start | bytes 995336 | tf_op jit(solution)/shard_map/ppermute | solution.py:209
  572.3 25.2 %collective-permute-start.30 = (bf16[1,512,1152]{2,1,0:T(8,128)(2,1)}, bf16[1,512,1152]{2,1,0:T(8,128)(2,1)}, u32[]{:S(2)}, u32[]{:S(2)}) collective-permute-start(bf16[1,512,1152]{2,1,0:T(8,128)(2,1)} %bitcast.104), channel_id=1, source_target_pairs={{1,2},{2,1},{5,6},{6,5},{9,10},{10,9},{13,14},{14,13},{17,18},{18,... | collective-permute-start | bytes 3538952 | tf_op jit(solution)/shard_map/ppermute | solution.py:68
  576.6 26.8 %collective-permute-start.29 = (bf16[1,512,1152]{2,1,0:T(8,128)(2,1)S(1)}, bf16[1,512,1152]{2,1,0:T(8,128)(2,1)}, u32[]{:S(2)}, u32[]{:S(2)}) collective-permute-start(bf16[1,512,1152]{2,1,0:T(8,128)(2,1)S(1)} %bitcast.103), channel_id=1, source_target_pairs={{1,2},{2,1},{5,6},{6,5},{9,10},{10,9},{13,14},{14,13},{17,18},{18,... | collective-permute-start | bytes 3538952 | tf_op jit(solution)/shard_map/ppermute | solution.py:68
  (60 other events, 473.0 us)
Sparse Core Ops, SparseCore 0:
  10.0 100.8 all-gather.2
  112.7 74.2 all-gather.4
  244.6 103.7 reduce-scatter.1
  385.7 78.0 all-reduce.1

commit v11 on v10

--- a/solution.py
+++ b/solution.py
@@ -180,10 +180,16 @@
         self.kept = pair(mine)
         self.received = permute(pair(mine ^ near), first_rule)
 
+    def add_third(self):
+        kept = self.kept.astype(jnp.float32) + self.received.astype(jnp.float32)
+        self.kept, self.sent = kept[0], kept[1].astype(self.low)
+
+    def send_third(self):
+        self.received = permute(self.sent, second_rule)
+
     def third(self):
-        kept = self.kept.astype(jnp.float32) + self.received.astype(jnp.float32)
-        self.kept = kept[0]
-        self.received = permute(kept[1].astype(self.low), second_rule)
+        self.add_third()
+        self.send_third()
 
     def result(self):
         return self.kept + self.received.astype(jnp.float32)
@@ -642,29 +648,35 @@
     d_query, d_attended, out_scatter.received = tie(left[0], d_attended, out_scatter.received)
     out_scatter.second()
     right = attend_back(query, pair_own, pair_other, d_attended, log_rows, halves[1])
-    *right, up_scatter.received = tie(*right, up_scatter.received)
-    up_scatter.third()
+    *right, up_scatter.received, out_scatter.received = tie(
+        *right, up_scatter.received, out_scatter.received
+    )
+    up_scatter.add_third()
+    out_scatter.add_third()
     d_query = join_heads(d_query, right[0], width)
     d_own = join_heads(left[1], right[1], width)
     d_other = permute(join_heads(left[2], right[2], width), core_rule)
     d_own = (d_own + d_other.astype(jnp.float32)).astype(jnp.bfloat16)
     d_projected = jnp.concatenate([d_query, d_own[0], d_own[1]], axis=-1)
 
-    d_projected, down_shard = tie(d_projected, down_shard)
+    d_projected, down_shard, up_scatter.sent, out_scatter.sent = tie(
+        d_projected, down_shard, up_scatter.sent, out_scatter.sent
+    )
+    up_scatter.send_third()
+    out_scatter.send_third()
+    down_total = lax.psum(down_shard, "rep")
     d_hidden_one, qkv_halves = product_back(hidden_one, d_projected, full_qkv)
     qkv_scatter = Scatter(qkv_halves)
-    column_sums = jnp.sum(d_projected.astype(jnp.float32), axis=0)
-    d_hidden_one, *arrived = tie(
+    d_hidden_one, d_projected, *arrived = tie(
         d_hidden_one,
+        d_projected,
         qkv_scatter.received,
         up_scatter.received,
-        out_scatter.received,
-    )
-    qkv_scatter.received, up_scatter.received, out_scatter.received = arrived
+    )
+    qkv_scatter.received, up_scatter.received = arrived
     qkv_scatter.second()
-    down_total = lax.psum(down_shard, "rep")
     up_sum = ReplicaSum(up_scatter.result(), replicas)
-    out_scatter.third()
+    column_sums = jnp.sum(d_projected.astype(jnp.float32), axis=0)
     d_shift_one = jnp.sum(d_hidden_one, axis=0)
     d_scale_one = jnp.sum(d_hidden_one * normed_one, axis=0)
     latent_grad = d_middle + norm_back(d_hidden_one * (1.0 + scale_one), normed_one, inverse_one)
@@ -688,11 +700,13 @@
     late_sum = ReplicaSum(
         jnp.concatenate([out_scatter.result(), qkv_shard], axis=1), replicas
     )
-    latent_grad = swap_halves(latent_grad[None]).astype(jnp.float32)
+    latent_grad = swap_halves(latent_grad[None])
     block_out = swap_halves(block_out[None])
     sums_all = gather_group(small_sums)
     up_sum.second()
-    down_total, sums_all, *late_sum.received = tie(down_total, sums_all, *late_sum.received)
+    down_total, sums_all, latent_grad, block_out, *late_sum.received = tie(
+        down_total, sums_all, latent_grad, block_out, *late_sum.received
+    )
     late_sum.second()
 
     d_group = sums_all[:, :ada_width].reshape(2, 2, 2, ada_width).sum(1).reshape(4, ada_width)
@@ -742,7 +756,7 @@
     )
     return (
         block_out,
-        latent_grad,
+        latent_grad.astype(jnp.float32),
         cond_grad,
         ada_total,
         ada_bias_total,

time: 620 us -> 611 us (0.985)
    ppermute x12, waiting for transfers between devices: 68.5 us -> 42.7 us  [send(): return lax.ppermute(values, 'rep', pairs)]
    ppermute x4, waiting for transfers between devices: 24.7 us -> 44.1 us  [swap_halves(): received = lax.ppermute(values, GROUP, pairs)]
    ppermute x3, waiting for transfers between devices: 0.01 us -> 14.1 us  [gather_replicas(): stacked.append(lax.ppermute(values, 'rep', pairs))]
    unnamed x124 -> x116, local copies, waits for them, and re-layouts: 11.8 us -> 13.4 us
  transfers between devices with their start and end apart: 53 -> 53, of which waited for: 19 -> 19; matrix products, arithmetic and copies ran while one was open for 19% -> 16% of each run, Pallas kernels for 14% -> 15%
where the time goes in v11:
time: 611 us; the launch traced here: 604 us
  waiting for transfers between devices  251 us (41%)
  Pallas kernels  154 us (25%)
  other arithmetic  67.1 us (11%)
  starting transfers between devices  61.2 us (10%)
  local copies, waits for them, and re-layouts  39.8 us (7%)
  between operations  16 us (3%)
  matrix products  15.7 us (3%)
    ppermute x30, waiting for transfers between devices, permute(): return lax.ppermute(values, GROUP, pairs_by(rule))  148 us
    pallas_call x2, Pallas kernels, attend_back(): pl.pallas_call(functools.partial(attend_back_kernel, heads[0], low), grid...  48.4 us
    pallas_call x1, Pallas kernels, mlp(): pl.pallas_call(mlp_kernel, grid=(units // block,), out_shape=(jax.ShapeDt...  47.7 us
    ppermute x4, waiting for transfers between devices, swap_halves(): received = lax.ppermute(values, GROUP, pairs)  44.1 us
    ppermute x12, waiting for transfers between devices, send(): return lax.ppermute(values, 'rep', pairs)  42.7 us
    ppermute x30, starting transfers between devices, permute(): return lax.ppermute(values, GROUP, pairs_by(rule))  33.5 us
    pallas_call x2, Pallas kernels, product_back(): pl.pallas_call(product_back_kernel, grid=(columns // block,), out_shape=(...  27.1 us
    pallas_call x1, Pallas kernels, attend(): pl.pallas_call(functools.partial(attend_kernel, heads[0], low), grid=(len...  26.9 us
  transfers between devices with their start and end apart: 53, of which 19 were waited for; matrix products, arithmetic and copies ran while one was open for 16% of the time, Pallas kernels for 15%

profile of v11, /device:TPU:9, one launch (start us, length us, event | category | flops | bytes accessed | tf_op | source)
XLA Modules:
  0.0 604.0 jit_solution(10022786555957858572)
XLA Ops:
  12.3 1.9 collective-permute-start.2
  18.3 2.0 collective-permute-start
  20.8 43.8 %collective-permute-done.3 = bf16[4,2432]{1,0:T(4,128)(2,1)S(1)} collective-permute-done((bf16[4,2432]{1,0:T(4,128)(2,1)S(1)}, bf16[4,2432]{1,0:T(4,128)(2,1)S(1)}, u32[]{:S(2)}, u32[]{:S(2)}) %collective-permute-start.3) | collective-permute-done | bytes 19488 | tf_op jit(solution)/shard_map/ppermute | solution.py:62
  65.3 2.2 collective-permute-start.4
  67.5 3.1 collective-permute-done.4
  72.5 35.0 %collective-permute-done.5 = f32[1,6912]{1,0:T(1,128)S(1)} collective-permute-done((f32[1,6912]{1,0:T(1,128)S(1)}, f32[1,6912]{1,0:T(1,128)S(1)}, u32[]{:S(2)}, u32[]{:S(2)}) %collective-permute-start.5) | collective-permute-done | bytes 27680 | tf_op jit(solution)/shard_map/ppermute | solution.py:62
  109.5 7.4 %collective-permute-start.13 = (bf16[144,4608]{1,0:T(8,128)(2,1)S(1)}, bf16[144,4608]{1,0:T(8,128)(2,1)S(1)}, u32[]{:S(2)}, u32[]{:S(2)}) collective-permute-start(bf16[144,4608]{1,0:T(8,128)(2,1)S(1)} %collective-permute-done.9.refs_3_), channel_id=1, source_target_pairs={{0,2},{1,3},{2,0},{3,1},{4,6},{5,7},{6,4},{7,5},{8,10},{9,11},{10,... | collective-permute-start | bytes 3981320 | tf_op jit(solution)/shard_map/ppermute | solution.py:62
  119.7 3.5 shard_map.237
  123.2 5.1 add_convert_fusion.2
  131.1 3.4 collective-permute-start.15
  136.1 22.8 %collective-permute-done.15 = bf16[1,512,1152]{2,1,0:T(8,128)(2,1)} collective-permute-done((bf16[1,512,1152]{2,1,0:T(8,128)(2,1)S(1)}, bf16[1,512,1152]{2,1,0:T(8,128)(2,1)}, u32[]{:S(2)}, u32[]{:S(2)}) %collective-permute-start.15) | collective-permute-done | bytes 1179680 | tf_op jit(solution)/shard_map/ppermute | solution.py:68
  158.9 3.5 convert_reduce_fusion.2
  163.8 26.9 %shard_map.238 = (bf16[512,1152]{1,0:T(8,128)(2,1)S(1)}, f32[512,128]{1,0:T(8,128)S(1)}) custom-call(bf16[512,1152]{1,0:T(8,128)(2,1)S(1)} %slice.226.query_ref, bf16[512,2304]{1,0:T(8,128)(2,1)} %slice.227.own_ref, bf16[512,2304]{1,0:T(8,128)(2,1)} %collective-permute-done.14.other_ref), custom_call_target="tpu_custom_call" | custom-call | flops 1048576 | bytes 1048576 | tf_op jit(solution)/shard_map/pallas_call | solution.py:303
  190.7 3.3 fusion.47
  196.8 47.7 %shard_map.239 = (f32[512,1152]{1,0:T(8,128)}, f32[512,1152]{1,0:T(8,128)}, bf16[4,144,4608]{2,1,0:T(8,128)(2,1)}, bf16[4,144,4608]{2,1,0:T(8,128)(2,1)}, bf16[4608,1152]{1,0:T(8,128)(2,1)}, /*index=5*/f32[1,4608]{1,0:T(1,128)}) custom-call(bf16[512,1152]{1,0:T(8,128)(2,1)} %add_convert_fusion.4.hidden_ref, ...), custom_call_target="tpu_custom_call" | custom-call | flops 1048576 | bytes 1048576 | tf_op jit(solution)/shard_map/pallas_call | solution.py:513
  245.0 3.5 multiply_reduce_fusion
  248.8 6.9 %fusion.21 = (f32[1152]{0:T(1024)S(1)}, bf16[512,1152]{1,0:T(8,128)(2,1)}, f32[1152]{0:T(1024)S(1)}, bf16[512,1152]{1,0:T(8,128)(2,1)}, f32[512,1152]{1,0:T(8,128)}) fusion(bf16[1,512,1152]{2,1,0:T(8,128)(2,1)S(1)} %get-tuple-element.165, f32[512,1152]{1,0:T(8,128)} %get-tuple-element.116, f32[1152]{0:T(1024)S(1)} %reshape.147, f32[]{:T(128)} %bitcast.10, ...), kind=kLoop, calls=%fused_computation.43 | loop fusion | flops 12384000 | bytes 13011972 | tf_op jit(solution)/shard_map/reduce_sum | solution.py:632
  255.7 9.1 %shard_map.240 = (f32[512,1152]{1,0:T(8,128)}, bf16[4,144,1152]{2,1,0:T(8,128)(2,1)}, bf16[4,144,1152]{2,1,0:T(8,128)(2,1)}) custom-call(bf16[512,1152]{1,0:T(8,128)(2,1)S(1)} %copy-done.8, bf16[512,1152]{1,0:T(8,128)(2,1)} %get-tuple-element.184.upstream_ref, bf16[1152,1152]{1,0:T(8,128)(2,1)} %copy-done.5), custom_call_target="tpu_custom_call" | custom-call | flops 1048576 | bytes 1048576 | tf_op jit(solution)/shard_map/pallas_call | solution.py:449
  264.8 3.0 convert_element_type.248.upstream_ref
  268.5 3.8 add_convert_fusion
  272.3 2.2 constant_dynamic-slice_fusion.13
  277.0 24.5 %shard_map.241 = (bf16[512,640]{1,0:T(8,128)(2,1)}, f32[2,512,640]{2,1,0:T(8,128)}, bf16[2,512,640]{2,1,0:T(8,128)(2,1)}) custom-call(bf16[512,1152]{1,0:T(8,128)(2,1)} %copy-done.1, bf16[512,2304]{1,0:T(8,128)(2,1)} %slice.227.own_ref, bf16[512,2304]{1,0:T(8,128)(2,1)} %collective-permute-done.14.other_ref, ...), custom_call_target="tpu_custom_call" | custom-call | flops 1048576 | bytes 1048576 | tf_op jit(solution)/shard_map/pallas_call | solution.py:375
  306.9 23.9 %shard_map.242 = (bf16[512,640]{1,0:T(8,128)(2,1)}, f32[2,512,640]{2,1,0:T(8,128)}, bf16[2,512,640]{2,1,0:T(8,128)(2,1)}) custom-call(bf16[512,1152]{1,0:T(8,128)(2,1)} %copy-done.1, bf16[512,2304]{1,0:T(8,128)(2,1)} %slice.227.own_ref, bf16[512,2304]{1,0:T(8,128)(2,1)} %collective-permute-done.14.other_ref, ...), custom_call_target="tpu_custom_call" | custom-call | flops 1048576 | bytes 1048576 | tf_op jit(solution)/shard_map/pallas_call | solution.py:375
  330.8 1.9 slice_dynamic-update-slice_fusion.1
  332.7 20.7 %collective-permute-done.19 = bf16[2,144,1152]{2,1,0:T(8,128)(2,1)} collective-permute-done((bf16[2,144,1152]{2,1,0:T(8,128)(2,1)}, bf16[2,144,1152]{2,1,0:T(8,128)(2,1)}, u32[]{:S(2)}, u32[]{:S(2)}) %collective-permute-start.19) | collective-permute-done | bytes 663584 | tf_op jit(solution)/shard_map/ppermute | solution.py:62
  362.8 2.5 convert_add_fusion
  365.3 2.3 copy-done.15
  371.8 18.0 %shard_map.243 = (f32[512,1152]{1,0:T(8,128)}, bf16[4,144,3456]{2,1,0:T(8,128)(2,1)}, bf16[4,144,3456]{2,1,0:T(8,128)(2,1)}) custom-call(bf16[512,1152]{1,0:T(8,128)(2,1)S(1)} %copy-done.4, bf16[512,3456]{1,0:T(8,128)(2,1)} %fusion.24.upstream_ref, bf16[1152,3456]{1,0:T(8,128)(2,1)} %copy-done.2), custom_call_target="tpu_custom_call" | custom-call | flops 1048576 | bytes 1048576 | tf_op jit(solution)/shard_map/pallas_call | solution.py:449
  391.9 15.6 %collective-permute-done.22 = bf16[144,4608]{1,0:T(8,128)(2,1)S(1)} collective-permute-done((bf16[144,4608]{1,0:T(8,128)(2,1)}, bf16[144,4608]{1,0:T(8,128)(2,1)S(1)}, u32[]{:S(2)}, u32[]{:S(2)}) %collective-permute-start.22) | collective-permute-done | bytes 1327136 | tf_op jit(solution)/shard_map/ppermute | solution.py:62
  407.5 3.8 fusion.44
  411.3 3.2 add_convert_fusion.1
  422.7 16.6 %collective-permute-done.23 = bf16[2,144,3456]{2,1,0:T(8,128)(2,1)S(1)} collective-permute-done((bf16[2,144,3456]{2,1,0:T(8,128)(2,1)S(1)}, bf16[2,144,3456]{2,1,0:T(8,128)(2,1)S(1)}, u32[]{:S(2)}, u32[]{:S(2)}) %collective-permute-start.23) | collective-permute-done | bytes 1990688 | tf_op jit(solution)/shard_map/ppermute | solution.py:62
  440.6 2.7 convert_reduce_fusion
  443.4 10.0 %collective-permute-done.25 = bf16[144,3456]{1,0:T(8,128)(2,1)S(1)} collective-permute-done((bf16[144,3456]{1,0:T(8,128)(2,1)S(1)}, bf16[144,3456]{1,0:T(8,128)(2,1)S(1)}, u32[]{:S(2)}, u32[]{:S(2)}) %collective-permute-start.25) | collective-permute-done | bytes 995360 | tf_op jit(solution)/shard_map/ppermute | solution.py:62
  453.6 3.2 collective-permute-done.27
  456.9 5.7 collective-permute-done.28
  466.4 2.8 collective-permute-start.30
  473.2 4.4 collective-permute-start.33
  477.9 3.6 collective-permute-start.32
  481.7 9.8 %collective-permute-done.33 = bf16[1,512,1152]{2,1,0:T(8,128)(2,1)S(1)} collective-permute-done((bf16[1,512,1152]{2,1,0:T(8,128)(2,1)S(1)}, bf16[1,512,1152]{2,1,0:T(8,128)(2,1)S(1)}, u32[]{:S(2)}, u32[]{:S(2)}) %collective-permute-start.33) | collective-permute-done | bytes 1179680 | tf_op jit(solution)/shard_map/ppermute | solution.py:68
  492.6 11.5 %collective-permute-done.32 = bf16[1,512,1152]{2,1,0:T(8,128)(2,1)S(1)} collective-permute-done((bf16[1,512,1152]{2,1,0:T(8,128)(2,1)S(1)}, bf16[1,512,1152]{2,1,0:T(8,128)(2,1)S(1)}, u32[]{:S(2)}, u32[]{:S(2)}) %collective-permute-start.32) | collective-permute-done | bytes 1179680 | tf_op jit(solution)/shard_map/ppermute | solution.py:68
  510.9 3.0 collective-permute-start.41
  513.9 3.0 collective-permute-start.38
  526.0 2.0 collective-permute-start.47
  530.8 14.1 %collective-permute-done.42 = f32[29376]{0:T(1024)} collective-permute-done((f32[29376]{0:T(1024)S(1)}, f32[29376]{0:T(1024)}, u32[]{:S(2)}, u32[]{:S(2)}) %collective-permute-start.42) | collective-permute-done | bytes 117536 | tf_op jit(solution)/shard_map/ppermute | solution.py:90
  546.6 32.0 %collective-permute-done.44 = bf16[144,1152]{1,0:T(8,128)(2,1)S(1)} collective-permute-done((bf16[144,1152]{1,0:T(8,128)(2,1)S(1)}, bf16[144,1152]{1,0:T(8,128)(2,1)S(1)}, u32[]{:S(2)}, u32[]{:S(2)}) %collective-permute-start.44) | collective-permute-done | bytes 331808 | tf_op jit(solution)/shard_map/ppermute | solution.py:215
  578.6 1.8 collective-permute-done.45
  588.0 5.2 fusion.51
  (336 shorter events, 100.3 us)
Async XLA Ops:
  7.2 189.6 %all-gather.3.cloned.1.call-start = ((), (), s32[]{:S(2)}) async-start(), calls=%async_computation.1 | async-start | bytes 11943936 | tf_op jit(solution)/shard_map/all_gather | solution.py:568
  8.0 188.8 %all-gather.5.cloned.1.call-start = ((), (), s32[]{:S(2)}) async-start(), calls=%async_computation.2 | async-start | bytes 11943936 | tf_op jit(solution)/shard_map/all_gather | solution.py:571
  8.7 363.1 %reduce-scatter.2.cloned.1.call-start = ((), (), s32[]{:S(2)}) async-start(), calls=%async_computation.3 | async-start | bytes 11943936 | tf_op jit(solution)/shard_map/reduce_scatter | solution.py:629
  12.3 8.0 %collective-permute-start.2 = (bf16[2,2432]{1,0:T(2,128)(2,1)S(1)}, bf16[2,2432]{1,0:T(2,128)(2,1)S(1)}, u32[]{:S(2)}, u32[]{:S(2)}) collective-permute-start(bf16[2,2432]{1,0:T(2,128)(2,1)S(1)} %broadcast_select_fusion.7), channel_id=1, source_target_pairs={{0,2},{1,3},{2,0},{3,1},{4,6},{5,7},{6,4},{7,5},{8,10},{9,11},{10,... | collective-permute-start | bytes 29192 | tf_op jit(solution)/shard_map/ppermute | solution.py:62
  15.2 55.8 %collective-permute-start.7 = (bf16[144,4608]{1,0:T(8,128)(2,1)S(1)}, bf16[144,4608]{1,0:T(8,128)(2,1)}, u32[]{:S(2)}, u32[]{:S(2)}) collective-permute-start(bf16[144,4608]{1,0:T(8,128)(2,1)S(1)} %constant_dynamic-update-slice_fusion.refs_0_), channel_id=1, source_target_pairs={{0,4},{1,5},{2,3},{3,2},{4,0},{5,1},{6,7},{7,6},{8,12},{9,13},{10,... | collective-permute-start | bytes 3981320 | tf_op jit(solution)/shard_map/ppermute | solution.py:62
  16.5 92.7 %collective-permute-start.8 = (bf16[144,4608]{1,0:T(8,128)(2,1)S(1)}, bf16[144,4608]{1,0:T(8,128)(2,1)}, u32[]{:S(2)}, u32[]{:S(2)}) collective-permute-start(bf16[144,4608]{1,0:T(8,128)(2,1)S(1)} %constant_dynamic-update-slice_fusion.refs_0_), channel_id=1, source_target_pairs={{0,1},{1,0},{2,6},{3,7},{4,5},{5,4},{6,2},{7,3},{8,9},{9,8},{10,14... | collective-permute-start | bytes 3981320 | tf_op jit(solution)/shard_map/ppermute | solution.py:62
  17.7 101.9 %collective-permute-start.10 = (bf16[144,4608]{1,0:T(8,128)(2,1)S(1)}, bf16[144,4608]{1,0:T(8,128)(2,1)}, u32[]{:S(2)}, u32[]{:S(2)}) collective-permute-start(bf16[144,4608]{1,0:T(8,128)(2,1)S(1)} %constant_dynamic-update-slice_fusion.refs_0_), channel_id=1, source_target_pairs={{0,2},{1,3},{2,0},{3,1},{4,6},{5,7},{6,4},{7,5},{8,10},{9,11},{10,... | collective-permute-start | bytes 3981320 | tf_op jit(solution)/shard_map/ppermute | solution.py:62
  18.3 98.6 %collective-permute-start = (bf16[1,512,1152]{2,1,0:T(8,128)(2,1)}, bf16[1,512,1152]{2,1,0:T(8,128)(2,1)}, u32[]{:S(2)}, u32[]{:S(2)}) collective-permute-start(bf16[1,512,1152]{2,1,0:T(8,128)(2,1)} %param.14), channel_id=1, source_target_pairs={{1,2},{2,1},{5,6},{6,5},{9,10},{10,9},{13,14},{14,13},{17,18},{18,... | collective-permute-start | bytes 3538952 | tf_op jit(solution)/shard_map/ppermute | solution.py:68
  20.3 44.3 %collective-permute-start.3 = (bf16[4,2432]{1,0:T(4,128)(2,1)S(1)}, bf16[4,2432]{1,0:T(4,128)(2,1)S(1)}, u32[]{:S(2)}, u32[]{:S(2)}) collective-permute-start(bf16[4,2432]{1,0:T(4,128)(2,1)S(1)} %maximum_select_fusion.4), channel_id=1, source_target_pairs={{0,4},{1,5},{2,6},{3,7},{4,0},{5,1},{6,2},{7,3},{8,12},{9,13},{10,... | collective-permute-start | bytes 58376 | tf_op jit(solution)/shard_map/ppermute | solution.py:62
  65.3 5.3 collective-permute-start.4
  70.7 36.8 %collective-permute-start.5 = (f32[1,6912]{1,0:T(1,128)S(1)}, f32[1,6912]{1,0:T(1,128)S(1)}, u32[]{:S(2)}, u32[]{:S(2)}) collective-permute-start(f32[1,6912]{1,0:T(1,128)S(1)} %broadcast_select_fusion.5), channel_id=1, source_target_pairs={{0,1},{1,0},{2,3},{3,2},{4,5},{5,4},{6,7},{7,6},{8,9},{9,8},{10,11... | collective-permute-start | bytes 82952 | tf_op jit(solution)/shard_map/ppermute | solution.py:62
  70.9 38.6 %collective-permute-start.9 = (bf16[144,4608]{1,0:T(8,128)(2,1)}, bf16[144,4608]{1,0:T(8,128)(2,1)S(1)}, u32[]{:S(2)}, u32[]{:S(2)}) collective-permute-start(bf16[144,4608]{1,0:T(8,128)(2,1)} %collective-permute-done.7.refs_1_), channel_id=1, source_target_pairs={{0,1},{1,0},{2,6},{3,7},{4,5},{5,4},{6,2},{7,3},{8,9},{9,8},{10,14... | collective-permute-start | bytes 3981320 | tf_op jit(solution)/shard_map/ppermute | solution.py:62
  108.9 10.7 %collective-permute-start.11 = (bf16[144,4608]{1,0:T(8,128)(2,1)}, bf16[144,4608]{1,0:T(8,128)(2,1)S(1)}, u32[]{:S(2)}, u32[]{:S(2)}) collective-permute-start(bf16[144,4608]{1,0:T(8,128)(2,1)} %collective-permute-done.7.refs_1_), channel_id=1, source_target_pairs={{0,2},{1,3},{2,0},{3,1},{4,6},{5,7},{6,4},{7,5},{8,10},{9,11},{10,... | collective-permute-start | bytes 3981320 | tf_op jit(solution)/shard_map/ppermute | solution.py:62
  109.2 10.4 %collective-permute-start.12 = (bf16[144,4608]{1,0:T(8,128)(2,1)}, bf16[144,4608]{1,0:T(8,128)(2,1)S(1)}, u32[]{:S(2)}, u32[]{:S(2)}) collective-permute-start(bf16[144,4608]{1,0:T(8,128)(2,1)} %collective-permute-done.8.refs_2_), channel_id=1, source_target_pairs={{0,2},{1,3},{2,0},{3,1},{4,6},{5,7},{6,4},{7,5},{8,10},{9,11},{10,... | collective-permute-start | bytes 3981320 | tf_op jit(solution)/shard_map/ppermute | solution.py:62
  109.5 10.2 %collective-permute-start.13 = (bf16[144,4608]{1,0:T(8,128)(2,1)S(1)}, bf16[144,4608]{1,0:T(8,128)(2,1)S(1)}, u32[]{:S(2)}, u32[]{:S(2)}) collective-permute-start(bf16[144,4608]{1,0:T(8,128)(2,1)S(1)} %collective-permute-done.9.refs_3_), channel_id=1, source_target_pairs={{0,2},{1,3},{2,0},{3,1},{4,6},{5,7},{6,4},{7,5},{8,10},{9,11},{10,... | collective-permute-start | bytes 3981320 | tf_op jit(solution)/shard_map/ppermute | solution.py:62
  130.9 32.9 %collective-permute-start.14 = (bf16[512,2304]{1,0:T(8,128)(2,1)}, bf16[512,2304]{1,0:T(8,128)(2,1)}, u32[]{:S(2)}, u32[]{:S(2)}) collective-permute-start(bf16[512,2304]{1,0:T(8,128)(2,1)} %slice.227.own_ref), channel_id=1, source_target_pairs={{0,2},{1,3},{2,0},{3,1},{4,6},{5,7},{6,4},{7,5},{8,10},{9,11},{10,... | collective-permute-start | bytes 7077896 | tf_op jit(solution)/shard_map/ppermute | solution.py:62
  131.1 27.7 %collective-permute-start.15 = (bf16[1,512,1152]{2,1,0:T(8,128)(2,1)S(1)}, bf16[1,512,1152]{2,1,0:T(8,128)(2,1)}, u32[]{:S(2)}, u32[]{:S(2)}) collective-permute-start(bf16[1,512,1152]{2,1,0:T(8,128)(2,1)S(1)} %copy-done.35), channel_id=1, source_target_pairs={{1,2},{2,1},{5,6},{6,5},{9,10},{10,9},{13,14},{14,13},{17,18},{18,... | collective-permute-start | bytes 3538952 | tf_op jit(solution)/shard_map/ppermute | solution.py:68
  244.5 24.0 %collective-permute-start.16 = (bf16[4,144,4608]{2,1,0:T(8,128)(2,1)}, bf16[4,144,4608]{2,1,0:T(8,128)(2,1)}, u32[]{:S(2)}, u32[]{:S(2)}) collective-permute-start(bf16[4,144,4608]{2,1,0:T(8,128)(2,1)} %get-tuple-element.84), channel_id=1, source_target_pairs={{0,2},{1,3},{2,0},{3,1},{4,6},{5,7},{6,4},{7,5},{8,10},{9,11},{10,... | collective-permute-start | bytes 15925256 | tf_op jit(solution)/shard_map/ppermute | solution.py:62
  244.6 260.7 %all-reduce.2.cloned.1.call-start = ((), (), s32[]{:S(2)}) async-start(), calls=%async_computation.4 | async-start | bytes 2654208 | tf_op jit(solution)/shard_map/psum | solution.py:667
  267.8 33.7 %collective-permute-start.17 = (bf16[4,144,1152]{2,1,0:T(8,128)(2,1)}, bf16[4,144,1152]{2,1,0:T(8,128)(2,1)}, u32[]{:S(2)}, u32[]{:S(2)}) collective-permute-start(bf16[4,144,1152]{2,1,0:T(8,128)(2,1)} %get-tuple-element.88), channel_id=1, source_target_pairs={{0,2},{1,3},{2,0},{3,1},{4,6},{5,7},{6,4},{7,5},{8,10},{9,11},{10,... | collective-permute-start | bytes 3981320 | tf_op jit(solution)/shard_map/ppermute | solution.py:62
  276.2 77.3 %collective-permute-start.18 = (bf16[2,144,4608]{2,1,0:T(8,128)(2,1)}, bf16[2,144,4608]{2,1,0:T(8,128)(2,1)}, u32[]{:S(2)}, u32[]{:S(2)}) collective-permute-start(bf16[2,144,4608]{2,1,0:T(8,128)(2,1)} %pad_maximum_fusion.1), channel_id=1, source_target_pairs={{0,4},{1,5},{2,3},{3,2},{4,0},{5,1},{6,7},{7,6},{8,12},{9,13},{10,... | collective-permute-start | bytes 7962632 | tf_op jit(solution)/shard_map/ppermute | solution.py:62
  304.9 48.5 %collective-permute-start.19 = (bf16[2,144,1152]{2,1,0:T(8,128)(2,1)}, bf16[2,144,1152]{2,1,0:T(8,128)(2,1)}, u32[]{:S(2)}, u32[]{:S(2)}) collective-permute-start(bf16[2,144,1152]{2,1,0:T(8,128)(2,1)} %pad_maximum_fusion.4), channel_id=1, source_target_pairs={{0,4},{1,5},{2,3},{3,2},{4,0},{5,1},{6,7},{7,6},{8,12},{9,13},{10,... | collective-permute-start | bytes 1990664 | tf_op jit(solution)/shard_map/ppermute | solution.py:62
  356.1 12.6 %collective-permute-start.20 = (bf16[2,512,1152]{2,1,0:T(8,128)(2,1)S(1)}, bf16[2,512,1152]{2,1,0:T(8,128)(2,1)S(1)}, u32[]{:S(2)}, u32[]{:S(2)}) collective-permute-start(bf16[2,512,1152]{2,1,0:T(8,128)(2,1)S(1)} %pad_maximum_fusion.2), channel_id=1, source_target_pairs={{0,2},{1,3},{2,0},{3,1},{4,6},{5,7},{6,4},{7,5},{8,10},{9,11},{10,... | collective-permute-start | bytes 7077896 | tf_op jit(solution)/shard_map/ppermute | solution.py:62
  389.8 17.7 %collective-permute-start.21 = (bf16[4,144,3456]{2,1,0:T(8,128)(2,1)}, bf16[4,144,3456]{2,1,0:T(8,128)(2,1)}, u32[]{:S(2)}, u32[]{:S(2)}) collective-permute-start(bf16[4,144,3456]{2,1,0:T(8,128)(2,1)} %get-tuple-element.110), channel_id=1, source_target_pairs={{0,2},{1,3},{2,0},{3,1},{4,6},{5,7},{6,4},{7,5},{8,10},{9,11},{10,... | collective-permute-start | bytes 11943944 | tf_op jit(solution)/shard_map/ppermute | solution.py:62
  390.3 17.2 %collective-permute-start.22 = (bf16[144,4608]{1,0:T(8,128)(2,1)}, bf16[144,4608]{1,0:T(8,128)(2,1)S(1)}, u32[]{:S(2)}, u32[]{:S(2)}) collective-permute-start(bf16[144,4608]{1,0:T(8,128)(2,1)} %fusion.23), channel_id=1, source_target_pairs={{0,1},{1,0},{2,6},{3,7},{4,5},{5,4},{6,2},{7,3},{8,9},{9,8},{10,14... | collective-permute-start | bytes 3981320 | tf_op jit(solution)/shard_map/ppermute | solution.py:62
  390.9 31.8 %collective-permute-start.24 = (bf16[144,1152]{1,0:T(8,128)(2,1)}, bf16[144,1152]{1,0:T(8,128)(2,1)}, u32[]{:S(2)}, u32[]{:S(2)}) collective-permute-start(bf16[144,1152]{1,0:T(8,128)(2,1)} %fusion.33), channel_id=1, source_target_pairs={{0,1},{1,0},{2,6},{3,7},{4,5},{5,4},{6,2},{7,3},{8,9},{9,8},{10,14... | collective-permute-start | bytes 995336 | tf_op jit(solution)/shard_map/ppermute | solution.py:62
  415.2 24.1 %collective-permute-start.23 = (bf16[2,144,3456]{2,1,0:T(8,128)(2,1)S(1)}, bf16[2,144,3456]{2,1,0:T(8,128)(2,1)S(1)}, u32[]{:S(2)}, u32[]{:S(2)}) collective-permute-start(bf16[2,144,3456]{2,1,0:T(8,128)(2,1)S(1)} %pad_maximum_fusion.3), channel_id=1, source_target_pairs={{0,4},{1,5},{2,3},{3,2},{4,0},{5,1},{6,7},{7,6},{8,12},{9,13},{10,... | collective-permute-start | bytes 5971976 | tf_op jit(solution)/shard_map/ppermute | solution.py:62
  416.6 37.0 %collective-permute-start.26 = (bf16[144,1152]{1,0:T(8,128)(2,1)S(1)}, bf16[144,1152]{1,0:T(8,128)(2,1)S(1)}, u32[]{:S(2)}, u32[]{:S(2)}) collective-permute-start(bf16[144,1152]{1,0:T(8,128)(2,1)S(1)} %get-tuple-element.193), channel_id=1, source_target_pairs={{0,8},{8,16},{16,24},{24,0},{1,9},{9,17},{17,25},{25,1},{2,10},{10... | collective-permute-start | bytes 995336 | tf_op jit(solution)/shard_map/ppermute | solution.py:215
  417.7 39.1 %collective-permute-start.27 = (bf16[144,1152]{1,0:T(8,128)(2,1)S(1)}, bf16[144,1152]{1,0:T(8,128)(2,1)S(1)}, u32[]{:S(2)}, u32[]{:S(2)}) collective-permute-start(bf16[144,1152]{1,0:T(8,128)(2,1)S(1)} %get-tuple-element.192), channel_id=1, source_target_pairs={{0,16},{8,24},{16,0},{24,8},{1,17},{9,25},{17,1},{25,9},{2,18},{10... | collective-permute-start | bytes 995336 | tf_op jit(solution)/shard_map/ppermute | solution.py:215
  419.0 43.6 %collective-permute-start.28 = (bf16[144,1152]{1,0:T(8,128)(2,1)S(1)}, bf16[144,1152]{1,0:T(8,128)(2,1)S(1)}, u32[]{:S(2)}, u32[]{:S(2)}) collective-permute-start(bf16[144,1152]{1,0:T(8,128)(2,1)S(1)} %get-tuple-element.191), channel_id=1, source_target_pairs={{0,24},{8,0},{16,8},{24,16},{1,25},{9,1},{17,9},{25,17},{2,26},{10... | collective-permute-start | bytes 995336 | tf_op jit(solution)/shard_map/ppermute | solution.py:215
  439.9 13.5 %collective-permute-start.25 = (bf16[144,3456]{1,0:T(8,128)(2,1)S(1)}, bf16[144,3456]{1,0:T(8,128)(2,1)S(1)}, u32[]{:S(2)}, u32[]{:S(2)}) collective-permute-start(bf16[144,3456]{1,0:T(8,128)(2,1)S(1)} %fusion.26), channel_id=1, source_target_pairs={{0,1},{1,0},{2,6},{3,7},{4,5},{5,4},{6,2},{7,3},{8,9},{9,8},{10,14... | collective-permute-start | bytes 2985992 | tf_op jit(solution)/shard_map/ppermute | solution.py:62
  470.3 7.6 %collective-permute-start.31 = (f32[4,16128]{1,0:T(4,128)S(1)}, f32[4,16128]{1,0:T(4,128)S(1)}, u32[]{:S(2)}, u32[]{:S(2)}) collective-permute-start(f32[4,16128]{1,0:T(4,128)S(1)} %maximum_select_fusion.1), channel_id=1, source_target_pairs={{0,4},{1,5},{2,6},{3,7},{4,0},{5,1},{6,2},{7,3},{8,12},{9,13},{10,... | collective-permute-start | bytes 774152 | tf_op jit(solution)/shard_map/ppermute | solution.py:62
  471.8 33.5 %collective-permute-start.34 = (bf16[144,1152]{1,0:T(8,128)(2,1)}, bf16[144,1152]{1,0:T(8,128)(2,1)}, u32[]{:S(2)}, u32[]{:S(2)}) collective-permute-start(bf16[144,1152]{1,0:T(8,128)(2,1)} %get-tuple-element.190), channel_id=1, source_target_pairs={{0,8},{8,16},{16,24},{24,0},{1,9},{9,17},{17,25},{25,1},{2,10},{10... | collective-permute-start | bytes 995336 | tf_op jit(solution)/shard_map/ppermute | solution.py:215
  471.8 33.5 %collective-permute-start.35 = (bf16[144,1152]{1,0:T(8,128)(2,1)}, bf16[144,1152]{1,0:T(8,128)(2,1)}, u32[]{:S(2)}, u32[]{:S(2)}) collective-permute-start(bf16[144,1152]{1,0:T(8,128)(2,1)} %get-tuple-element.189), channel_id=1, source_target_pairs={{0,16},{8,24},{16,0},{24,8},{1,17},{9,25},{17,1},{25,9},{2,18},{10... | collective-permute-start | bytes 995336 | tf_op jit(solution)/shard_map/ppermute | solution.py:215
  471.8 33.5 %collective-permute-start.36 = (bf16[144,1152]{1,0:T(8,128)(2,1)S(1)}, bf16[144,1152]{1,0:T(8,128)(2,1)}, u32[]{:S(2)}, u32[]{:S(2)}) collective-permute-start(bf16[144,1152]{1,0:T(8,128)(2,1)S(1)} %get-tuple-element.188), channel_id=1, source_target_pairs={{0,24},{8,0},{16,8},{24,16},{1,25},{9,1},{17,9},{25,17},{2,26},{10... | collective-permute-start | bytes 995336 | tf_op jit(solution)/shard_map/ppermute | solution.py:215
  473.2 18.2 %collective-permute-start.33 = (bf16[1,512,1152]{2,1,0:T(8,128)(2,1)S(1)}, bf16[1,512,1152]{2,1,0:T(8,128)(2,1)S(1)}, u32[]{:S(2)}, u32[]{:S(2)}) collective-permute-start(bf16[1,512,1152]{2,1,0:T(8,128)(2,1)S(1)} %bitcast.103), channel_id=1, source_target_pairs={{1,2},{2,1},{5,6},{6,5},{9,10},{10,9},{13,14},{14,13},{17,18},{18,... | collective-permute-start | bytes 3538952 | tf_op jit(solution)/shard_map/ppermute | solution.py:68
  477.9 26.2 %collective-permute-start.32 = (bf16[1,512,1152]{2,1,0:T(8,128)(2,1)S(1)}, bf16[1,512,1152]{2,1,0:T(8,128)(2,1)S(1)}, u32[]{:S(2)}, u32[]{:S(2)}) collective-permute-start(bf16[1,512,1152]{2,1,0:T(8,128)(2,1)S(1)} %bitcast.104), channel_id=1, source_target_pairs={{1,2},{2,1},{5,6},{6,5},{9,10},{10,9},{13,14},{14,13},{17,18},{18,... | collective-permute-start | bytes 3538952 | tf_op jit(solution)/shard_map/ppermute | solution.py:68
  509.7 16.3 %collective-permute-start.40 = (f32[29376]{0:T(1024)S(1)}, f32[29376]{0:T(1024)}, u32[]{:S(2)}, u32[]{:S(2)}) collective-permute-start(f32[29376]{0:T(1024)S(1)} %concatenate.131), channel_id=1, source_target_pairs={{0,8},{8,16},{16,24},{24,0},{1,9},{9,17},{17,25},{25,1},{2,10},{10... | collective-permute-start | bytes 352520 | tf_op jit(solution)/shard_map/ppermute | solution.py:90
  510.9 18.1 %collective-permute-start.41 = (f32[29376]{0:T(1024)S(1)}, f32[29376]{0:T(1024)}, u32[]{:S(2)}, u32[]{:S(2)}) collective-permute-start(f32[29376]{0:T(1024)S(1)} %concatenate.131), channel_id=1, source_target_pairs={{0,16},{8,24},{16,0},{24,8},{1,17},{9,25},{17,1},{25,9},{2,18},{10... | collective-permute-start | bytes 352520 | tf_op jit(solution)/shard_map/ppermute | solution.py:90
  513.8 31.1 %collective-permute-start.42 = (f32[29376]{0:T(1024)S(1)}, f32[29376]{0:T(1024)}, u32[]{:S(2)}, u32[]{:S(2)}) collective-permute-start(f32[29376]{0:T(1024)S(1)} %concatenate.131), channel_id=1, source_target_pairs={{0,24},{8,0},{16,8},{24,16},{1,25},{9,1},{17,9},{25,17},{2,26},{10... | collective-permute-start | bytes 352520 | tf_op jit(solution)/shard_map/ppermute | solution.py:90
  513.9 6.2 %collective-permute-start.38 = (f32[2,4,144]{2,1,0:T(4,128)S(1)}, f32[2,4,144]{2,1,0:T(4,128)S(1)}, u32[]{:S(2)}, u32[]{:S(2)}) collective-permute-start(f32[2,4,144]{2,1,0:T(4,128)S(1)} %maximum_select_fusion.6), channel_id=1, source_target_pairs={{0,2},{1,3},{2,0},{3,1},{4,6},{5,7},{6,4},{7,5},{8,10},{9,11},{10,... | collective-permute-start | bytes 13832 | tf_op jit(solution)/shard_map/ppermute | solution.py:62
  518.4 27.5 %collective-permute-start.43 = (bf16[144,1152]{1,0:T(8,128)(2,1)S(1)}, bf16[144,1152]{1,0:T(8,128)(2,1)}, u32[]{:S(2)}, u32[]{:S(2)}) collective-permute-start(bf16[144,1152]{1,0:T(8,128)(2,1)S(1)} %fusion.31), channel_id=1, source_target_pairs={{0,8},{8,16},{16,24},{24,0},{1,9},{9,17},{17,25},{25,1},{2,10},{10... | collective-permute-start | bytes 995336 | tf_op jit(solution)/shard_map/ppermute | solution.py:215
  520.0 5.2 collective-permute-start.39
  525.3 55.2 %collective-permute-start.46 = (bf16[144,1152]{1,0:T(8,128)(2,1)S(1)}, bf16[144,1152]{1,0:T(8,128)(2,1)}, u32[]{:S(2)}, u32[]{:S(2)}) collective-permute-start(bf16[144,1152]{1,0:T(8,128)(2,1)S(1)} %add_convert_fusion.5), channel_id=1, source_target_pairs={{0,8},{8,16},{16,24},{24,0},{1,9},{9,17},{17,25},{25,1},{2,10},{10... | collective-permute-start | bytes 995336 | tf_op jit(solution)/shard_map/ppermute | solution.py:215
  526.0 54.4 %collective-permute-start.47 = (bf16[144,1152]{1,0:T(8,128)(2,1)S(1)}, bf16[144,1152]{1,0:T(8,128)(2,1)S(1)}, u32[]{:S(2)}, u32[]{:S(2)}) collective-permute-start(bf16[144,1152]{1,0:T(8,128)(2,1)S(1)} %add_convert_fusion.5), channel_id=1, source_target_pairs={{0,16},{8,24},{16,0},{24,8},{1,17},{9,25},{17,1},{25,9},{2,18},{10... | collective-permute-start | bytes 995336 | tf_op jit(solution)/shard_map/ppermute | solution.py:215
  529.0 52.2 %collective-permute-start.48 = (bf16[144,1152]{1,0:T(8,128)(2,1)S(1)}, bf16[144,1152]{1,0:T(8,128)(2,1)}, u32[]{:S(2)}, u32[]{:S(2)}) collective-permute-start(bf16[144,1152]{1,0:T(8,128)(2,1)S(1)} %add_convert_fusion.5), channel_id=1, source_target_pairs={{0,24},{8,0},{16,8},{24,16},{1,25},{9,1},{17,9},{25,17},{2,26},{10... | collective-permute-start | bytes 995336 | tf_op jit(solution)/shard_map/ppermute | solution.py:215
  544.9 33.7 %collective-permute-start.44 = (bf16[144,1152]{1,0:T(8,128)(2,1)S(1)}, bf16[144,1152]{1,0:T(8,128)(2,1)S(1)}, u32[]{:S(2)}, u32[]{:S(2)}) collective-permute-start(bf16[144,1152]{1,0:T(8,128)(2,1)S(1)} %fusion.31), channel_id=1, source_target_pairs={{0,16},{8,24},{16,0},{24,8},{1,17},{9,25},{17,1},{25,9},{2,18},{10... | collective-permute-start | bytes 995336 | tf_op jit(solution)/shard_map/ppermute | solution.py:215
  545.9 34.5 %collective-permute-start.45 = (bf16[144,1152]{1,0:T(8,128)(2,1)S(1)}, bf16[144,1152]{1,0:T(8,128)(2,1)S(1)}, u32[]{:S(2)}, u32[]{:S(2)}) collective-permute-start(bf16[144,1152]{1,0:T(8,128)(2,1)S(1)} %fusion.31), channel_id=1, source_target_pairs={{0,24},{8,0},{16,8},{24,16},{1,25},{9,1},{17,9},{25,17},{2,26},{10... | collective-permute-start | bytes 995336 | tf_op jit(solution)/shard_map/ppermute | solution.py:215
  (56 other events, 441.1 us)
Sparse Core Ops, SparseCore 0:
  10.0 100.8 all-gather.2
  112.7 74.2 all-gather.4
  244.7 103.7 reduce-scatter.1
  392.0 79.3 all-reduce.1

commit v12 on v11

--- a/solution.py
+++ b/solution.py
@@ -648,14 +648,14 @@
     d_query, d_attended, out_scatter.received = tie(left[0], d_attended, out_scatter.received)
     out_scatter.second()
     right = attend_back(query, pair_own, pair_other, d_attended, log_rows, halves[1])
-    *right, up_scatter.received, out_scatter.received = tie(
-        *right, up_scatter.received, out_scatter.received
+    d_other = permute(join_heads(left[2], right[2], width), core_rule)
+    d_right, up_scatter.received, out_scatter.received = tie(
+        right[1], up_scatter.received, out_scatter.received
     )
     up_scatter.add_third()
     out_scatter.add_third()
     d_query = join_heads(d_query, right[0], width)
-    d_own = join_heads(left[1], right[1], width)
-    d_other = permute(join_heads(left[2], right[2], width), core_rule)
+    d_own = join_heads(left[1], d_right, width)
     d_own = (d_own + d_other.astype(jnp.float32)).astype(jnp.bfloat16)
     d_projected = jnp.concatenate([d_query, d_own[0], d_own[1]], axis=-1)
 

time: 611 us -> 606 us (level)
  transfers between devices with their start and end apart: 53 -> 53, of which waited for: 19 -> 19; matrix products, arithmetic and copies ran while one was open for 16% -> 15% of each run, Pallas kernels for 15% -> 15%
where the time goes in v12:
time: 606 us; the launch traced here: 598 us
  waiting for transfers between devices  252 us (42%)
  Pallas kernels  153 us (25%)
  other arithmetic  63.1 us (10%)
  starting transfers between devices  61.5 us (10%)
  local copies, waits for them, and re-layouts  36.8 us (6%)
  between operations  16.1 us (3%)
  matrix products  15.7 us (3%)
    ppermute x30, waiting for transfers between devices, permute(): return lax.ppermute(values, GROUP, pairs_by(rule))  149 us
    pallas_call x2, Pallas kernels, attend_back(): pl.pallas_call(functools.partial(attend_back_kernel, heads[0], low), grid...  48.4 us
    pallas_call x1, Pallas kernels, mlp(): pl.pallas_call(mlp_kernel, grid=(units // block,), out_shape=(jax.ShapeDt...  47.7 us
    ppermute x4, waiting for transfers between devices, swap_halves(): received = lax.ppermute(values, GROUP, pairs)  44.1 us
    ppermute x12, waiting for transfers between devices, send(): return lax.ppermute(values, 'rep', pairs)  42.7 us
    ppermute x30, starting transfers between devices, permute(): return lax.ppermute(values, GROUP, pairs_by(rule))  33.8 us
    pallas_call x2, Pallas kernels, product_back(): pl.pallas_call(product_back_kernel, grid=(columns // block,), out_shape=(...  27 us
    pallas_call x1, Pallas kernels, attend(): pl.pallas_call(functools.partial(attend_kernel, heads[0], low), grid=(len...  26.9 us
  transfers between devices with their start and end apart: 53, of which 19 were waited for; matrix products, arithmetic and copies ran while one was open for 15% of the time, Pallas kernels for 15%

profile of v12, /device:TPU:9, one launch (start us, length us, event | category | flops | bytes accessed | tf_op | source)
XLA Modules:
  0.0 598.0 jit_solution(3914987874971780724)
XLA Ops:
  12.3 1.9 collective-permute-start.2
  18.3 2.0 collective-permute-start
  20.8 43.8 %collective-permute-done.3 = bf16[4,2432]{1,0:T(4,128)(2,1)S(1)} collective-permute-done((bf16[4,2432]{1,0:T(4,128)(2,1)S(1)}, bf16[4,2432]{1,0:T(4,128)(2,1)S(1)}, u32[]{:S(2)}, u32[]{:S(2)}) %collective-permute-start.3) | collective-permute-done | bytes 19488 | tf_op jit(solution)/shard_map/ppermute | solution.py:62
  65.3 2.2 collective-permute-start.4
  67.5 3.1 collective-permute-done.4
  72.5 35.0 %collective-permute-done.5 = f32[1,6912]{1,0:T(1,128)S(1)} collective-permute-done((f32[1,6912]{1,0:T(1,128)S(1)}, f32[1,6912]{1,0:T(1,128)S(1)}, u32[]{:S(2)}, u32[]{:S(2)}) %collective-permute-start.5) | collective-permute-done | bytes 27680 | tf_op jit(solution)/shard_map/ppermute | solution.py:62
  109.5 7.4 %collective-permute-start.13 = (bf16[144,4608]{1,0:T(8,128)(2,1)S(1)}, bf16[144,4608]{1,0:T(8,128)(2,1)S(1)}, u32[]{:S(2)}, u32[]{:S(2)}) collective-permute-start(bf16[144,4608]{1,0:T(8,128)(2,1)S(1)} %collective-permute-done.9.refs_3_), channel_id=1, source_target_pairs={{0,2},{1,3},{2,0},{3,1},{4,6},{5,7},{6,4},{7,5},{8,10},{9,11},{10,... | collective-permute-start | bytes 3981320 | tf_op jit(solution)/shard_map/ppermute | solution.py:62
  116.9 1.7 convert_reduce_fusion.1
  119.7 3.5 shard_map.237
  123.2 5.1 add_convert_fusion.2
  131.1 3.4 collective-permute-start.15
  136.1 22.8 %collective-permute-done.15 = bf16[1,512,1152]{2,1,0:T(8,128)(2,1)} collective-permute-done((bf16[1,512,1152]{2,1,0:T(8,128)(2,1)S(1)}, bf16[1,512,1152]{2,1,0:T(8,128)(2,1)}, u32[]{:S(2)}, u32[]{:S(2)}) %collective-permute-start.15) | collective-permute-done | bytes 1179680 | tf_op jit(solution)/shard_map/ppermute | solution.py:68
  158.9 3.5 convert_reduce_fusion.2
  163.8 26.9 %shard_map.238 = (bf16[512,1152]{1,0:T(8,128)(2,1)S(1)}, f32[512,128]{1,0:T(8,128)S(1)}) custom-call(bf16[512,1152]{1,0:T(8,128)(2,1)S(1)} %slice.226.query_ref, bf16[512,2304]{1,0:T(8,128)(2,1)} %slice.227.own_ref, bf16[512,2304]{1,0:T(8,128)(2,1)} %collective-permute-done.14.other_ref), custom_call_target="tpu_custom_call" | custom-call | flops 1048576 | bytes 1048576 | tf_op jit(solution)/shard_map/pallas_call | solution.py:303
  190.7 3.3 fusion.47
  196.8 47.7 %shard_map.239 = (f32[512,1152]{1,0:T(8,128)}, f32[512,1152]{1,0:T(8,128)}, bf16[4,144,4608]{2,1,0:T(8,128)(2,1)}, bf16[4,144,4608]{2,1,0:T(8,128)(2,1)}, bf16[4608,1152]{1,0:T(8,128)(2,1)}, /*index=5*/f32[1,4608]{1,0:T(1,128)}) custom-call(bf16[512,1152]{1,0:T(8,128)(2,1)} %add_convert_fusion.4.hidden_ref, ...), custom_call_target="tpu_custom_call" | custom-call | flops 1048576 | bytes 1048576 | tf_op jit(solution)/shard_map/pallas_call | solution.py:513
  245.8 3.5 multiply_reduce_fusion
  249.6 7.1 %fusion.21 = (f32[1152]{0:T(1024)S(1)}, bf16[512,1152]{1,0:T(8,128)(2,1)}, f32[1152]{0:T(1024)S(1)}, bf16[512,1152]{1,0:T(8,128)(2,1)}, f32[512,1152]{1,0:T(8,128)}) fusion(bf16[1,512,1152]{2,1,0:T(8,128)(2,1)S(1)} %get-tuple-element.161, f32[512,1152]{1,0:T(8,128)} %get-tuple-element.112, f32[1152]{0:T(1024)S(1)} %reshape.147, f32[]{:T(128)} %bitcast.10, ...), kind=kLoop, calls=%fused_computation.43 | loop fusion | flops 12384000 | bytes 13011972 | tf_op jit(solution)/shard_map/reduce_sum | solution.py:632
  256.7 9.0 %shard_map.240 = (f32[512,1152]{1,0:T(8,128)}, bf16[4,144,1152]{2,1,0:T(8,128)(2,1)}, bf16[4,144,1152]{2,1,0:T(8,128)(2,1)}) custom-call(bf16[512,1152]{1,0:T(8,128)(2,1)S(1)} %copy-done.8, bf16[512,1152]{1,0:T(8,128)(2,1)} %get-tuple-element.180.upstream_ref, bf16[1152,1152]{1,0:T(8,128)(2,1)} %copy-done.5), custom_call_target="tpu_custom_call" | custom-call | flops 1048576 | bytes 1048576 | tf_op jit(solution)/shard_map/pallas_call | solution.py:449
  265.7 2.9 convert_element_type.248.upstream_ref
  269.2 3.8 add_convert_fusion
  275.4 24.4 %shard_map.241 = (bf16[512,640]{1,0:T(8,128)(2,1)}, f32[2,512,640]{2,1,0:T(8,128)}, bf16[2,512,640]{2,1,0:T(8,128)(2,1)}) custom-call(bf16[512,1152]{1,0:T(8,128)(2,1)} %copy-done.1, bf16[512,2304]{1,0:T(8,128)(2,1)} %slice.227.own_ref, bf16[512,2304]{1,0:T(8,128)(2,1)} %collective-permute-done.14.other_ref, ...), custom_call_target="tpu_custom_call" | custom-call | flops 1048576 | bytes 1048576 | tf_op jit(solution)/shard_map/pallas_call | solution.py:375
  299.8 24.0 %shard_map.242 = (bf16[512,640]{1,0:T(8,128)(2,1)}, f32[2,512,640]{2,1,0:T(8,128)}, bf16[2,512,640]{2,1,0:T(8,128)(2,1)}) custom-call(bf16[512,1152]{1,0:T(8,128)(2,1)} %copy-done.1, bf16[512,2304]{1,0:T(8,128)(2,1)} %slice.227.own_ref, bf16[512,2304]{1,0:T(8,128)(2,1)} %collective-permute-done.14.other_ref, ...), custom_call_target="tpu_custom_call" | custom-call | flops 1048576 | bytes 1048576 | tf_op jit(solution)/shard_map/pallas_call | solution.py:375
  333.1 20.3 %collective-permute-done.19 = bf16[2,144,1152]{2,1,0:T(8,128)(2,1)S(1)} collective-permute-done((bf16[2,144,1152]{2,1,0:T(8,128)(2,1)S(1)}, bf16[2,144,1152]{2,1,0:T(8,128)(2,1)S(1)}, u32[]{:S(2)}, u32[]{:S(2)}) %collective-permute-start.19) | collective-permute-done | bytes 663584 | tf_op jit(solution)/shard_map/ppermute | solution.py:62
  355.1 2.5 fusion
  357.9 3.9 convert_add_fusion
  361.8 2.3 copy-done.17
  365.9 18.0 %shard_map.243 = (f32[512,1152]{1,0:T(8,128)}, bf16[4,144,3456]{2,1,0:T(8,128)(2,1)}, bf16[4,144,3456]{2,1,0:T(8,128)(2,1)}) custom-call(bf16[512,1152]{1,0:T(8,128)(2,1)S(1)} %copy-done.4, bf16[512,3456]{1,0:T(8,128)(2,1)} %copy-done.15, bf16[1152,3456]{1,0:T(8,128)(2,1)} %copy-done.2), custom_call_target="tpu_custom_call" | custom-call | flops 1048576 | bytes 1048576 | tf_op jit(solution)/shard_map/pallas_call | solution.py:449
  385.9 15.6 %collective-permute-done.22 = bf16[144,4608]{1,0:T(8,128)(2,1)S(1)} collective-permute-done((bf16[144,4608]{1,0:T(8,128)(2,1)}, bf16[144,4608]{1,0:T(8,128)(2,1)S(1)}, u32[]{:S(2)}, u32[]{:S(2)}) %collective-permute-start.22) | collective-permute-done | bytes 1327136 | tf_op jit(solution)/shard_map/ppermute | solution.py:62
  401.6 3.8 fusion.44
  405.4 3.2 add_convert_fusion.1
  416.7 16.6 %collective-permute-done.23 = bf16[2,144,3456]{2,1,0:T(8,128)(2,1)S(1)} collective-permute-done((bf16[2,144,3456]{2,1,0:T(8,128)(2,1)S(1)}, bf16[2,144,3456]{2,1,0:T(8,128)(2,1)S(1)}, u32[]{:S(2)}, u32[]{:S(2)}) %collective-permute-start.23) | collective-permute-done | bytes 1990688 | tf_op jit(solution)/shard_map/ppermute | solution.py:62
  436.1 11.3 %collective-permute-done.25 = bf16[144,3456]{1,0:T(8,128)(2,1)S(1)} collective-permute-done((bf16[144,3456]{1,0:T(8,128)(2,1)S(1)}, bf16[144,3456]{1,0:T(8,128)(2,1)S(1)}, u32[]{:S(2)}, u32[]{:S(2)}) %collective-permute-start.25) | collective-permute-done | bytes 995360 | tf_op jit(solution)/shard_map/ppermute | solution.py:62
  447.7 3.2 collective-permute-done.27
  450.9 5.7 collective-permute-done.28
  460.4 2.8 collective-permute-start.30
  467.2 4.4 collective-permute-start.33
  472.0 3.5 collective-permute-start.32
  475.7 9.8 %collective-permute-done.33 = bf16[1,512,1152]{2,1,0:T(8,128)(2,1)S(1)} collective-permute-done((bf16[1,512,1152]{2,1,0:T(8,128)(2,1)S(1)}, bf16[1,512,1152]{2,1,0:T(8,128)(2,1)S(1)}, u32[]{:S(2)}, u32[]{:S(2)}) %collective-permute-start.33) | collective-permute-done | bytes 1179680 | tf_op jit(solution)/shard_map/ppermute | solution.py:68
  486.6 11.5 %collective-permute-done.32 = bf16[1,512,1152]{2,1,0:T(8,128)(2,1)S(1)} collective-permute-done((bf16[1,512,1152]{2,1,0:T(8,128)(2,1)S(1)}, bf16[1,512,1152]{2,1,0:T(8,128)(2,1)S(1)}, u32[]{:S(2)}, u32[]{:S(2)}) %collective-permute-start.32) | collective-permute-done | bytes 1179680 | tf_op jit(solution)/shard_map/ppermute | solution.py:68
  504.9 3.0 collective-permute-start.41
  507.9 3.0 collective-permute-start.38
  516.0 1.7 convert_element_type.298
  520.0 2.0 collective-permute-start.47
  524.8 14.1 %collective-permute-done.42 = f32[29376]{0:T(1024)} collective-permute-done((f32[29376]{0:T(1024)S(1)}, f32[29376]{0:T(1024)}, u32[]{:S(2)}, u32[]{:S(2)}) %collective-permute-start.42) | collective-permute-done | bytes 117536 | tf_op jit(solution)/shard_map/ppermute | solution.py:90
  540.6 32.0 %collective-permute-done.44 = bf16[144,1152]{1,0:T(8,128)(2,1)S(1)} collective-permute-done((bf16[144,1152]{1,0:T(8,128)(2,1)S(1)}, bf16[144,1152]{1,0:T(8,128)(2,1)S(1)}, u32[]{:S(2)}, u32[]{:S(2)}) %collective-permute-start.44) | collective-permute-done | bytes 331808 | tf_op jit(solution)/shard_map/ppermute | solution.py:215
  572.6 1.8 collective-permute-done.45
  582.0 5.2 fusion.51
  (336 shorter events, 93.1 us)
Async XLA Ops:
  7.2 189.6 %all-gather.3.cloned.1.call-start = ((), (), s32[]{:S(2)}) async-start(), calls=%async_computation.1 | async-start | bytes 11943936 | tf_op jit(solution)/shard_map/all_gather | solution.py:568
  8.0 188.8 %all-gather.5.cloned.1.call-start = ((), (), s32[]{:S(2)}) async-start(), calls=%async_computation.2 | async-start | bytes 11943936 | tf_op jit(solution)/shard_map/all_gather | solution.py:571
  8.7 356.6 %reduce-scatter.2.cloned.1.call-start = ((), (), s32[]{:S(2)}) async-start(), calls=%async_computation.3 | async-start | bytes 11943936 | tf_op jit(solution)/shard_map/reduce_scatter | solution.py:629
  12.3 8.0 %collective-permute-start.2 = (bf16[2,2432]{1,0:T(2,128)(2,1)S(1)}, bf16[2,2432]{1,0:T(2,128)(2,1)S(1)}, u32[]{:S(2)}, u32[]{:S(2)}) collective-permute-start(bf16[2,2432]{1,0:T(2,128)(2,1)S(1)} %broadcast_select_fusion.7), channel_id=1, source_target_pairs={{0,2},{1,3},{2,0},{3,1},{4,6},{5,7},{6,4},{7,5},{8,10},{9,11},{10,... | collective-permute-start | bytes 29192 | tf_op jit(solution)/shard_map/ppermute | solution.py:62
  15.2 55.8 %collective-permute-start.7 = (bf16[144,4608]{1,0:T(8,128)(2,1)S(1)}, bf16[144,4608]{1,0:T(8,128)(2,1)}, u32[]{:S(2)}, u32[]{:S(2)}) collective-permute-start(bf16[144,4608]{1,0:T(8,128)(2,1)S(1)} %constant_dynamic-update-slice_fusion.refs_0_), channel_id=1, source_target_pairs={{0,4},{1,5},{2,3},{3,2},{4,0},{5,1},{6,7},{7,6},{8,12},{9,13},{10,... | collective-permute-start | bytes 3981320 | tf_op jit(solution)/shard_map/ppermute | solution.py:62
  16.5 92.7 %collective-permute-start.8 = (bf16[144,4608]{1,0:T(8,128)(2,1)S(1)}, bf16[144,4608]{1,0:T(8,128)(2,1)}, u32[]{:S(2)}, u32[]{:S(2)}) collective-permute-start(bf16[144,4608]{1,0:T(8,128)(2,1)S(1)} %constant_dynamic-update-slice_fusion.refs_0_), channel_id=1, source_target_pairs={{0,1},{1,0},{2,6},{3,7},{4,5},{5,4},{6,2},{7,3},{8,9},{9,8},{10,14... | collective-permute-start | bytes 3981320 | tf_op jit(solution)/shard_map/ppermute | solution.py:62
  17.7 101.9 %collective-permute-start.10 = (bf16[144,4608]{1,0:T(8,128)(2,1)S(1)}, bf16[144,4608]{1,0:T(8,128)(2,1)}, u32[]{:S(2)}, u32[]{:S(2)}) collective-permute-start(bf16[144,4608]{1,0:T(8,128)(2,1)S(1)} %constant_dynamic-update-slice_fusion.refs_0_), channel_id=1, source_target_pairs={{0,2},{1,3},{2,0},{3,1},{4,6},{5,7},{6,4},{7,5},{8,10},{9,11},{10,... | collective-permute-start | bytes 3981320 | tf_op jit(solution)/shard_map/ppermute | solution.py:62
  18.3 98.6 %collective-permute-start = (bf16[1,512,1152]{2,1,0:T(8,128)(2,1)}, bf16[1,512,1152]{2,1,0:T(8,128)(2,1)}, u32[]{:S(2)}, u32[]{:S(2)}) collective-permute-start(bf16[1,512,1152]{2,1,0:T(8,128)(2,1)} %param.14), channel_id=1, source_target_pairs={{1,2},{2,1},{5,6},{6,5},{9,10},{10,9},{13,14},{14,13},{17,18},{18,... | collective-permute-start | bytes 3538952 | tf_op jit(solution)/shard_map/ppermute | solution.py:68
  20.3 44.3 %collective-permute-start.3 = (bf16[4,2432]{1,0:T(4,128)(2,1)S(1)}, bf16[4,2432]{1,0:T(4,128)(2,1)S(1)}, u32[]{:S(2)}, u32[]{:S(2)}) collective-permute-start(bf16[4,2432]{1,0:T(4,128)(2,1)S(1)} %maximum_select_fusion.4), channel_id=1, source_target_pairs={{0,4},{1,5},{2,6},{3,7},{4,0},{5,1},{6,2},{7,3},{8,12},{9,13},{10,... | collective-permute-start | bytes 58376 | tf_op jit(solution)/shard_map/ppermute | solution.py:62
  65.3 5.3 collective-permute-start.4
  70.7 36.8 %collective-permute-start.5 = (f32[1,6912]{1,0:T(1,128)S(1)}, f32[1,6912]{1,0:T(1,128)S(1)}, u32[]{:S(2)}, u32[]{:S(2)}) collective-permute-start(f32[1,6912]{1,0:T(1,128)S(1)} %broadcast_select_fusion.5), channel_id=1, source_target_pairs={{0,1},{1,0},{2,3},{3,2},{4,5},{5,4},{6,7},{7,6},{8,9},{9,8},{10,11... | collective-permute-start | bytes 82952 | tf_op jit(solution)/shard_map/ppermute | solution.py:62
  70.9 38.6 %collective-permute-start.9 = (bf16[144,4608]{1,0:T(8,128)(2,1)}, bf16[144,4608]{1,0:T(8,128)(2,1)S(1)}, u32[]{:S(2)}, u32[]{:S(2)}) collective-permute-start(bf16[144,4608]{1,0:T(8,128)(2,1)} %collective-permute-done.7.refs_1_), channel_id=1, source_target_pairs={{0,1},{1,0},{2,6},{3,7},{4,5},{5,4},{6,2},{7,3},{8,9},{9,8},{10,14... | collective-permute-start | bytes 3981320 | tf_op jit(solution)/shard_map/ppermute | solution.py:62
  108.9 10.7 %collective-permute-start.11 = (bf16[144,4608]{1,0:T(8,128)(2,1)}, bf16[144,4608]{1,0:T(8,128)(2,1)S(1)}, u32[]{:S(2)}, u32[]{:S(2)}) collective-permute-start(bf16[144,4608]{1,0:T(8,128)(2,1)} %collective-permute-done.7.refs_1_), channel_id=1, source_target_pairs={{0,2},{1,3},{2,0},{3,1},{4,6},{5,7},{6,4},{7,5},{8,10},{9,11},{10,... | collective-permute-start | bytes 3981320 | tf_op jit(solution)/shard_map/ppermute | solution.py:62
  109.2 10.4 %collective-permute-start.12 = (bf16[144,4608]{1,0:T(8,128)(2,1)}, bf16[144,4608]{1,0:T(8,128)(2,1)S(1)}, u32[]{:S(2)}, u32[]{:S(2)}) collective-permute-start(bf16[144,4608]{1,0:T(8,128)(2,1)} %collective-permute-done.8.refs_2_), channel_id=1, source_target_pairs={{0,2},{1,3},{2,0},{3,1},{4,6},{5,7},{6,4},{7,5},{8,10},{9,11},{10,... | collective-permute-start | bytes 3981320 | tf_op jit(solution)/shard_map/ppermute | solution.py:62
  109.5 10.2 %collective-permute-start.13 = (bf16[144,4608]{1,0:T(8,128)(2,1)S(1)}, bf16[144,4608]{1,0:T(8,128)(2,1)S(1)}, u32[]{:S(2)}, u32[]{:S(2)}) collective-permute-start(bf16[144,4608]{1,0:T(8,128)(2,1)S(1)} %collective-permute-done.9.refs_3_), channel_id=1, source_target_pairs={{0,2},{1,3},{2,0},{3,1},{4,6},{5,7},{6,4},{7,5},{8,10},{9,11},{10,... | collective-permute-start | bytes 3981320 | tf_op jit(solution)/shard_map/ppermute | solution.py:62
  130.9 32.9 %collective-permute-start.14 = (bf16[512,2304]{1,0:T(8,128)(2,1)}, bf16[512,2304]{1,0:T(8,128)(2,1)}, u32[]{:S(2)}, u32[]{:S(2)}) collective-permute-start(bf16[512,2304]{1,0:T(8,128)(2,1)} %slice.227.own_ref), channel_id=1, source_target_pairs={{0,2},{1,3},{2,0},{3,1},{4,6},{5,7},{6,4},{7,5},{8,10},{9,11},{10,... | collective-permute-start | bytes 7077896 | tf_op jit(solution)/shard_map/ppermute | solution.py:62
  131.1 27.7 %collective-permute-start.15 = (bf16[1,512,1152]{2,1,0:T(8,128)(2,1)S(1)}, bf16[1,512,1152]{2,1,0:T(8,128)(2,1)}, u32[]{:S(2)}, u32[]{:S(2)}) collective-permute-start(bf16[1,512,1152]{2,1,0:T(8,128)(2,1)S(1)} %copy-done.34), channel_id=1, source_target_pairs={{1,2},{2,1},{5,6},{6,5},{9,10},{10,9},{13,14},{14,13},{17,18},{18,... | collective-permute-start | bytes 3538952 | tf_op jit(solution)/shard_map/ppermute | solution.py:68
  244.5 24.7 %collective-permute-start.16 = (bf16[4,144,4608]{2,1,0:T(8,128)(2,1)}, bf16[4,144,4608]{2,1,0:T(8,128)(2,1)}, u32[]{:S(2)}, u32[]{:S(2)}) collective-permute-start(bf16[4,144,4608]{2,1,0:T(8,128)(2,1)} %get-tuple-element.82), channel_id=1, source_target_pairs={{0,2},{1,3},{2,0},{3,1},{4,6},{5,7},{6,4},{7,5},{8,10},{9,11},{10,... | collective-permute-start | bytes 15925256 | tf_op jit(solution)/shard_map/ppermute | solution.py:62
  244.6 254.7 %all-reduce.2.cloned.1.call-start = ((), (), s32[]{:S(2)}) async-start(), calls=%async_computation.4 | async-start | bytes 2654208 | tf_op jit(solution)/shard_map/psum | solution.py:667
  268.6 31.2 %collective-permute-start.17 = (bf16[4,144,1152]{2,1,0:T(8,128)(2,1)}, bf16[4,144,1152]{2,1,0:T(8,128)(2,1)}, u32[]{:S(2)}, u32[]{:S(2)}) collective-permute-start(bf16[4,144,1152]{2,1,0:T(8,128)(2,1)} %get-tuple-element.86), channel_id=1, source_target_pairs={{0,2},{1,3},{2,0},{3,1},{4,6},{5,7},{6,4},{7,5},{8,10},{9,11},{10,... | collective-permute-start | bytes 3981320 | tf_op jit(solution)/shard_map/ppermute | solution.py:62
  273.8 79.6 %collective-permute-start.18 = (bf16[2,144,4608]{2,1,0:T(8,128)(2,1)S(1)}, bf16[2,144,4608]{2,1,0:T(8,128)(2,1)}, u32[]{:S(2)}, u32[]{:S(2)}) collective-permute-start(bf16[2,144,4608]{2,1,0:T(8,128)(2,1)S(1)} %pad_maximum_fusion.1), channel_id=1, source_target_pairs={{0,4},{1,5},{2,3},{3,2},{4,0},{5,1},{6,7},{7,6},{8,12},{9,13},{10,... | collective-permute-start | bytes 7962632 | tf_op jit(solution)/shard_map/ppermute | solution.py:62
  327.3 27.7 %collective-permute-start.20 = (bf16[2,512,1152]{2,1,0:T(8,128)(2,1)S(1)}, bf16[2,512,1152]{2,1,0:T(8,128)(2,1)}, u32[]{:S(2)}, u32[]{:S(2)}) collective-permute-start(bf16[2,512,1152]{2,1,0:T(8,128)(2,1)S(1)} %pad_maximum_fusion.2), channel_id=1, source_target_pairs={{0,2},{1,3},{2,0},{3,1},{4,6},{5,7},{6,4},{7,5},{8,10},{9,11},{10,... | collective-permute-start | bytes 7077896 | tf_op jit(solution)/shard_map/ppermute | solution.py:62
  330.4 23.0 %collective-permute-start.19 = (bf16[2,144,1152]{2,1,0:T(8,128)(2,1)S(1)}, bf16[2,144,1152]{2,1,0:T(8,128)(2,1)S(1)}, u32[]{:S(2)}, u32[]{:S(2)}) collective-permute-start(bf16[2,144,1152]{2,1,0:T(8,128)(2,1)S(1)} %pad_maximum_fusion.4), channel_id=1, source_target_pairs={{0,4},{1,5},{2,3},{3,2},{4,0},{5,1},{6,7},{7,6},{8,12},{9,13},{10,... | collective-permute-start | bytes 1990664 | tf_op jit(solution)/shard_map/ppermute | solution.py:62
  383.9 17.7 %collective-permute-start.21 = (bf16[4,144,3456]{2,1,0:T(8,128)(2,1)}, bf16[4,144,3456]{2,1,0:T(8,128)(2,1)}, u32[]{:S(2)}, u32[]{:S(2)}) collective-permute-start(bf16[4,144,3456]{2,1,0:T(8,128)(2,1)} %get-tuple-element.106), channel_id=1, source_target_pairs={{0,2},{1,3},{2,0},{3,1},{4,6},{5,7},{6,4},{7,5},{8,10},{9,11},{10,... | collective-permute-start | bytes 11943944 | tf_op jit(solution)/shard_map/ppermute | solution.py:62
  384.3 17.2 %collective-permute-start.22 = (bf16[144,4608]{1,0:T(8,128)(2,1)}, bf16[144,4608]{1,0:T(8,128)(2,1)S(1)}, u32[]{:S(2)}, u32[]{:S(2)}) collective-permute-start(bf16[144,4608]{1,0:T(8,128)(2,1)} %fusion.23), channel_id=1, source_target_pairs={{0,1},{1,0},{2,6},{3,7},{4,5},{5,4},{6,2},{7,3},{8,9},{9,8},{10,14... | collective-permute-start | bytes 3981320 | tf_op jit(solution)/shard_map/ppermute | solution.py:62
  385.0 31.8 %collective-permute-start.24 = (bf16[144,1152]{1,0:T(8,128)(2,1)}, bf16[144,1152]{1,0:T(8,128)(2,1)}, u32[]{:S(2)}, u32[]{:S(2)}) collective-permute-start(bf16[144,1152]{1,0:T(8,128)(2,1)} %fusion.33), channel_id=1, source_target_pairs={{0,1},{1,0},{2,6},{3,7},{4,5},{5,4},{6,2},{7,3},{8,9},{9,8},{10,14... | collective-permute-start | bytes 995336 | tf_op jit(solution)/shard_map/ppermute | solution.py:62
  409.2 24.1 %collective-permute-start.23 = (bf16[2,144,3456]{2,1,0:T(8,128)(2,1)S(1)}, bf16[2,144,3456]{2,1,0:T(8,128)(2,1)S(1)}, u32[]{:S(2)}, u32[]{:S(2)}) collective-permute-start(bf16[2,144,3456]{2,1,0:T(8,128)(2,1)S(1)} %pad_maximum_fusion.3), channel_id=1, source_target_pairs={{0,4},{1,5},{2,3},{3,2},{4,0},{5,1},{6,7},{7,6},{8,12},{9,13},{10,... | collective-permute-start | bytes 5971976 | tf_op jit(solution)/shard_map/ppermute | solution.py:62
  410.6 37.0 %collective-permute-start.26 = (bf16[144,1152]{1,0:T(8,128)(2,1)S(1)}, bf16[144,1152]{1,0:T(8,128)(2,1)S(1)}, u32[]{:S(2)}, u32[]{:S(2)}) collective-permute-start(bf16[144,1152]{1,0:T(8,128)(2,1)S(1)} %get-tuple-element.189), channel_id=1, source_target_pairs={{0,8},{8,16},{16,24},{24,0},{1,9},{9,17},{17,25},{25,1},{2,10},{10... | collective-permute-start | bytes 995336 | tf_op jit(solution)/shard_map/ppermute | solution.py:215
  411.8 39.1 %collective-permute-start.27 = (bf16[144,1152]{1,0:T(8,128)(2,1)S(1)}, bf16[144,1152]{1,0:T(8,128)(2,1)S(1)}, u32[]{:S(2)}, u32[]{:S(2)}) collective-permute-start(bf16[144,1152]{1,0:T(8,128)(2,1)S(1)} %get-tuple-element.188), channel_id=1, source_target_pairs={{0,16},{8,24},{16,0},{24,8},{1,17},{9,25},{17,1},{25,9},{2,18},{10... | collective-permute-start | bytes 995336 | tf_op jit(solution)/shard_map/ppermute | solution.py:215
  413.0 43.6 %collective-permute-start.28 = (bf16[144,1152]{1,0:T(8,128)(2,1)S(1)}, bf16[144,1152]{1,0:T(8,128)(2,1)S(1)}, u32[]{:S(2)}, u32[]{:S(2)}) collective-permute-start(bf16[144,1152]{1,0:T(8,128)(2,1)S(1)} %get-tuple-element.187), channel_id=1, source_target_pairs={{0,24},{8,0},{16,8},{24,16},{1,25},{9,1},{17,9},{25,17},{2,26},{10... | collective-permute-start | bytes 995336 | tf_op jit(solution)/shard_map/ppermute | solution.py:215
  433.9 13.5 %collective-permute-start.25 = (bf16[144,3456]{1,0:T(8,128)(2,1)S(1)}, bf16[144,3456]{1,0:T(8,128)(2,1)S(1)}, u32[]{:S(2)}, u32[]{:S(2)}) collective-permute-start(bf16[144,3456]{1,0:T(8,128)(2,1)S(1)} %fusion.26), channel_id=1, source_target_pairs={{0,1},{1,0},{2,6},{3,7},{4,5},{5,4},{6,2},{7,3},{8,9},{9,8},{10,14... | collective-permute-start | bytes 2985992 | tf_op jit(solution)/shard_map/ppermute | solution.py:62
  464.4 7.6 %collective-permute-start.31 = (f32[4,16128]{1,0:T(4,128)S(1)}, f32[4,16128]{1,0:T(4,128)S(1)}, u32[]{:S(2)}, u32[]{:S(2)}) collective-permute-start(f32[4,16128]{1,0:T(4,128)S(1)} %maximum_select_fusion.1), channel_id=1, source_target_pairs={{0,4},{1,5},{2,6},{3,7},{4,0},{5,1},{6,2},{7,3},{8,12},{9,13},{10,... | collective-permute-start | bytes 774152 | tf_op jit(solution)/shard_map/ppermute | solution.py:62
  465.8 33.5 %collective-permute-start.34 = (bf16[144,1152]{1,0:T(8,128)(2,1)}, bf16[144,1152]{1,0:T(8,128)(2,1)}, u32[]{:S(2)}, u32[]{:S(2)}) collective-permute-start(bf16[144,1152]{1,0:T(8,128)(2,1)} %get-tuple-element.186), channel_id=1, source_target_pairs={{0,8},{8,16},{16,24},{24,0},{1,9},{9,17},{17,25},{25,1},{2,10},{10... | collective-permute-start | bytes 995336 | tf_op jit(solution)/shard_map/ppermute | solution.py:215
  465.8 33.5 %collective-permute-start.35 = (bf16[144,1152]{1,0:T(8,128)(2,1)}, bf16[144,1152]{1,0:T(8,128)(2,1)}, u32[]{:S(2)}, u32[]{:S(2)}) collective-permute-start(bf16[144,1152]{1,0:T(8,128)(2,1)} %get-tuple-element.185), channel_id=1, source_target_pairs={{0,16},{8,24},{16,0},{24,8},{1,17},{9,25},{17,1},{25,9},{2,18},{10... | collective-permute-start | bytes 995336 | tf_op jit(solution)/shard_map/ppermute | solution.py:215
  465.8 33.5 %collective-permute-start.36 = (bf16[144,1152]{1,0:T(8,128)(2,1)S(1)}, bf16[144,1152]{1,0:T(8,128)(2,1)}, u32[]{:S(2)}, u32[]{:S(2)}) collective-permute-start(bf16[144,1152]{1,0:T(8,128)(2,1)S(1)} %get-tuple-element.184), channel_id=1, source_target_pairs={{0,24},{8,0},{16,8},{24,16},{1,25},{9,1},{17,9},{25,17},{2,26},{10... | collective-permute-start | bytes 995336 | tf_op jit(solution)/shard_map/ppermute | solution.py:215
  467.2 18.3 %collective-permute-start.33 = (bf16[1,512,1152]{2,1,0:T(8,128)(2,1)S(1)}, bf16[1,512,1152]{2,1,0:T(8,128)(2,1)S(1)}, u32[]{:S(2)}, u32[]{:S(2)}) collective-permute-start(bf16[1,512,1152]{2,1,0:T(8,128)(2,1)S(1)} %bitcast.103), channel_id=1, source_target_pairs={{1,2},{2,1},{5,6},{6,5},{9,10},{10,9},{13,14},{14,13},{17,18},{18,... | collective-permute-start | bytes 3538952 | tf_op jit(solution)/shard_map/ppermute | solution.py:68
  472.0 26.2 %collective-permute-start.32 = (bf16[1,512,1152]{2,1,0:T(8,128)(2,1)S(1)}, bf16[1,512,1152]{2,1,0:T(8,128)(2,1)S(1)}, u32[]{:S(2)}, u32[]{:S(2)}) collective-permute-start(bf16[1,512,1152]{2,1,0:T(8,128)(2,1)S(1)} %bitcast.104), channel_id=1, source_target_pairs={{1,2},{2,1},{5,6},{6,5},{9,10},{10,9},{13,14},{14,13},{17,18},{18,... | collective-permute-start | bytes 3538952 | tf_op jit(solution)/shard_map/ppermute | solution.py:68
  503.7 16.2 %collective-permute-start.40 = (f32[29376]{0:T(1024)S(1)}, f32[29376]{0:T(1024)}, u32[]{:S(2)}, u32[]{:S(2)}) collective-permute-start(f32[29376]{0:T(1024)S(1)} %concatenate.131), channel_id=1, source_target_pairs={{0,8},{8,16},{16,24},{24,0},{1,9},{9,17},{17,25},{25,1},{2,10},{10... | collective-permute-start | bytes 352520 | tf_op jit(solution)/shard_map/ppermute | solution.py:90
  504.9 18.1 %collective-permute-start.41 = (f32[29376]{0:T(1024)S(1)}, f32[29376]{0:T(1024)}, u32[]{:S(2)}, u32[]{:S(2)}) collective-permute-start(f32[29376]{0:T(1024)S(1)} %concatenate.131), channel_id=1, source_target_pairs={{0,16},{8,24},{16,0},{24,8},{1,17},{9,25},{17,1},{25,9},{2,18},{10... | collective-permute-start | bytes 352520 | tf_op jit(solution)/shard_map/ppermute | solution.py:90
  507.8 31.1 %collective-permute-start.42 = (f32[29376]{0:T(1024)S(1)}, f32[29376]{0:T(1024)}, u32[]{:S(2)}, u32[]{:S(2)}) collective-permute-start(f32[29376]{0:T(1024)S(1)} %concatenate.131), channel_id=1, source_target_pairs={{0,24},{8,0},{16,8},{24,16},{1,25},{9,1},{17,9},{25,17},{2,26},{10... | collective-permute-start | bytes 352520 | tf_op jit(solution)/shard_map/ppermute | solution.py:90
  507.9 6.2 %collective-permute-start.38 = (f32[2,4,144]{2,1,0:T(4,128)S(1)}, f32[2,4,144]{2,1,0:T(4,128)S(1)}, u32[]{:S(2)}, u32[]{:S(2)}) collective-permute-start(f32[2,4,144]{2,1,0:T(4,128)S(1)} %maximum_select_fusion.6), channel_id=1, source_target_pairs={{0,2},{1,3},{2,0},{3,1},{4,6},{5,7},{6,4},{7,5},{8,10},{9,11},{10,... | collective-permute-start | bytes 13832 | tf_op jit(solution)/shard_map/ppermute | solution.py:62
  512.4 27.5 %collective-permute-start.43 = (bf16[144,1152]{1,0:T(8,128)(2,1)S(1)}, bf16[144,1152]{1,0:T(8,128)(2,1)}, u32[]{:S(2)}, u32[]{:S(2)}) collective-permute-start(bf16[144,1152]{1,0:T(8,128)(2,1)S(1)} %fusion.31), channel_id=1, source_target_pairs={{0,8},{8,16},{16,24},{24,0},{1,9},{9,17},{17,25},{25,1},{2,10},{10... | collective-permute-start | bytes 995336 | tf_op jit(solution)/shard_map/ppermute | solution.py:215
  514.0 5.2 collective-permute-start.39
  519.2 55.2 %collective-permute-start.46 = (bf16[144,1152]{1,0:T(8,128)(2,1)S(1)}, bf16[144,1152]{1,0:T(8,128)(2,1)}, u32[]{:S(2)}, u32[]{:S(2)}) collective-permute-start(bf16[144,1152]{1,0:T(8,128)(2,1)S(1)} %add_convert_fusion.5), channel_id=1, source_target_pairs={{0,8},{8,16},{16,24},{24,0},{1,9},{9,17},{17,25},{25,1},{2,10},{10... | collective-permute-start | bytes 995336 | tf_op jit(solution)/shard_map/ppermute | solution.py:215
  520.0 54.4 %collective-permute-start.47 = (bf16[144,1152]{1,0:T(8,128)(2,1)S(1)}, bf16[144,1152]{1,0:T(8,128)(2,1)S(1)}, u32[]{:S(2)}, u32[]{:S(2)}) collective-permute-start(bf16[144,1152]{1,0:T(8,128)(2,1)S(1)} %add_convert_fusion.5), channel_id=1, source_target_pairs={{0,16},{8,24},{16,0},{24,8},{1,17},{9,25},{17,1},{25,9},{2,18},{10... | collective-permute-start | bytes 995336 | tf_op jit(solution)/shard_map/ppermute | solution.py:215
  523.0 52.2 %collective-permute-start.48 = (bf16[144,1152]{1,0:T(8,128)(2,1)S(1)}, bf16[144,1152]{1,0:T(8,128)(2,1)}, u32[]{:S(2)}, u32[]{:S(2)}) collective-permute-start(bf16[144,1152]{1,0:T(8,128)(2,1)S(1)} %add_convert_fusion.5), channel_id=1, source_target_pairs={{0,24},{8,0},{16,8},{24,16},{1,25},{9,1},{17,9},{25,17},{2,26},{10... | collective-permute-start | bytes 995336 | tf_op jit(solution)/shard_map/ppermute | solution.py:215
  538.9 33.7 %collective-permute-start.44 = (bf16[144,1152]{1,0:T(8,128)(2,1)S(1)}, bf16[144,1152]{1,0:T(8,128)(2,1)S(1)}, u32[]{:S(2)}, u32[]{:S(2)}) collective-permute-start(bf16[144,1152]{1,0:T(8,128)(2,1)S(1)} %fusion.31), channel_id=1, source_target_pairs={{0,16},{8,24},{16,0},{24,8},{1,17},{9,25},{17,1},{25,9},{2,18},{10... | collective-permute-start | bytes 995336 | tf_op jit(solution)/shard_map/ppermute | solution.py:215
  539.9 34.5 %collective-permute-start.45 = (bf16[144,1152]{1,0:T(8,128)(2,1)S(1)}, bf16[144,1152]{1,0:T(8,128)(2,1)S(1)}, u32[]{:S(2)}, u32[]{:S(2)}) collective-permute-start(bf16[144,1152]{1,0:T(8,128)(2,1)S(1)} %fusion.31), channel_id=1, source_target_pairs={{0,24},{8,0},{16,8},{24,16},{1,25},{9,1},{17,9},{25,17},{2,26},{10... | collective-permute-start | bytes 995336 | tf_op jit(solution)/shard_map/ppermute | solution.py:215
  (56 other events, 434.2 us)
Sparse Core Ops, SparseCore 0:
  10.0 100.8 all-gather.2
  112.7 74.2 all-gather.4
  244.7 104.7 reduce-scatter.1
  386.0 79.3 all-reduce.1

commit v13 on v12

--- a/solution.py
+++ b/solution.py
@@ -667,15 +667,10 @@
     down_total = lax.psum(down_shard, "rep")
     d_hidden_one, qkv_halves = product_back(hidden_one, d_projected, full_qkv)
     qkv_scatter = Scatter(qkv_halves)
-    d_hidden_one, d_projected, *arrived = tie(
-        d_hidden_one,
-        d_projected,
-        qkv_scatter.received,
-        up_scatter.received,
-    )
-    qkv_scatter.received, up_scatter.received = arrived
+    d_hidden_one, d_projected, qkv_scatter.received = tie(
+        d_hidden_one, d_projected, qkv_scatter.received
+    )
     qkv_scatter.second()
-    up_sum = ReplicaSum(up_scatter.result(), replicas)
     column_sums = jnp.sum(d_projected.astype(jnp.float32), axis=0)
     d_shift_one = jnp.sum(d_hidden_one, axis=0)
     d_scale_one = jnp.sum(d_hidden_one * normed_one, axis=0)
@@ -689,13 +684,14 @@
     sums = [d_shift_one, d_scale_one, d_gate_one, d_shift_two, d_scale_two, d_gate_two]
     ada_width = 6 * width
     small_sums = jnp.concatenate(sums + list(bias_grads))
-    qkv_scatter.received, out_scatter.received = tie(
-        qkv_scatter.received, out_scatter.received
-    )
+    qkv_scatter.received, out_scatter.received, up_scatter.received = tie(
+        qkv_scatter.received, out_scatter.received, up_scatter.received
+    )
+    up_shard = up_scatter.result().astype(jnp.bfloat16)
     qkv_scatter.third()
     qkv_shard = qkv_scatter.result()
-    qkv_shard, latent_grad, block_out, small_sums, *up_sum.received = tie(
-        qkv_shard, latent_grad.astype(jnp.bfloat16), block_out, small_sums, *up_sum.received
+    qkv_shard, latent_grad, block_out, small_sums = tie(
+        qkv_shard, latent_grad.astype(jnp.bfloat16), block_out, small_sums
     )
     late_sum = ReplicaSum(
         jnp.concatenate([out_scatter.result(), qkv_shard], axis=1), replicas
@@ -703,10 +699,10 @@
     latent_grad = swap_halves(latent_grad[None])
     block_out = swap_halves(block_out[None])
     sums_all = gather_group(small_sums)
-    up_sum.second()
-    down_total, sums_all, latent_grad, block_out, *late_sum.received = tie(
-        down_total, sums_all, latent_grad, block_out, *late_sum.received
-    )
+    down_total, up_shard, sums_all, latent_grad, block_out, *late_sum.received = tie(
+        down_total, up_shard, sums_all, latent_grad, block_out, *late_sum.received
+    )
+    up_total = lax.psum(up_shard, "rep")
     late_sum.second()
 
     d_group = sums_all[:, :ada_width].reshape(2, 2, 2, ada_width).sum(1).reshape(4, ada_width)
@@ -734,8 +730,6 @@
     )
     packed_all = gather_replicas(packed, replicas)
     packed_all, *late_sum.received = tie(packed_all, *late_sum.received)
-    late_sum.received[0], *up_sum.received = tie(late_sum.received[0], *up_sum.received)
-    up_total = up_sum.result()
     late_total = late_sum.result()
     out_total, qkv_total = late_total[:, :width], late_total[:, width:]
 

time: 606 us -> 613 us (1.012)
  starting transfers between devices: 61.5 us -> 54.7 us
    psum x0 -> x1, waiting for transfers between devices: none -> 19.4 us  [per_device(): up_total = lax.psum(up_shard, 'rep')]
    ppermute x12 -> x6, waiting for transfers between devices: 42.7 us -> 32.9 us  [send(): return lax.ppermute(values, 'rep', pairs)]
  transfers between devices with their start and end apart: 53 -> 48, of which waited for: 19 -> 20; matrix products, arithmetic and copies ran while one was open for 15% -> 17% of each run, Pallas kernels for 15% -> 15%
where the time goes in v13:
time: 613 us; the launch traced here: 604 us
  waiting for transfers between devices  258 us (42%)
  Pallas kernels  153 us (25%)
  other arithmetic  66.1 us (11%)
  starting transfers between devices  54.7 us (9%)
  local copies, waits for them, and re-layouts  39.6 us (6%)
  between operations  15.9 us (3%)
  matrix products  15.7 us (3%)
    ppermute x30, waiting for transfers between devices, permute(): return lax.ppermute(values, GROUP, pairs_by(rule))  149 us
    pallas_call x2, Pallas kernels, attend_back(): pl.pallas_call(functools.partial(attend_back_kernel, heads[0], low), grid...  48.4 us
    pallas_call x1, Pallas kernels, mlp(): pl.pallas_call(mlp_kernel, grid=(units // block,), out_shape=(jax.ShapeDt...  47.7 us
    ppermute x4, waiting for transfers between devices, swap_halves(): received = lax.ppermute(values, GROUP, pairs)  45.4 us
    ppermute x6, waiting for transfers between devices, send(): return lax.ppermute(values, 'rep', pairs)  32.9 us
    ppermute x30, starting transfers between devices, permute(): return lax.ppermute(values, GROUP, pairs_by(rule))  32.3 us
    pallas_call x2, Pallas kernels, product_back(): pl.pallas_call(product_back_kernel, grid=(columns // block,), out_shape=(...  27 us
    pallas_call x1, Pallas kernels, attend(): pl.pallas_call(functools.partial(attend_kernel, heads[0], low), grid=(len...  26.9 us
  transfers between devices with their start and end apart: 48, of which 20 were waited for; matrix products, arithmetic and copies ran while one was open for 17% of the time, Pallas kernels for 15%

profile of v13, /device:TPU:9, one launch (start us, length us, event | category | flops | bytes accessed | tf_op | source)
XLA Modules:
  0.0 603.6 jit_solution(5943157664740414502)
XLA Ops:
  12.3 1.9 collective-permute-start.2
  18.3 2.0 collective-permute-start
  20.8 43.8 %collective-permute-done.3 = bf16[4,2432]{1,0:T(4,128)(2,1)S(1)} collective-permute-done((bf16[4,2432]{1,0:T(4,128)(2,1)S(1)}, bf16[4,2432]{1,0:T(4,128)(2,1)S(1)}, u32[]{:S(2)}, u32[]{:S(2)}) %collective-permute-start.3) | collective-permute-done | bytes 19488 | tf_op jit(solution)/shard_map/ppermute | solution.py:62
  65.3 2.2 collective-permute-start.4
  67.5 3.1 collective-permute-done.4
  72.5 35.0 %collective-permute-done.5 = f32[1,6912]{1,0:T(1,128)S(1)} collective-permute-done((f32[1,6912]{1,0:T(1,128)S(1)}, f32[1,6912]{1,0:T(1,128)S(1)}, u32[]{:S(2)}, u32[]{:S(2)}) %collective-permute-start.5) | collective-permute-done | bytes 27680 | tf_op jit(solution)/shard_map/ppermute | solution.py:62
  109.5 7.4 %collective-permute-start.13 = (bf16[144,4608]{1,0:T(8,128)(2,1)S(1)}, bf16[144,4608]{1,0:T(8,128)(2,1)S(1)}, u32[]{:S(2)}, u32[]{:S(2)}) collective-permute-start(bf16[144,4608]{1,0:T(8,128)(2,1)S(1)} %collective-permute-done.9.refs_3_), channel_id=1, source_target_pairs={{0,2},{1,3},{2,0},{3,1},{4,6},{5,7},{6,4},{7,5},{8,10},{9,11},{10,... | collective-permute-start | bytes 3981320 | tf_op jit(solution)/shard_map/ppermute | solution.py:62
  119.7 3.5 shard_map.237
  123.2 5.1 add_convert_fusion.2
  131.1 3.4 collective-permute-start.15
  136.1 22.8 %collective-permute-done.15 = bf16[1,512,1152]{2,1,0:T(8,128)(2,1)} collective-permute-done((bf16[1,512,1152]{2,1,0:T(8,128)(2,1)S(1)}, bf16[1,512,1152]{2,1,0:T(8,128)(2,1)}, u32[]{:S(2)}, u32[]{:S(2)}) %collective-permute-start.15) | collective-permute-done | bytes 1179680 | tf_op jit(solution)/shard_map/ppermute | solution.py:68
  158.9 3.5 convert_reduce_fusion.2
  163.8 26.9 %shard_map.238 = (bf16[512,1152]{1,0:T(8,128)(2,1)S(1)}, f32[512,128]{1,0:T(8,128)S(1)}) custom-call(bf16[512,1152]{1,0:T(8,128)(2,1)S(1)} %slice.226.query_ref, bf16[512,2304]{1,0:T(8,128)(2,1)} %slice.227.own_ref, bf16[512,2304]{1,0:T(8,128)(2,1)} %collective-permute-done.14.other_ref), custom_call_target="tpu_custom_call" | custom-call | flops 1048576 | bytes 1048576 | tf_op jit(solution)/shard_map/pallas_call | solution.py:303
  190.7 3.3 fusion.46
  196.8 47.7 %shard_map.239 = (f32[512,1152]{1,0:T(8,128)}, f32[512,1152]{1,0:T(8,128)}, bf16[4,144,4608]{2,1,0:T(8,128)(2,1)}, bf16[4,144,4608]{2,1,0:T(8,128)(2,1)}, bf16[4608,1152]{1,0:T(8,128)(2,1)}, /*index=5*/f32[1,4608]{1,0:T(1,128)}) custom-call(bf16[512,1152]{1,0:T(8,128)(2,1)} %add_convert_fusion.4.hidden_ref, ...), custom_call_target="tpu_custom_call" | custom-call | flops 1048576 | bytes 1048576 | tf_op jit(solution)/shard_map/pallas_call | solution.py:513
  245.9 3.5 multiply_reduce_fusion
  249.6 7.1 %fusion.22 = (f32[1152]{0:T(1024)S(1)}, bf16[512,1152]{1,0:T(8,128)(2,1)}, f32[1152]{0:T(1024)S(1)}, bf16[512,1152]{1,0:T(8,128)(2,1)}, f32[512,1152]{1,0:T(8,128)}) fusion(bf16[1,512,1152]{2,1,0:T(8,128)(2,1)S(1)} %get-tuple-element.145, f32[512,1152]{1,0:T(8,128)} %get-tuple-element.106, f32[1152]{0:T(1024)S(1)} %reshape.147, f32[]{:T(128)} %bitcast.10, ...), kind=kLoop, calls=%fused_computation.44 | loop fusion | flops 12384000 | bytes 13011972 | tf_op jit(solution)/shard_map/reduce_sum | solution.py:632
  256.8 9.0 %shard_map.240 = (f32[512,1152]{1,0:T(8,128)}, bf16[4,144,1152]{2,1,0:T(8,128)(2,1)}, bf16[4,144,1152]{2,1,0:T(8,128)(2,1)}) custom-call(bf16[512,1152]{1,0:T(8,128)(2,1)S(1)} %copy-done.8, bf16[512,1152]{1,0:T(8,128)(2,1)} %get-tuple-element.164.upstream_ref, bf16[1152,1152]{1,0:T(8,128)(2,1)} %copy-done.5), custom_call_target="tpu_custom_call" | custom-call | flops 1048576 | bytes 1048576 | tf_op jit(solution)/shard_map/pallas_call | solution.py:449
  265.8 2.9 convert_element_type.227.upstream_ref
  269.3 3.8 add_convert_fusion
  275.5 24.4 %shard_map.241 = (bf16[512,640]{1,0:T(8,128)(2,1)}, f32[2,512,640]{2,1,0:T(8,128)}, bf16[2,512,640]{2,1,0:T(8,128)(2,1)}) custom-call(bf16[512,1152]{1,0:T(8,128)(2,1)} %copy-done.1, bf16[512,2304]{1,0:T(8,128)(2,1)} %slice.227.own_ref, bf16[512,2304]{1,0:T(8,128)(2,1)} %collective-permute-done.14.other_ref, ...), custom_call_target="tpu_custom_call" | custom-call | flops 1048576 | bytes 1048576 | tf_op jit(solution)/shard_map/pallas_call | solution.py:375
  299.8 24.0 %shard_map.242 = (bf16[512,640]{1,0:T(8,128)(2,1)}, f32[2,512,640]{2,1,0:T(8,128)}, bf16[2,512,640]{2,1,0:T(8,128)(2,1)}) custom-call(bf16[512,1152]{1,0:T(8,128)(2,1)} %copy-done.1, bf16[512,2304]{1,0:T(8,128)(2,1)} %slice.227.own_ref, bf16[512,2304]{1,0:T(8,128)(2,1)} %collective-permute-done.14.other_ref, ...), custom_call_target="tpu_custom_call" | custom-call | flops 1048576 | bytes 1048576 | tf_op jit(solution)/shard_map/pallas_call | solution.py:375
  333.1 20.3 %collective-permute-done.19 = bf16[2,144,1152]{2,1,0:T(8,128)(2,1)S(1)} collective-permute-done((bf16[2,144,1152]{2,1,0:T(8,128)(2,1)S(1)}, bf16[2,144,1152]{2,1,0:T(8,128)(2,1)S(1)}, u32[]{:S(2)}, u32[]{:S(2)}) %collective-permute-start.19) | collective-permute-done | bytes 663584 | tf_op jit(solution)/shard_map/ppermute | solution.py:62
  355.1 2.5 fusion
  358.0 3.9 convert_add_fusion
  361.9 2.3 copy-done.17
  366.0 18.0 %shard_map.243 = (f32[512,1152]{1,0:T(8,128)}, bf16[4,144,3456]{2,1,0:T(8,128)(2,1)}, bf16[4,144,3456]{2,1,0:T(8,128)(2,1)}) custom-call(bf16[512,1152]{1,0:T(8,128)(2,1)S(1)} %copy-done.4, bf16[512,3456]{1,0:T(8,128)(2,1)} %copy-done.15, bf16[1152,3456]{1,0:T(8,128)(2,1)} %copy-done.2), custom_call_target="tpu_custom_call" | custom-call | flops 1048576 | bytes 1048576 | tf_op jit(solution)/shard_map/pallas_call | solution.py:449
  386.1 5.2 collective-permute-done.21
  391.2 4.5 add_convert_fusion.1
  399.6 2.2 multiply_reduce_fusion.1
  402.6 7.8 %collective-permute-done.23 = bf16[144,1152]{1,0:T(8,128)(2,1)} collective-permute-done((bf16[144,1152]{1,0:T(8,128)(2,1)}, bf16[144,1152]{1,0:T(8,128)(2,1)}, u32[]{:S(2)}, u32[]{:S(2)}) %collective-permute-start.23) | collective-permute-done | bytes 331808 | tf_op jit(solution)/shard_map/ppermute | solution.py:62
  410.5 16.8 %collective-permute-done.22 = bf16[2,144,3456]{2,1,0:T(8,128)(2,1)S(1)} collective-permute-done((bf16[2,144,3456]{2,1,0:T(8,128)(2,1)S(1)}, bf16[2,144,3456]{2,1,0:T(8,128)(2,1)S(1)}, u32[]{:S(2)}, u32[]{:S(2)}) %collective-permute-start.22) | collective-permute-done | bytes 1990688 | tf_op jit(solution)/shard_map/ppermute | solution.py:62
  427.7 2.0 copy-done.18
  433.0 11.5 %collective-permute-done.25 = bf16[144,3456]{1,0:T(8,128)(2,1)} collective-permute-done((bf16[144,3456]{1,0:T(8,128)(2,1)}, bf16[144,3456]{1,0:T(8,128)(2,1)}, u32[]{:S(2)}, u32[]{:S(2)}) %collective-permute-start.25) | collective-permute-done | bytes 995360 | tf_op jit(solution)/shard_map/ppermute | solution.py:62
  444.5 2.0 fusion.23
  458.1 4.1 collective-permute-start.30
  462.2 2.5 collective-permute-start.29
  465.0 11.1 %collective-permute-done.30 = bf16[1,512,1152]{2,1,0:T(8,128)(2,1)S(1)} collective-permute-done((bf16[1,512,1152]{2,1,0:T(8,128)(2,1)S(1)}, bf16[1,512,1152]{2,1,0:T(8,128)(2,1)S(1)}, u32[]{:S(2)}, u32[]{:S(2)}) %collective-permute-start.30) | collective-permute-done | bytes 1179680 | tf_op jit(solution)/shard_map/ppermute | solution.py:68
  477.2 11.5 %collective-permute-done.29 = bf16[1,512,1152]{2,1,0:T(8,128)(2,1)S(1)} collective-permute-done((bf16[1,512,1152]{2,1,0:T(8,128)(2,1)S(1)}, bf16[1,512,1152]{2,1,0:T(8,128)(2,1)S(1)}, u32[]{:S(2)}, u32[]{:S(2)}) %collective-permute-start.29) | collective-permute-done | bytes 1179680 | tf_op jit(solution)/shard_map/ppermute | solution.py:68
  493.7 2.4 collective-permute-done.34
  498.8 3.0 collective-permute-start.38
  507.8 3.0 convert_element_type.270
  516.8 10.3 %collective-permute-done.39 = f32[29376]{0:T(1024)} collective-permute-done((f32[29376]{0:T(1024)}, f32[29376]{0:T(1024)}, u32[]{:S(2)}, u32[]{:S(2)}) %collective-permute-start.39) | collective-permute-done | bytes 117536 | tf_op jit(solution)/shard_map/ppermute | solution.py:90
  530.1 28.6 %collective-permute-done.41 = bf16[144,1152]{1,0:T(8,128)(2,1)S(1)} collective-permute-done((bf16[144,1152]{1,0:T(8,128)(2,1)S(1)}, bf16[144,1152]{1,0:T(8,128)(2,1)S(1)}, u32[]{:S(2)}, u32[]{:S(2)}) %collective-permute-start.41) | collective-permute-done | bytes 331808 | tf_op jit(solution)/shard_map/ppermute | solution.py:215
  558.7 3.6 collective-permute-done.42
  569.2 5.2 fusion.50
  574.4 19.4 %all-reduce.5.cloned.1.call-done = bf16[144,4608]{1,0:T(8,128)(2,1)} async-done(((bf16[144,4608]{1,0:T(8,128)(2,1)}), bf16[144,4608]{1,0:T(8,128)(2,1)}) %all-reduce.5.cloned.1.call-update) | async-done | bytes 1327120 | tf_op jit(solution)/shard_map/psum | solution.py:705
  593.8 3.1 convert_element_type.269
  (314 shorter events, 94.7 us)
Async XLA Ops:
  7.2 189.6 %all-gather.3.cloned.1.call-start = ((), (), s32[]{:S(2)}) async-start(), calls=%async_computation.1 | async-start | bytes 11943936 | tf_op jit(solution)/shard_map/all_gather | solution.py:568
  8.0 188.8 %all-gather.5.cloned.1.call-start = ((), (), s32[]{:S(2)}) async-start(), calls=%async_computation.2 | async-start | bytes 11943936 | tf_op jit(solution)/shard_map/all_gather | solution.py:571
  8.7 356.7 %reduce-scatter.2.cloned.1.call-start = ((), (), s32[]{:S(2)}) async-start(), calls=%async_computation.3 | async-start | bytes 11943936 | tf_op jit(solution)/shard_map/reduce_scatter | solution.py:629
  9.6 2.6 collective-permute-start.1
  12.3 8.0 %collective-permute-start.2 = (bf16[2,2432]{1,0:T(2,128)(2,1)S(1)}, bf16[2,2432]{1,0:T(2,128)(2,1)S(1)}, u32[]{:S(2)}, u32[]{:S(2)}) collective-permute-start(bf16[2,2432]{1,0:T(2,128)(2,1)S(1)} %broadcast_select_fusion.7), channel_id=1, source_target_pairs={{0,2},{1,3},{2,0},{3,1},{4,6},{5,7},{6,4},{7,5},{8,10},{9,11},{10,... | collective-permute-start | bytes 29192 | tf_op jit(solution)/shard_map/ppermute | solution.py:62
  15.2 55.8 %collective-permute-start.7 = (bf16[144,4608]{1,0:T(8,128)(2,1)S(1)}, bf16[144,4608]{1,0:T(8,128)(2,1)}, u32[]{:S(2)}, u32[]{:S(2)}) collective-permute-start(bf16[144,4608]{1,0:T(8,128)(2,1)S(1)} %constant_dynamic-update-slice_fusion.refs_0_), channel_id=1, source_target_pairs={{0,4},{1,5},{2,3},{3,2},{4,0},{5,1},{6,7},{7,6},{8,12},{9,13},{10,... | collective-permute-start | bytes 3981320 | tf_op jit(solution)/shard_map/ppermute | solution.py:62
  16.5 92.7 %collective-permute-start.8 = (bf16[144,4608]{1,0:T(8,128)(2,1)S(1)}, bf16[144,4608]{1,0:T(8,128)(2,1)}, u32[]{:S(2)}, u32[]{:S(2)}) collective-permute-start(bf16[144,4608]{1,0:T(8,128)(2,1)S(1)} %constant_dynamic-update-slice_fusion.refs_0_), channel_id=1, source_target_pairs={{0,1},{1,0},{2,6},{3,7},{4,5},{5,4},{6,2},{7,3},{8,9},{9,8},{10,14... | collective-permute-start | bytes 3981320 | tf_op jit(solution)/shard_map/ppermute | solution.py:62
  17.7 101.9 %collective-permute-start.10 = (bf16[144,4608]{1,0:T(8,128)(2,1)S(1)}, bf16[144,4608]{1,0:T(8,128)(2,1)}, u32[]{:S(2)}, u32[]{:S(2)}) collective-permute-start(bf16[144,4608]{1,0:T(8,128)(2,1)S(1)} %constant_dynamic-update-slice_fusion.refs_0_), channel_id=1, source_target_pairs={{0,2},{1,3},{2,0},{3,1},{4,6},{5,7},{6,4},{7,5},{8,10},{9,11},{10,... | collective-permute-start | bytes 3981320 | tf_op jit(solution)/shard_map/ppermute | solution.py:62
  18.3 98.6 %collective-permute-start = (bf16[1,512,1152]{2,1,0:T(8,128)(2,1)}, bf16[1,512,1152]{2,1,0:T(8,128)(2,1)}, u32[]{:S(2)}, u32[]{:S(2)}) collective-permute-start(bf16[1,512,1152]{2,1,0:T(8,128)(2,1)} %param.14), channel_id=1, source_target_pairs={{1,2},{2,1},{5,6},{6,5},{9,10},{10,9},{13,14},{14,13},{17,18},{18,... | collective-permute-start | bytes 3538952 | tf_op jit(solution)/shard_map/ppermute | solution.py:68
  20.3 44.3 %collective-permute-start.3 = (bf16[4,2432]{1,0:T(4,128)(2,1)S(1)}, bf16[4,2432]{1,0:T(4,128)(2,1)S(1)}, u32[]{:S(2)}, u32[]{:S(2)}) collective-permute-start(bf16[4,2432]{1,0:T(4,128)(2,1)S(1)} %maximum_select_fusion.4), channel_id=1, source_target_pairs={{0,4},{1,5},{2,6},{3,7},{4,0},{5,1},{6,2},{7,3},{8,12},{9,13},{10,... | collective-permute-start | bytes 58376 | tf_op jit(solution)/shard_map/ppermute | solution.py:62
  65.3 5.3 collective-permute-start.4
  70.7 36.8 %collective-permute-start.5 = (f32[1,6912]{1,0:T(1,128)S(1)}, f32[1,6912]{1,0:T(1,128)S(1)}, u32[]{:S(2)}, u32[]{:S(2)}) collective-permute-start(f32[1,6912]{1,0:T(1,128)S(1)} %broadcast_select_fusion.5), channel_id=1, source_target_pairs={{0,1},{1,0},{2,3},{3,2},{4,5},{5,4},{6,7},{7,6},{8,9},{9,8},{10,11... | collective-permute-start | bytes 82952 | tf_op jit(solution)/shard_map/ppermute | solution.py:62
  70.9 38.6 %collective-permute-start.9 = (bf16[144,4608]{1,0:T(8,128)(2,1)}, bf16[144,4608]{1,0:T(8,128)(2,1)S(1)}, u32[]{:S(2)}, u32[]{:S(2)}) collective-permute-start(bf16[144,4608]{1,0:T(8,128)(2,1)} %collective-permute-done.7.refs_1_), channel_id=1, source_target_pairs={{0,1},{1,0},{2,6},{3,7},{4,5},{5,4},{6,2},{7,3},{8,9},{9,8},{10,14... | collective-permute-start | bytes 3981320 | tf_op jit(solution)/shard_map/ppermute | solution.py:62
  107.6 1.3 collective-permute-start.6
  108.9 10.7 %collective-permute-start.11 = (bf16[144,4608]{1,0:T(8,128)(2,1)}, bf16[144,4608]{1,0:T(8,128)(2,1)S(1)}, u32[]{:S(2)}, u32[]{:S(2)}) collective-permute-start(bf16[144,4608]{1,0:T(8,128)(2,1)} %collective-permute-done.7.refs_1_), channel_id=1, source_target_pairs={{0,2},{1,3},{2,0},{3,1},{4,6},{5,7},{6,4},{7,5},{8,10},{9,11},{10,... | collective-permute-start | bytes 3981320 | tf_op jit(solution)/shard_map/ppermute | solution.py:62
  109.2 10.4 %collective-permute-start.12 = (bf16[144,4608]{1,0:T(8,128)(2,1)}, bf16[144,4608]{1,0:T(8,128)(2,1)S(1)}, u32[]{:S(2)}, u32[]{:S(2)}) collective-permute-start(bf16[144,4608]{1,0:T(8,128)(2,1)} %collective-permute-done.8.refs_2_), channel_id=1, source_target_pairs={{0,2},{1,3},{2,0},{3,1},{4,6},{5,7},{6,4},{7,5},{8,10},{9,11},{10,... | collective-permute-start | bytes 3981320 | tf_op jit(solution)/shard_map/ppermute | solution.py:62
  109.5 10.2 %collective-permute-start.13 = (bf16[144,4608]{1,0:T(8,128)(2,1)S(1)}, bf16[144,4608]{1,0:T(8,128)(2,1)S(1)}, u32[]{:S(2)}, u32[]{:S(2)}) collective-permute-start(bf16[144,4608]{1,0:T(8,128)(2,1)S(1)} %collective-permute-done.9.refs_3_), channel_id=1, source_target_pairs={{0,2},{1,3},{2,0},{3,1},{4,6},{5,7},{6,4},{7,5},{8,10},{9,11},{10,... | collective-permute-start | bytes 3981320 | tf_op jit(solution)/shard_map/ppermute | solution.py:62
  130.9 32.9 %collective-permute-start.14 = (bf16[512,2304]{1,0:T(8,128)(2,1)}, bf16[512,2304]{1,0:T(8,128)(2,1)}, u32[]{:S(2)}, u32[]{:S(2)}) collective-permute-start(bf16[512,2304]{1,0:T(8,128)(2,1)} %slice.227.own_ref), channel_id=1, source_target_pairs={{0,2},{1,3},{2,0},{3,1},{4,6},{5,7},{6,4},{7,5},{8,10},{9,11},{10,... | collective-permute-start | bytes 7077896 | tf_op jit(solution)/shard_map/ppermute | solution.py:62
  131.1 27.7 %collective-permute-start.15 = (bf16[1,512,1152]{2,1,0:T(8,128)(2,1)S(1)}, bf16[1,512,1152]{2,1,0:T(8,128)(2,1)}, u32[]{:S(2)}, u32[]{:S(2)}) collective-permute-start(bf16[1,512,1152]{2,1,0:T(8,128)(2,1)S(1)} %copy-done.33), channel_id=1, source_target_pairs={{1,2},{2,1},{5,6},{6,5},{9,10},{10,9},{13,14},{14,13},{17,18},{18,... | collective-permute-start | bytes 3538952 | tf_op jit(solution)/shard_map/ppermute | solution.py:68
  244.5 24.7 %collective-permute-start.16 = (bf16[4,144,4608]{2,1,0:T(8,128)(2,1)}, bf16[4,144,4608]{2,1,0:T(8,128)(2,1)}, u32[]{:S(2)}, u32[]{:S(2)}) collective-permute-start(bf16[4,144,4608]{2,1,0:T(8,128)(2,1)} %get-tuple-element.75), channel_id=1, source_target_pairs={{0,2},{1,3},{2,0},{3,1},{4,6},{5,7},{6,4},{7,5},{8,10},{9,11},{10,... | collective-permute-start | bytes 15925256 | tf_op jit(solution)/shard_map/ppermute | solution.py:62
  244.6 245.2 %all-reduce.3.cloned.1.call-start = ((), (), s32[]{:S(2)}) async-start(), calls=%async_computation.4 | async-start | bytes 2654208 | tf_op jit(solution)/shard_map/psum | solution.py:667
  268.7 31.2 %collective-permute-start.17 = (bf16[4,144,1152]{2,1,0:T(8,128)(2,1)}, bf16[4,144,1152]{2,1,0:T(8,128)(2,1)}, u32[]{:S(2)}, u32[]{:S(2)}) collective-permute-start(bf16[4,144,1152]{2,1,0:T(8,128)(2,1)} %get-tuple-element.79), channel_id=1, source_target_pairs={{0,2},{1,3},{2,0},{3,1},{4,6},{5,7},{6,4},{7,5},{8,10},{9,11},{10,... | collective-permute-start | bytes 3981320 | tf_op jit(solution)/shard_map/ppermute | solution.py:62
  273.8 79.6 %collective-permute-start.18 = (bf16[2,144,4608]{2,1,0:T(8,128)(2,1)S(1)}, bf16[2,144,4608]{2,1,0:T(8,128)(2,1)}, u32[]{:S(2)}, u32[]{:S(2)}) collective-permute-start(bf16[2,144,4608]{2,1,0:T(8,128)(2,1)S(1)} %pad_maximum_fusion.1), channel_id=1, source_target_pairs={{0,4},{1,5},{2,3},{3,2},{4,0},{5,1},{6,7},{7,6},{8,12},{9,13},{10,... | collective-permute-start | bytes 7962632 | tf_op jit(solution)/shard_map/ppermute | solution.py:62
  327.4 27.8 %collective-permute-start.20 = (bf16[2,512,1152]{2,1,0:T(8,128)(2,1)S(1)}, bf16[2,512,1152]{2,1,0:T(8,128)(2,1)}, u32[]{:S(2)}, u32[]{:S(2)}) collective-permute-start(bf16[2,512,1152]{2,1,0:T(8,128)(2,1)S(1)} %pad_maximum_fusion.2), channel_id=1, source_target_pairs={{0,2},{1,3},{2,0},{3,1},{4,6},{5,7},{6,4},{7,5},{8,10},{9,11},{10,... | collective-permute-start | bytes 7077896 | tf_op jit(solution)/shard_map/ppermute | solution.py:62
  330.4 23.0 %collective-permute-start.19 = (bf16[2,144,1152]{2,1,0:T(8,128)(2,1)S(1)}, bf16[2,144,1152]{2,1,0:T(8,128)(2,1)S(1)}, u32[]{:S(2)}, u32[]{:S(2)}) collective-permute-start(bf16[2,144,1152]{2,1,0:T(8,128)(2,1)S(1)} %pad_maximum_fusion.4), channel_id=1, source_target_pairs={{0,4},{1,5},{2,3},{3,2},{4,0},{5,1},{6,7},{7,6},{8,12},{9,13},{10,... | collective-permute-start | bytes 1990664 | tf_op jit(solution)/shard_map/ppermute | solution.py:62
  383.9 7.3 %collective-permute-start.21 = (bf16[4,144,3456]{2,1,0:T(8,128)(2,1)}, bf16[4,144,3456]{2,1,0:T(8,128)(2,1)}, u32[]{:S(2)}, u32[]{:S(2)}) collective-permute-start(bf16[4,144,3456]{2,1,0:T(8,128)(2,1)} %get-tuple-element.99), channel_id=1, source_target_pairs={{0,2},{1,3},{2,0},{3,1},{4,6},{5,7},{6,4},{7,5},{8,10},{9,11},{10,... | collective-permute-start | bytes 11943944 | tf_op jit(solution)/shard_map/ppermute | solution.py:62
  384.5 26.0 %collective-permute-start.24 = (bf16[144,4608]{1,0:T(8,128)(2,1)}, bf16[144,4608]{1,0:T(8,128)(2,1)S(1)}, u32[]{:S(2)}, u32[]{:S(2)}) collective-permute-start(bf16[144,4608]{1,0:T(8,128)(2,1)} %fusion.24), channel_id=1, source_target_pairs={{0,1},{1,0},{2,6},{3,7},{4,5},{5,4},{6,2},{7,3},{8,9},{9,8},{10,14... | collective-permute-start | bytes 3981320 | tf_op jit(solution)/shard_map/ppermute | solution.py:62
  385.2 25.3 %collective-permute-start.23 = (bf16[144,1152]{1,0:T(8,128)(2,1)}, bf16[144,1152]{1,0:T(8,128)(2,1)}, u32[]{:S(2)}, u32[]{:S(2)}) collective-permute-start(bf16[144,1152]{1,0:T(8,128)(2,1)} %fusion.34), channel_id=1, source_target_pairs={{0,1},{1,0},{2,6},{3,7},{4,5},{5,4},{6,2},{7,3},{8,9},{9,8},{10,14... | collective-permute-start | bytes 995336 | tf_op jit(solution)/shard_map/ppermute | solution.py:62
  386.0 207.8 %all-reduce.5.cloned.1.call-start = ((), (), s32[]{:S(2)}) async-start(), calls=%async_computation.5 | async-start | bytes 2654208 | tf_op jit(solution)/shard_map/psum | solution.py:705
  396.5 30.8 %collective-permute-start.22 = (bf16[2,144,3456]{2,1,0:T(8,128)(2,1)S(1)}, bf16[2,144,3456]{2,1,0:T(8,128)(2,1)S(1)}, u32[]{:S(2)}, u32[]{:S(2)}) collective-permute-start(bf16[2,144,3456]{2,1,0:T(8,128)(2,1)S(1)} %pad_maximum_fusion.3), channel_id=1, source_target_pairs={{0,4},{1,5},{2,3},{3,2},{4,0},{5,1},{6,7},{7,6},{8,12},{9,13},{10,... | collective-permute-start | bytes 5971976 | tf_op jit(solution)/shard_map/ppermute | solution.py:62
  430.8 13.7 %collective-permute-start.25 = (bf16[144,3456]{1,0:T(8,128)(2,1)}, bf16[144,3456]{1,0:T(8,128)(2,1)}, u32[]{:S(2)}, u32[]{:S(2)}) collective-permute-start(bf16[144,3456]{1,0:T(8,128)(2,1)} %fusion.27), channel_id=1, source_target_pairs={{0,1},{1,0},{2,6},{3,7},{4,5},{5,4},{6,2},{7,3},{8,9},{9,8},{10,14... | collective-permute-start | bytes 2985992 | tf_op jit(solution)/shard_map/ppermute | solution.py:62
  446.6 3.2 collective-permute-start.26
  449.9 2.7 collective-permute-start.27
  452.9 9.3 %collective-permute-start.28 = (f32[4,16128]{1,0:T(4,128)S(1)}, f32[4,16128]{1,0:T(4,128)S(1)}, u32[]{:S(2)}, u32[]{:S(2)}) collective-permute-start(f32[4,16128]{1,0:T(4,128)S(1)} %maximum_select_fusion.1), channel_id=1, source_target_pairs={{0,4},{1,5},{2,6},{3,7},{4,0},{5,1},{6,2},{7,3},{8,12},{9,13},{10,... | collective-permute-start | bytes 774152 | tf_op jit(solution)/shard_map/ppermute | solution.py:62
  454.5 35.3 %collective-permute-start.31 = (bf16[144,1152]{1,0:T(8,128)(2,1)}, bf16[144,1152]{1,0:T(8,128)(2,1)}, u32[]{:S(2)}, u32[]{:S(2)}) collective-permute-start(bf16[144,1152]{1,0:T(8,128)(2,1)} %get-tuple-element.170), channel_id=1, source_target_pairs={{0,8},{8,16},{16,24},{24,0},{1,9},{9,17},{17,25},{25,1},{2,10},{10... | collective-permute-start | bytes 995336 | tf_op jit(solution)/shard_map/ppermute | solution.py:215
  455.7 34.1 %collective-permute-start.32 = (bf16[144,1152]{1,0:T(8,128)(2,1)}, bf16[144,1152]{1,0:T(8,128)(2,1)}, u32[]{:S(2)}, u32[]{:S(2)}) collective-permute-start(bf16[144,1152]{1,0:T(8,128)(2,1)} %get-tuple-element.169), channel_id=1, source_target_pairs={{0,16},{8,24},{16,0},{24,8},{1,17},{9,25},{17,1},{25,9},{2,18},{10... | collective-permute-start | bytes 995336 | tf_op jit(solution)/shard_map/ppermute | solution.py:215
  456.9 33.0 %collective-permute-start.33 = (bf16[144,1152]{1,0:T(8,128)(2,1)S(1)}, bf16[144,1152]{1,0:T(8,128)(2,1)}, u32[]{:S(2)}, u32[]{:S(2)}) collective-permute-start(bf16[144,1152]{1,0:T(8,128)(2,1)S(1)} %get-tuple-element.168), channel_id=1, source_target_pairs={{0,24},{8,0},{16,8},{24,16},{1,25},{9,1},{17,9},{25,17},{2,26},{10... | collective-permute-start | bytes 995336 | tf_op jit(solution)/shard_map/ppermute | solution.py:215
  458.1 17.9 %collective-permute-start.30 = (bf16[1,512,1152]{2,1,0:T(8,128)(2,1)S(1)}, bf16[1,512,1152]{2,1,0:T(8,128)(2,1)S(1)}, u32[]{:S(2)}, u32[]{:S(2)}) collective-permute-start(bf16[1,512,1152]{2,1,0:T(8,128)(2,1)S(1)} %bitcast.106), channel_id=1, source_target_pairs={{1,2},{2,1},{5,6},{6,5},{9,10},{10,9},{13,14},{14,13},{17,18},{18,... | collective-permute-start | bytes 3538952 | tf_op jit(solution)/shard_map/ppermute | solution.py:68
  462.2 26.5 %collective-permute-start.29 = (bf16[1,512,1152]{2,1,0:T(8,128)(2,1)S(1)}, bf16[1,512,1152]{2,1,0:T(8,128)(2,1)S(1)}, u32[]{:S(2)}, u32[]{:S(2)}) collective-permute-start(bf16[1,512,1152]{2,1,0:T(8,128)(2,1)S(1)} %bitcast.107), channel_id=1, source_target_pairs={{1,2},{2,1},{5,6},{6,5},{9,10},{10,9},{13,14},{14,13},{17,18},{18,... | collective-permute-start | bytes 3538952 | tf_op jit(solution)/shard_map/ppermute | solution.py:68
  493.6 2.5 collective-permute-start.34
  496.1 5.8 collective-permute-start.35
  498.6 16.2 %collective-permute-start.37 = (f32[29376]{0:T(1024)}, f32[29376]{0:T(1024)}, u32[]{:S(2)}, u32[]{:S(2)}) collective-permute-start(f32[29376]{0:T(1024)} %concatenate.131), channel_id=1, source_target_pairs={{0,8},{8,16},{16,24},{24,0},{1,9},{9,17},{17,25},{25,1},{2,10},{10... | collective-permute-start | bytes 352520 | tf_op jit(solution)/shard_map/ppermute | solution.py:90
  498.8 17.0 %collective-permute-start.38 = (f32[29376]{0:T(1024)}, f32[29376]{0:T(1024)}, u32[]{:S(2)}, u32[]{:S(2)}) collective-permute-start(f32[29376]{0:T(1024)} %concatenate.131), channel_id=1, source_target_pairs={{0,16},{8,24},{16,0},{24,8},{1,17},{9,25},{17,1},{25,9},{2,18},{10... | collective-permute-start | bytes 352520 | tf_op jit(solution)/shard_map/ppermute | solution.py:90
  501.9 25.2 %collective-permute-start.39 = (f32[29376]{0:T(1024)}, f32[29376]{0:T(1024)}, u32[]{:S(2)}, u32[]{:S(2)}) collective-permute-start(f32[29376]{0:T(1024)} %concatenate.131), channel_id=1, source_target_pairs={{0,24},{8,0},{16,8},{24,16},{1,25},{9,1},{17,9},{25,17},{2,26},{10... | collective-permute-start | bytes 352520 | tf_op jit(solution)/shard_map/ppermute | solution.py:90
  501.9 10.5 %collective-permute-start.36 = (f32[4,4,144]{2,1,0:T(4,128)S(1)}, f32[4,4,144]{2,1,0:T(4,128)S(1)}, u32[]{:S(2)}, u32[]{:S(2)}) collective-permute-start(f32[4,4,144]{2,1,0:T(4,128)S(1)} %maximum_select_fusion.5), channel_id=1, source_target_pairs={{0,4},{1,5},{2,6},{3,7},{4,0},{5,1},{6,2},{7,3},{8,12},{9,13},{10,... | collective-permute-start | bytes 27656 | tf_op jit(solution)/shard_map/ppermute | solution.py:62
  506.4 23.7 %collective-permute-start.40 = (bf16[144,1152]{1,0:T(8,128)(2,1)S(1)}, bf16[144,1152]{1,0:T(8,128)(2,1)}, u32[]{:S(2)}, u32[]{:S(2)}) collective-permute-start(bf16[144,1152]{1,0:T(8,128)(2,1)S(1)} %fusion.32), channel_id=1, source_target_pairs={{0,8},{8,16},{16,24},{24,0},{1,9},{9,17},{17,25},{25,1},{2,10},{10... | collective-permute-start | bytes 995336 | tf_op jit(solution)/shard_map/ppermute | solution.py:215
  512.4 46.3 %collective-permute-start.41 = (bf16[144,1152]{1,0:T(8,128)(2,1)S(1)}, bf16[144,1152]{1,0:T(8,128)(2,1)S(1)}, u32[]{:S(2)}, u32[]{:S(2)}) collective-permute-start(bf16[144,1152]{1,0:T(8,128)(2,1)S(1)} %fusion.32), channel_id=1, source_target_pairs={{0,16},{8,24},{16,0},{24,8},{1,17},{9,25},{17,1},{25,9},{2,18},{10... | collective-permute-start | bytes 995336 | tf_op jit(solution)/shard_map/ppermute | solution.py:215
  514.8 47.5 %collective-permute-start.42 = (bf16[144,1152]{1,0:T(8,128)(2,1)S(1)}, bf16[144,1152]{1,0:T(8,128)(2,1)S(1)}, u32[]{:S(2)}, u32[]{:S(2)}) collective-permute-start(bf16[144,1152]{1,0:T(8,128)(2,1)S(1)} %fusion.32), channel_id=1, source_target_pairs={{0,24},{8,0},{16,8},{24,16},{1,25},{9,1},{17,9},{25,17},{2,26},{10... | collective-permute-start | bytes 995336 | tf_op jit(solution)/shard_map/ppermute | solution.py:215
  (47 other events, 393.2 us)
Sparse Core Ops, SparseCore 0:
  10.0 100.8 all-gather.2
  112.7 74.2 all-gather.4
  244.7 104.7 reduce-scatter.1
  386.1 60.7 all-reduce.2
  508.0 85.7 all-reduce.4
